TPU v7x, 128 devices: a whole 4x4x4 slice. The times are simulated.
128 devices in a mesh: segment: 2 (over x_lo), dp: 32 (over z, y, core), mp: 2 (over x_hi).
Axes of the slice: x: 4 (x_hi: 2, x_lo: 2; x = x_hi * 2 + x_lo), y: 4, z: 4, core: 2. Of those that a mesh axis runs over, the one named last changes fastest.
Arguments:
- segment_inputs: bfloat16 [2, 16384, 4096], P('segment', 'dp', 'mp'), may hold values from -68 to 68
- cotangent: bfloat16 [16384, 4096], P('dp', 'mp'), may hold values from -6 to 6
- report_lengths: int32 [128], P('dp'), may hold values from 64 to 128
- norm_gain: float32 [2, 4096], P('segment', 'mp'), may hold values from 0.25 to 1.75
- attn_gate: float32 [2], P('segment'), may hold values from 0.3 to 1.5
- w_query: bfloat16 [2, 4096, 1024], P('segment', 'mp', 'dp'), may hold values from -0.09375 to 0.09375
- w_out: bfloat16 [2, 1024, 4096], P('segment', 'dp', 'mp'), may hold values from -0.1875 to 0.1875
- w_key: bfloat16 [2, 1536, 1024], P('segment', None, 'mp'), may hold values from -0.15625 to 0.15625
- w_value: bfloat16 [2, 1536, 1024], P('segment', None, 'mp'), may hold values from -0.15625 to 0.15625
- tiles: bfloat16 [128, 64, 1536], P('dp')
- tile_counts: int32 [32, 4], P('dp'), may hold values from 1 to 64, 160 in all within a row
- lat_query: bfloat16 [32, 1536], replicated
- request_source: int32 [128, 6, 1], replicated, may hold values from 0 to 31; in each aligned block of 24 rows (0 to 23, 24 to 47, ..., all dimensions but the last counted through in order) at most 2 rows name the same one
- request_slide: int32 [128, 6], replicated, may hold values from 0 to 3
- cross_pattern: int32 [128, 4, 6], P('dp'), may hold values from 0 to 1, as said below
Outputs:
- grad_inputs: bfloat16 [2, 16384, 4096], P('segment', 'dp', 'mp')
- latent_grad: float32 [128, 192, 1536], P('dp', ('segment', 'mp'))
Inputs may be any that keep to these rules, and one draw needn't show every extreme that they name: `request_source`: among the 24 requests of one dp index's reports, no encoder shard is named more than 2 times, a bound that some block reaches. `cross_pattern`: every query block of every report attends to at least one slide.
All inputs are finite; a program needn't handle non-finite values.
Results may differ from a plain program's by a relative error of at most 0.022.
The roundings to bfloat16 on the way count: a program that leaves them out, or rounds other values in their place, can miss the bound.
Values may be sent and summed in bfloat16 or wider, within the bound.
No kernel may reach another device: no remote copies, remote signals or barrier semaphores. Data moves between devices by JAX's collectives and lax.ppermute only.
A program may use at most 192 MiB of HBM per device.

v0:
```python
import jax
import jax.numpy as jnp
from jax import lax
from jax.sharding import PartitionSpec as P

MODEL_WIDTH = 4096
E = 1536
HEAD = 128
LAT = 32
SPR = 6
L = 128
QBLK = 32
MICRO = 2


def from_behind(array, axis, by):
    devices = lax.axis_size(axis)
    pairs = [(i, i + by) for i in range(devices) if 0 <= i + by < devices]
    return lax.ppermute(array, axis, pairs)


def pool_slides(slides, counts, queries):
    heads = E // HEAD
    lead = slides.shape[:-2]
    slots = slides.shape[-2]
    keys = slides.reshape(lead + (slots, heads, HEAD))
    qry = queries.reshape(LAT, heads, HEAD)
    scores = jnp.einsum(
        "lhd,...thd->...hlt", qry, keys, preferred_element_type=jnp.float32
    ) * HEAD ** (-0.5)
    live = jnp.arange(slots) < counts[..., None, None, None]
    scores = jnp.where(live, scores, -1e30)
    weights = jax.nn.softmax(scores, axis=-1).astype(jnp.bfloat16)
    pooled = jnp.einsum("...hlt,...thd->...lhd", weights, keys, preferred_element_type=jnp.float32)
    return (queries.astype(jnp.float32) + pooled.reshape(lead + (LAT, E))).astype(jnp.bfloat16)


def per_device(
    segment_inputs,
    cotangent,
    report_lengths,
    norm_gain,
    attn_gate,
    w_query,
    w_out,
    w_key,
    w_value,
    tiles,
    tile_counts,
    lat_query,
    request_source,
    request_slide,
    cross_pattern,
):
    ndp = lax.axis_size("dp")
    sections = lax.axis_size("segment")
    me_dp = lax.axis_index("dp")
    me_mp = lax.axis_index("mp")
    my_section = lax.axis_index("segment")
    rep_dev = request_source.shape[0] // ndp
    wanted = rep_dev * SPR
    cap = max(2, -(-wanted // ndp))
    source = request_source[:, :, 0].reshape(ndp, wanted)
    slide_ids = request_slide.reshape(ndp, wanted)
    earlier = jnp.arange(wanted)[:, None] < jnp.arange(wanted)[None, :]
    same = source[:, :, None] == source[:, None, :]
    rank = jnp.sum(jnp.where(same & earlier[None], 1, 0), axis=1)
    match = (source[:, None, :] == me_dp) & (rank[:, None, :] == jnp.arange(cap)[None, :, None])
    slot_slide = jnp.sum(jnp.where(match, slide_ids[:, None, :], 0), axis=2)
    slot_live = jnp.any(match, axis=2)
    my_source = lax.dynamic_index_in_dim(source, me_dp, 0, keepdims=False)
    my_rank = lax.dynamic_index_in_dim(rank, me_dp, 0, keepdims=False)
    pick = my_source * cap + my_rank
    counts = tile_counts[0]
    stored = counts.shape[0]
    sent = jnp.where(slot_live[:, :, None, None], tiles[slot_slide], jnp.zeros((), jnp.bfloat16))
    slot_hot = slot_slide[:, :, None] == jnp.arange(stored)[None, None, :]
    sent_counts = jnp.sum(
        jnp.where(slot_hot & slot_live[:, :, None], counts[None, None, :], 0), axis=2
    )
    pooled = pool_slides(
        lax.all_to_all(sent, "dp", split_axis=0, concat_axis=0, tiled=True),
        lax.all_to_all(sent_counts, "dp", split_axis=0, concat_axis=0, tiled=True),
        lat_query,
    )
    latents = pooled.reshape(ndp * cap, LAT, E)[pick].reshape(wanted * LAT, E)
    key_w = w_key[0]
    value_w = w_value[0]
    keys = jnp.dot(latents, key_w, preferred_element_type=jnp.float32).astype(jnp.bfloat16)
    vals = jnp.dot(latents, value_w, preferred_element_type=jnp.float32).astype(jnp.bfloat16)
    local_width = key_w.shape[1]
    local_heads = local_width // HEAD
    report_keys = SPR * LAT
    total_keys = wanted * LAT
    key_heads = keys.reshape(rep_dev, report_keys, local_heads, HEAD)
    val_heads = vals.reshape(rep_dev, report_keys, local_heads, HEAD)
    hidden_state = segment_inputs[0]
    tokens_here = hidden_state.shape[0]
    width = hidden_state.shape[1]
    hidden_single_precision = hidden_state.astype(jnp.float32)
    squares = lax.psum(jnp.sum(hidden_single_precision * hidden_single_precision, axis=1), "mp")
    inverse_root_mean = lax.rsqrt(squares / MODEL_WIDTH + 1e-05)
    normalized_input = hidden_single_precision * inverse_root_mean[:, None]
    scale_factor = norm_gain[0]
    normalized_rows = (normalized_input * scale_factor).astype(jnp.bfloat16)
    query_rows, out_cols = (
        lax.all_gather(w_query[0], "dp", axis=1, tiled=True),
        lax.all_gather(w_out[0], "dp", axis=0, tiled=True),
    )
    queries = lax.psum(
        jnp.dot(normalized_rows, query_rows, preferred_element_type=jnp.float32), "mp"
    )
    queries_b = queries.astype(jnp.bfloat16)
    local_q = lax.dynamic_slice_in_dim(queries_b, me_mp * local_width, local_width, 1)
    query_heads = local_q.reshape(tokens_here, local_heads, HEAD)
    query_report = query_heads.reshape(rep_dev, L, local_heads, HEAD)
    scale = HEAD ** (-0.5)
    nblocks = cross_pattern.shape[1]
    pattern_wide = jnp.broadcast_to(
        cross_pattern[:, :, None, :, None], (rep_dev, nblocks, QBLK, SPR, LAT)
    )
    allowed = pattern_wide.reshape(rep_dev, L, report_keys) == 1
    scores = (
        jnp.einsum("rthd,rkhd->rthk", query_report, key_heads, preferred_element_type=jnp.float32)
        * scale
    )
    scores = jnp.where(allowed[:, :, None, :], scores, -1e30)
    probs = jax.nn.softmax(scores, axis=-1).reshape(tokens_here, local_heads, report_keys)
    probs_b = probs.astype(jnp.bfloat16)
    token_pos = jnp.arange(tokens_here)
    lengths_tok = jnp.repeat(report_lengths, L)
    top = jnp.where((token_pos % L < lengths_tok)[:, None], cotangent, jnp.zeros((), jnp.bfloat16))
    gate = jnp.tanh(attn_gate[0])
    row_count = tokens_here // MICRO
    blk_reps = max(1, row_count // L)
    blk_len = row_count // blk_reps

    def step(turn, carry):
        incoming, grads, key_acc, val_acc = carry
        index = turn - (sections - 1 - my_section)
        valid = (index >= 0) & (index < MICRO)
        begin_offset = jnp.clip(index, 0, MICRO - 1) * row_count
        first_report = begin_offset // L
        top_block = lax.dynamic_slice_in_dim(
            top, jnp.clip(turn, 0, MICRO - 1) * row_count, row_count, 0
        )
        top_block = jnp.where(turn < MICRO, top_block, jnp.zeros((), jnp.bfloat16))
        upstream = jnp.where(my_section == sections - 1, top_block, incoming)
        out_sum = lax.psum_scatter(
            jnp.einsum("id,td->it", out_cols, upstream, preferred_element_type=jnp.float32).astype(
                jnp.bfloat16
            ),
            "mp",
            scatter_dimension=0,
            tiled=True,
        ).astype(jnp.float32)
        out_grad = (
            (gate * out_sum).astype(jnp.bfloat16).reshape(local_heads, HEAD, blk_reps, blk_len)
        )
        keys_blk = lax.dynamic_slice_in_dim(key_heads, first_report, blk_reps, 0)
        vals_blk = lax.dynamic_slice_in_dim(val_heads, first_report, blk_reps, 0)
        probs_blk = lax.dynamic_slice_in_dim(probs, begin_offset, row_count, 0).reshape(
            blk_reps, blk_len, local_heads, report_keys
        )
        probs_blk_b = lax.dynamic_slice_in_dim(probs_b, begin_offset, row_count, 0).reshape(
            blk_reps, blk_len, local_heads, report_keys
        )
        query_blk = lax.dynamic_slice_in_dim(query_heads, begin_offset, row_count, 0).reshape(
            blk_reps, blk_len, local_heads, HEAD
        )
        dprob = jnp.einsum(
            "hdrt,rkhd->rthk", out_grad, vals_blk, preferred_element_type=jnp.float32
        )
        rowdot = jnp.sum(probs_blk * dprob, axis=3, keepdims=True)
        dscore = (probs_blk * (dprob - rowdot)).astype(jnp.bfloat16)
        dquery = (
            (
                jnp.einsum("rthk,rkhd->rthd", dscore, keys_blk, preferred_element_type=jnp.float32)
                * scale
            )
            .astype(jnp.bfloat16)
            .reshape(row_count, local_width)
        )
        weight_live = jnp.where(valid, 1.0, 0.0)
        key_term = (
            jnp.einsum("rthk,rthd->rkhd", dscore, query_blk, preferred_element_type=jnp.float32)
            * scale
        )
        val_term = jnp.einsum(
            "rthk,hdrt->rkhd", probs_blk_b, out_grad, preferred_element_type=jnp.float32
        )
        key_now = lax.dynamic_slice_in_dim(key_acc, first_report, blk_reps, 0)
        val_now = lax.dynamic_slice_in_dim(val_acc, first_report, blk_reps, 0)
        key_acc = lax.dynamic_update_slice_in_dim(
            key_acc, key_now + weight_live * key_term, first_report, 0
        )
        val_acc = lax.dynamic_update_slice_in_dim(
            val_acc, val_now + weight_live * val_term, first_report, 0
        )
        query_blk32 = lax.dynamic_slice_in_dim(queries, begin_offset, row_count, 0)
        piece = lax.all_gather(dquery, "mp", axis=1, tiled=True)
        accum = jnp.einsum("tj,dj->td", piece, query_rows, preferred_element_type=jnp.float32)
        norm_statistic = jnp.sum(query_blk32 * piece.astype(jnp.float32), axis=1)
        normalized_gradient, norm_statistic = (accum, norm_statistic)
        normalized_input_block = lax.dynamic_slice_in_dim(
            normalized_input, begin_offset, row_count, 0
        )
        inverse_root_block = lax.dynamic_slice_in_dim(inverse_root_mean, begin_offset, row_count, 0)
        input_gradient = inverse_root_block[:, None] * (
            scale_factor * normalized_gradient
            - normalized_input_block * (norm_statistic / MODEL_WIDTH)[:, None]
        )
        grad_here = (upstream.astype(jnp.float32) + input_gradient).astype(jnp.bfloat16)
        grads = jnp.where(
            valid, lax.dynamic_update_slice_in_dim(grads, grad_here, begin_offset, 0), grads
        )
        incoming = from_behind(grad_here, "segment", -1)
        return (incoming, grads, key_acc, val_acc)

    acc_shape = (rep_dev, report_keys, local_heads, HEAD)
    start_carry = (
        jnp.zeros((row_count, width), jnp.bfloat16),
        jnp.zeros((tokens_here, width), jnp.bfloat16),
        jnp.zeros(acc_shape, jnp.float32),
        jnp.zeros(acc_shape, jnp.float32),
    )
    final = lax.fori_loop(0, MICRO + sections - 1, step, start_carry)
    grads = final[1]
    key_b = final[2].reshape(total_keys, local_width).astype(jnp.bfloat16)
    val_b = final[3].reshape(total_keys, local_width).astype(jnp.bfloat16)
    latent_term = jnp.einsum("kj,ej->ke", key_b, key_w, preferred_element_type=jnp.float32)
    latent_term = latent_term + jnp.einsum(
        "kj,ej->ke", val_b, value_w, preferred_element_type=jnp.float32
    )
    latent_term = latent_term.reshape(rep_dev, SPR * LAT, E)
    latent_grad = lax.psum_scatter(latent_term, ("segment", "mp"), scatter_dimension=1, tiled=True)
    return (grads[None], latent_grad)


def solution(mesh):
    return jax.shard_map(
        per_device,
        mesh=mesh,
        in_specs=(
            P("segment", "dp", "mp"),
            P("dp", "mp"),
            P("dp"),
            P("segment", "mp"),
            P("segment"),
            P("segment", "mp", "dp"),
            P("segment", "dp", "mp"),
            P("segment", None, "mp"),
            P("segment", None, "mp"),
            P("dp", None, None),
            P("dp", None),
            P(),
            P(),
            P(),
            P("dp", None, None),
        ),
        out_specs=(P("segment", "dp", "mp"), P("dp", ("segment", "mp"), None)),
        check_vma=False,
    )
```

profile of v0, /device:TPU:0, one launch (start us, length us, event | category | flops | bytes accessed | tf_op | source)
XLA Modules:
  0.0 666.8 jit_solution(11233674536599041828)
XLA Ops:
  11.0 8.4 %all-to-all-start.1 = ((s32[32,1,2]{2,1,0:T(1,128)}), s32[32,1,2]{2,1,0:T(1,128)S(1)}, u32[]{:S(2)}, u32[]{:S(2)}) async-start(s32[32,1,2]{2,1,0:T(1,128)} %copy.164), calls=%async_computation.2 | async-start | bytes 32768 | tf_op jit(solution)/shard_map/all_to_all | solution.py:83
  20.4 8.2 %gather_fusion = bf16[64,64,1536]{2,1,0:T(8,128)(2,1)} fusion(bf16[4,64,1536]{2,1,0:T(8,128)(2,1)} %param.26, s32[1024]{0:T(1024)S(1)} %pad_clamp_fusion.1), kind=kCustom, calls=%fused_computation | custom fusion | bytes 25166080 | tf_op jit(solution)/shard_map/gather | solution.py:76
  28.7 10.8 %broadcast_select_fusion = bf16[32,2,64,1536]{3,2,1,0:T(8,128)(2,1)} fusion(bf16[32,2,64,1536]{3,2,1,0:T(8,128)(2,1)} %bitcast.199, pred[32,2]{1,0:T(8,128)(4,1)S(1)} %copy.160), kind=kLoop, calls=%fused_computation.59 | loop fusion | flops 6291456 | bytes 25165888 | tf_op jit(solution)/shard_map/jit(_where)/select_n | solution.py:76
  39.4 7.5 %all-to-all-start = ((bf16[32,2,64,1536]{3,2,1,0:T(8,128)(2,1)}), bf16[32,2,64,1536]{3,2,1,0:T(8,128)(2,1)}, u32[]{:S(2)}, u32[]{:S(2)}) async-start(bf16[32,2,64,1536]{3,2,1,0:T(8,128)(2,1)} %broadcast_select_fusion), calls=%async_computation.1 | async-start | bytes 25165824 | tf_op jit(solution)/shard_map/all_to_all | solution.py:82
  55.5 88.1 %all-gather.5.cloned.1.call-done = bf16[1,2048,1024]{1,2,0:T(8,128)(2,1)} async-done(((bf16[1,2048,32]{1,2,0:T(8,128)(2,1)}), bf16[1,2048,1024]{1,2,0:T(8,128)(2,1)}) %all-gather.5.cloned.1.call-update) | async-done | bytes 4194320 | tf_op jit(solution)/shard_map/all_gather | solution.py:107
  143.6 6.6 fusion.46
  165.3 55.1 %all-reduce.2.cloned.1.call-done = f32[512,1024]{1,0:T(8,128)} async-done(((f32[512,1024]{1,0:T(8,128)}), f32[512,1024]{1,0:T(8,128)}) %all-reduce.2.cloned.1.call-update) | async-done | bytes 2097168 | tf_op jit(solution)/shard_map/psum | solution.py:110
  223.6 17.6 %fusion.29 = f32[12,32,2,64,32]{3,4,2,1,0:T(8,128)} fusion(bf16[32,12,128,1,1]{2,1,0,4,3:T(8,128)(2,1)S(1)} %bitcast.212, bf16[32,2,64,1536]{3,2,1,0:T(8,128)(2,1)} %all-to-all-done), kind=kOutput, calls=%fused_computation.49 | convolution fusion | flops 402653184 | bytes 18972672 | tf_op jit(solution)/shard_map/lhd,...thd->...hlt/dot_general | solution.py:28
  241.2 16.0 %fusion.85 = (f32[32,2,12,32]{3,1,0,2:T(2,128)S(1)}, f32[32,2,12,32,64]{4,3,1,0,2:T(8,128)}) fusion(f32[12,32,2,64,32]{3,4,2,1,0:T(8,128)} %fusion.29, pred[32,2,64]{2,1,0:T(4,128)(4,1)S(1)} %iota_compare_fusion), kind=kOutput, calls=%fused_computation.126 | output fusion | flops 9437247 | bytes 12685312 | tf_op jit(solution)/shard_map/sub | solution.py:33
  257.2 15.4 %fusion.40 = f32[32,2,32,12,128]{4,2,3,1,0:T(8,128)} fusion(bf16[32,2,64,1536]{3,2,1,0:T(8,128)(2,1)} %all-to-all-done, f32[32,2,12,32,64]{4,3,1,0,2:T(8,128)} %get-tuple-element.620, f32[32,2,12,32]{3,1,0,2:T(2,128)S(1)} %get-tuple-element.619), kind=kOutput, calls=%fused_computation.66 | convolution fusion | flops 405798912 | bytes 31555584 | tf_op jit(solution)/shard_map/...hlt,...thd->...lhd/dot_general | solution.py:34
  272.7 22.5 %copy.171 = f32[32,2,32,12,128]{4,3,2,1,0:T(8,128)} copy(f32[32,2,32,12,128]{4,2,3,1,0:T(8,128)} %fusion.40) | data formatting | bytes 25165824 | tf_op jit(solution)/shard_map/...hlt,...thd->...lhd/transpose | solution.py:34
  295.1 15.6 %reshape.216 = f32[64,32,1536]{2,1,0:T(8,128)} reshape(f32[32,2,32,12,128]{4,3,2,1,0:T(8,128)} %copy.171) | data formatting | bytes 25165824 | tf_op jit(solution)/shard_map/reshape | solution.py:35
  310.7 9.1 %add_convert_fusion = bf16[64,32,1536]{2,1,0:T(8,128)(2,1)} fusion(f32[64,32,1536]{2,1,0:T(8,128)} %reshape.216, f32[32,1536]{1,0:T(8,128)S(1)} %convert_element_type.131), kind=kLoop, calls=%fused_computation.56 | loop fusion | flops 6291456 | bytes 19070976 | tf_op jit(solution)/shard_map/convert_element_type | solution.py:35
  344.2 218.7 %while.21 = (s32[]{:T(128)}, bf16[256,2048]{1,0:T(8,128)(2,1)}, bf16[512,2048]{1,0:T(8,128)(2,1)}, f32[4,192,4,128]{3,1,2,0:T(8,128)}, f32[4,192,4,128]{3,1,2,0:...) while((s32[]{:T(128)}, bf16[256,2048]{1,0:T(8,128)(2,1)}, ...), condition=%wide.region_15.16_spmd, body=%wide.region_11.15_spmd.sunk | while | flops 2358574080 | bytes 74473896 | solution.py:227
  350.4 16.5 %reduce-scatter.5.cloned.1.call-done = bf16[512,256]{0,1:T(8,128)(2,1)} async-done(((bf16[1024,256]{0,1:T(8,128)(2,1)}), bf16[512,256]{0,1:T(8,128)(2,1)}) %reduce-scatter.5.cloned.1.call-update) | async-done | bytes 262160 | tf_op jit(solution)/shard_map/while/body/eval_jaxpr/reduce_scatter | solution.py:149
  371.5 10.4 %all_gather.19 = bf16[256,1024]{1,0:T(8,128)(2,1)S(1)} all-gather(bf16[256,512]{1,0:T(8,128)(2,1)S(1)} %bitcast.200), channel_id=1, replica_groups=mesh['segment'=2,'dp'=32,'mp'=2] {'mp'}, dimensions={1}, use_global_device_ids=true | all-gather | bytes 786432 | tf_op jit(solution)/shard_map/while/body/eval_jaxpr/all_gather | solution.py:201
  396.2 21.0 %collective-permute-done = bf16[256,2048]{1,0:T(8,128)(2,1)} collective-permute-done((bf16[256,2048]{1,0:T(8,128)(2,1)}, bf16[256,2048]{1,0:T(8,128)(2,1)}, u32[]{:S(2)}, u32[]{:S(2)}) %collective-permute-start) | collective-permute-done | bytes 1048608 | tf_op jit(solution)/shard_map/while/body/eval_jaxpr/ppermute | solution.py:19
  423.4 16.3 %reduce-scatter.5.cloned.1.call-done = bf16[512,256]{0,1:T(8,128)(2,1)} async-done(((bf16[1024,256]{0,1:T(8,128)(2,1)}), bf16[512,256]{0,1:T(8,128)(2,1)}) %reduce-scatter.5.cloned.1.call-update) | async-done | bytes 262160 | tf_op jit(solution)/shard_map/while/body/eval_jaxpr/reduce_scatter | solution.py:149
  444.4 10.4 %all_gather.19 = bf16[256,1024]{1,0:T(8,128)(2,1)S(1)} all-gather(bf16[256,512]{1,0:T(8,128)(2,1)S(1)} %bitcast.200), channel_id=1, replica_groups=mesh['segment'=2,'dp'=32,'mp'=2] {'mp'}, dimensions={1}, use_global_device_ids=true | all-gather | bytes 786432 | tf_op jit(solution)/shard_map/while/body/eval_jaxpr/all_gather | solution.py:201
  469.0 21.0 %collective-permute-done = bf16[256,2048]{1,0:T(8,128)(2,1)} collective-permute-done((bf16[256,2048]{1,0:T(8,128)(2,1)}, bf16[256,2048]{1,0:T(8,128)(2,1)}, u32[]{:S(2)}, u32[]{:S(2)}) %collective-permute-start) | collective-permute-done | bytes 1048608 | tf_op jit(solution)/shard_map/while/body/eval_jaxpr/ppermute | solution.py:19
  496.2 16.3 %reduce-scatter.5.cloned.1.call-done = bf16[512,256]{0,1:T(8,128)(2,1)} async-done(((bf16[1024,256]{0,1:T(8,128)(2,1)}), bf16[512,256]{0,1:T(8,128)(2,1)}) %reduce-scatter.5.cloned.1.call-update) | async-done | bytes 262160 | tf_op jit(solution)/shard_map/while/body/eval_jaxpr/reduce_scatter | solution.py:149
  517.2 10.4 %all_gather.19 = bf16[256,1024]{1,0:T(8,128)(2,1)S(1)} all-gather(bf16[256,512]{1,0:T(8,128)(2,1)S(1)} %bitcast.200), channel_id=1, replica_groups=mesh['segment'=2,'dp'=32,'mp'=2] {'mp'}, dimensions={1}, use_global_device_ids=true | all-gather | bytes 786432 | tf_op jit(solution)/shard_map/while/body/eval_jaxpr/all_gather | solution.py:201
  541.8 21.1 %collective-permute-done = bf16[256,2048]{1,0:T(8,128)(2,1)} collective-permute-done((bf16[256,2048]{1,0:T(8,128)(2,1)}, bf16[256,2048]{1,0:T(8,128)(2,1)}, u32[]{:S(2)}, u32[]{:S(2)}) %collective-permute-start) | collective-permute-done | bytes 1048608 | tf_op jit(solution)/shard_map/while/body/eval_jaxpr/ppermute | solution.py:19
  571.7 88.0 %reduce-scatter.3.cloned.1.call-done = f32[4,48,1536]{2,1,0:T(8,128)} async-done(((f32[4,192,1536]{2,1,0:T(8,128)}), f32[4,48,1536]{2,1,0:T(8,128)}) %reduce-scatter.3.cloned.1.call-update) | async-done | bytes 1179664 | tf_op jit(solution)/shard_map/reduce_scatter | solution.py:236
  (186 shorter events, 138.6 us)
Async XLA Ops:
  7.2 317.7 %copy-start = (bf16[1,1536,512]{2,1,0:T(8,128)(2,1)S(1)}, bf16[1,1536,512]{2,1,0:T(8,128)(2,1)}, u32[]{:S(2)}) copy-start(bf16[1,1536,512]{2,1,0:T(8,128)(2,1)} %param.24) | copy-start | bytes 4718596
  11.0 28.5 %all-to-all-start.1 = ((s32[32,1,2]{2,1,0:T(1,128)}), s32[32,1,2]{2,1,0:T(1,128)S(1)}, u32[]{:S(2)}, u32[]{:S(2)}) async-start(s32[32,1,2]{2,1,0:T(1,128)} %copy.164), calls=%async_computation.2 | async-start | bytes 32768 | tf_op jit(solution)/shard_map/all_to_all | solution.py:83
  19.4 124.3 %all-gather.5.cloned.1.call-start = ((), (), s32[]{:S(2)}) async-start(), calls=%async_computation.6 | async-start | bytes 4325376 | tf_op jit(solution)/shard_map/all_gather | solution.py:107
  39.4 104.2 %copy-start.15 = (f32[1,2048]{1,0:T(1,128)S(1)}, f32[1,2048]{1,0:T(1,128)}, u32[]{:S(2)}) copy-start(f32[1,2048]{1,0:T(1,128)} %param.20) | copy-start | bytes 24580
  39.4 184.2 %all-to-all-start = ((bf16[32,2,64,1536]{3,2,1,0:T(8,128)(2,1)}), bf16[32,2,64,1536]{3,2,1,0:T(8,128)(2,1)}, u32[]{:S(2)}, u32[]{:S(2)}) async-start(bf16[32,2,64,1536]{3,2,1,0:T(8,128)(2,1)} %broadcast_select_fusion), calls=%async_computation.1 | async-start | bytes 25165824 | tf_op jit(solution)/shard_map/all_to_all | solution.py:82
  47.0 173.5 %all-reduce.2.cloned.1.call-start = ((), (), s32[]{:S(2)}) async-start(), calls=%async_computation.4 | async-start | bytes 4194304 | tf_op jit(solution)/shard_map/psum | solution.py:110
  143.6 7.3 %copy-start.13 = (bf16[32,1536]{1,0:T(8,128)(2,1)S(1)}, bf16[32,1536]{1,0:T(8,128)(2,1)}, u32[]{:S(2)}) copy-start(bf16[32,1536]{1,0:T(8,128)(2,1)} %param.28) | copy-start | bytes 294916
  150.2 188.6 %all-gather.7.cloned.1.call-start = ((), (), s32[]{:S(2)}) async-start(), calls=%async_computation.7 | async-start | bytes 4325376 | tf_op jit(solution)/shard_map/all_gather | solution.py:108
  152.7 3.6 copy-start.5
  332.2 3.1 copy-start.7
  333.6 2.8 copy-start.11
  344.2 22.7 %reduce-scatter.5.cloned.1.call-start = ((), (), s32[]{:S(2)}) async-start(), calls=%async_computation.8 | async-start | bytes 786432 | tf_op jit(solution)/shard_map/while/body/eval_jaxpr/reduce_scatter | solution.py:149
  371.5 11.9 %copy-start.9 = (bf16[512,2048]{1,0:T(8,128)(2,1)S(1)}, bf16[512,2048]{1,0:T(8,128)(2,1)}, u32[]{:S(2)}) copy-start(bf16[512,2048]{1,0:T(8,128)(2,1)} %get-tuple-element.784) | copy-start | bytes 6291460 | tf_op jit(solution)/shard_map/while
  391.0 26.2 %collective-permute-start = (bf16[256,2048]{1,0:T(8,128)(2,1)}, bf16[256,2048]{1,0:T(8,128)(2,1)}, u32[]{:S(2)}, u32[]{:S(2)}) collective-permute-start(bf16[256,2048]{1,0:T(8,128)(2,1)} %get-tuple-element.748), channel_id=1, source_target_pairs={{64,0},{65,1},{66,2},{67,3},{68,4},{69,5},{70,6},{71,7},{72,8},{73... | collective-permute-start | bytes 3145736 | tf_op jit(solution)/shard_map/while/body/eval_jaxpr/ppermute | solution.py:19
  396.1 21.1 %copy-start.3 = (f32[4,192,4,128]{3,1,2,0:T(8,128)}, f32[4,192,4,128]{3,1,2,0:T(8,128)S(1)}, u32[]{:S(2)}) copy-start(f32[4,192,4,128]{3,1,2,0:T(8,128)S(1)} %fusion.135) | copy-start | bytes 4718596 | tf_op jit(solution)/shard_map/while
  417.2 22.5 %reduce-scatter.5.cloned.1.call-start = ((), (), s32[]{:S(2)}) async-start(), calls=%async_computation.8 | async-start | bytes 786432 | tf_op jit(solution)/shard_map/while/body/eval_jaxpr/reduce_scatter | solution.py:149
  444.3 11.9 %copy-start.9 = (bf16[512,2048]{1,0:T(8,128)(2,1)S(1)}, bf16[512,2048]{1,0:T(8,128)(2,1)}, u32[]{:S(2)}) copy-start(bf16[512,2048]{1,0:T(8,128)(2,1)} %get-tuple-element.784) | copy-start | bytes 6291460 | tf_op jit(solution)/shard_map/while
  463.8 26.2 %collective-permute-start = (bf16[256,2048]{1,0:T(8,128)(2,1)}, bf16[256,2048]{1,0:T(8,128)(2,1)}, u32[]{:S(2)}, u32[]{:S(2)}) collective-permute-start(bf16[256,2048]{1,0:T(8,128)(2,1)} %get-tuple-element.748), channel_id=1, source_target_pairs={{64,0},{65,1},{66,2},{67,3},{68,4},{69,5},{70,6},{71,7},{72,8},{73... | collective-permute-start | bytes 3145736 | tf_op jit(solution)/shard_map/while/body/eval_jaxpr/ppermute | solution.py:19
  469.0 21.1 %copy-start.3 = (f32[4,192,4,128]{3,1,2,0:T(8,128)}, f32[4,192,4,128]{3,1,2,0:T(8,128)S(1)}, u32[]{:S(2)}) copy-start(f32[4,192,4,128]{3,1,2,0:T(8,128)S(1)} %fusion.135) | copy-start | bytes 4718596 | tf_op jit(solution)/shard_map/while
  490.0 22.5 %reduce-scatter.5.cloned.1.call-start = ((), (), s32[]{:S(2)}) async-start(), calls=%async_computation.8 | async-start | bytes 786432 | tf_op jit(solution)/shard_map/while/body/eval_jaxpr/reduce_scatter | solution.py:149
  517.1 11.9 %copy-start.9 = (bf16[512,2048]{1,0:T(8,128)(2,1)S(1)}, bf16[512,2048]{1,0:T(8,128)(2,1)}, u32[]{:S(2)}) copy-start(bf16[512,2048]{1,0:T(8,128)(2,1)} %get-tuple-element.784) | copy-start | bytes 6291460 | tf_op jit(solution)/shard_map/while
  536.6 26.2 %collective-permute-start = (bf16[256,2048]{1,0:T(8,128)(2,1)}, bf16[256,2048]{1,0:T(8,128)(2,1)}, u32[]{:S(2)}, u32[]{:S(2)}) collective-permute-start(bf16[256,2048]{1,0:T(8,128)(2,1)} %get-tuple-element.748), channel_id=1, source_target_pairs={{64,0},{65,1},{66,2},{67,3},{68,4},{69,5},{70,6},{71,7},{72,8},{73... | collective-permute-start | bytes 3145736 | tf_op jit(solution)/shard_map/while/body/eval_jaxpr/ppermute | solution.py:19
  541.8 21.1 %copy-start.3 = (f32[4,192,4,128]{3,1,2,0:T(8,128)}, f32[4,192,4,128]{3,1,2,0:T(8,128)S(1)}, u32[]{:S(2)}) copy-start(f32[4,192,4,128]{3,1,2,0:T(8,128)S(1)} %fusion.135) | copy-start | bytes 4718596 | tf_op jit(solution)/shard_map/while
  562.9 96.8 %reduce-scatter.3.cloned.1.call-start = ((), (), s32[]{:S(2)}) async-start(), calls=%async_computation.5 | async-start | bytes 5898240 | tf_op jit(solution)/shard_map/reduce_scatter | solution.py:236
  (15 other events, 30.0 us)
Sparse Core Ops, SparseCore 0:
  22.5 121.1 all-gather.4
  150.4 70.0 all-reduce.1
  222.9 45.8 all-gather.6
  349.2 17.6 reduce-scatter.4
  422.3 17.4 reduce-scatter.4
  495.1 17.3 reduce-scatter.4
  571.8 87.8 reduce-scatter.2
where the time goes:
time: 674 us; the launch traced here: 667 us
  waiting for transfers between devices  344 us (51%)
  matrix products  98.4 us (15%)
  local copies, waits for them, and re-layouts  92.1 us (14%)
  other arithmetic  57.7 us (9%)
  blocking collectives  37.5 us (6%)
  starting transfers between devices  20.7 us (3%)
  between operations  15.3 us (2%)
    all_gather x1, waiting for transfers between devices, per_device(): lax.all_gather(w_query[0], 'dp', axis=1, tiled=True)  88.1 us
    reduce_scatter x1, waiting for transfers between devices, per_device(): lax.psum_scatter(latent_term, ('segment', 'mp'), scatter_dimension=1, til...  88 us
    ppermute x3, waiting for transfers between devices, from_behind(): return lax.ppermute(array, axis, pairs)  63.1 us
    psum x1, waiting for transfers between devices, per_device(): lax.psum(jnp.dot(normalized_rows, query_rows, preferred_element_type=jnp....  55.1 us
    reduce_scatter x3, waiting for transfers between devices, step(): lax.psum_scatter(jnp.einsum('id,td->it', out_cols, upstream, preferred_el...  49.2 us
    all_gather x3, blocking collectives, step(): piece = lax.all_gather(dquery, 'mp', axis=1, tiled=True)  31.1 us
    transpose x1, local copies, waits for them, and re-layouts, pool_slides(): jnp.einsum('...hlt,...thd->...lhd', weights, keys, preferred_element_type...  22.5 us
    dot_general x3, matrix products, step(): jnp.einsum('tj,dj->td', piece, query_rows, preferred_element_type=jnp.flo...  18.9 us
  transfers between devices with their start and end apart: 12, of which 9 were waited for; matrix products, arithmetic and copies ran while one was open for 26% of the time, Pallas kernels for 0%

commit v1 on v0

v1 whole, which is shorter than its diff:
```python
import functools

import jax
import jax.numpy as jnp
from jax import lax
from jax.experimental import pallas as pl
from jax.experimental.pallas import tpu as pltpu
from jax.sharding import Mesh
from jax.sharding import PartitionSpec as P

MODEL_WIDTH = 4096
E = 1536
HEAD = 128
LAT = 32
SPR = 6
L = 128
QBLK = 32
MAXT = 64
QUARTER = E // 4
SCALE = HEAD ** (-0.5)
DP = ("z", "y", "core")
X = ("segment", "mp")
BF = jnp.bfloat16
F32 = jnp.float32
LIMIT = 48 * 1024 * 1024
NT = (((1,), (1,)), ((), ()))
NN = (((1,), (0,)), ((), ()))
TN = (((0,), (0,)), ((), ()))

SWAP_MP = [(0, 1), (1, 0), (2, 3), (3, 2)]
LAST_TO_SAME = [(2, 0), (3, 1)]
LAST_TO_CROSS = [(2, 1), (3, 0)]
LAST_SWAP = [(2, 3), (3, 2)]
FIRST_TO_SAME = [(0, 2), (1, 3)]
FIRST_TO_CROSS = [(0, 3), (1, 2)]
FIRST_SWAP = [(0, 1), (1, 0)]
AT_X = (0, 2, 1, 3)


def x_perm(k):
    return [(AT_X[x], AT_X[(x + k) % 4]) for x in range(4)]


def yz_perm(stage, k):
    pairs = []
    for z in range(4):
        for y in range(4):
            for core in range(2):
                along_y = (core == 0) == (stage == 1)
                to_z = z if along_y else (z + k) % 4
                to_y = (y + k) % 4 if along_y else y
                pairs.append(((z * 4 + y) * 2 + core, (to_z * 4 + to_y) * 2 + core))
    return pairs


def dot(a, b, dims):
    return lax.dot_general(a, b, dims, preferred_element_type=F32)


def params(**kwargs):
    return pltpu.CompilerParams(vmem_limit_bytes=LIMIT, **kwargs)


def whole(shape):
    return pl.BlockSpec(shape, lambda *_: (0,) * len(shape))


SMEM = pl.BlockSpec(memory_space=pltpu.SMEM)
ANY = pl.BlockSpec(memory_space=pl.ANY)


def pool_kernel(which, counts, tiles, queries, out):
    for slide in range(4):
        live = lax.broadcasted_iota(jnp.int32, (LAT, MAXT), 1) < counts[slide]
        for head in range(QUARTER // HEAD):
            cols = slice(head * HEAD, (head + 1) * HEAD)
            tile = tiles[slide, :, cols]
            query = queries[:, cols]
            scores = dot(query, tile, NT) * SCALE
            scores = jnp.where(live, scores, -1e30)
            exps = jnp.exp(scores - jnp.max(scores, axis=1, keepdims=True))
            weights = (exps / jnp.sum(exps, axis=1, keepdims=True)).astype(BF)
            pooled = dot(weights, tile, NN)
            out[slide * LAT : (slide + 1) * LAT, cols] = (query.astype(F32) + pooled).astype(BF)


def pool(which, counts, tiles, queries):
    return pl.pallas_call(
        pool_kernel,
        grid_spec=pltpu.PrefetchScalarGridSpec(
            num_scalar_prefetch=2,
            grid=(1,),
            in_specs=[
                pl.BlockSpec((4, MAXT, QUARTER), lambda i, which, counts: (0, 0, which[0])),
                pl.BlockSpec((LAT, QUARTER), lambda i, which, counts: (0, which[0])),
            ],
            out_specs=pl.BlockSpec((4 * LAT, QUARTER), lambda i, which, counts: (0, 0)),
        ),
        out_shape=jax.ShapeDtypeStruct((4 * LAT, QUARTER), BF),
        compiler_params=params(),
    )(which, counts, tiles, queries)


def gather_dp(block):
    parts = [block] + [lax.ppermute(block, DP, yz_perm(1, k)) for k in (1, 2, 3)]
    bundle = jnp.stack(parts)
    mine = [bundle] + [lax.ppermute(bundle, DP, yz_perm(2, k)) for k in (1, 2, 3)]
    others = [lax.ppermute(b, "core", [(0, 1), (1, 0)]) for b in mine]
    return mine + others


def places():
    z, y, core = (lax.axis_index(name) for name in DP)
    table = []
    for a in range(8):
        c = core if a < 4 else 1 - core
        for k in range(4):
            j = a % 4
            at_z = lax.rem(z - jnp.where(c == 0, j, k) + 4, 4)
            at_y = lax.rem(y - jnp.where(c == 0, k, j) + 4, 4)
            table.append((at_z * 4 + at_y) * 2 + c)
    return jnp.stack(table).astype(jnp.int32)


def assemble_kernel(kinds, rows, *refs):
    ins, outs, sems = refs[:8], refs[8 : 8 + kinds], refs[8 + kinds]
    copies = []
    for a in range(8):
        for k in range(4):
            at = pl.multiple_of(rows[a * 4 + k], 32)
            for kind in range(kinds):
                copies.append(
                    pltpu.make_async_copy(
                        ins[a].at[k, pl.ds(kind * 32, 32)],
                        outs[kind].at[pl.ds(at, 32)],
                        sems.at[(a * 4 + k) * kinds + kind],
                    )
                )
    for copy in copies:
        copy.start()
    for copy in copies:
        copy.wait()


def assemble(rows, blocks, kinds):
    width = blocks[0].shape[2]
    out = jax.ShapeDtypeStruct((1024, width), BF)
    return pl.pallas_call(
        functools.partial(assemble_kernel, kinds),
        in_specs=[SMEM] + [ANY] * 8,
        out_specs=[ANY] * kinds,
        out_shape=[out] * kinds,
        scratch_shapes=[pltpu.SemaphoreType.DMA((32 * kinds,))],
        compiler_params=params(),
    )(rows, *blocks)


def select_kernel(wanted, array, block, slide, *refs):
    ins, out, sems = refs[:8], refs[8], refs[9]
    for i in range(wanted):
        for a in range(8):

            @pl.when(array[i] == a)
            def _():
                pltpu.make_async_copy(
                    ins[a].at[block[i], pl.ds(pl.multiple_of(slide[i] * LAT, LAT), LAT)],
                    out.at[pl.ds(i * LAT, LAT)],
                    sems.at[i],
                ).start()

    for i in range(wanted):
        pltpu.make_async_copy(
            ins[0].at[0, pl.ds(0, LAT)], out.at[pl.ds(i * LAT, LAT)], sems.at[i]
        ).wait()


def select(array, block, slide, blocks):
    wanted = array.shape[0]
    return pl.pallas_call(
        functools.partial(select_kernel, wanted),
        in_specs=[SMEM] * 3 + [ANY] * 8,
        out_specs=ANY,
        out_shape=jax.ShapeDtypeStruct((wanted * LAT, QUARTER), BF),
        scratch_shapes=[pltpu.SemaphoreType.DMA((wanted,))],
        compiler_params=params(),
    )(array, block, slide, *blocks)


def front_kernel(h, rinv, gain, cot, live, wq, wo, q_own, q_send, o_own, o_send, q_acc, o_acc):
    step = pl.program_id(0)
    normed = (h[...].astype(F32) * rinv[...] * gain[...]).astype(BF)
    upstream = jnp.where(live[...] > 0, cot[...], jnp.zeros((), BF))
    q_term = dot(normed, wq[...], NT)
    o_term = dot(upstream, wo[...], NT)

    @pl.when(step == 0)
    def _():
        q_acc[...] = q_term
        o_acc[...] = o_term

    @pl.when(step > 0)
    def _():
        q_acc[...] += q_term
        o_acc[...] += o_term

    @pl.when(step == pl.num_programs(0) - 1)
    def _():
        half = q_own.shape[1]
        q_own[...] = q_acc[:, :half]
        q_send[...] = q_acc[:, half:].astype(BF)
        o_own[...] = o_acc[:, :half].astype(BF)
        o_send[...] = o_acc[:, half:].astype(BF)


TILE = 512


def front(h, rinv, gain, cot, live, wq, wo):
    tokens, width = h.shape
    inner = wq.shape[0]
    half = inner // 2
    act = pl.BlockSpec((tokens, TILE), lambda i: (0, i))
    weight = pl.BlockSpec((inner, TILE), lambda i: (0, i))
    column = whole((tokens, 1))
    result = whole((tokens, half))
    return pl.pallas_call(
        front_kernel,
        grid=(width // TILE,),
        in_specs=[act, column, pl.BlockSpec((1, TILE), lambda i: (0, i)), act, column, weight, weight],
        out_specs=[result] * 4,
        out_shape=[jax.ShapeDtypeStruct((tokens, half), t) for t in (F32, BF, BF, BF)],
        scratch_shapes=[pltpu.VMEM((tokens, inner), F32)] * 2,
        compiler_params=params(),
        cost_estimate=pl.CostEstimate(
            flops=4 * tokens * width * inner, bytes_accessed=14 << 20, transcendentals=0
        ),
    )(h, rinv, gain, cot, live, wq, wo)


def attend_kernel(slot, gate, q_own, q_got, o_own, o_got, keys, vals, allowed, dq_out, dkv_out):
    report = pl.program_id(0)
    rows = pl.ds(pl.multiple_of(report * L, L), L)
    local = q_own.shape[1]
    mask = allowed[...] > 0
    stat = jnp.zeros((L, HEAD), F32)
    for head in range(local // HEAD):
        cols = slice(head * HEAD, (head + 1) * HEAD)
        q = q_own[:, cols] + q_got[:, cols].astype(F32)
        qb = q.astype(BF)
        og = (gate[0] * (o_own[:, cols].astype(F32) + o_got[:, cols].astype(F32))).astype(BF)
        key = keys[:, cols]
        val = vals[:, cols]
        scores = jnp.where(mask, dot(qb, key, NT) * SCALE, -1e30)
        exps = jnp.exp(scores - jnp.max(scores, axis=1, keepdims=True))
        probs = exps / jnp.sum(exps, axis=1, keepdims=True)
        dprob = dot(og, val, NT)
        rowdot = jnp.sum(probs * dprob, axis=1, keepdims=True)
        dscore = (probs * (dprob - rowdot)).astype(BF)
        dq = (dot(dscore, key, NN) * SCALE).astype(BF)
        dkey = (dot(dscore, qb, TN) * SCALE).astype(BF)
        dval = dot(probs.astype(BF), og, TN).astype(BF)
        dq_out[rows, cols] = dq
        stat += q * dq.astype(F32)
        for part in range(4):
            into = pl.ds(pl.multiple_of(report * 48, 16), 48)
            dkv_out[slot[part], into, cols] = dkey[part * 48 : (part + 1) * 48]
            dkv_out[slot[part], into, slice(local + head * HEAD, local + (head + 1) * HEAD)] = dval[
                part * 48 : (part + 1) * 48
            ]
    total = jnp.sum(stat.T, axis=0, keepdims=True)
    high = total.astype(BF)
    rest = total - high.astype(F32)
    low = rest.astype(BF)
    lower = (rest - low.astype(F32)).astype(BF)
    zero = jnp.zeros((13, L), F32)
    extra = jnp.concatenate([high.astype(F32), low.astype(F32), lower.astype(F32), zero], axis=0)
    tokens = q_own.shape[0] * pl.num_programs(0)
    dq_out[4 * L : 4 * L + 16, rows] = extra.astype(BF)


def attend(slot, gate, q_own, q_got, o_own, o_got, keys, vals, allowed):
    tokens, local = q_own.shape
    reports = tokens // L
    span = keys.shape[0] // reports
    token = pl.BlockSpec((L, local), lambda i: (i, 0))
    latent = pl.BlockSpec((span, local), lambda i: (i, 0))
    return pl.pallas_call(
        attend_kernel,
        grid=(reports,),
        in_specs=[SMEM, SMEM, token, token, token, token, latent, latent]
        + [pl.BlockSpec((L, span), lambda i: (i, 0))],
        out_specs=[whole((tokens + 16, local)), whole((4, reports * 48, 2 * local))],
        out_shape=[
            jax.ShapeDtypeStruct((tokens + 16, local), BF),
            jax.ShapeDtypeStruct((4, reports * 48, 2 * local), BF),
        ],
        compiler_params=params(),
        cost_estimate=pl.CostEstimate(
            flops=10 * tokens * span * local, bytes_accessed=6 << 20, transcendentals=tokens * span * 4
        ),
    )(slot, gate, q_own, q_got, o_own, o_got, keys, vals, allowed)


def back_kernel(following, dq_own, dq_got, stat, up, live, h, rinv, gain, wq, *refs):
    half = dq_own.shape[1]
    if following:
        wo, grad, o_own, o_send, o_acc = refs
    else:
        (grad,) = refs
    step = pl.program_id(0)
    dnormed = dot(dq_own[...], wq[:half], NN) + dot(dq_got[...], wq[half:], NN)
    upstream = jnp.where(live[...] > 0, up[...].astype(F32), 0.0)
    xhat = h[...].astype(F32) * rinv[...]
    value = upstream + rinv[...] * (gain[...] * dnormed - xhat * (stat[...] / MODEL_WIDTH))
    value = value.astype(BF)
    grad[...] = value
    if not following:
        return
    o_term = dot(value, wo[...], NT)

    @pl.when(step == 0)
    def _():
        o_acc[...] = o_term

    @pl.when(step > 0)
    def _():
        o_acc[...] += o_term

    @pl.when(step == pl.num_programs(0) - 1)
    def _():
        o_own[...] = o_acc[:, :half].astype(BF)
        o_send[...] = o_acc[:, half:].astype(BF)


def back(dq_own, dq_got, stat, up, live, h, rinv, gain, wq, wo=None):
    tokens, width = h.shape
    inner = wq.shape[0]
    half = inner // 2
    act = pl.BlockSpec((tokens, TILE), lambda i: (0, i))
    weight = pl.BlockSpec((inner, TILE), lambda i: (0, i))
    column = whole((tokens, 1))
    inputs = [dq_own, dq_got, stat, up, live, h, rinv, gain, wq]
    specs = [whole((tokens, half))] * 2 + [column, act, column, act, column]
    specs += [pl.BlockSpec((1, TILE), lambda i: (0, i)), weight]
    out_specs = [act]
    out_shape = [jax.ShapeDtypeStruct((tokens, width), BF)]
    scratch = []
    if wo is not None:
        inputs.append(wo)
        specs.append(weight)
        out_specs += [whole((tokens, half))] * 2
        out_shape += [jax.ShapeDtypeStruct((tokens, half), BF)] * 2
        scratch = [pltpu.VMEM((tokens, inner), F32)]
    return pl.pallas_call(
        functools.partial(back_kernel, wo is not None),
        grid=(width // TILE,),
        in_specs=specs,
        out_specs=out_specs,
        out_shape=out_shape,
        scratch_shapes=scratch,
        compiler_params=params(),
        cost_estimate=pl.CostEstimate(
            flops=(4 if wo is not None else 2) * tokens * width * inner,
            bytes_accessed=14 << 20,
            transcendentals=0,
        ),
    )(*inputs)


def per_device(
    segment_inputs,
    cotangent,
    report_lengths,
    norm_gain,
    attn_gate,
    w_query,
    w_out,
    w_key,
    w_value,
    tiles,
    tile_counts,
    lat_query,
    request_source,
    request_slide,
    cross_pattern,
):
    z, y, core = (lax.axis_index(name) for name in DP)
    me_dp = (z * 4 + y) * 2 + core
    me_mp = lax.axis_index("mp")
    seg = lax.axis_index("segment")
    me_x = me_mp * 2 + seg
    last = seg == 1
    reports = cross_pattern.shape[0]
    wanted = reports * SPR

    pooled = pool(
        me_x.reshape(1).astype(jnp.int32), tile_counts.reshape(4), tiles, lat_query
    )
    lat_blocks = gather_dp(pooled)

    wq_t = w_query[0].T
    w_blocks = gather_dp(jnp.concatenate([w_out[0], wq_t], axis=0))

    place = places()
    rows = lax.rem(place * 32 - me_mp * 512 + 1024, 1024).astype(jnp.int32)
    where_is = jnp.zeros((32,), jnp.int32).at[place].set(jnp.arange(32, dtype=jnp.int32))
    source = lax.dynamic_index_in_dim(
        request_source.reshape(32, wanted), me_dp, 0, keepdims=False
    )
    slide = lax.dynamic_index_in_dim(request_slide.reshape(32, wanted), me_dp, 0, keepdims=False)
    found = where_is[source]
    chosen = select(found // 4, found % 4, slide, lat_blocks)
    lat_parts = [chosen] + [lax.ppermute(chosen, X, x_perm(k)) for k in (1, 2, 3)]
    latents = jnp.concatenate(lat_parts, axis=1)
    w_kv = jnp.concatenate([w_key[0], w_value[0]], axis=1)
    w_kv_x = jnp.concatenate(
        [
            lax.dynamic_slice_in_dim(w_kv, lax.rem(me_x - k + 4, 4) * QUARTER, QUARTER, 0)
            for k in range(4)
        ],
        axis=0,
    )
    kv = dot(latents, w_kv_x, NN).astype(BF)
    local = w_key.shape[2]
    keys, vals = kv[:, :local], kv[:, local:]

    h = segment_inputs[0]
    h32 = h.astype(F32)
    squares = lax.psum(jnp.sum(h32 * h32, axis=1), "mp")
    both = lax.all_gather(jnp.concatenate([squares, norm_gain[0]]), "segment")
    tokens, width = h.shape
    squares1, gain1 = both[1, :tokens], both[1, tokens:]
    rinv = lax.rsqrt(squares / MODEL_WIDTH + 1e-05)[:, None]
    rinv1 = lax.rsqrt(squares1 / MODEL_WIDTH + 1e-05)[:, None]
    gain = norm_gain[0][None, :]
    gain1 = gain1[None, :]
    h1 = jnp.where(last, h, lax.ppermute(h, "segment", [(1, 0)]))
    wq1_t = jnp.where(last, wq_t, lax.ppermute(wq_t, "segment", [(1, 0)]))
    live = (jnp.arange(tokens) % L < jnp.repeat(report_lengths, L)).astype(F32)[:, None]
    allowed = jnp.broadcast_to(
        cross_pattern[:, :, None, :, None], (reports, cross_pattern.shape[1], QBLK, SPR, LAT)
    ).reshape(tokens, SPR * LAT).astype(F32)
    gate = jnp.tanh(attn_gate)
    slot = []
    for part in range(4):
        same_seg, same_mp = seg == part // 2, me_mp == part % 2
        slot.append(jnp.where(same_seg, jnp.where(same_mp, 0, 3), jnp.where(same_mp, 1, 2)))
    slot = jnp.stack(slot).astype(jnp.int32)

    wo, wq = assemble(rows, w_blocks, 2)
    (wq1,) = assemble(rows, gather_dp(wq1_t), 1)

    q_own, q_send, o_own, o_send = front(h, rinv, gain, cotangent, live, wq, wo)
    q_got = lax.ppermute(q_send, X, SWAP_MP)
    o_got = lax.ppermute(o_send, X, LAST_SWAP)
    dq, dkv = attend(slot, gate, q_own, q_got, o_own, o_got, keys, vals, allowed)
    dq_same = jnp.where(last, dq, lax.ppermute(dq, X, LAST_TO_SAME))
    dq_cross = lax.ppermute(dq, X, LAST_TO_CROSS) + lax.ppermute(dq, X, LAST_SWAP)

    def split(own, got):
        stat = jnp.sum(
            own[tokens : tokens + 3].astype(F32) + got[tokens : tokens + 3].astype(F32), axis=0
        )
        return own[:tokens], got[:tokens], stat[:, None]

    def latent_terms(dkv):
        own = dot(dkv[0], w_kv, NT)
        return own, [dot(dkv[k], w_kv, NT).astype(BF) for k in (1, 2, 3)]

    own1, terms = latent_terms(dkv)
    got = [
        lax.ppermute(t, X, p)
        for t, p in zip(terms, (LAST_TO_SAME, LAST_TO_CROSS, LAST_SWAP))
    ]
    grad1, o_own, o_send = back(
        *split(dq_same, dq_cross), cotangent, live, h1, rinv1, gain1, wq1, wo
    )

    o_got = lax.ppermute(o_send, X, FIRST_SWAP)
    dq, dkv = attend(slot, gate, q_own, q_got, o_own, o_got, keys, vals, allowed)
    dq_got = lax.ppermute(dq, X, FIRST_SWAP)
    own0, terms = latent_terms(dkv)
    got += [
        lax.ppermute(t, X, p)
        for t, p in zip(terms, (FIRST_TO_SAME, FIRST_TO_CROSS, FIRST_SWAP))
    ]
    (grad0,) = back(*split(dq, dq_got), grad1, jnp.ones_like(live), h, rinv, gain, wq)

    grads = jnp.where(last, grad1, grad0)
    latent_grad = jnp.where(last, own1, own0)
    for term in got:
        latent_grad = latent_grad + term.astype(F32)
    return grads[None], latent_grad.reshape(reports, 48, E)


def solution(mesh):
    fine = Mesh(mesh.devices.reshape(2, 4, 4, 2, 2), ("segment", "z", "y", "core", "mp"))
    return jax.shard_map(
        per_device,
        mesh=fine,
        in_specs=(
            P("segment", DP, "mp"),
            P(DP, "mp"),
            P(DP),
            P("segment", "mp"),
            P("segment"),
            P("segment", "mp", DP),
            P("segment", DP, "mp"),
            P("segment", None, "mp"),
            P("segment", None, "mp"),
            P(DP, None, None),
            P(DP, None),
            P(),
            P(),
            P(),
            P(DP, None, None),
        ),
        out_specs=(P("segment", DP, "mp"), P(DP, X, None)),
        check_vma=False,
    )
```

time: 674 us -> 601 us (0.89)
  Pallas kernels: 0 us -> 357 us
  waiting for transfers between devices: 344 us -> 68.4 us
  matrix products: 98.4 us -> 25.3 us
  starting transfers between devices: 20.7 us -> 78 us
  local copies, waits for them, and re-layouts: 92.1 us -> 35.3 us
  other arithmetic: 57.7 us -> 13.5 us
  blocking collectives: 37.5 us -> 10.8 us
  between operations: 15.3 us -> 2.69 us
    pallas_call x0 -> x9, Pallas kernels: none -> 357 us  [the longest x2 306 us: assemble(): pl.pallas_call(functools.partial(assemble_kernel, kinds), in_specs=[SMEM]...]
    reduce_scatter x4 -> x0, waiting for transfers between devices: 137 us -> none  [the longest x1 88 us: per_device(): lax.psum_scatter(latent_term, ('segment', 'mp'), scatter_dimension=1, til...]
    all_gather x2 -> x0, waiting for transfers between devices: 88.1 us -> none  [the longest x1 88.1 us: per_device(): lax.all_gather(w_query[0], 'dp', axis=1, tiled=True)]
    ppermute x3 -> x48, starting transfers between devices: 3.84 us -> 78 us  [the longest x9 20.1 us: gather_dp(): lax.ppermute(bundle, DP, yz_perm(2, k))]
    dot_general x25 -> x9, matrix products: 96.3 us -> 25.3 us  [dot(): return lax.dot_general(a, b, dims, preferred_element_type=F32)]
    psum x1 -> x0, waiting for transfers between devices: 55.1 us -> none  [per_device(): lax.psum(jnp.dot(normalized_rows, query_rows, preferred_element_type=jnp....]
    all_gather x3 -> x1, blocking collectives: 31.1 us -> 4.39 us  [per_device(): both = lax.all_gather(jnp.concatenate([squares, norm_gain[0]]), 'segment')]
    transpose x1 -> x0, local copies, waits for them, and re-layouts: 22.5 us -> none  [pool_slides(): jnp.einsum('...hlt,...thd->...lhd', weights, keys, preferred_element_type...]
  transfers between devices with their start and end apart: 12 -> 48, of which waited for: 9 -> 13; matrix products, arithmetic and copies ran while one was open for 26% -> 9% of each run, Pallas kernels for 0% -> 60%
where the time goes in v1:
time: 601 us; the launch traced here: 591 us
  Pallas kernels  357 us (59%)
  starting transfers between devices  78 us (13%)
  waiting for transfers between devices  68.4 us (11%)
  local copies, waits for them, and re-layouts  35.3 us (6%)
  matrix products  25.3 us (4%)
  other arithmetic  13.5 us (2%)
  blocking collectives  10.8 us (2%)
    pallas_call x2, Pallas kernels, assemble(): pl.pallas_call(functools.partial(assemble_kernel, kinds), in_specs=[SMEM]...  306 us
    dot_general x9, matrix products, dot(): return lax.dot_general(a, b, dims, preferred_element_type=F32)  25.3 us
    ppermute x9, starting transfers between devices, gather_dp(): lax.ppermute(bundle, DP, yz_perm(2, k))  20.1 us
    pallas_call x2, Pallas kernels, attend(): pl.pallas_call(attend_kernel, grid=(reports,), in_specs=[SMEM, SMEM, toke...  19.6 us
    unnamed x106, local copies, waits for them, and re-layouts  17 us
    ppermute x1, waiting for transfers between devices, per_device(): lax.ppermute(dq, X, LAST_TO_CROSS) + lax.ppermute(dq, X, LAST_SWAP)  15.6 us
    ppermute x1, waiting for transfers between devices, per_device(): dq_same = jnp.where(last, dq, lax.ppermute(dq, X, LAST_TO_SAME))  15.4 us
    ppermute x6, starting transfers between devices, per_device(): lax.ppermute(t, X, p)  15.3 us
  transfers between devices with their start and end apart: 48, of which 13 were waited for; matrix products, arithmetic and copies ran while one was open for 9% of the time, Pallas kernels for 60%

profile of v1, /device:TPU:0, one launch (start us, length us, event | category | flops | bytes accessed | tf_op | source)
XLA Modules:
  0.0 590.6 jit_solution(7191767227130948240)
XLA Ops:
  3.3 4.3 shard_map.160
  23.3 4.1 collective-permute-start.31
  34.5 5.4 collective-permute-done.32
  53.3 4.9 collective-permute-start.3
  68.6 6.4 %psum.7 = f32[512]{0:T(512)S(1)} all-reduce(f32[512]{0:T(512)S(1)} %multiply_reduce_fusion), channel_id=1, replica_groups=mesh['segment'=2,'z'=4,'y'=4,'core'=2,'mp'=2] {'mp'}, use_global_device_ids=true, to_apply=%region_1.2 | all-reduce | flops 512 | bytes 4096 | tf_op jit(solution)/shard_map/psum | solution.py:429
  75.0 4.4 all-gather.1
  111.6 4.2 collective-permute-start.22
  120.7 81.4 %shard_map.163.wq = bf16[1024,2048]{1,0:T(8,128)(2,1)} custom-call(s32[32]{0:T(128)S(1)} %compare_select_fusion.2.rows, bf16[4,32,2048]{2,1,0:T(8,128)(2,1)S(1)} %copy-done.10, bf16[4,32,2048]{2,1,0:T(8,128)(2,1)} %collective-permute-done.33.refs_1_, bf16[4,32,2048]{2,1,0:T(8,128)(2,1)} %collective-permute-done.34.refs_2_, ...), custom_call_target="tpu_custom_call" | custom-call | tf_op jit(solution)/shard_map/pallas_call | solution.py:148
  202.1 224.6 %shard_map.158 = (bf16[1024,2048]{1,0:T(8,128)(2,1)}, bf16[1024,2048]{1,0:T(8,128)(2,1)}) custom-call(s32[32]{0:T(128)S(1)} %compare_select_fusion.2.rows, bf16[4,64,2048]{2,1,0:T(8,128)(2,1)S(1)} %copy-done.6, bf16[4,64,2048]{2,1,0:T(8,128)(2,1)} %collective-permute-done.3.refs_1_, bf16[4,64,2048]{2,1,0:T(8,128)(2,1)} %collective-permute-done.4.refs_2_, ...), custom_call_target="tpu_custom_call" | custom-call | tf_op jit(solution)/shard_map/pallas_call | solution.py:148
  426.7 9.2 %shard_map.159 = (f32[512,512]{1,0:T(8,128)S(1)}, bf16[512,512]{1,0:T(8,128)(2,1)S(1)}, bf16[512,512]{1,0:T(8,128)(2,1)S(1)}, bf16[512,512]{1,0:T(8,128)(2,1)S(1)}) custom-call(bf16[512,2048]{1,0:T(8,128)(2,1)S(1)} %bitcast.148, f32[512,1]{1,0:T(8,128)S(1)} %copy-done.13, f32[1,2048]{1,0:T(1,128)S(1)} %copy-done.35, bf16[512,2048]{1,0:T(8,128)(2,1)} %up.1, ...), custom_call_target="tpu_custom_call" | custom-call | flops 4294967296 | bytes 14680064 | tf_op jit(solution)/shard_map/pallas_call | solution.py:226
  438.4 4.6 fusion.21
  443.1 7.8 %collective-permute-done.10.q_got = bf16[512,512]{1,0:T(8,128)(2,1)S(1)} collective-permute-done((bf16[512,512]{1,0:T(8,128)(2,1)S(1)}, bf16[512,512]{1,0:T(8,128)(2,1)S(1)}, u32[]{:S(2)}, u32[]{:S(2)}) %collective-permute-start.10) | collective-permute-done | bytes 524320 | tf_op jit(solution)/shard_map/ppermute | solution.py:454
  450.9 9.8 %shard_map.162 = (bf16[528,512]{1,0:T(8,128)(2,1)S(1)}, bf16[4,192,1024]{2,1,0:T(8,128)(2,1)}) custom-call(s32[4]{0:T(128)S(1)} %pad_add_fusion.slot, f32[1]{0:T(128)S(6)} %tanh.3.gate, f32[512,512]{1,0:T(8,128)S(1)} %get-tuple-element.17.q_own, bf16[512,512]{1,0:T(8,128)(2,1)S(1)} %collective-permute-done.10.q_got, ...), custom_call_target="tpu_custom_call" | custom-call | flops 503316480 | bytes 6291456 | tf_op jit(solution)/shard_map/pallas_call | solution.py:287
  469.9 15.6 %collective-permute-done.26 = bf16[528,512]{1,0:T(8,128)(2,1)S(1)} collective-permute-done((bf16[528,512]{1,0:T(8,128)(2,1)S(1)}, bf16[528,512]{1,0:T(8,128)(2,1)S(1)}, u32[]{:S(2)}, u32[]{:S(2)}) %collective-permute-start.26) | collective-permute-done | bytes 540704 | tf_op jit(solution)/shard_map/ppermute | solution.py:458
  486.5 15.4 %collective-permute-done.25 = bf16[528,512]{1,0:T(8,128)(2,1)S(1)} collective-permute-done((bf16[528,512]{1,0:T(8,128)(2,1)S(1)}, bf16[528,512]{1,0:T(8,128)(2,1)S(1)}, u32[]{:S(2)}, u32[]{:S(2)}) %collective-permute-start.25) | collective-permute-done | bytes 540704 | tf_op jit(solution)/shard_map/ppermute | solution.py:457
  508.7 8.7 %shard_map.164 = (bf16[512,2048]{1,0:T(8,128)(2,1)S(1)}, bf16[512,512]{1,0:T(8,128)(2,1)S(1)}, bf16[512,512]{1,0:T(8,128)(2,1)S(1)}) custom-call(bf16[512,512]{1,0:T(8,128)(2,1)S(1)} %copy-done.19, bf16[512,512]{1,0:T(8,128)(2,1)S(1)} %copy-done.18, f32[512,1]{1,0:T(8,128)S(1)} %copy-done.33, bf16[512,2048]{1,0:T(8,128)(2,1)} %up.1, ...), custom_call_target="tpu_custom_call" | custom-call | flops 4294967296 | bytes 14680064 | tf_op jit(solution)/shard_map/pallas_call | solution.py:354
  517.4 5.8 collective-permute-start.40
  530.4 9.8 %shard_map.165 = (bf16[528,512]{1,0:T(8,128)(2,1)S(1)}, bf16[4,192,1024]{2,1,0:T(8,128)(2,1)}) custom-call(s32[4]{0:T(128)S(1)} %pad_add_fusion.slot, f32[1]{0:T(128)S(6)} %tanh.3.gate, f32[512,512]{1,0:T(8,128)S(1)} %copy-done.4, bf16[512,512]{1,0:T(8,128)(2,1)S(1)} %copy-done.8, bf16[512,512]{1,0:T(8,128)(2,1)S(1)} %get-tuple-element.23.o_own, ...), custom_call_target="tpu_custom_call" | custom-call | flops 503316480 | bytes 6291456 | tf_op jit(solution)/shard_map/pallas_call | solution.py:287
  545.4 5.4 collective-permute-start.41
  558.9 4.7 collective-permute-done.41
  567.0 5.5 shard_map.166
  572.5 5.1 collective-permute-start.47
  579.2 6.8 %collective-permute-done.47 = bf16[192,1536]{1,0:T(8,128)(2,1)S(1)} collective-permute-done((bf16[192,1536]{1,0:T(8,128)(2,1)S(1)}, bf16[192,1536]{1,0:T(8,128)(2,1)S(1)}, u32[]{:S(2)}, u32[]{:S(2)}) %collective-permute-start.47) | collective-permute-done | bytes 589856 | tf_op jit(solution)/shard_map/ppermute | solution.py:484
  586.1 4.3 fusion.13
  (247 shorter events, 130.0 us)
Async XLA Ops:
  27.5 16.4 %collective-permute-start.15 = (bf16[4,128,384]{2,1,0:T(8,128)(2,1)S(1)}, bf16[4,128,384]{2,1,0:T(8,128)(2,1)S(1)}, u32[]{:S(2)}, u32[]{:S(2)}) collective-permute-start(bf16[4,128,384]{2,1,0:T(8,128)(2,1)S(1)} %pad_maximum_fusion.3.refs_0_), channel_id=1, source_target_pairs={{0,16},{2,6},{4,20},{6,10},{8,24},{10,14},{12,28},{14,2},{16,32},{... | collective-permute-start | bytes 1179656 | tf_op jit(solution)/shard_map/ppermute | solution.py:107
  28.6 18.9 %collective-permute-start.16 = (bf16[4,128,384]{2,1,0:T(8,128)(2,1)S(1)}, bf16[4,128,384]{2,1,0:T(8,128)(2,1)S(1)}, u32[]{:S(2)}, u32[]{:S(2)}) collective-permute-start(bf16[4,128,384]{2,1,0:T(8,128)(2,1)S(1)} %pad_maximum_fusion.3.refs_0_), channel_id=1, source_target_pairs={{0,32},{2,10},{4,36},{6,14},{8,40},{10,2},{12,44},{14,6},{16,48},{... | collective-permute-start | bytes 1179656 | tf_op jit(solution)/shard_map/ppermute | solution.py:107
  32.1 16.4 %collective-permute-start.17 = (bf16[4,128,384]{2,1,0:T(8,128)(2,1)S(1)}, bf16[4,128,384]{2,1,0:T(8,128)(2,1)}, u32[]{:S(2)}, u32[]{:S(2)}) collective-permute-start(bf16[4,128,384]{2,1,0:T(8,128)(2,1)S(1)} %pad_maximum_fusion.3.refs_0_), channel_id=1, source_target_pairs={{0,48},{2,14},{4,52},{6,2},{8,56},{10,6},{12,60},{14,10},{16,0},{1... | collective-permute-start | bytes 1179656 | tf_op jit(solution)/shard_map/ppermute | solution.py:107
  43.9 16.6 %collective-permute-start.34 = (bf16[4,32,2048]{2,1,0:T(8,128)(2,1)S(1)}, bf16[4,32,2048]{2,1,0:T(8,128)(2,1)}, u32[]{:S(2)}, u32[]{:S(2)}) collective-permute-start(bf16[4,32,2048]{2,1,0:T(8,128)(2,1)S(1)} %pad_maximum_fusion.2.refs_0_), channel_id=1, source_target_pairs={{0,32},{2,10},{4,36},{6,14},{8,40},{10,2},{12,44},{14,6},{16,48},{... | collective-permute-start | bytes 1572872 | tf_op jit(solution)/shard_map/ppermute | solution.py:107
  53.3 30.3 %collective-permute-start.3 = (bf16[4,64,2048]{2,1,0:T(8,128)(2,1)S(1)}, bf16[4,64,2048]{2,1,0:T(8,128)(2,1)}, u32[]{:S(2)}, u32[]{:S(2)}) collective-permute-start(bf16[4,64,2048]{2,1,0:T(8,128)(2,1)S(1)} %pad_maximum_fusion.1.refs_0_), channel_id=1, source_target_pairs={{0,16},{2,6},{4,20},{6,10},{8,24},{10,14},{12,28},{14,2},{16,32},{... | collective-permute-start | bytes 3145736 | tf_op jit(solution)/shard_map/ppermute | solution.py:107
  60.5 24.4 %collective-permute-start.4 = (bf16[4,64,2048]{2,1,0:T(8,128)(2,1)S(1)}, bf16[4,64,2048]{2,1,0:T(8,128)(2,1)}, u32[]{:S(2)}, u32[]{:S(2)}) collective-permute-start(bf16[4,64,2048]{2,1,0:T(8,128)(2,1)S(1)} %pad_maximum_fusion.1.refs_0_), channel_id=1, source_target_pairs={{0,32},{2,10},{4,36},{6,14},{8,40},{10,2},{12,44},{14,6},{16,48},{... | collective-permute-start | bytes 3145736 | tf_op jit(solution)/shard_map/ppermute | solution.py:107
  60.8 25.7 %collective-permute-start.5 = (bf16[4,64,2048]{2,1,0:T(8,128)(2,1)S(1)}, bf16[4,64,2048]{2,1,0:T(8,128)(2,1)}, u32[]{:S(2)}, u32[]{:S(2)}) collective-permute-start(bf16[4,64,2048]{2,1,0:T(8,128)(2,1)S(1)} %pad_maximum_fusion.1.refs_0_), channel_id=1, source_target_pairs={{0,48},{2,14},{4,52},{6,2},{8,56},{10,6},{12,60},{14,10},{16,0},{1... | collective-permute-start | bytes 3145736 | tf_op jit(solution)/shard_map/ppermute | solution.py:107
  64.2 22.8 %collective-permute-start.6 = (bf16[4,64,2048]{2,1,0:T(8,128)(2,1)S(1)}, bf16[4,64,2048]{2,1,0:T(8,128)(2,1)}, u32[]{:S(2)}, u32[]{:S(2)}) collective-permute-start(bf16[4,64,2048]{2,1,0:T(8,128)(2,1)S(1)} %pad_maximum_fusion.1.refs_0_), channel_id=1, source_target_pairs={{0,2},{2,0},{1,3},{3,1},{4,6},{6,4},{5,7},{7,5},{8,10},{10,8},{9,1... | collective-permute-start | bytes 3145736 | tf_op jit(solution)/shard_map/ppermute | solution.py:108
  83.4 17.7 %collective-permute-start.37 = (bf16[4,32,2048]{2,1,0:T(8,128)(2,1)}, bf16[4,32,2048]{2,1,0:T(8,128)(2,1)}, u32[]{:S(2)}, u32[]{:S(2)}) collective-permute-start(bf16[4,32,2048]{2,1,0:T(8,128)(2,1)} %collective-permute-done.33.refs_1_), channel_id=1, source_target_pairs={{0,2},{2,0},{1,3},{3,1},{4,6},{6,4},{5,7},{7,5},{8,10},{10,8},{9,1... | collective-permute-start | bytes 1572872 | tf_op jit(solution)/shard_map/ppermute | solution.py:108
  83.6 32.2 %collective-permute-start.7 = (bf16[4,64,2048]{2,1,0:T(8,128)(2,1)}, bf16[4,64,2048]{2,1,0:T(8,128)(2,1)}, u32[]{:S(2)}, u32[]{:S(2)}) collective-permute-start(bf16[4,64,2048]{2,1,0:T(8,128)(2,1)} %collective-permute-done.3.refs_1_), channel_id=1, source_target_pairs={{0,2},{2,0},{1,3},{3,1},{4,6},{6,4},{5,7},{7,5},{8,10},{10,8},{9,1... | collective-permute-start | bytes 3145736 | tf_op jit(solution)/shard_map/ppermute | solution.py:108
  84.9 33.9 %collective-permute-start.8 = (bf16[4,64,2048]{2,1,0:T(8,128)(2,1)}, bf16[4,64,2048]{2,1,0:T(8,128)(2,1)}, u32[]{:S(2)}, u32[]{:S(2)}) collective-permute-start(bf16[4,64,2048]{2,1,0:T(8,128)(2,1)} %collective-permute-done.4.refs_2_), channel_id=1, source_target_pairs={{0,2},{2,0},{1,3},{3,1},{4,6},{6,4},{5,7},{7,5},{8,10},{10,8},{9,1... | collective-permute-start | bytes 3145736 | tf_op jit(solution)/shard_map/ppermute | solution.py:108
  87.0 115.0 %collective-permute-start.9 = (bf16[4,64,2048]{2,1,0:T(8,128)(2,1)}, bf16[4,64,2048]{2,1,0:T(8,128)(2,1)}, u32[]{:S(2)}, u32[]{:S(2)}) collective-permute-start(bf16[4,64,2048]{2,1,0:T(8,128)(2,1)} %collective-permute-done.5.refs_3_), channel_id=1, source_target_pairs={{0,2},{2,0},{1,3},{3,1},{4,6},{6,4},{5,7},{7,5},{8,10},{10,8},{9,1... | collective-permute-start | bytes 3145736 | tf_op jit(solution)/shard_map/ppermute | solution.py:108
  101.7 362.3 %collective-permute-start.28 = (bf16[512,2048]{1,0:T(8,128)(2,1)S(1)}, bf16[512,2048]{1,0:T(8,128)(2,1)S(1)}, u32[]{:S(2)}, u32[]{:S(2)}) collective-permute-start(bf16[512,2048]{1,0:T(8,128)(2,1)S(1)} %bitcast.147), channel_id=1, source_target_pairs={{64,0},{65,1},{66,2},{67,3},{68,4},{69,5},{70,6},{71,7},{72,8},{73... | collective-permute-start | bytes 6291464 | tf_op jit(solution)/shard_map/ppermute | solution.py:437
  111.6 325.9 %collective-permute-start.22 = (bf16[768,384]{1,0:T(8,128)(2,1)S(1)}, bf16[768,384]{1,0:T(8,128)(2,1)S(1)}, u32[]{:S(2)}, u32[]{:S(2)}) collective-permute-start(bf16[768,384]{1,0:T(8,128)(2,1)S(1)} %shard_map.161), channel_id=1, source_target_pairs={{0,64},{64,1},{1,65},{65,0},{2,66},{66,3},{3,67},{67,2},{4,68},{68... | collective-permute-start | bytes 1769480 | tf_op jit(solution)/shard_map/ppermute | solution.py:413
  115.8 322.6 %collective-permute-start.23 = (bf16[768,384]{1,0:T(8,128)(2,1)S(1)}, bf16[768,384]{1,0:T(8,128)(2,1)}, u32[]{:S(2)}, u32[]{:S(2)}) collective-permute-start(bf16[768,384]{1,0:T(8,128)(2,1)S(1)} %shard_map.161), channel_id=1, source_target_pairs={{0,1},{64,65},{1,0},{65,64},{2,3},{66,67},{3,2},{67,66},{4,5},{68,... | collective-permute-start | bytes 1769480 | tf_op jit(solution)/shard_map/ppermute | solution.py:413
  118.8 319.6 %collective-permute-start.24 = (bf16[768,384]{1,0:T(8,128)(2,1)S(1)}, bf16[768,384]{1,0:T(8,128)(2,1)}, u32[]{:S(2)}, u32[]{:S(2)}) collective-permute-start(bf16[768,384]{1,0:T(8,128)(2,1)S(1)} %shard_map.161), channel_id=1, source_target_pairs={{0,65},{64,0},{1,64},{65,1},{2,67},{66,2},{3,66},{67,3},{4,69},{68... | collective-permute-start | bytes 1769480 | tf_op jit(solution)/shard_map/ppermute | solution.py:413
  460.7 24.8 %collective-permute-start.26 = (bf16[528,512]{1,0:T(8,128)(2,1)S(1)}, bf16[528,512]{1,0:T(8,128)(2,1)S(1)}, u32[]{:S(2)}, u32[]{:S(2)}) collective-permute-start(bf16[528,512]{1,0:T(8,128)(2,1)S(1)} %get-tuple-element.21), channel_id=1, source_target_pairs={{64,1},{65,0},{66,3},{67,2},{68,5},{69,4},{70,7},{71,6},{72,9},{73... | collective-permute-start | bytes 1622024 | tf_op jit(solution)/shard_map/ppermute | solution.py:458
  462.0 23.5 %collective-permute-start.27 = (bf16[528,512]{1,0:T(8,128)(2,1)S(1)}, bf16[528,512]{1,0:T(8,128)(2,1)S(1)}, u32[]{:S(2)}, u32[]{:S(2)}) collective-permute-start(bf16[528,512]{1,0:T(8,128)(2,1)S(1)} %get-tuple-element.21), channel_id=1, source_target_pairs={{64,65},{65,64},{66,67},{67,66},{68,69},{69,68},{70,71},{71,70},{7... | collective-permute-start | bytes 1622024 | tf_op jit(solution)/shard_map/ppermute | solution.py:458
  462.7 39.2 %collective-permute-start.25 = (bf16[528,512]{1,0:T(8,128)(2,1)S(1)}, bf16[528,512]{1,0:T(8,128)(2,1)S(1)}, u32[]{:S(2)}, u32[]{:S(2)}) collective-permute-start(bf16[528,512]{1,0:T(8,128)(2,1)S(1)} %get-tuple-element.21), channel_id=1, source_target_pairs={{64,0},{65,1},{66,2},{67,3},{68,4},{69,5},{70,6},{71,7},{72,8},{73... | collective-permute-start | bytes 1622024 | tf_op jit(solution)/shard_map/ppermute | solution.py:457
  468.6 103.9 %collective-permute-start.42 = (bf16[192,1536]{1,0:T(8,128)(2,1)}, bf16[192,1536]{1,0:T(8,128)(2,1)}, u32[]{:S(2)}, u32[]{:S(2)}) collective-permute-start(bf16[192,1536]{1,0:T(8,128)(2,1)} %convolution_convert_fusion.5), channel_id=1, source_target_pairs={{64,0},{65,1},{66,2},{67,3},{68,4},{69,5},{70,6},{71,7},{72,8},{73... | collective-permute-start | bytes 1769480 | tf_op jit(solution)/shard_map/ppermute | solution.py:472
  525.2 54.0 %collective-permute-start.43 = (bf16[192,1536]{1,0:T(8,128)(2,1)}, bf16[192,1536]{1,0:T(8,128)(2,1)}, u32[]{:S(2)}, u32[]{:S(2)}) collective-permute-start(bf16[192,1536]{1,0:T(8,128)(2,1)} %convolution_convert_fusion.4), channel_id=1, source_target_pairs={{64,1},{65,0},{66,3},{67,2},{68,5},{69,4},{70,7},{71,6},{72,9},{73... | collective-permute-start | bytes 1769480 | tf_op jit(solution)/shard_map/ppermute | solution.py:472
  528.6 50.6 %collective-permute-start.44 = (bf16[192,1536]{1,0:T(8,128)(2,1)}, bf16[192,1536]{1,0:T(8,128)(2,1)}, u32[]{:S(2)}, u32[]{:S(2)}) collective-permute-start(bf16[192,1536]{1,0:T(8,128)(2,1)} %convolution_convert_fusion.3), channel_id=1, source_target_pairs={{64,65},{65,64},{66,67},{67,66},{68,69},{69,68},{70,71},{71,70},{7... | collective-permute-start | bytes 1769480 | tf_op jit(solution)/shard_map/ppermute | solution.py:472
  545.4 18.2 %collective-permute-start.41 = (bf16[528,512]{1,0:T(8,128)(2,1)S(1)}, bf16[528,512]{1,0:T(8,128)(2,1)S(1)}, u32[]{:S(2)}, u32[]{:S(2)}) collective-permute-start(bf16[528,512]{1,0:T(8,128)(2,1)S(1)} %get-tuple-element.25), channel_id=1, source_target_pairs={{0,1},{1,0},{2,3},{3,2},{4,5},{5,4},{6,7},{7,6},{8,9},{9,8},{10,11... | collective-permute-start | bytes 1622024 | tf_op jit(solution)/shard_map/ppermute | solution.py:481
  550.8 28.5 %collective-permute-start.45 = (bf16[192,1536]{1,0:T(8,128)(2,1)}, bf16[192,1536]{1,0:T(8,128)(2,1)}, u32[]{:S(2)}, u32[]{:S(2)}) collective-permute-start(bf16[192,1536]{1,0:T(8,128)(2,1)} %convolution_convert_fusion.2), channel_id=1, source_target_pairs={{0,64},{1,65},{2,66},{3,67},{4,68},{5,69},{6,70},{7,71},{8,72},{9,... | collective-permute-start | bytes 1769480 | tf_op jit(solution)/shard_map/ppermute | solution.py:484
  (75 other events, 1385.9 us)

commit v2 on v1

v2 whole, which is shorter than its diff:
```python
import functools

import jax
import jax.numpy as jnp
from jax import lax
from jax.experimental import pallas as pl
from jax.experimental.pallas import tpu as pltpu
from jax.sharding import Mesh
from jax.sharding import PartitionSpec as P

MODEL_WIDTH = 4096
E = 1536
HEAD = 128
LAT = 32
SPR = 6
L = 128
QBLK = 32
MAXT = 64
QUARTER = E // 4
SCALE = HEAD ** (-0.5)
DP = ("z", "y", "core")
X = ("segment", "mp")
BF = jnp.bfloat16
F32 = jnp.float32
LIMIT = 60 * 1024 * 1024
NT = (((1,), (1,)), ((), ()))
NN = (((1,), (0,)), ((), ()))
TN = (((0,), (0,)), ((), ()))

SWAP_MP = [(0, 1), (1, 0), (2, 3), (3, 2)]
LAST_TO_SAME = [(2, 0), (3, 1)]
LAST_TO_CROSS = [(2, 1), (3, 0)]
LAST_SWAP = [(2, 3), (3, 2)]
FIRST_TO_SAME = [(0, 2), (1, 3)]
FIRST_TO_CROSS = [(0, 3), (1, 2)]
FIRST_SWAP = [(0, 1), (1, 0)]
AT_X = (0, 2, 1, 3)


def x_perm(k):
    return [(AT_X[x], AT_X[(x + k) % 4]) for x in range(4)]


def yz_perm(stage, k):
    pairs = []
    for z in range(4):
        for y in range(4):
            for core in range(2):
                along_y = (core == 0) == (stage == 1)
                to_z = z if along_y else (z + k) % 4
                to_y = (y + k) % 4 if along_y else y
                pairs.append(((z * 4 + y) * 2 + core, (to_z * 4 + to_y) * 2 + core))
    return pairs


def dot(a, b, dims):
    return lax.dot_general(a, b, dims, preferred_element_type=F32)


def params(**kwargs):
    return pltpu.CompilerParams(vmem_limit_bytes=LIMIT, **kwargs)


def whole(shape):
    return pl.BlockSpec(shape, lambda *_: (0,) * len(shape))


SMEM = pl.BlockSpec(memory_space=pltpu.SMEM)
ANY = pl.BlockSpec(memory_space=pl.ANY)
VMEM = pl.BlockSpec(memory_space=pltpu.VMEM)
TILE = 512


def pool_kernel(which, counts, tiles, queries, out):
    for slide in range(4):
        live = lax.broadcasted_iota(jnp.int32, (LAT, MAXT), 1) < counts[slide]
        for head in range(QUARTER // HEAD):
            cols = slice(head * HEAD, (head + 1) * HEAD)
            tile = tiles[slide, :, cols]
            query = queries[:, cols]
            scores = dot(query, tile, NT) * SCALE
            scores = jnp.where(live, scores, -1e30)
            exps = jnp.exp(scores - jnp.max(scores, axis=1, keepdims=True))
            weights = (exps / jnp.sum(exps, axis=1, keepdims=True)).astype(BF)
            pooled = dot(weights, tile, NN)
            out[slide * LAT : (slide + 1) * LAT, cols] = (query.astype(F32) + pooled).astype(BF)


def pool(which, counts, tiles, queries):
    return pl.pallas_call(
        pool_kernel,
        grid_spec=pltpu.PrefetchScalarGridSpec(
            num_scalar_prefetch=2,
            grid=(1,),
            in_specs=[
                pl.BlockSpec((4, MAXT, QUARTER), lambda i, which, counts: (0, 0, which[0])),
                pl.BlockSpec((LAT, QUARTER), lambda i, which, counts: (0, which[0])),
            ],
            out_specs=pl.BlockSpec((4 * LAT, QUARTER), lambda i, which, counts: (0, 0)),
        ),
        out_shape=jax.ShapeDtypeStruct((4 * LAT, QUARTER), BF),
        compiler_params=params(),
    )(which, counts, tiles, queries)


def gather_chips(block):
    parts = [block] + [lax.ppermute(block, DP, yz_perm(1, k)) for k in (1, 2, 3)]
    bundle = jnp.stack(parts)
    return [bundle] + [lax.ppermute(bundle, DP, yz_perm(2, k)) for k in (1, 2, 3)]


def places(z, y, core):
    table = []
    for a in range(8):
        c = core if a < 4 else 1 - core
        for k in range(4):
            j = a % 4
            at_z = lax.rem(z - jnp.where(c == 0, j, k) + 4, 4)
            at_y = lax.rem(y - jnp.where(c == 0, k, j) + 4, 4)
            table.append((at_z * 4 + at_y) * 2 + c)
    return jnp.stack(table).astype(jnp.int32)


def select_kernel(wanted, array, block, slide, *refs):
    ins, outs, sems = refs[:4], refs[4:6], refs[6]

    def copy(a, which, i):
        at = which * wanted + i
        return pltpu.make_async_copy(
            ins[a].at[block[at], pl.ds(pl.multiple_of(slide[at] * LAT, LAT), LAT)],
            outs[which].at[pl.ds(i * LAT, LAT)],
            sems.at[at],
        )

    for act in ("start", "wait"):
        for which in range(2):
            for i in range(wanted):
                for a in range(4):

                    @pl.when(array[which * wanted + i] == a)
                    def _():
                        getattr(copy(a, which, i), act)()


def select(array, block, slide, blocks):
    wanted = array.shape[0] // 2
    out = jax.ShapeDtypeStruct((wanted * LAT, QUARTER), BF)
    return pl.pallas_call(
        functools.partial(select_kernel, wanted),
        in_specs=[SMEM] * 3 + [ANY] * 4,
        out_specs=[VMEM, VMEM],
        out_shape=[out, out],
        scratch_shapes=[pltpu.SemaphoreType.DMA((2 * wanted,))],
        compiler_params=params(),
    )(array, block, slide, *blocks)


def column(row):
    return jnp.broadcast_to(row, (HEAD, row.shape[1])).T[:, :1]


def live_tokens(lengths, tokens):
    index = lax.broadcasted_iota(jnp.int32, (tokens, 1), 0)
    parts = [index[r * L : (r + 1) * L] < r * L + lengths[r] for r in range(tokens // L)]
    return jnp.concatenate([p.astype(F32) for p in parts], axis=0) > 0


def project_kernel(kind, rows, lengths, rinv, gain, x, *refs):
    ins, (send, weight, left), (w_v, x_v, sems) = refs[:8], refs[8:11], refs[11:]
    load = pltpu.make_async_copy(x, x_v, sems.at[2])
    load.start()
    half = w_v.shape[0] // 2
    for part in (1, 0):
        for a in range(8):
            for k in range(4):
                at = pl.multiple_of(rows[a * 4 + k], 32)
                group = (at >= half).astype(jnp.int32)

                @pl.when(group == part)
                def _():
                    pltpu.make_async_copy(
                        ins[a].at[k, pl.ds(kind * 32, 32)], w_v.at[pl.ds(at, 32)], sems.at[part]
                    ).start()

    load.wait()
    if kind == 0:
        live = live_tokens(lengths, x_v.shape[0])
        x_v[...] = jnp.where(live, x_v[...].astype(F32), 0.0).astype(BF)
    else:
        x_v[...] = (x_v[...].astype(F32) * column(rinv[...]) * gain[...]).astype(BF)
    store_x = pltpu.make_async_copy(x_v, left, sems.at[2])
    store_x.start()

    def group(part):
        return w_v.at[pl.ds(part * half, half)]

    pltpu.make_async_copy(group(1), group(1), sems.at[1]).wait()
    store1 = pltpu.make_async_copy(group(1), weight.at[pl.ds(half, half)], sems.at[1])
    store1.start()
    send[...] = dot(x_v[...], w_v[half:], NT).astype(BF)
    pltpu.make_async_copy(group(0), group(0), sems.at[0]).wait()
    store0 = pltpu.make_async_copy(group(0), weight.at[pl.ds(0, half)], sems.at[0])
    store0.start()
    store_x.wait()
    store1.wait()
    store0.wait()


def project(kind, rows, lengths, rinv, gain, x, blocks):
    tokens, width = x.shape
    inner = 32 * 32
    return pl.pallas_call(
        functools.partial(project_kernel, kind),
        in_specs=[SMEM, SMEM, VMEM, VMEM, ANY] + [ANY] * 8,
        out_specs=[VMEM, ANY, ANY],
        out_shape=[
            jax.ShapeDtypeStruct((tokens, inner // 2), BF),
            jax.ShapeDtypeStruct((inner, width), BF),
            jax.ShapeDtypeStruct((tokens, width), BF),
        ],
        scratch_shapes=[
            pltpu.VMEM((inner, width), BF),
            pltpu.VMEM((tokens, width), BF),
            pltpu.SemaphoreType.DMA((3,)),
        ],
        compiler_params=params(),
        cost_estimate=pl.CostEstimate(
            flops=tokens * width * inner, bytes_accessed=12 << 20, transcendentals=0
        ),
    )(rows, lengths, rinv, gain, x, *blocks)


def forward_kernel(pattern, q_own, q_got, keys, probs):
    report = pl.program_id(0)
    span = keys.shape[0]
    slide = lax.broadcasted_iota(jnp.int32, (QBLK, span), 1) // LAT
    masks = []
    for block in range(L // QBLK):
        seen = jnp.zeros((QBLK, span), jnp.int32)
        for j in range(SPR):
            seen = jnp.where(slide == j, pattern[(report * (L // QBLK) + block) * SPR + j], seen)
        masks.append(seen)
    mask = jnp.concatenate(masks, axis=0) == 1
    for head in range(probs.shape[0]):
        cols = slice(head * HEAD, (head + 1) * HEAD)
        qb = (q_own[:, cols] + q_got[:, cols].astype(F32)).astype(BF)
        scores = jnp.where(mask, dot(qb, keys[:, cols], NT) * SCALE, -1e30)
        exps = jnp.exp(scores - jnp.max(scores, axis=1, keepdims=True))
        probs[head] = exps / jnp.sum(exps, axis=1, keepdims=True)


def forward(pattern, q_own, q_got, kv):
    tokens, local = q_own.shape
    reports = tokens // L
    span = kv.shape[0] // reports
    heads = local // HEAD
    token = pl.BlockSpec((L, local), lambda i: (i, 0))
    return pl.pallas_call(
        forward_kernel,
        grid=(reports,),
        in_specs=[SMEM, token, token, pl.BlockSpec((span, local), lambda i: (i, 0))],
        out_specs=pl.BlockSpec((heads, L, span), lambda i: (0, i, 0)),
        out_shape=jax.ShapeDtypeStruct((heads, tokens, span), F32),
        compiler_params=params(),
        cost_estimate=pl.CostEstimate(
            flops=2 * tokens * span * local, bytes_accessed=6 << 20, transcendentals=tokens * span * 4
        ),
    )(pattern, q_own, q_got, kv)


def backward_kernel(slot, gate, q_own, q_got, o_own, o_got, keys, vals, probs, dq_out, dkv_out):
    report = pl.program_id(0)
    rows = pl.ds(pl.multiple_of(report * L, L), L)
    local = q_own.shape[1]
    stat = jnp.zeros((L, HEAD), F32)
    for head in range(local // HEAD):
        cols = slice(head * HEAD, (head + 1) * HEAD)
        q = q_own[:, cols] + q_got[:, cols].astype(F32)
        qb = q.astype(BF)
        og = (gate[0] * (o_own[:, cols].astype(F32) + o_got[:, cols].astype(F32))).astype(BF)
        key = keys[:, cols]
        prob = probs[head]
        dprob = dot(og, vals[:, cols], NT)
        rowdot = jnp.sum(prob * dprob, axis=1, keepdims=True)
        dscore = (prob * (dprob - rowdot)).astype(BF)
        dq = (dot(dscore, key, NN) * SCALE).astype(BF)
        dkey = (dot(dscore, qb, TN) * SCALE).astype(BF)
        dval = dot(prob.astype(BF), og, TN).astype(BF)
        dq_out[rows, cols] = dq
        stat += q * dq.astype(F32)
        for part in range(4):
            into = pl.ds(pl.multiple_of(report * 48, 16), 48)
            piece = slice(part * 48, (part + 1) * 48)
            dkv_out[slot[part], into, cols] = dkey[piece]
            dkv_out[slot[part], into, local + head * HEAD : local + (head + 1) * HEAD] = dval[piece]
    total = jnp.sum(stat.T, axis=0, keepdims=True)
    high = total.astype(BF)
    rest = total - high.astype(F32)
    low = rest.astype(BF)
    lower = (rest - low.astype(F32)).astype(BF)
    zero = jnp.zeros((13, L), F32)
    extra = jnp.concatenate([high.astype(F32), low.astype(F32), lower.astype(F32), zero], axis=0)
    dq_out[4 * L : 4 * L + 16, rows] = extra.astype(BF)


def backward(slot, gate, q_own, q_got, o_own, o_got, kv, probs):
    tokens, local = q_own.shape
    reports = tokens // L
    heads, _, span = probs.shape
    token = pl.BlockSpec((L, local), lambda i: (i, 0))
    return pl.pallas_call(
        backward_kernel,
        grid=(reports,),
        in_specs=[SMEM, SMEM, token, token, token, token]
        + [
            pl.BlockSpec((span, local), lambda i: (i, 0)),
            pl.BlockSpec((span, local), lambda i: (i, 1)),
            pl.BlockSpec((heads, L, span), lambda i: (0, i, 0)),
        ],
        out_specs=[whole((tokens + 16, local)), whole((4, reports * 48, 2 * local))],
        out_shape=[
            jax.ShapeDtypeStruct((tokens + 16, local), BF),
            jax.ShapeDtypeStruct((4, reports * 48, 2 * local), BF),
        ],
        compiler_params=params(),
        cost_estimate=pl.CostEstimate(
            flops=8 * tokens * span * local, bytes_accessed=8 << 20, transcendentals=0
        ),
    )(slot, gate, q_own, q_got, o_own, o_got, kv, kv, probs)


def back_kernel(following, info, lengths, dq_own, dq_got, rinv, gain, up, h, wq, *refs):
    if following:
        wo, grad, o_send, wq_v, up_v, h_v, wo_v, sems = refs
    else:
        grad, wq_v, up_v, h_v, sems = refs
    inner, width = wq_v.shape
    half = inner // 2
    tokens = up_v.shape[0]
    tiles = width // TILE

    def copies(tile):
        cols = slice(tile * TILE, (tile + 1) * TILE)
        out = []
        for part in range(2):
            at = pl.multiple_of(info[1 + part], half)
            into = slice(part * half, (part + 1) * half)
            out.append((wq.at[pl.ds(at, half), cols], wq_v.at[into, cols]))
        out.append((up.at[:, cols], up_v.at[:, cols]))
        out.append((h.at[:, cols], h_v.at[:, cols]))
        return [
            pltpu.make_async_copy(a, b, sems.at[tile * 4 + i]) for i, (a, b) in enumerate(out)
        ]

    for tile in range(tiles):
        for copy in copies(tile):
            copy.start()
    if following:
        load = pltpu.make_async_copy(wo.at[pl.ds(half, half)], wo_v, sems.at[tiles * 4])
        load.start()
    stat = column(
        jnp.sum(dq_own[tokens:].astype(F32) + dq_got[tokens:].astype(F32), axis=0, keepdims=True)
    )
    scale = column(rinv[...])
    share = scale * scale * stat / MODEL_WIDTH
    if following:
        live = live_tokens(lengths, tokens)
    stores = []
    for tile in range(tiles):
        for copy in copies(tile):
            copy.wait()
        cols = slice(tile * TILE, (tile + 1) * TILE)
        dnormed = dot(dq_own[:tokens], wq_v[:half, cols], NN)
        dnormed += dot(dq_got[:tokens], wq_v[half:, cols], NN)
        upstream = up_v[:, cols].astype(F32)
        if following:
            upstream = jnp.where(live, upstream, 0.0)
        value = upstream + (scale * (gain[:, cols] * dnormed) - h_v[:, cols].astype(F32) * share)
        if following:
            value = jnp.where(info[0] == 1, upstream, value)
        up_v[:, cols] = value.astype(BF)
        store = pltpu.make_async_copy(up_v.at[:, cols], grad.at[:, cols], sems.at[tile * 4])
        store.start()
        stores.append(store)
    if following:
        load.wait()
        o_send[...] = dot(up_v[...], wo_v[...], NT).astype(BF)
    for store in stores:
        store.wait()


def back(info, lengths, dq_own, dq_got, rinv, gain, up, h, wq, wo=None):
    tokens, width = h.shape
    inner = wq.shape[0]
    half = inner // 2
    inputs = [info, lengths, dq_own, dq_got, rinv, gain, up, h, wq]
    in_specs = [SMEM, SMEM, VMEM, VMEM, VMEM, VMEM, ANY, ANY, ANY]
    out_specs = [ANY]
    out_shape = [jax.ShapeDtypeStruct((tokens, width), BF)]
    scratch = [pltpu.VMEM((inner, width), BF)] + [pltpu.VMEM((tokens, width), BF)] * 2
    if wo is not None:
        inputs.append(wo)
        in_specs.append(ANY)
        out_specs.append(VMEM)
        out_shape.append(jax.ShapeDtypeStruct((tokens, half), BF))
        scratch.append(pltpu.VMEM((half, width), BF))
    return pl.pallas_call(
        functools.partial(back_kernel, wo is not None),
        in_specs=in_specs,
        out_specs=out_specs,
        out_shape=out_shape,
        scratch_shapes=scratch + [pltpu.SemaphoreType.DMA((width // TILE * 4 + 1,))],
        compiler_params=params(),
        cost_estimate=pl.CostEstimate(
            flops=(3 if wo is not None else 2) * tokens * width * inner,
            bytes_accessed=12 << 20,
            transcendentals=0,
        ),
    )(*inputs)


def term_kernel(dkv, w_kv, own, *terms):
    for k in range(4):
        value = dot(dkv[k], w_kv[...], NT)
        if k == 0:
            own[...] = value
        else:
            terms[k - 1][...] = value.astype(BF)


def latent_terms(dkv, w_kv):
    rows, inner = dkv.shape[1:]
    features = w_kv.shape[0]
    tile = features // 3
    result = pl.BlockSpec((rows, tile), lambda i: (0, i))
    return pl.pallas_call(
        term_kernel,
        grid=(features // tile,),
        in_specs=[whole(dkv.shape), pl.BlockSpec((tile, inner), lambda i: (i, 0))],
        out_specs=[result] * 4,
        out_shape=[jax.ShapeDtypeStruct((rows, features), t) for t in (F32, BF, BF, BF)],
        compiler_params=params(),
        cost_estimate=pl.CostEstimate(
            flops=8 * rows * inner * features, bytes_accessed=8 << 20, transcendentals=0
        ),
    )(dkv, w_kv)


def per_device(
    segment_inputs,
    cotangent,
    report_lengths,
    norm_gain,
    attn_gate,
    w_query,
    w_out,
    w_key,
    w_value,
    tiles,
    tile_counts,
    lat_query,
    request_source,
    request_slide,
    cross_pattern,
):
    z, y, core = (lax.axis_index(name) for name in DP)
    me_dp = (z * 4 + y) * 2 + core
    me_mp = lax.axis_index("mp")
    seg = lax.axis_index("segment")
    me_x = me_mp * 2 + seg
    last = seg == 1
    reports = cross_pattern.shape[0]
    wanted = reports * SPR
    h = segment_inputs[0]
    tokens, width = h.shape
    half = 512

    wq_t = w_query[0].T
    h1 = lax.ppermute(h, "segment", [(1, 0)])
    wq1 = lax.all_gather(lax.ppermute(wq_t, "segment", [(1, 0)]), DP, axis=0, tiled=True)

    pooled = pool(me_x.reshape(1).astype(jnp.int32), tile_counts.reshape(4), tiles, lat_query)
    lat_blocks = gather_chips(pooled)
    pair = me_dp - core
    sources = request_source.reshape(32, wanted)
    slides = request_slide.reshape(32, wanted)
    order = jnp.stack([me_dp, me_dp + 1 - 2 * core])
    source = sources[order]
    slide = slides[order].reshape(-1)
    source_core = source % 2
    far_z = lax.rem(z - source // 8 + 4, 4)
    far_y = lax.rem(y - source // 2 % 4 + 4, 4)
    first = jnp.where(core == 0, far_y, far_z)
    second = jnp.where(core == 0, far_z, far_y)
    array = jnp.where(source_core == core, second, 4)
    near, across = select(array.reshape(-1), first.reshape(-1), slide, lat_blocks)
    crossed = lax.ppermute(across, "core", [(0, 1), (1, 0)])
    is_near = jnp.repeat(source_core[0] == core, LAT)[:, None]
    chosen = jnp.where(is_near, near, crossed)
    latents = jnp.concatenate(
        [chosen] + [lax.ppermute(chosen, X, x_perm(k)) for k in (1, 2, 3)], axis=1
    )
    w_kv = jnp.concatenate([w_key[0], w_value[0]], axis=1)
    w_kv_x = jnp.concatenate(
        [
            lax.dynamic_slice_in_dim(w_kv, lax.rem(me_x - k + 4, 4) * QUARTER, QUARTER, 0)
            for k in range(4)
        ],
        axis=0,
    )
    kv = dot(latents, w_kv_x, NN).astype(BF)

    blocks = gather_chips(jnp.concatenate([w_out[0], wq_t], axis=0))
    blocks = blocks + [lax.ppermute(b, "core", [(0, 1), (1, 0)]) for b in blocks]
    rows = lax.rem(places(z, y, core) * 32 - me_mp * half + 2 * half, 2 * half)

    h32 = h.astype(F32)
    message = jnp.concatenate([jnp.sum(h32 * h32, axis=1), norm_gain[0]])
    messages = lax.all_gather(message, X)
    squares = messages[:, :tokens].reshape(2, 2, tokens).sum(axis=1)
    rinvs = lax.rsqrt(squares / MODEL_WIDTH + 1e-05)
    rinv = lax.dynamic_index_in_dim(rinvs, seg, 0)
    rinv1 = rinvs[1:]
    gain = norm_gain
    gain1 = lax.dynamic_index_in_dim(messages[2:, tokens:], me_mp, 0)
    gate = jnp.tanh(attn_gate)
    slot = []
    for part in range(4):
        same_seg, same_mp = seg == part // 2, me_mp == part % 2
        slot.append(jnp.where(same_seg, jnp.where(same_mp, 0, 3), jnp.where(same_mp, 1, 2)))
    slot = jnp.stack(slot).astype(jnp.int32)
    pattern = cross_pattern.reshape(-1)

    q_send, wq, normed = project(1, rows, report_lengths, rinv, gain, h, blocks)
    q_got = lax.ppermute(q_send, X, SWAP_MP)
    o_send, wo, up1 = project(0, rows, report_lengths, rinv, gain, cotangent, blocks)
    o_got = lax.ppermute(o_send, X, LAST_SWAP)
    q_own = dot(normed, wq[:half], NT)
    o_own = dot(up1, wo[:half], NT).astype(BF)
    probs = forward(pattern, q_own, q_got, kv)
    dq1, dkv1 = backward(slot, gate, q_own, q_got, o_own, o_got, kv, probs)
    dq_same = lax.ppermute(dq1, X, LAST_TO_SAME)
    dq_cross = lax.ppermute(dq1, X, LAST_TO_CROSS)
    info1 = jnp.stack([seg, me_mp * half, (1 - me_mp) * half]).astype(jnp.int32)
    up, o_send = back(
        info1, report_lengths, dq_same, dq_cross, rinv1, gain1, cotangent, h1, wq1, wo
    )
    o_got = lax.ppermute(o_send, X, FIRST_SWAP)
    o_own = dot(up, wo[:half], NT).astype(BF)
    dq1, dkv1, _ = lax.optimization_barrier((dq1, dkv1, o_send))
    dq1_got = lax.ppermute(dq1, X, LAST_SWAP)
    own1, *terms = latent_terms(dkv1, w_kv)
    moves = (LAST_TO_SAME, LAST_TO_CROSS, LAST_SWAP)
    got = [lax.ppermute(t, X, p) for t, p in zip(terms, moves)]

    dq0, dkv0 = backward(slot, gate, q_own, q_got, o_own, o_got, kv, probs)
    dq0_got = lax.ppermute(dq0, X, FIRST_SWAP)
    own0, *terms = latent_terms(dkv0, w_kv)
    moves = (FIRST_TO_SAME, FIRST_TO_CROSS, FIRST_SWAP)
    got += [lax.ppermute(t, X, p) for t, p in zip(terms, moves)]
    dq = jnp.where(last, dq1, dq0)
    dq_got = jnp.where(last, dq1_got, dq0_got)
    info = jnp.array([0, 0, half], jnp.int32)
    (grads,) = back(info, report_lengths, dq, dq_got, rinv, gain, up, h, wq)

    latent_grad = jnp.where(last, own1, own0)
    for term in got:
        latent_grad = latent_grad + term.astype(F32)
    return grads[None], latent_grad.reshape(reports, 48, E)


def solution(mesh):
    fine = Mesh(mesh.devices.reshape(2, 4, 4, 2, 2), ("segment", "z", "y", "core", "mp"))
    return jax.shard_map(
        per_device,
        mesh=fine,
        in_specs=(
            P("segment", DP, "mp"),
            P(DP, "mp"),
            P(DP),
            P("segment", "mp"),
            P("segment"),
            P("segment", "mp", DP),
            P("segment", DP, "mp"),
            P("segment", None, "mp"),
            P("segment", None, "mp"),
            P(DP, None, None),
            P(DP, None),
            P(),
            P(),
            P(),
            P(DP, None, None),
        ),
        out_specs=(P("segment", DP, "mp"), P(DP, X, None)),
        check_vma=False,
    )
```

time: 601 us -> 294 us (0.49); the launches traced: 591 us -> 292 us
  Pallas kernels: 357 us -> 74.3 us
  local copies, waits for them, and re-layouts: 35.3 us -> 6.58 us
  starting transfers between devices: 78 us -> 56.6 us
  waiting for transfers between devices: 68.4 us -> 89.4 us
  between operations: 2.69 us -> 15.3 us
  matrix products: 25.3 us -> 16.8 us
  other arithmetic: 13.5 us -> 20.8 us
    pallas_call x7 -> x9, Pallas kernels: 349 us -> 65 us  [the longest x2 17.8 us: backward(): pl.pallas_call(backward_kernel, grid=(reports,), in_specs=[SMEM, SMEM, to...]
    ppermute x42 -> x29, waiting for transfers between devices: 60.3 us -> 84.8 us  [the longest x1 45.1 us: per_device(): dq_same = lax.ppermute(dq1, X, LAST_TO_SAME)]
    ppermute x42 -> x29, starting transfers between devices: 62.6 us -> 46.1 us  [the longest x6 12.3 us: gather_chips(): lax.ppermute(bundle, DP, yz_perm(2, k))]
    unnamed x106 -> x40, local copies, waits for them, and re-layouts: 17 us -> 2.49 us
    dot_general x9 -> x4, matrix products: 25.3 us -> 16.8 us  [dot(): return lax.dot_general(a, b, dims, preferred_element_type=F32)]
    all_gather x1, blocking collectives: 4.39 us -> 12.6 us  [per_device(): messages = lax.all_gather(message, X)]
    ppermute x1, waiting for transfers between devices: 7.77 us -> 0.52 us  [per_device(): q_got = lax.ppermute(q_send, X, SWAP_MP)]
    psum x1 -> x0, blocking collectives: 6.42 us -> none  [per_device(): squares = lax.psum(jnp.sum(h32 * h32, axis=1), 'mp')]
  transfers between devices with their start and end apart: 48 -> 36, of which waited for: 13 -> 12; matrix products, arithmetic and copies ran while one was open for 9% -> 13% of each run, Pallas kernels for 60% -> 23%
where the time goes in v2:
time: 294 us; the launch traced here: 292 us
  waiting for transfers between devices  89.4 us (30%)
  Pallas kernels  74.3 us (25%)
  starting transfers between devices  56.6 us (19%)
  other arithmetic  20.8 us (7%)
  matrix products  16.8 us (6%)
  between operations  15.3 us (5%)
  blocking collectives  12.6 us (4%)
  local copies, waits for them, and re-layouts  6.58 us (2%)
    ppermute x1, waiting for transfers between devices, per_device(): dq_same = lax.ppermute(dq1, X, LAST_TO_SAME)  45.1 us
    ppermute x6, waiting for transfers between devices, gather_chips(): lax.ppermute(bundle, DP, yz_perm(2, k))  20.3 us
    pallas_call x2, Pallas kernels, backward(): pl.pallas_call(backward_kernel, grid=(reports,), in_specs=[SMEM, SMEM, to...  17.8 us
    dot_general x4, matrix products, dot(): return lax.dot_general(a, b, dims, preferred_element_type=F32)  16.8 us
    pallas_call x2, Pallas kernels, back(): pl.pallas_call(functools.partial(back_kernel, wo is not None), in_specs=i...  15.4 us
    pallas_call x2, Pallas kernels, latent_terms(): pl.pallas_call(term_kernel, grid=(features // tile,), in_specs=[whole(dkv...  14.3 us
    pallas_call x2, Pallas kernels, project(): pl.pallas_call(functools.partial(project_kernel, kind), in_specs=[SMEM, S...  12.8 us
    all_gather x1, blocking collectives, per_device(): messages = lax.all_gather(message, X)  12.6 us
  transfers between devices with their start and end apart: 36, of which 12 were waited for; matrix products, arithmetic and copies ran while one was open for 13% of the time, Pallas kernels for 23%

profile of v2, /device:TPU:0, one launch (start us, length us, event | category | flops | bytes accessed | tf_op | source)
XLA Modules:
  0.0 292.4 jit_solution(3667638296128226506)
XLA Ops:
  8.5 5.8 %collective-permute-done.25 = bf16[32,2048]{1,0:T(8,128)(2,1)S(1)} collective-permute-done((bf16[32,2048]{1,0:T(8,128)(2,1)}, bf16[32,2048]{1,0:T(8,128)(2,1)S(1)}, u32[]{:S(2)}, u32[]{:S(2)}) %collective-permute-start.25) | collective-permute-done | bytes 131104 | tf_op jit(solution)/shard_map/ppermute | solution.py:480
  20.2 6.0 %shard_map.169 = bf16[128,384]{1,0:T(8,128)(2,1)} custom-call(s32[1]{0:T(128)} %bitcast.49.which, s32[4]{0:T(128)} %bitcast.94, bf16[4,64,1536]{2,1,0:T(8,128)(2,1)} %tiles.1, bf16[32,1536]{1,0:T(8,128)(2,1)} %queries.1), custom_call_target="tpu_custom_call" | custom-call | tf_op jit(solution)/shard_map/pallas_call | solution.py:90
  38.9 3.7 %collective-permute-start.16 = (bf16[4,128,384]{2,1,0:T(8,128)(2,1)S(1)}, bf16[4,128,384]{2,1,0:T(8,128)(2,1)}, u32[]{:S(2)}, u32[]{:S(2)}) collective-permute-start(bf16[4,128,384]{2,1,0:T(8,128)(2,1)S(1)} %pad_maximum_fusion.2.refs_0_), channel_id=1, source_target_pairs={{0,32},{2,10},{4,36},{6,14},{8,40},{10,2},{12,44},{14,6},{16,48},{... | collective-permute-start | bytes 1179656 | tf_op jit(solution)/shard_map/ppermute | solution.py:109
  48.5 6.4 %collective-permute-done.16.refs_2_ = bf16[4,128,384]{2,1,0:T(8,128)(2,1)} collective-permute-done((bf16[4,128,384]{2,1,0:T(8,128)(2,1)S(1)}, bf16[4,128,384]{2,1,0:T(8,128)(2,1)}, u32[]{:S(2)}, u32[]{:S(2)}) %collective-permute-start.16) | collective-permute-done | bytes 393248 | tf_op jit(solution)/shard_map/ppermute | solution.py:109
  59.8 12.6 %all-gather.1 = f32[4,1,2560]{2,1,0:T(1,128)S(1)} all-gather(f32[1,1,2560]{2,1,0:T(1,128)S(1)} %reshape.145), channel_id=2, replica_groups=mesh['segment'=2,'z'=4,'y'=4,'core'=2,'mp'=2] {'segment','mp'}, dimensions={0}, use_global_device_ids=true | all-gather | bytes 51200 | tf_op jit(solution)/shard_map/all_gather | solution.py:519
  88.9 11.8 %collective-permute-done.5.refs_3_ = bf16[4,64,2048]{2,1,0:T(8,128)(2,1)} collective-permute-done((bf16[4,64,2048]{2,1,0:T(8,128)(2,1)S(1)}, bf16[4,64,2048]{2,1,0:T(8,128)(2,1)}, u32[]{:S(2)}, u32[]{:S(2)}) %collective-permute-start.5) | collective-permute-done | bytes 1048608 | tf_op jit(solution)/shard_map/ppermute | solution.py:109
  100.7 4.0 %collective-permute-done.21 = bf16[768,384]{1,0:T(8,128)(2,1)} collective-permute-done((bf16[768,384]{1,0:T(8,128)(2,1)}, bf16[768,384]{1,0:T(8,128)(2,1)}, u32[]{:S(2)}, u32[]{:S(2)}) %collective-permute-start.21) | collective-permute-done | bytes 589856 | tf_op jit(solution)/shard_map/ppermute | solution.py:501
  109.9 6.3 %fusion.21.keys.vals = bf16[768,1024]{1,0:T(8,128)(2,1)} fusion(bf16[384,1024]{1,0:T(8,128)(2,1)} %get-tuple-element.56, bf16[384,1024]{1,0:T(8,128)(2,1)} %get-tuple-element.55, bf16[384,1024]{1,0:T(8,128)(2,1)} %get-tuple-element.54, bf16[384,1024]{1,0:T(8,128)(2,1)} %get-tuple-element.53, bf16[768,384]{1,0:T(8,128)(2,1)} %collective-permute-done.21, ...), kind=kOutput, calls=%fused_computation.33 | convolution fusion | flops 2438725632 | bytes 7077888 | tf_op jit(solution)/shard_map/dot_general | solution.py:57
  116.3 6.5 %shard_map.167 = (bf16[512,512]{1,0:T(8,128)(2,1)}, bf16[1024,2048]{1,0:T(8,128)(2,1)}, bf16[512,2048]{1,0:T(8,128)(2,1)}) custom-call(s32[32]{0:T(128)} %compare_select_fusion.9.rows, s32[4]{0:T(128)} %lengths.7, f32[1,512]{1,0:T(1,128)} %get-tuple-element.60.rinv, f32[1,2048]{1,0:T(1,128)} %gain.5, bf16[512,2048]{1,0:T(8,128)(2,1)} %bitcast.75, ...), custom_call_target="tpu_custom_call" | custom-call | flops 1073741824 | bytes 12582912 | tf_op jit(solution)/shard_map/pallas_call | solution.py:212
  123.4 6.3 %shard_map.168 = (bf16[512,512]{1,0:T(8,128)(2,1)}, bf16[1024,2048]{1,0:T(8,128)(2,1)}, bf16[512,2048]{1,0:T(8,128)(2,1)}) custom-call(s32[32]{0:T(128)} %compare_select_fusion.9.rows, s32[4]{0:T(128)} %lengths.7, f32[1,512]{1,0:T(1,128)} %get-tuple-element.60.rinv, f32[1,2048]{1,0:T(1,128)} %gain.5, bf16[512,2048]{1,0:T(8,128)(2,1)} %up.1, ...), custom_call_target="tpu_custom_call" | custom-call | flops 1073741824 | bytes 12582912 | tf_op jit(solution)/shard_map/pallas_call | solution.py:212
  131.2 4.6 %fusion.15.q_own = f32[512,512]{1,0:T(8,128)} fusion(bf16[512,2048]{1,0:T(8,128)(2,1)} %get-tuple-element.26, bf16[1024,2048]{1,0:T(8,128)(2,1)} %get-tuple-element.27.wq), kind=kOutput, calls=%fused_computation.27 | convolution fusion | flops 1073741824 | bytes 5242880 | tf_op jit(solution)/shard_map/dot_general | solution.py:57
  139.3 4.7 %shard_map.171.probs = f32[4,512,192]{2,1,0:T(8,128)} custom-call(s32[96]{0:T(128)} %reshape.126.pattern, f32[512,512]{1,0:T(8,128)} %fusion.15.q_own, bf16[512,512]{1,0:T(8,128)(2,1)} %copy-done.4, bf16[768,1024]{1,0:T(8,128)(2,1)} %fusion.21.keys.vals), custom_call_target="tpu_custom_call" | custom-call | flops 100663296 | bytes 6291456 | tf_op jit(solution)/shard_map/pallas_call | solution.py:258
  144.0 8.9 %shard_map.172 = (bf16[528,512]{1,0:T(8,128)(2,1)}, bf16[4,192,1024]{2,1,0:T(8,128)(2,1)}) custom-call(s32[4]{0:T(128)} %pad_add_fusion.slot, f32[1]{0:T(128)S(6)} %tanh.3.gate, f32[512,512]{1,0:T(8,128)} %fusion.15.q_own, bf16[512,512]{1,0:T(8,128)(2,1)} %copy-done.4, bf16[512,512]{1,0:T(8,128)(2,1)} %fusion.26.o_own, ...), custom_call_target="tpu_custom_call" | custom-call | flops 402653184 | bytes 8388608 | tf_op jit(solution)/shard_map/pallas_call | solution.py:311
  159.8 45.1 %collective-permute-done.22.dq_own = bf16[528,512]{1,0:T(8,128)(2,1)} collective-permute-done((bf16[528,512]{1,0:T(8,128)(2,1)}, bf16[528,512]{1,0:T(8,128)(2,1)}, u32[]{:S(2)}, u32[]{:S(2)}) %collective-permute-start.22) | collective-permute-done | bytes 540704 | tf_op jit(solution)/shard_map/ppermute | solution.py:542
  207.2 8.4 %shard_map.173 = (bf16[512,2048]{1,0:T(8,128)(2,1)}, bf16[512,512]{1,0:T(8,128)(2,1)}) custom-call(s32[3]{0:T(128)} %pad_add_fusion.1.info, s32[4]{0:T(128)} %lengths.7, bf16[528,512]{1,0:T(8,128)(2,1)} %collective-permute-done.22.dq_own, bf16[528,512]{1,0:T(8,128)(2,1)} %collective-permute-done.23.dq_got, f32[1,512]{1,0:T(1,128)} %get-tuple-element.59.rinv, ...), custom_call_target="tpu_custom_call" | custom-call | flops 3221225472 | bytes 12582912 | tf_op jit(solution)/shard_map/pallas_call | solution.py:407
  215.6 3.8 %collective-permute-start.26 = (bf16[512,512]{1,0:T(8,128)(2,1)}, bf16[512,512]{1,0:T(8,128)(2,1)}, u32[]{:S(2)}, u32[]{:S(2)}) collective-permute-start(bf16[512,512]{1,0:T(8,128)(2,1)} %get-tuple-element.36), channel_id=1, source_target_pairs={{0,1},{1,0},{2,3},{3,2},{4,5},{5,4},{6,7},{7,6},{8,9},{9,8},{10,11... | collective-permute-start | bytes 1572872 | tf_op jit(solution)/shard_map/ppermute | solution.py:548
  219.4 7.2 %shard_map.176 = (f32[192,1536]{1,0:T(8,128)}, bf16[192,1536]{1,0:T(8,128)(2,1)}, bf16[192,1536]{1,0:T(8,128)(2,1)}, bf16[192,1536]{1,0:T(8,128)(2,1)}) custom-call(bf16[4,192,1024]{2,1,0:T(8,128)(2,1)} %get-tuple-element.40.dkv, bf16[1536,1024]{1,0:T(8,128)(2,1)} %pad_maximum_fusion.w_kv), custom_call_target="tpu_custom_call" | custom-call | flops 2415919104 | bytes 8388608 | tf_op jit(solution)/shard_map/pallas_call | solution.py:436
  227.3 3.7 %fusion.29.o_own = bf16[512,512]{1,0:T(8,128)(2,1)} fusion(bf16[512,2048]{1,0:T(8,128)(2,1)S(1)} %copy-done.6, bf16[1024,2048]{1,0:T(8,128)(2,1)} %get-tuple-element.30.refs_0_), kind=kOutput, calls=%fused_computation.35 | convolution fusion | flops 1074003968 | bytes 4718592 | tf_op jit(solution)/shard_map/dot_general | solution.py:57
  231.8 8.9 %shard_map.174 = (bf16[528,512]{1,0:T(8,128)(2,1)}, bf16[4,192,1024]{2,1,0:T(8,128)(2,1)}) custom-call(s32[4]{0:T(128)} %pad_add_fusion.slot, f32[1]{0:T(128)S(6)} %tanh.3.gate, f32[512,512]{1,0:T(8,128)} %fusion.15.q_own, bf16[512,512]{1,0:T(8,128)(2,1)} %copy-done.4, bf16[512,512]{1,0:T(8,128)(2,1)} %fusion.29.o_own, ...), custom_call_target="tpu_custom_call" | custom-call | flops 402653184 | bytes 8388608 | tf_op jit(solution)/shard_map/pallas_call | solution.py:311
  240.6 4.0 %collective-permute-start.28 = (bf16[528,512]{1,0:T(8,128)(2,1)}, bf16[528,512]{1,0:T(8,128)(2,1)S(1)}, u32[]{:S(2)}, u32[]{:S(2)}) collective-permute-start(bf16[528,512]{1,0:T(8,128)(2,1)} %get-tuple-element.39), channel_id=1, source_target_pairs={{0,1},{1,0},{2,3},{3,2},{4,5},{5,4},{6,7},{7,6},{8,9},{9,8},{10,11... | collective-permute-start | bytes 1622024 | tf_op jit(solution)/shard_map/ppermute | solution.py:557
  247.3 7.1 %shard_map.177 = (f32[192,1536]{1,0:T(8,128)}, bf16[192,1536]{1,0:T(8,128)(2,1)}, bf16[192,1536]{1,0:T(8,128)(2,1)}, bf16[192,1536]{1,0:T(8,128)(2,1)}) custom-call(bf16[4,192,1024]{2,1,0:T(8,128)(2,1)} %get-tuple-element.42.dkv, bf16[1536,1024]{1,0:T(8,128)(2,1)} %pad_maximum_fusion.w_kv), custom_call_target="tpu_custom_call" | custom-call | flops 2415919104 | bytes 8388608 | tf_op jit(solution)/shard_map/pallas_call | solution.py:436
  257.7 5.6 %collective-permute-start.33 = (bf16[192,1536]{1,0:T(8,128)(2,1)}, bf16[192,1536]{1,0:T(8,128)(2,1)}, u32[]{:S(2)}, u32[]{:S(2)}) collective-permute-start(bf16[192,1536]{1,0:T(8,128)(2,1)} %get-tuple-element.48), channel_id=1, source_target_pairs={{0,65},{1,64},{2,67},{3,66},{4,69},{5,68},{6,71},{7,70},{8,73},{9,... | collective-permute-start | bytes 1769480 | tf_op jit(solution)/shard_map/ppermute | solution.py:560
  267.1 7.0 %shard_map.175 = bf16[512,2048]{1,0:T(8,128)(2,1)} custom-call(s32[3]{0:T(128)} %constant.268.clone.info, s32[4]{0:T(128)} %lengths.7, bf16[528,512]{1,0:T(8,128)(2,1)} %broadcast_select_fusion.2.dq_own, bf16[528,512]{1,0:T(8,128)(2,1)} %broadcast_select_fusion.1.dq_got, f32[1,512]{1,0:T(1,128)} %get-tuple-element.60.rinv, f32[1,2048]{1,0:T(1,128)} %gain.5, ...), custom_call_target="tpu_custom_call" | custom-call | flops 2147483648 | bytes 12582912 | tf_op jit(solution)/shard_map/pallas_call | solution.py:407
  274.1 8.1 %collective-permute-done.30 = bf16[192,1536]{1,0:T(8,128)(2,1)S(1)} collective-permute-done((bf16[192,1536]{1,0:T(8,128)(2,1)}, bf16[192,1536]{1,0:T(8,128)(2,1)S(1)}, u32[]{:S(2)}, u32[]{:S(2)}) %collective-permute-start.30) | collective-permute-done | bytes 589856 | tf_op jit(solution)/shard_map/ppermute | solution.py:554
  (142 shorter events, 80.5 us)
Async XLA Ops:
  7.2 200.0 %all-gather.4.cloned.1.call-start = ((), (), s32[]{:S(2)}) async-start(), calls=%async_computation | async-start | bytes 4325376 | tf_op jit(solution)/shard_map/all_gather | solution.py:480
  16.2 42.2 %collective-permute-start.2 = (bf16[64,2048]{1,0:T(8,128)(2,1)S(1)}, bf16[64,2048]{1,0:T(8,128)(2,1)}, u32[]{:S(2)}, u32[]{:S(2)}) collective-permute-start(bf16[64,2048]{1,0:T(8,128)(2,1)S(1)} %get-tuple-element.58), channel_id=1, source_target_pairs={{0,12},{2,50},{4,0},{6,54},{8,4},{10,58},{12,8},{14,62},{16,28},{1... | collective-permute-start | bytes 786440 | tf_op jit(solution)/shard_map/ppermute | solution.py:107
  19.6 38.8 %collective-permute-start.1 = (bf16[64,2048]{1,0:T(8,128)(2,1)S(1)}, bf16[64,2048]{1,0:T(8,128)(2,1)}, u32[]{:S(2)}, u32[]{:S(2)}) collective-permute-start(bf16[64,2048]{1,0:T(8,128)(2,1)S(1)} %get-tuple-element.58), channel_id=1, source_target_pairs={{0,8},{2,34},{4,12},{6,38},{8,0},{10,42},{12,4},{14,46},{16,24},{1... | collective-permute-start | bytes 786440 | tf_op jit(solution)/shard_map/ppermute | solution.py:107
  38.9 16.0 %collective-permute-start.16 = (bf16[4,128,384]{2,1,0:T(8,128)(2,1)S(1)}, bf16[4,128,384]{2,1,0:T(8,128)(2,1)}, u32[]{:S(2)}, u32[]{:S(2)}) collective-permute-start(bf16[4,128,384]{2,1,0:T(8,128)(2,1)S(1)} %pad_maximum_fusion.2.refs_0_), channel_id=1, source_target_pairs={{0,32},{2,10},{4,36},{6,14},{8,40},{10,2},{12,44},{14,6},{16,48},{... | collective-permute-start | bytes 1179656 | tf_op jit(solution)/shard_map/ppermute | solution.py:109
  58.3 19.7 %collective-permute-start.18 = (bf16[768,384]{1,0:T(8,128)(2,1)}, bf16[768,384]{1,0:T(8,128)(2,1)}, u32[]{:S(2)}, u32[]{:S(2)}) collective-permute-start(bf16[768,384]{1,0:T(8,128)(2,1)} %get-tuple-element.33), channel_id=1, source_target_pairs={{0,2},{2,0},{1,3},{3,1},{4,6},{6,4},{5,7},{7,5},{8,10},{10,8},{9,1... | collective-permute-start | bytes 1769480 | tf_op jit(solution)/shard_map/ppermute | solution.py:497
  59.7 24.3 %collective-permute-start.3 = (bf16[4,64,2048]{2,1,0:T(8,128)(2,1)S(1)}, bf16[4,64,2048]{2,1,0:T(8,128)(2,1)}, u32[]{:S(2)}, u32[]{:S(2)}) collective-permute-start(bf16[4,64,2048]{2,1,0:T(8,128)(2,1)S(1)} %pad_maximum_fusion.1.refs_0_), channel_id=1, source_target_pairs={{0,16},{2,6},{4,20},{6,10},{8,24},{10,14},{12,28},{14,2},{16,32},{... | collective-permute-start | bytes 3145736 | tf_op jit(solution)/shard_map/ppermute | solution.py:109
  72.4 16.5 %collective-permute-start.4 = (bf16[4,64,2048]{2,1,0:T(8,128)(2,1)S(1)}, bf16[4,64,2048]{2,1,0:T(8,128)(2,1)}, u32[]{:S(2)}, u32[]{:S(2)}) collective-permute-start(bf16[4,64,2048]{2,1,0:T(8,128)(2,1)S(1)} %pad_maximum_fusion.1.refs_0_), channel_id=1, source_target_pairs={{0,32},{2,10},{4,36},{6,14},{8,40},{10,2},{12,44},{14,6},{16,48},{... | collective-permute-start | bytes 3145736 | tf_op jit(solution)/shard_map/ppermute | solution.py:109
  75.0 25.7 %collective-permute-start.5 = (bf16[4,64,2048]{2,1,0:T(8,128)(2,1)S(1)}, bf16[4,64,2048]{2,1,0:T(8,128)(2,1)}, u32[]{:S(2)}, u32[]{:S(2)}) collective-permute-start(bf16[4,64,2048]{2,1,0:T(8,128)(2,1)S(1)} %pad_maximum_fusion.1.refs_0_), channel_id=1, source_target_pairs={{0,48},{2,14},{4,52},{6,2},{8,56},{10,6},{12,60},{14,10},{16,0},{1... | collective-permute-start | bytes 3145736 | tf_op jit(solution)/shard_map/ppermute | solution.py:109
  80.3 24.4 %collective-permute-start.21 = (bf16[768,384]{1,0:T(8,128)(2,1)}, bf16[768,384]{1,0:T(8,128)(2,1)}, u32[]{:S(2)}, u32[]{:S(2)}) collective-permute-start(bf16[768,384]{1,0:T(8,128)(2,1)} %broadcast_select_fusion), channel_id=1, source_target_pairs={{0,65},{64,0},{1,64},{65,1},{2,67},{66,2},{3,66},{67,3},{4,69},{68... | collective-permute-start | bytes 1769480 | tf_op jit(solution)/shard_map/ppermute | solution.py:501
  83.2 21.6 %collective-permute-start.20 = (bf16[768,384]{1,0:T(8,128)(2,1)}, bf16[768,384]{1,0:T(8,128)(2,1)}, u32[]{:S(2)}, u32[]{:S(2)}) collective-permute-start(bf16[768,384]{1,0:T(8,128)(2,1)} %broadcast_select_fusion), channel_id=1, source_target_pairs={{0,1},{64,65},{1,0},{65,64},{2,3},{66,67},{3,2},{67,66},{4,5},{68,... | collective-permute-start | bytes 1769480 | tf_op jit(solution)/shard_map/ppermute | solution.py:501
  84.0 24.5 %collective-permute-start.19 = (bf16[768,384]{1,0:T(8,128)(2,1)}, bf16[768,384]{1,0:T(8,128)(2,1)}, u32[]{:S(2)}, u32[]{:S(2)}) collective-permute-start(bf16[768,384]{1,0:T(8,128)(2,1)} %broadcast_select_fusion), channel_id=1, source_target_pairs={{0,64},{64,1},{1,65},{65,0},{2,66},{66,3},{3,67},{67,2},{4,68},{68... | collective-permute-start | bytes 1769480 | tf_op jit(solution)/shard_map/ppermute | solution.py:501
  88.9 27.4 %collective-permute-start.6 = (bf16[4,64,2048]{2,1,0:T(8,128)(2,1)S(1)}, bf16[4,64,2048]{2,1,0:T(8,128)(2,1)}, u32[]{:S(2)}, u32[]{:S(2)}) collective-permute-start(bf16[4,64,2048]{2,1,0:T(8,128)(2,1)S(1)} %pad_maximum_fusion.1.refs_0_), channel_id=1, source_target_pairs={{0,2},{2,0},{1,3},{3,1},{4,6},{6,4},{5,7},{7,5},{8,10},{10,8},{9,1... | collective-permute-start | bytes 3145736 | tf_op jit(solution)/shard_map/ppermute | solution.py:514
  108.5 51.3 %collective-permute-start.24 = (bf16[512,2048]{1,0:T(8,128)(2,1)S(1)}, bf16[512,2048]{1,0:T(8,128)(2,1)}, u32[]{:S(2)}, u32[]{:S(2)}) collective-permute-start(bf16[512,2048]{1,0:T(8,128)(2,1)S(1)} %bitcast.77), channel_id=1, source_target_pairs={{64,0},{65,1},{66,2},{67,3},{68,4},{69,5},{70,6},{71,7},{72,8},{73... | collective-permute-start | bytes 6291464 | tf_op jit(solution)/shard_map/ppermute | solution.py:479
  152.9 52.0 %collective-permute-start.22 = (bf16[528,512]{1,0:T(8,128)(2,1)}, bf16[528,512]{1,0:T(8,128)(2,1)}, u32[]{:S(2)}, u32[]{:S(2)}) collective-permute-start(bf16[528,512]{1,0:T(8,128)(2,1)} %get-tuple-element.37), channel_id=1, source_target_pairs={{64,0},{65,1},{66,2},{67,3},{68,4},{69,5},{70,6},{71,7},{72,8},{73... | collective-permute-start | bytes 1622024 | tf_op jit(solution)/shard_map/ppermute | solution.py:542
  154.2 53.0 %collective-permute-start.23 = (bf16[528,512]{1,0:T(8,128)(2,1)}, bf16[528,512]{1,0:T(8,128)(2,1)}, u32[]{:S(2)}, u32[]{:S(2)}) collective-permute-start(bf16[528,512]{1,0:T(8,128)(2,1)} %get-tuple-element.37), channel_id=1, source_target_pairs={{64,1},{65,0},{66,3},{67,2},{68,5},{69,4},{70,7},{71,6},{72,9},{73... | collective-permute-start | bytes 1622024 | tf_op jit(solution)/shard_map/ppermute | solution.py:543
  215.6 16.1 %collective-permute-start.26 = (bf16[512,512]{1,0:T(8,128)(2,1)}, bf16[512,512]{1,0:T(8,128)(2,1)}, u32[]{:S(2)}, u32[]{:S(2)}) collective-permute-start(bf16[512,512]{1,0:T(8,128)(2,1)} %get-tuple-element.36), channel_id=1, source_target_pairs={{0,1},{1,0},{2,3},{3,2},{4,5},{5,4},{6,7},{7,6},{8,9},{9,8},{10,11... | collective-permute-start | bytes 1572872 | tf_op jit(solution)/shard_map/ppermute | solution.py:548
  226.6 31.1 %collective-permute-start.31 = (bf16[192,1536]{1,0:T(8,128)(2,1)}, bf16[192,1536]{1,0:T(8,128)(2,1)S(1)}, u32[]{:S(2)}, u32[]{:S(2)}) collective-permute-start(bf16[192,1536]{1,0:T(8,128)(2,1)} %get-tuple-element.46), channel_id=1, source_target_pairs={{64,65},{65,64},{66,67},{67,66},{68,69},{69,68},{70,71},{71,70},{7... | collective-permute-start | bytes 1769480 | tf_op jit(solution)/shard_map/ppermute | solution.py:554
  231.1 23.3 %collective-permute-start.27 = (bf16[528,512]{1,0:T(8,128)(2,1)S(1)}, bf16[528,512]{1,0:T(8,128)(2,1)S(1)}, u32[]{:S(2)}, u32[]{:S(2)}) collective-permute-start(bf16[528,512]{1,0:T(8,128)(2,1)S(1)} %copy-done.10), channel_id=1, source_target_pairs={{64,65},{65,64},{66,67},{67,66},{68,69},{69,68},{70,71},{71,70},{7... | collective-permute-start | bytes 1622024 | tf_op jit(solution)/shard_map/ppermute | solution.py:551
  240.6 22.6 %collective-permute-start.28 = (bf16[528,512]{1,0:T(8,128)(2,1)}, bf16[528,512]{1,0:T(8,128)(2,1)S(1)}, u32[]{:S(2)}, u32[]{:S(2)}) collective-permute-start(bf16[528,512]{1,0:T(8,128)(2,1)} %get-tuple-element.39), channel_id=1, source_target_pairs={{0,1},{1,0},{2,3},{3,2},{4,5},{5,4},{6,7},{7,6},{8,9},{9,8},{10,11... | collective-permute-start | bytes 1622024 | tf_op jit(solution)/shard_map/ppermute | solution.py:557
  244.7 37.6 %collective-permute-start.30 = (bf16[192,1536]{1,0:T(8,128)(2,1)}, bf16[192,1536]{1,0:T(8,128)(2,1)S(1)}, u32[]{:S(2)}, u32[]{:S(2)}) collective-permute-start(bf16[192,1536]{1,0:T(8,128)(2,1)} %get-tuple-element.45), channel_id=1, source_target_pairs={{64,1},{65,0},{66,3},{67,2},{68,5},{69,4},{70,7},{71,6},{72,9},{73... | collective-permute-start | bytes 1769480 | tf_op jit(solution)/shard_map/ppermute | solution.py:554
  246.0 36.3 %collective-permute-start.29 = (bf16[192,1536]{1,0:T(8,128)(2,1)}, bf16[192,1536]{1,0:T(8,128)(2,1)}, u32[]{:S(2)}, u32[]{:S(2)}) collective-permute-start(bf16[192,1536]{1,0:T(8,128)(2,1)} %get-tuple-element.44), channel_id=1, source_target_pairs={{64,0},{65,1},{66,2},{67,3},{68,4},{69,5},{70,6},{71,7},{72,8},{73... | collective-permute-start | bytes 1769480 | tf_op jit(solution)/shard_map/ppermute | solution.py:554
  254.4 27.9 %collective-permute-start.34 = (bf16[192,1536]{1,0:T(8,128)(2,1)}, bf16[192,1536]{1,0:T(8,128)(2,1)}, u32[]{:S(2)}, u32[]{:S(2)}) collective-permute-start(bf16[192,1536]{1,0:T(8,128)(2,1)} %get-tuple-element.49), channel_id=1, source_target_pairs={{0,1},{1,0},{2,3},{3,2},{4,5},{5,4},{6,7},{7,6},{8,9},{9,8},{10,11... | collective-permute-start | bytes 1769480 | tf_op jit(solution)/shard_map/ppermute | solution.py:560
  257.7 24.6 %collective-permute-start.33 = (bf16[192,1536]{1,0:T(8,128)(2,1)}, bf16[192,1536]{1,0:T(8,128)(2,1)}, u32[]{:S(2)}, u32[]{:S(2)}) collective-permute-start(bf16[192,1536]{1,0:T(8,128)(2,1)} %get-tuple-element.48), channel_id=1, source_target_pairs={{0,65},{1,64},{2,67},{3,66},{4,69},{5,68},{6,71},{7,70},{8,73},{9,... | collective-permute-start | bytes 1769480 | tf_op jit(solution)/shard_map/ppermute | solution.py:560
  263.2 19.0 %collective-permute-start.32 = (bf16[192,1536]{1,0:T(8,128)(2,1)}, bf16[192,1536]{1,0:T(8,128)(2,1)}, u32[]{:S(2)}, u32[]{:S(2)}) collective-permute-start(bf16[192,1536]{1,0:T(8,128)(2,1)} %get-tuple-element.47), channel_id=1, source_target_pairs={{0,64},{1,65},{2,66},{3,67},{4,68},{5,69},{6,70},{7,71},{8,72},{9,... | collective-permute-start | bytes 1769480 | tf_op jit(solution)/shard_map/ppermute | solution.py:560
  (30 other events, 381.1 us)
Sparse Core Ops, SparseCore 0:
  15.1 53.0 all-gather.3

commit v3 on v2

--- a/solution.py
+++ b/solution.py
@@ -69,6 +69,7 @@
 ANY = pl.BlockSpec(memory_space=pl.ANY)
 VMEM = pl.BlockSpec(memory_space=pltpu.VMEM)
 TILE = 512
+ROWS, SLOT, INFO, LENGTHS, PATTERN = 0, 32, 36, 39, 43
 
 
 def pool_kernel(which, counts, tiles, queries, out):
@@ -121,13 +122,14 @@
     return jnp.stack(table).astype(jnp.int32)
 
 
-def select_kernel(wanted, array, block, slide, *refs):
+def select_kernel(wanted, picks, *refs):
     ins, outs, sems = refs[:4], refs[4:6], refs[6]
 
     def copy(a, which, i):
         at = which * wanted + i
+        slide = pl.multiple_of(picks[4 * wanted + at] * LAT, LAT)
         return pltpu.make_async_copy(
-            ins[a].at[block[at], pl.ds(pl.multiple_of(slide[at] * LAT, LAT), LAT)],
+            ins[a].at[picks[2 * wanted + at], pl.ds(slide, LAT)],
             outs[which].at[pl.ds(i * LAT, LAT)],
             sems.at[at],
         )
@@ -137,63 +139,54 @@
             for i in range(wanted):
                 for a in range(4):
 
-                    @pl.when(array[which * wanted + i] == a)
+                    @pl.when(picks[which * wanted + i] == a)
                     def _():
                         getattr(copy(a, which, i), act)()
 
 
-def select(array, block, slide, blocks):
-    wanted = array.shape[0] // 2
+def select(picks, blocks):
+    wanted = picks.shape[0] // 6
     out = jax.ShapeDtypeStruct((wanted * LAT, QUARTER), BF)
     return pl.pallas_call(
         functools.partial(select_kernel, wanted),
-        in_specs=[SMEM] * 3 + [ANY] * 4,
+        in_specs=[SMEM] + [ANY] * 4,
         out_specs=[VMEM, VMEM],
         out_shape=[out, out],
         scratch_shapes=[pltpu.SemaphoreType.DMA((2 * wanted,))],
         compiler_params=params(),
-    )(array, block, slide, *blocks)
+    )(picks, *blocks)
 
 
 def column(row):
     return jnp.broadcast_to(row, (HEAD, row.shape[1])).T[:, :1]
 
 
-def live_tokens(lengths, tokens):
+def live_tokens(meta, tokens):
     index = lax.broadcasted_iota(jnp.int32, (tokens, 1), 0)
-    parts = [index[r * L : (r + 1) * L] < r * L + lengths[r] for r in range(tokens // L)]
+    parts = [index[r * L : (r + 1) * L] < r * L + meta[LENGTHS + r] for r in range(tokens // L)]
     return jnp.concatenate([p.astype(F32) for p in parts], axis=0) > 0
 
 
-def project_kernel(kind, rows, lengths, rinv, gain, x, *refs):
-    ins, (send, weight, left), (w_v, x_v, sems) = refs[:8], refs[8:11], refs[11:]
+def project_kernel(kind, meta, x, *refs):
+    ins, (send, weight), (w_v, x_v, sems) = refs[:8], refs[8:10], refs[10:]
     load = pltpu.make_async_copy(x, x_v, sems.at[2])
     load.start()
     half = w_v.shape[0] // 2
     for part in (1, 0):
         for a in range(8):
             for k in range(4):
-                at = pl.multiple_of(rows[a * 4 + k], 32)
-                group = (at >= half).astype(jnp.int32)
-
-                @pl.when(group == part)
+                at = pl.multiple_of(meta[ROWS + a * 4 + k], 32)
+
+                @pl.when((at >= half) == (part == 1))
                 def _():
                     pltpu.make_async_copy(
                         ins[a].at[k, pl.ds(kind * 32, 32)], w_v.at[pl.ds(at, 32)], sems.at[part]
                     ).start()
 
-    load.wait()
-    if kind == 0:
-        live = live_tokens(lengths, x_v.shape[0])
-        x_v[...] = jnp.where(live, x_v[...].astype(F32), 0.0).astype(BF)
-    else:
-        x_v[...] = (x_v[...].astype(F32) * column(rinv[...]) * gain[...]).astype(BF)
-    store_x = pltpu.make_async_copy(x_v, left, sems.at[2])
-    store_x.start()
-
     def group(part):
         return w_v.at[pl.ds(part * half, half)]
 
+    load.wait()
     pltpu.make_async_copy(group(1), group(1), sems.at[1]).wait()
     store1 = pltpu.make_async_copy(group(1), weight.at[pl.ds(half, half)], sems.at[1])
     store1.start()
@@ -201,22 +194,20 @@
     pltpu.make_async_copy(group(0), group(0), sems.at[0]).wait()
     store0 = pltpu.make_async_copy(group(0), weight.at[pl.ds(0, half)], sems.at[0])
     store0.start()
-    store_x.wait()
     store1.wait()
     store0.wait()
 
 
-def project(kind, rows, lengths, rinv, gain, x, blocks):
+def project(kind, meta, x, blocks):
     tokens, width = x.shape
     inner = 32 * 32
     return pl.pallas_call(
         functools.partial(project_kernel, kind),
-        in_specs=[SMEM, SMEM, VMEM, VMEM, ANY] + [ANY] * 8,
-        out_specs=[VMEM, ANY, ANY],
+        in_specs=[SMEM, ANY] + [ANY] * 8,
+        out_specs=[VMEM, ANY],
         out_shape=[
             jax.ShapeDtypeStruct((tokens, inner // 2), BF),
             jax.ShapeDtypeStruct((inner, width), BF),
-            jax.ShapeDtypeStruct((tokens, width), BF),
         ],
         scratch_shapes=[
             pltpu.VMEM((inner, width), BF),
@@ -227,10 +218,10 @@
         cost_estimate=pl.CostEstimate(
             flops=tokens * width * inner, bytes_accessed=12 << 20, transcendentals=0
         ),
-    )(rows, lengths, rinv, gain, x, *blocks)
-
-
-def forward_kernel(pattern, q_own, q_got, keys, probs):
+    )(meta, x, *blocks)
+
+
+def forward_kernel(meta, q_own, q_got, keys, probs):
     report = pl.program_id(0)
     span = keys.shape[0]
     slide = lax.broadcasted_iota(jnp.int32, (QBLK, span), 1) // LAT
@@ -238,18 +229,21 @@
     for block in range(L // QBLK):
         seen = jnp.zeros((QBLK, span), jnp.int32)
         for j in range(SPR):
-            seen = jnp.where(slide == j, pattern[(report * (L // QBLK) + block) * SPR + j], seen)
+            at = PATTERN + (report * (L // QBLK) + block) * SPR + j
+            seen = jnp.where(slide == j, meta[at], seen)
         masks.append(seen)
     mask = jnp.concatenate(masks, axis=0) == 1
-    for head in range(probs.shape[0]):
-        cols = slice(head * HEAD, (head + 1) * HEAD)
-        qb = (q_own[:, cols] + q_got[:, cols].astype(F32)).astype(BF)
-        scores = jnp.where(mask, dot(qb, keys[:, cols], NT) * SCALE, -1e30)
-        exps = jnp.exp(scores - jnp.max(scores, axis=1, keepdims=True))
-        probs[head] = exps / jnp.sum(exps, axis=1, keepdims=True)
-
-
-def forward(pattern, q_own, q_got, kv):
+    heads = [slice(head * HEAD, (head + 1) * HEAD) for head in range(probs.shape[0])]
+    qb = [(q_own[:, c] + q_got[:, c].astype(F32)).astype(BF) for c in heads]
+    scores = [dot(q, keys[:, c], NT) * SCALE for q, c in zip(qb, heads)]
+    scores = [jnp.where(mask, s, -1e30) for s in scores]
+    exps = [jnp.exp(s - jnp.max(s, axis=1, keepdims=True)) for s in scores]
+    totals = [jnp.sum(e, axis=1, keepdims=True) for e in exps]
+    for head, (e, total) in enumerate(zip(exps, totals)):
+        probs[head] = e / total
+
+
+def forward(meta, q_own, q_got, kv):
     tokens, local = q_own.shape
     reports = tokens // L
     span = kv.shape[0] // reports
@@ -265,34 +259,33 @@
         cost_estimate=pl.CostEstimate(
             flops=2 * tokens * span * local, bytes_accessed=6 << 20, transcendentals=tokens * span * 4
         ),
-    )(pattern, q_own, q_got, kv)
-
-
-def backward_kernel(slot, gate, q_own, q_got, o_own, o_got, keys, vals, probs, dq_out, dkv_out):
+    )(meta, q_own, q_got, kv)
+
+
+def backward_kernel(meta, gate, q_own, q_got, o_own, o_got, keys, vals, probs, dq_out, dkv_out):
     report = pl.program_id(0)
     rows = pl.ds(pl.multiple_of(report * L, L), L)
     local = q_own.shape[1]
+    heads = [slice(head * HEAD, (head + 1) * HEAD) for head in range(local // HEAD)]
+    og = [
+        (gate[0] * (o_own[:, c].astype(F32) + o_got[:, c].astype(F32))).astype(BF) for c in heads
+    ]
+    dprob = [dot(g, vals[:, c], NT) for g, c in zip(og, heads)]
+    prob = [probs[head] for head in range(len(heads))]
+    rowdot = [jnp.sum(p * d, axis=1, keepdims=True) for p, d in zip(prob, dprob)]
+    dscore = [(p * (d - r)).astype(BF) for p, d, r in zip(prob, dprob, rowdot)]
+    dq = [(dot(d, keys[:, c], NN) * SCALE).astype(BF) for d, c in zip(dscore, heads)]
+    q = [q_own[:, c] + q_got[:, c].astype(F32) for c in heads]
+    dkey = [(dot(d, x.astype(BF), TN) * SCALE).astype(BF) for d, x in zip(dscore, q)]
+    dval = [dot(p.astype(BF), g, TN).astype(BF) for p, g in zip(prob, og)]
     stat = jnp.zeros((L, HEAD), F32)
-    for head in range(local // HEAD):
-        cols = slice(head * HEAD, (head + 1) * HEAD)
-        q = q_own[:, cols] + q_got[:, cols].astype(F32)
-        qb = q.astype(BF)
-        og = (gate[0] * (o_own[:, cols].astype(F32) + o_got[:, cols].astype(F32))).astype(BF)
-        key = keys[:, cols]
-        prob = probs[head]
-        dprob = dot(og, vals[:, cols], NT)
-        rowdot = jnp.sum(prob * dprob, axis=1, keepdims=True)
-        dscore = (prob * (dprob - rowdot)).astype(BF)
-        dq = (dot(dscore, key, NN) * SCALE).astype(BF)
-        dkey = (dot(dscore, qb, TN) * SCALE).astype(BF)
-        dval = dot(prob.astype(BF), og, TN).astype(BF)
-        dq_out[rows, cols] = dq
-        stat += q * dq.astype(F32)
-        for part in range(4):
-            into = pl.ds(pl.multiple_of(report * 48, 16), 48)
-            piece = slice(part * 48, (part + 1) * 48)
-            dkv_out[slot[part], into, cols] = dkey[piece]
-            dkv_out[slot[part], into, local + head * HEAD : local + (head + 1) * HEAD] = dval[piece]
+    for c, d, x in zip(heads, dq, q):
+        dq_out[rows, c] = d
+        stat += x * d.astype(F32)
+    into = pl.ds(pl.multiple_of(report * 48, 16), 48)
+    both = jnp.concatenate(dkey + dval, axis=1)
+    for part in range(4):
+        dkv_out[meta[SLOT + part], into, :] = both[part * 48 : (part + 1) * 48]
     total = jnp.sum(stat.T, axis=0, keepdims=True)
     high = total.astype(BF)
     rest = total - high.astype(F32)
@@ -303,7 +296,7 @@
     dq_out[4 * L : 4 * L + 16, rows] = extra.astype(BF)
 
 
-def backward(slot, gate, q_own, q_got, o_own, o_got, kv, probs):
+def backward(meta, gate, q_own, q_got, o_own, o_got, kv, probs):
     tokens, local = q_own.shape
     reports = tokens // L
     heads, _, span = probs.shape
@@ -326,14 +319,19 @@
         cost_estimate=pl.CostEstimate(
             flops=8 * tokens * span * local, bytes_accessed=8 << 20, transcendentals=0
         ),
-    )(slot, gate, q_own, q_got, o_own, o_got, kv, kv, probs)
-
-
-def back_kernel(following, info, lengths, dq_own, dq_got, rinv, gain, up, h, wq, *refs):
+    )(meta, gate, q_own, q_got, o_own, o_got, kv, kv, probs)
+
+
+def back_kernel(following, meta, rinv, gain, *refs):
     if following:
-        wo, grad, o_send, wq_v, up_v, h_v, wo_v, sems = refs
+        dq_own, dq_got, up, h, wq, wo, grad, o_send, wq_v, up_v, h_v, wo_v, sems = refs
+        left, right = dq_own[...], dq_got[...]
     else:
-        grad, wq_v, up_v, h_v, sems = refs
+        dq1, dq0, got1, got0, up, h, wq, grad, wq_v, up_v, h_v, sems = refs
+        left = jnp.where(meta[INFO] == 1, dq1[...].astype(F32), dq0[...].astype(F32)).astype(BF)
+        right = (got1[...].astype(F32) + got0[...].astype(F32)).astype(BF)
+    if len(h.shape) == 3:
+        h = h.at[1]
     inner, width = wq_v.shape
     half = inner // 2
     tokens = up_v.shape[0]
@@ -343,7 +341,7 @@
         cols = slice(tile * TILE, (tile + 1) * TILE)
         out = []
         for part in range(2):
-            at = pl.multiple_of(info[1 + part], half)
+            at = pl.multiple_of(meta[INFO + 1 + part], half) if following else part * half
             into = slice(part * half, (part + 1) * half)
             out.append((wq.at[pl.ds(at, half), cols], wq_v.at[into, cols]))
         out.append((up.at[:, cols], up_v.at[:, cols]))
@@ -359,25 +357,25 @@
         load = pltpu.make_async_copy(wo.at[pl.ds(half, half)], wo_v, sems.at[tiles * 4])
         load.start()
     stat = column(
-        jnp.sum(dq_own[tokens:].astype(F32) + dq_got[tokens:].astype(F32), axis=0, keepdims=True)
+        jnp.sum(left[tokens:].astype(F32) + right[tokens:].astype(F32), axis=0, keepdims=True)
     )
+    left, right = left[:tokens], right[:tokens]
     scale = column(rinv[...])
     share = scale * scale * stat / MODEL_WIDTH
     if following:
-        live = live_tokens(lengths, tokens)
+        live = live_tokens(meta, tokens)
     stores = []
     for tile in range(tiles):
         for copy in copies(tile):
             copy.wait()
         cols = slice(tile * TILE, (tile + 1) * TILE)
-        dnormed = dot(dq_own[:tokens], wq_v[:half, cols], NN)
-        dnormed += dot(dq_got[:tokens], wq_v[half:, cols], NN)
+        dnormed = dot(left, wq_v[:half, cols], NN) + dot(right, wq_v[half:, cols], NN)
         upstream = up_v[:, cols].astype(F32)
         if following:
             upstream = jnp.where(live, upstream, 0.0)
         value = upstream + (scale * (gain[:, cols] * dnormed) - h_v[:, cols].astype(F32) * share)
         if following:
-            value = jnp.where(info[0] == 1, upstream, value)
+            value = jnp.where(meta[INFO] == 1, upstream, value)
         up_v[:, cols] = value.astype(BF)
         store = pltpu.make_async_copy(up_v.at[:, cols], grad.at[:, cols], sems.at[tile * 4])
         store.start()
@@ -389,12 +387,12 @@
         store.wait()
 
 
-def back(info, lengths, dq_own, dq_got, rinv, gain, up, h, wq, wo=None):
-    tokens, width = h.shape
+def back(meta, rinv, gain, dqs, up, h, wq, wo=None):
+    tokens, width = up.shape
     inner = wq.shape[0]
     half = inner // 2
-    inputs = [info, lengths, dq_own, dq_got, rinv, gain, up, h, wq]
-    in_specs = [SMEM, SMEM, VMEM, VMEM, VMEM, VMEM, ANY, ANY, ANY]
+    inputs = [meta, rinv, gain, *dqs, up, h, wq]
+    in_specs = [SMEM] + [VMEM] * (2 + len(dqs)) + [ANY] * 3
     out_specs = [ANY]
     out_shape = [jax.ShapeDtypeStruct((tokens, width), BF)]
     scratch = [pltpu.VMEM((inner, width), BF)] + [pltpu.VMEM((tokens, width), BF)] * 2
@@ -475,25 +473,38 @@
     tokens, width = h.shape
     half = 512
 
-    wq_t = w_query[0].T
-    h1 = lax.ppermute(h, "segment", [(1, 0)])
-    wq1 = lax.all_gather(lax.ppermute(wq_t, "segment", [(1, 0)]), DP, axis=0, tiled=True)
-
-    pooled = pool(me_x.reshape(1).astype(jnp.int32), tile_counts.reshape(4), tiles, lat_query)
-    lat_blocks = gather_chips(pooled)
-    pair = me_dp - core
-    sources = request_source.reshape(32, wanted)
-    slides = request_slide.reshape(32, wanted)
+    slot = []
+    for part in range(4):
+        same_seg, same_mp = seg == part // 2, me_mp == part % 2
+        slot.append(jnp.where(same_seg, jnp.where(same_mp, 0, 3), jnp.where(same_mp, 1, 2)))
+    rows = lax.rem(places(z, y, core) * 32 - me_mp * half + 2 * half, 2 * half)
+    info = [seg, me_mp * half, (1 - me_mp) * half]
+    meta = jnp.concatenate(
+        [rows, jnp.stack(slot + info).astype(jnp.int32), report_lengths, cross_pattern.reshape(-1)]
+    )
     order = jnp.stack([me_dp, me_dp + 1 - 2 * core])
-    source = sources[order]
-    slide = slides[order].reshape(-1)
+    source = request_source.reshape(32, wanted)[order]
+    slide = request_slide.reshape(32, wanted)[order]
     source_core = source % 2
     far_z = lax.rem(z - source // 8 + 4, 4)
     far_y = lax.rem(y - source // 2 % 4 + 4, 4)
     first = jnp.where(core == 0, far_y, far_z)
     second = jnp.where(core == 0, far_z, far_y)
     array = jnp.where(source_core == core, second, 4)
-    near, across = select(array.reshape(-1), first.reshape(-1), slide, lat_blocks)
+    picks = jnp.concatenate([array.reshape(-1), first.reshape(-1), slide.reshape(-1)])
+
+    h_all = lax.all_gather(h, "segment")
+
+    wq_t = w_query[0].T
+    block = jnp.concatenate([w_out[0], wq_t], axis=0)
+    blocks = gather_chips(block)
+
+    pooled = pool(me_x.reshape(1).astype(jnp.int32), tile_counts.reshape(4), tiles, lat_query)
+    lat_blocks = gather_chips(pooled)
+    lat_blocks[3], blocks[1], blocks[3] = lax.optimization_barrier(
+        (lat_blocks[3], blocks[1], blocks[3])
+    )
+    near, across = select(picks, lat_blocks)
     crossed = lax.ppermute(across, "core", [(0, 1), (1, 0)])
     is_near = jnp.repeat(source_core[0] == core, LAT)[:, None]
     chosen = jnp.where(is_near, near, crossed)
@@ -509,59 +520,49 @@
         axis=0,
     )
     kv = dot(latents, w_kv_x, NN).astype(BF)
-
-    blocks = gather_chips(jnp.concatenate([w_out[0], wq_t], axis=0))
     blocks = blocks + [lax.ppermute(b, "core", [(0, 1), (1, 0)]) for b in blocks]
-    rows = lax.rem(places(z, y, core) * 32 - me_mp * half + 2 * half, 2 * half)
+
+    wq_t, _ = lax.optimization_barrier((wq_t, lat_blocks[0]))
+    wq1 = lax.all_gather(lax.ppermute(wq_t, "segment", [(1, 0)]), DP, axis=0, tiled=True)
 
     h32 = h.astype(F32)
-    message = jnp.concatenate([jnp.sum(h32 * h32, axis=1), norm_gain[0]])
-    messages = lax.all_gather(message, X)
-    squares = messages[:, :tokens].reshape(2, 2, tokens).sum(axis=1)
-    rinvs = lax.rsqrt(squares / MODEL_WIDTH + 1e-05)
-    rinv = lax.dynamic_index_in_dim(rinvs, seg, 0)
-    rinv1 = rinvs[1:]
+    partial = jnp.sum(h32 * h32, axis=1)
+    squares = partial + lax.ppermute(partial, "mp", [(0, 1), (1, 0)])
+    rinv = lax.rsqrt(squares / MODEL_WIDTH + 1e-05)
     gain = norm_gain
-    gain1 = lax.dynamic_index_in_dim(messages[2:, tokens:], me_mp, 0)
+    message = lax.ppermute(jnp.concatenate([rinv, gain[0]]), "segment", [(1, 0)])[None]
+    rinv1, gain1 = message[:, :tokens], message[:, tokens:]
+    normed = (h32 * rinv[:, None] * gain).astype(BF)
+    position = jnp.arange(tokens)
+    live = position % L < jnp.repeat(report_lengths, L)
+    up1 = jnp.where(live[:, None], cotangent, jnp.zeros((), BF))
+    rinv = rinv[None]
     gate = jnp.tanh(attn_gate)
-    slot = []
-    for part in range(4):
-        same_seg, same_mp = seg == part // 2, me_mp == part % 2
-        slot.append(jnp.where(same_seg, jnp.where(same_mp, 0, 3), jnp.where(same_mp, 1, 2)))
-    slot = jnp.stack(slot).astype(jnp.int32)
-    pattern = cross_pattern.reshape(-1)
-
-    q_send, wq, normed = project(1, rows, report_lengths, rinv, gain, h, blocks)
+
+    q_send, wq = project(1, meta, normed, blocks)
     q_got = lax.ppermute(q_send, X, SWAP_MP)
-    o_send, wo, up1 = project(0, rows, report_lengths, rinv, gain, cotangent, blocks)
+    o_send, wo = project(0, meta, up1, blocks)
     o_got = lax.ppermute(o_send, X, LAST_SWAP)
     q_own = dot(normed, wq[:half], NT)
     o_own = dot(up1, wo[:half], NT).astype(BF)
-    probs = forward(pattern, q_own, q_got, kv)
-    dq1, dkv1 = backward(slot, gate, q_own, q_got, o_own, o_got, kv, probs)
-    dq_same = lax.ppermute(dq1, X, LAST_TO_SAME)
-    dq_cross = lax.ppermute(dq1, X, LAST_TO_CROSS)
-    info1 = jnp.stack([seg, me_mp * half, (1 - me_mp) * half]).astype(jnp.int32)
-    up, o_send = back(
-        info1, report_lengths, dq_same, dq_cross, rinv1, gain1, cotangent, h1, wq1, wo
-    )
+    probs = forward(meta, q_own, q_got, kv)
+    dq1, dkv1 = backward(meta, gate, q_own, q_got, o_own, o_got, kv, probs)
+    dqs = [lax.ppermute(dq1, X, LAST_TO_SAME), lax.ppermute(dq1, X, LAST_TO_CROSS)]
+    up, o_send = back(meta, rinv1, gain1, dqs, cotangent, h_all, wq1, wo)
     o_got = lax.ppermute(o_send, X, FIRST_SWAP)
     o_own = dot(up, wo[:half], NT).astype(BF)
     dq1, dkv1, _ = lax.optimization_barrier((dq1, dkv1, o_send))
-    dq1_got = lax.ppermute(dq1, X, LAST_SWAP)
+    got1 = lax.ppermute(dq1, X, LAST_SWAP)
     own1, *terms = latent_terms(dkv1, w_kv)
     moves = (LAST_TO_SAME, LAST_TO_CROSS, LAST_SWAP)
     got = [lax.ppermute(t, X, p) for t, p in zip(terms, moves)]
 
-    dq0, dkv0 = backward(slot, gate, q_own, q_got, o_own, o_got, kv, probs)
-    dq0_got = lax.ppermute(dq0, X, FIRST_SWAP)
+    dq0, dkv0 = backward(meta, gate, q_own, q_got, o_own, o_got, kv, probs)
+    got0 = lax.ppermute(dq0, X, FIRST_SWAP)
     own0, *terms = latent_terms(dkv0, w_kv)
     moves = (FIRST_TO_SAME, FIRST_TO_CROSS, FIRST_SWAP)
     got += [lax.ppermute(t, X, p) for t, p in zip(terms, moves)]
-    dq = jnp.where(last, dq1, dq0)
-    dq_got = jnp.where(last, dq1_got, dq0_got)
-    info = jnp.array([0, 0, half], jnp.int32)
-    (grads,) = back(info, report_lengths, dq, dq_got, rinv, gain, up, h, wq)
+    (grads,) = back(meta, rinv, gain, [dq1, dq0, got1, got0], up, h, wq)
 
     latent_grad = jnp.where(last, own1, own0)
     for term in got:

time: 294 us -> 259 us (0.88)
  waiting for transfers between devices: 89.4 us -> 66 us
  blocking collectives: 12.6 us -> 0 us
  local copies, waits for them, and re-layouts: 6.58 us -> 12.7 us
  Pallas kernels: 74.3 us -> 69.6 us
    ppermute x5 -> x6, waiting for transfers between devices: 47.5 us -> 13.8 us  [the longest x1 13.6 us: per_device(): lax.ppermute(jnp.concatenate([rinv, gain[0]]), 'segment', [(1, 0)])[None]]
    all_gather x1 -> x0, blocking collectives: 12.6 us -> none  [per_device(): messages = lax.all_gather(message, X)]
    ppermute x6, waiting for transfers between devices: 20.3 us -> 14.5 us  [gather_chips(): lax.ppermute(bundle, DP, yz_perm(2, k))]
    pallas_call x2, Pallas kernels: 17.8 us -> 12.8 us  [backward(): pl.pallas_call(backward_kernel, grid=(reports,), in_specs=[SMEM, SMEM, to...]
    ppermute x6, waiting for transfers between devices: 3.11 us -> 8.05 us  [gather_chips(): lax.ppermute(block, DP, yz_perm(1, k))]
    ppermute x1, waiting for transfers between devices: 0.52 us -> 5.09 us  [per_device(): q_got = lax.ppermute(q_send, X, SWAP_MP)]
    ppermute x1, waiting for transfers between devices: 5.77 us -> 9.22 us  [per_device(): lax.ppermute(wq_t, 'segment', [(1, 0)])]
    ppermute x5 -> x6, starting transfers between devices: 8.95 us -> 11.3 us  [the longest x1 3.58 us: per_device(): got0 = lax.ppermute(dq0, X, FIRST_SWAP)]
  transfers between devices with their start and end apart: 36 -> 38, of which waited for: 12 -> 14; matrix products, arithmetic and copies ran while one was open for 13% -> 17% of each run, Pallas kernels for 23% -> 24%
where the time goes in v3:
time: 259 us; the launch traced here: 256 us
  Pallas kernels  69.6 us (27%)
  waiting for transfers between devices  66 us (25%)
  starting transfers between devices  56.8 us (22%)
  other arithmetic  19.2 us (7%)
  matrix products  16.8 us (6%)
  between operations  15.2 us (6%)
  local copies, waits for them, and re-layouts  12.7 us (5%)
    dot_general x4, matrix products, dot(): return lax.dot_general(a, b, dims, preferred_element_type=F32)  16.8 us
    pallas_call x2, Pallas kernels, back(): pl.pallas_call(functools.partial(back_kernel, wo is not None), in_specs=i...  15.8 us
    ppermute x6, waiting for transfers between devices, gather_chips(): lax.ppermute(bundle, DP, yz_perm(2, k))  14.5 us
    pallas_call x2, Pallas kernels, latent_terms(): pl.pallas_call(term_kernel, grid=(features // tile,), in_specs=[whole(dkv...  14.2 us
    ppermute x1, waiting for transfers between devices, per_device(): lax.ppermute(jnp.concatenate([rinv, gain[0]]), 'segment', [(1, 0)])[None]  13.6 us
    pallas_call x2, Pallas kernels, backward(): pl.pallas_call(backward_kernel, grid=(reports,), in_specs=[SMEM, SMEM, to...  12.8 us
    pallas_call x2, Pallas kernels, project(): pl.pallas_call(functools.partial(project_kernel, kind), in_specs=[SMEM, A...  12.6 us
    ppermute x6, starting transfers between devices, gather_chips(): lax.ppermute(bundle, DP, yz_perm(2, k))  10.9 us
  transfers between devices with their start and end apart: 38, of which 14 were waited for; matrix products, arithmetic and copies ran while one was open for 17% of the time, Pallas kernels for 24%

profile of v3, /device:TPU:0, one launch (start us, length us, event | category | flops | bytes accessed | tf_op | source)
XLA Modules:
  0.0 256.4 jit_solution(5832200614186052317)
XLA Ops:
  8.0 6.0 %shard_map.158 = bf16[128,384]{1,0:T(8,128)(2,1)} custom-call(s32[1]{0:T(128)} %bitcast.49.which, s32[4]{0:T(128)} %bitcast.95, bf16[4,64,1536]{2,1,0:T(8,128)(2,1)} %tiles.1, bf16[32,1536]{1,0:T(8,128)(2,1)} %queries.1), custom_call_target="tpu_custom_call" | custom-call | tf_op jit(solution)/shard_map/pallas_call | solution.py:91
  19.7 3.8 %collective-permute-done.5 = bf16[128,384]{1,0:T(8,128)(2,1)S(1)} collective-permute-done((bf16[128,384]{1,0:T(8,128)(2,1)}, bf16[128,384]{1,0:T(8,128)(2,1)S(1)}, u32[]{:S(2)}, u32[]{:S(2)}) %collective-permute-start.5) | collective-permute-done | bytes 98336 | tf_op jit(solution)/shard_map/ppermute | solution.py:108
  26.7 9.2 %collective-permute-done.26 = bf16[32,2048]{1,0:T(8,128)(2,1)S(1)} collective-permute-done((bf16[32,2048]{1,0:T(8,128)(2,1)S(1)}, bf16[32,2048]{1,0:T(8,128)(2,1)S(1)}, u32[]{:S(2)}, u32[]{:S(2)}) %collective-permute-start.26) | collective-permute-done | bytes 131104 | tf_op jit(solution)/shard_map/ppermute | solution.py:526
  73.5 8.4 %collective-permute-done.9.refs_3_ = bf16[4,64,2048]{2,1,0:T(8,128)(2,1)} collective-permute-done((bf16[4,64,2048]{2,1,0:T(8,128)(2,1)S(1)}, bf16[4,64,2048]{2,1,0:T(8,128)(2,1)}, u32[]{:S(2)}, u32[]{:S(2)}) %collective-permute-start.9) | collective-permute-done | bytes 1048608 | tf_op jit(solution)/shard_map/ppermute | solution.py:110
  82.4 5.6 %collective-permute-done.18.refs_2_ = bf16[4,128,384]{2,1,0:T(8,128)(2,1)} collective-permute-done((bf16[4,128,384]{2,1,0:T(8,128)(2,1)S(1)}, bf16[4,128,384]{2,1,0:T(8,128)(2,1)}, u32[]{:S(2)}, u32[]{:S(2)}) %collective-permute-start.18) | collective-permute-done | bytes 393248 | tf_op jit(solution)/shard_map/ppermute | solution.py:110
  101.5 6.3 %shard_map.159 = (bf16[512,512]{1,0:T(8,128)(2,1)}, bf16[1024,2048]{1,0:T(8,128)(2,1)}) custom-call(s32[139]{0:T(256)} %concatenate.40.meta, bf16[512,2048]{1,0:T(8,128)(2,1)} %fusion.2.x, bf16[4,64,2048]{2,1,0:T(8,128)(2,1)} %copy-done.1, bf16[4,64,2048]{2,1,0:T(8,128)(2,1)} %collective-permute-done.8.refs_1_, ...), custom_call_target="tpu_custom_call" | custom-call | flops 1073741824 | bytes 12582912 | tf_op jit(solution)/shard_map/pallas_call | solution.py:204
  107.8 3.9 %fusion.18.q_own = f32[512,512]{1,0:T(8,128)} fusion(bf16[512,2048]{1,0:T(8,128)(2,1)S(1)} %copy-done.4, bf16[1024,2048]{1,0:T(8,128)(2,1)} %get-tuple-element.30.refs_6_), kind=kOutput, calls=%fused_computation.31 | convolution fusion | flops 1073741824 | bytes 5242880 | tf_op jit(solution)/shard_map/dot_general | solution.py:57
  113.4 6.4 %shard_map.160 = (bf16[512,512]{1,0:T(8,128)(2,1)}, bf16[1024,2048]{1,0:T(8,128)(2,1)}) custom-call(s32[139]{0:T(256)} %concatenate.40.meta, bf16[512,2048]{1,0:T(8,128)(2,1)} %broadcast_select_fusion.x, bf16[4,64,2048]{2,1,0:T(8,128)(2,1)} %copy-done.1, bf16[4,64,2048]{2,1,0:T(8,128)(2,1)} %collective-permute-done.8.refs_1_, ...), custom_call_target="tpu_custom_call" | custom-call | flops 1073741824 | bytes 12582912 | tf_op jit(solution)/shard_map/pallas_call | solution.py:204
  121.3 3.9 %fusion.29.o_own = bf16[512,512]{1,0:T(8,128)(2,1)} fusion(bf16[512,2048]{1,0:T(8,128)(2,1)S(1)} %copy-done.3, bf16[1024,2048]{1,0:T(8,128)(2,1)} %get-tuple-element.32.refs_5_), kind=kOutput, calls=%fused_computation.39 | convolution fusion | flops 1074003968 | bytes 4718592 | tf_op jit(solution)/shard_map/dot_general | solution.py:57
  128.8 5.4 %fusion.24.keys.vals = bf16[768,1024]{1,0:T(8,128)(2,1)} fusion(bf16[384,1024]{1,0:T(8,128)(2,1)S(1)} %copy-done.17, bf16[384,1024]{1,0:T(8,128)(2,1)S(1)} %copy-done.16, bf16[384,1024]{1,0:T(8,128)(2,1)S(1)} %copy-done.15, bf16[384,1024]{1,0:T(8,128)(2,1)S(1)} %copy-done.14, bf16[768,384]{1,0:T(8,128)(2,1)} %collective-permute-done.22, ...), kind=kOutput, calls=%fused_computation.38 | convolution fusion | flops 2438725632 | bytes 7077888 | tf_op jit(solution)/shard_map/dot_general | solution.py:57
  134.1 5.1 %collective-permute-done.15.q_got = bf16[512,512]{1,0:T(8,128)(2,1)S(1)} collective-permute-done((bf16[512,512]{1,0:T(8,128)(2,1)}, bf16[512,512]{1,0:T(8,128)(2,1)S(1)}, u32[]{:S(2)}, u32[]{:S(2)}) %collective-permute-start.15) | collective-permute-done | bytes 524320 | tf_op jit(solution)/shard_map/ppermute | solution.py:543
  140.0 4.7 %shard_map.162.probs = f32[4,512,192]{2,1,0:T(8,128)} custom-call(s32[139]{0:T(256)} %concatenate.40.meta, f32[512,512]{1,0:T(8,128)} %fusion.18.q_own, bf16[512,512]{1,0:T(8,128)(2,1)} %copy-done.9, bf16[768,1024]{1,0:T(8,128)(2,1)} %fusion.24.keys.vals), custom_call_target="tpu_custom_call" | custom-call | flops 100663296 | bytes 6291456 | tf_op jit(solution)/shard_map/pallas_call | solution.py:252
  144.7 6.5 %shard_map.163 = (bf16[528,512]{1,0:T(8,128)(2,1)}, bf16[4,192,1024]{2,1,0:T(8,128)(2,1)}) custom-call(s32[139]{0:T(256)} %concatenate.40.meta, f32[1]{0:T(128)S(6)} %tanh.3.gate, f32[512,512]{1,0:T(8,128)} %fusion.18.q_own, bf16[512,512]{1,0:T(8,128)(2,1)} %copy-done.9, bf16[512,512]{1,0:T(8,128)(2,1)} %fusion.29.o_own, ...), custom_call_target="tpu_custom_call" | custom-call | flops 402653184 | bytes 8388608 | tf_op jit(solution)/shard_map/pallas_call | solution.py:304
  157.3 13.6 %collective-permute-done.23 = f32[2560]{0:T(1024)S(1)} collective-permute-done((f32[2560]{0:T(1024)S(1)}, f32[2560]{0:T(1024)S(1)}, u32[]{:S(2)}, u32[]{:S(2)}) %collective-permute-start.23) | collective-permute-done | bytes 10272 | tf_op jit(solution)/shard_map/ppermute | solution.py:533
  172.8 8.5 %shard_map.164 = (bf16[512,2048]{1,0:T(8,128)(2,1)}, bf16[512,512]{1,0:T(8,128)(2,1)}) custom-call(s32[139]{0:T(256)} %concatenate.40.meta, f32[1,512]{1,0:T(1,128)} %slice.25.rinv, f32[1,2048]{1,0:T(1,128)} %slice.26.gain, bf16[528,512]{1,0:T(8,128)(2,1)} %copy-done.21, bf16[528,512]{1,0:T(8,128)(2,1)} %collective-permute-done.25.refs_1_, ...), custom_call_target="tpu_custom_call" | custom-call | flops 3221225472 | bytes 12582912 | tf_op jit(solution)/shard_map/pallas_call | solution.py:405
  181.3 3.8 %collective-permute-start.27 = (bf16[512,512]{1,0:T(8,128)(2,1)}, bf16[512,512]{1,0:T(8,128)(2,1)S(1)}, u32[]{:S(2)}, u32[]{:S(2)}) collective-permute-start(bf16[512,512]{1,0:T(8,128)(2,1)} %get-tuple-element.40), channel_id=1, source_target_pairs={{0,1},{1,0},{2,3},{3,2},{4,5},{5,4},{6,7},{7,6},{8,9},{9,8},{10,11... | collective-permute-start | bytes 1572872 | tf_op jit(solution)/shard_map/ppermute | solution.py:552
  185.1 7.2 %shard_map.167 = (f32[192,1536]{1,0:T(8,128)}, bf16[192,1536]{1,0:T(8,128)(2,1)}, bf16[192,1536]{1,0:T(8,128)(2,1)}, bf16[192,1536]{1,0:T(8,128)(2,1)}) custom-call(bf16[4,192,1024]{2,1,0:T(8,128)(2,1)} %get-tuple-element.44.dkv, bf16[1536,1024]{1,0:T(8,128)(2,1)} %pad_maximum_fusion.w_kv), custom_call_target="tpu_custom_call" | custom-call | flops 2415919104 | bytes 8388608 | tf_op jit(solution)/shard_map/pallas_call | solution.py:434
  193.0 3.7 %fusion.32.o_own = bf16[512,512]{1,0:T(8,128)(2,1)} fusion(bf16[512,2048]{1,0:T(8,128)(2,1)S(1)} %copy-done.10, bf16[1024,2048]{1,0:T(8,128)(2,1)} %get-tuple-element.32.refs_5_), kind=kOutput, calls=%fused_computation.40 | convolution fusion | flops 1074003968 | bytes 4718592 | tf_op jit(solution)/shard_map/dot_general | solution.py:57
  198.7 6.3 %shard_map.165 = (bf16[528,512]{1,0:T(8,128)(2,1)}, bf16[4,192,1024]{2,1,0:T(8,128)(2,1)}) custom-call(s32[139]{0:T(256)} %concatenate.40.meta, f32[1]{0:T(128)S(6)} %tanh.3.gate, f32[512,512]{1,0:T(8,128)} %fusion.18.q_own, bf16[512,512]{1,0:T(8,128)(2,1)} %copy-done.9, bf16[512,512]{1,0:T(8,128)(2,1)} %fusion.32.o_own, bf16[512,512]{1,0:T(8,128)(2,1)} %copy-done.22, ...), custom_call_target="tpu_custom_call" | custom-call | flops 402653184 | bytes 8388608 | tf_op jit(solution)/shard_map/pallas_call | solution.py:304
  211.2 7.1 %shard_map.168 = (f32[192,1536]{1,0:T(8,128)}, bf16[192,1536]{1,0:T(8,128)(2,1)}, bf16[192,1536]{1,0:T(8,128)(2,1)}, bf16[192,1536]{1,0:T(8,128)(2,1)}) custom-call(bf16[4,192,1024]{2,1,0:T(8,128)(2,1)} %get-tuple-element.46.dkv, bf16[1536,1024]{1,0:T(8,128)(2,1)} %pad_maximum_fusion.w_kv), custom_call_target="tpu_custom_call" | custom-call | flops 2415919104 | bytes 8388608 | tf_op jit(solution)/shard_map/pallas_call | solution.py:434
  218.3 3.8 %collective-permute-start.35 = (bf16[192,1536]{1,0:T(8,128)(2,1)}, bf16[192,1536]{1,0:T(8,128)(2,1)}, u32[]{:S(2)}, u32[]{:S(2)}) collective-permute-start(bf16[192,1536]{1,0:T(8,128)(2,1)} %get-tuple-element.53), channel_id=1, source_target_pairs={{0,1},{1,0},{2,3},{3,2},{4,5},{5,4},{6,7},{7,6},{8,9},{9,8},{10,11... | collective-permute-start | bytes 1769480 | tf_op jit(solution)/shard_map/ppermute | solution.py:564
  222.0 4.4 %collective-permute-start.34 = (bf16[192,1536]{1,0:T(8,128)(2,1)}, bf16[192,1536]{1,0:T(8,128)(2,1)}, u32[]{:S(2)}, u32[]{:S(2)}) collective-permute-start(bf16[192,1536]{1,0:T(8,128)(2,1)} %get-tuple-element.52), channel_id=1, source_target_pairs={{0,65},{1,64},{2,67},{3,66},{4,69},{5,68},{6,71},{7,70},{8,73},{9,... | collective-permute-start | bytes 1769480 | tf_op jit(solution)/shard_map/ppermute | solution.py:564
  228.5 7.4 %shard_map.166 = bf16[512,2048]{1,0:T(8,128)(2,1)} custom-call(s32[139]{0:T(256)} %concatenate.40.meta, f32[1,512]{1,0:T(1,128)} %bitcast.94, f32[1,2048]{1,0:T(1,128)} %gain.1, bf16[528,512]{1,0:T(8,128)(2,1)} %get-tuple-element.41.refs_0_, bf16[528,512]{1,0:T(8,128)(2,1)} %get-tuple-element.43.refs_1_, bf16[528,512]{1,0:T(8,128)(2,1)} %copy-done.19, ...), custom_call_target="tpu_custom_call" | custom-call | flops 2147483648 | bytes 12582912 | tf_op jit(solution)/shard_map/pallas_call | solution.py:405
  235.9 10.5 %collective-permute-done.31 = bf16[192,1536]{1,0:T(8,128)(2,1)S(1)} collective-permute-done((bf16[192,1536]{1,0:T(8,128)(2,1)}, bf16[192,1536]{1,0:T(8,128)(2,1)S(1)}, u32[]{:S(2)}, u32[]{:S(2)}) %collective-permute-start.31) | collective-permute-done | bytes 589856 | tf_op jit(solution)/shard_map/ppermute | solution.py:558
  (176 shorter events, 90.0 us)
Async XLA Ops:
  7.2 165.1 %all-gather.3.cloned.1.call-start = ((), (), s32[]{:S(2)}) async-start(), calls=%async_computation | async-start | bytes 6291456 | tf_op jit(solution)/shard_map/all_gather | solution.py:496
  7.9 164.3 %all-gather.5.cloned.1.call-start = ((), (), s32[]{:S(2)}) async-start(), calls=%async_computation.1 | async-start | bytes 4325376 | tf_op jit(solution)/shard_map/all_gather | solution.py:526
  51.9 29.9 %collective-permute-start.9 = (bf16[4,64,2048]{2,1,0:T(8,128)(2,1)S(1)}, bf16[4,64,2048]{2,1,0:T(8,128)(2,1)}, u32[]{:S(2)}, u32[]{:S(2)}) collective-permute-start(bf16[4,64,2048]{2,1,0:T(8,128)(2,1)S(1)} %pad_maximum_fusion.1.refs_0_), channel_id=1, source_target_pairs={{0,48},{2,14},{4,52},{6,2},{8,56},{10,6},{12,60},{14,10},{16,0},{1... | collective-permute-start | bytes 3145736 | tf_op jit(solution)/shard_map/ppermute | solution.py:110
  54.1 34.0 %collective-permute-start.10 = (bf16[4,64,2048]{2,1,0:T(8,128)(2,1)S(1)}, bf16[4,64,2048]{2,1,0:T(8,128)(2,1)}, u32[]{:S(2)}, u32[]{:S(2)}) collective-permute-start(bf16[4,64,2048]{2,1,0:T(8,128)(2,1)S(1)} %pad_maximum_fusion.1.refs_0_), channel_id=1, source_target_pairs={{0,32},{2,10},{4,36},{6,14},{8,40},{10,2},{12,44},{14,6},{16,48},{... | collective-permute-start | bytes 3145736 | tf_op jit(solution)/shard_map/ppermute | solution.py:110
  57.4 24.9 %collective-permute-start.17 = (bf16[4,128,384]{2,1,0:T(8,128)(2,1)S(1)}, bf16[4,128,384]{2,1,0:T(8,128)(2,1)}, u32[]{:S(2)}, u32[]{:S(2)}) collective-permute-start(bf16[4,128,384]{2,1,0:T(8,128)(2,1)S(1)} %pad_maximum_fusion.2.refs_0_), channel_id=1, source_target_pairs={{0,16},{2,6},{4,20},{6,10},{8,24},{10,14},{12,28},{14,2},{16,32},{... | collective-permute-start | bytes 1179656 | tf_op jit(solution)/shard_map/ppermute | solution.py:110
  58.4 29.6 %collective-permute-start.18 = (bf16[4,128,384]{2,1,0:T(8,128)(2,1)S(1)}, bf16[4,128,384]{2,1,0:T(8,128)(2,1)}, u32[]{:S(2)}, u32[]{:S(2)}) collective-permute-start(bf16[4,128,384]{2,1,0:T(8,128)(2,1)S(1)} %pad_maximum_fusion.2.refs_0_), channel_id=1, source_target_pairs={{0,32},{2,10},{4,36},{6,14},{8,40},{10,2},{12,44},{14,6},{16,48},{... | collective-permute-start | bytes 1179656 | tf_op jit(solution)/shard_map/ppermute | solution.py:110
  66.9 26.4 %collective-permute-start = (f32[512]{0:T(512)S(1)}, f32[512]{0:T(512)}, u32[]{:S(2)}, u32[]{:S(2)}) collective-permute-start(f32[512]{0:T(512)S(1)} %fusion), channel_id=1, source_target_pairs={{0,1},{1,0},{2,3},{3,2},{4,5},{5,4},{6,7},{7,6},{8,9},{9,8},{10,11... | collective-permute-start | bytes 6152 | tf_op jit(solution)/shard_map/ppermute | solution.py:530
  82.3 17.9 %collective-permute-start.12 = (bf16[4,64,2048]{2,1,0:T(8,128)(2,1)}, bf16[4,64,2048]{2,1,0:T(8,128)(2,1)}, u32[]{:S(2)}, u32[]{:S(2)}) collective-permute-start(bf16[4,64,2048]{2,1,0:T(8,128)(2,1)} %collective-permute-done.8.refs_1_), channel_id=1, source_target_pairs={{0,2},{2,0},{1,3},{3,1},{4,6},{6,4},{5,7},{7,5},{8,10},{10,8},{9,1... | collective-permute-start | bytes 3145736 | tf_op jit(solution)/shard_map/ppermute | solution.py:523
  97.0 28.2 %collective-permute-start.22 = (bf16[768,384]{1,0:T(8,128)(2,1)}, bf16[768,384]{1,0:T(8,128)(2,1)}, u32[]{:S(2)}, u32[]{:S(2)}) collective-permute-start(bf16[768,384]{1,0:T(8,128)(2,1)} %broadcast_select_fusion.1), channel_id=1, source_target_pairs={{0,65},{64,0},{1,64},{65,1},{2,67},{66,2},{3,66},{67,3},{4,69},{68... | collective-permute-start | bytes 1769480 | tf_op jit(solution)/shard_map/ppermute | solution.py:512
  98.2 27.0 %collective-permute-start.21 = (bf16[768,384]{1,0:T(8,128)(2,1)}, bf16[768,384]{1,0:T(8,128)(2,1)}, u32[]{:S(2)}, u32[]{:S(2)}) collective-permute-start(bf16[768,384]{1,0:T(8,128)(2,1)} %broadcast_select_fusion.1), channel_id=1, source_target_pairs={{0,1},{64,65},{1,0},{65,64},{2,3},{66,67},{3,2},{67,66},{4,5},{68,... | collective-permute-start | bytes 1769480 | tf_op jit(solution)/shard_map/ppermute | solution.py:512
  100.2 28.6 %collective-permute-start.20 = (bf16[768,384]{1,0:T(8,128)(2,1)}, bf16[768,384]{1,0:T(8,128)(2,1)}, u32[]{:S(2)}, u32[]{:S(2)}) collective-permute-start(bf16[768,384]{1,0:T(8,128)(2,1)} %broadcast_select_fusion.1), channel_id=1, source_target_pairs={{0,64},{64,1},{1,65},{65,0},{2,66},{66,3},{3,67},{67,2},{4,68},{68... | collective-permute-start | bytes 1769480 | tf_op jit(solution)/shard_map/ppermute | solution.py:512
  111.7 27.6 %collective-permute-start.15 = (bf16[512,512]{1,0:T(8,128)(2,1)}, bf16[512,512]{1,0:T(8,128)(2,1)S(1)}, u32[]{:S(2)}, u32[]{:S(2)}) collective-permute-start(bf16[512,512]{1,0:T(8,128)(2,1)} %get-tuple-element.31), channel_id=1, source_target_pairs={{0,1},{1,0},{64,65},{65,64},{2,3},{3,2},{66,67},{67,66},{4,5},{5,4... | collective-permute-start | bytes 1572872 | tf_op jit(solution)/shard_map/ppermute | solution.py:543
  119.8 24.9 %collective-permute-start.16 = (bf16[512,512]{1,0:T(8,128)(2,1)}, bf16[512,512]{1,0:T(8,128)(2,1)}, u32[]{:S(2)}, u32[]{:S(2)}) collective-permute-start(bf16[512,512]{1,0:T(8,128)(2,1)} %get-tuple-element.33), channel_id=1, source_target_pairs={{64,65},{65,64},{66,67},{67,66},{68,69},{69,68},{70,71},{71,70},{7... | collective-permute-start | bytes 1572872 | tf_op jit(solution)/shard_map/ppermute | solution.py:545
  151.2 20.8 %collective-permute-start.24 = (bf16[528,512]{1,0:T(8,128)(2,1)}, bf16[528,512]{1,0:T(8,128)(2,1)S(1)}, u32[]{:S(2)}, u32[]{:S(2)}) collective-permute-start(bf16[528,512]{1,0:T(8,128)(2,1)} %get-tuple-element.41.refs_0_), channel_id=1, source_target_pairs={{64,0},{65,1},{66,2},{67,3},{68,4},{69,5},{70,6},{71,7},{72,8},{73... | collective-permute-start | bytes 1622024 | tf_op jit(solution)/shard_map/ppermute | solution.py:550
  152.5 19.7 %collective-permute-start.25 = (bf16[528,512]{1,0:T(8,128)(2,1)}, bf16[528,512]{1,0:T(8,128)(2,1)}, u32[]{:S(2)}, u32[]{:S(2)}) collective-permute-start(bf16[528,512]{1,0:T(8,128)(2,1)} %get-tuple-element.41.refs_0_), channel_id=1, source_target_pairs={{64,1},{65,0},{66,3},{67,2},{68,5},{69,4},{70,7},{71,6},{72,9},{73... | collective-permute-start | bytes 1622024 | tf_op jit(solution)/shard_map/ppermute | solution.py:550
  153.8 17.0 %collective-permute-start.23 = (f32[2560]{0:T(1024)S(1)}, f32[2560]{0:T(1024)S(1)}, u32[]{:S(2)}, u32[]{:S(2)}) collective-permute-start(f32[2560]{0:T(1024)S(1)} %pad_maximum_fusion.4), channel_id=1, source_target_pairs={{64,0},{65,1},{66,2},{67,3},{68,4},{69,5},{70,6},{71,7},{72,8},{73... | collective-permute-start | bytes 30728 | tf_op jit(solution)/shard_map/ppermute | solution.py:533
  192.3 29.7 %collective-permute-start.32 = (bf16[192,1536]{1,0:T(8,128)(2,1)}, bf16[192,1536]{1,0:T(8,128)(2,1)S(1)}, u32[]{:S(2)}, u32[]{:S(2)}) collective-permute-start(bf16[192,1536]{1,0:T(8,128)(2,1)} %get-tuple-element.50), channel_id=1, source_target_pairs={{64,65},{65,64},{66,67},{67,66},{68,69},{69,68},{70,71},{71,70},{7... | collective-permute-start | bytes 1769480 | tf_op jit(solution)/shard_map/ppermute | solution.py:558
  196.7 21.5 %collective-permute-start.28 = (bf16[528,512]{1,0:T(8,128)(2,1)}, bf16[528,512]{1,0:T(8,128)(2,1)S(1)}, u32[]{:S(2)}, u32[]{:S(2)}) collective-permute-start(bf16[528,512]{1,0:T(8,128)(2,1)} %get-tuple-element.41.refs_0_), channel_id=1, source_target_pairs={{64,65},{65,64},{66,67},{67,66},{68,69},{69,68},{70,71},{71,70},{7... | collective-permute-start | bytes 1622024 | tf_op jit(solution)/shard_map/ppermute | solution.py:555
  205.0 21.4 %collective-permute-start.29 = (bf16[528,512]{1,0:T(8,128)(2,1)}, bf16[528,512]{1,0:T(8,128)(2,1)S(1)}, u32[]{:S(2)}, u32[]{:S(2)}) collective-permute-start(bf16[528,512]{1,0:T(8,128)(2,1)} %get-tuple-element.43.refs_1_), channel_id=1, source_target_pairs={{0,1},{1,0},{2,3},{3,2},{4,5},{5,4},{6,7},{7,6},{8,9},{9,8},{10,11... | collective-permute-start | bytes 1622024 | tf_op jit(solution)/shard_map/ppermute | solution.py:561
  208.6 37.8 %collective-permute-start.31 = (bf16[192,1536]{1,0:T(8,128)(2,1)}, bf16[192,1536]{1,0:T(8,128)(2,1)S(1)}, u32[]{:S(2)}, u32[]{:S(2)}) collective-permute-start(bf16[192,1536]{1,0:T(8,128)(2,1)} %get-tuple-element.49), channel_id=1, source_target_pairs={{64,1},{65,0},{66,3},{67,2},{68,5},{69,4},{70,7},{71,6},{72,9},{73... | collective-permute-start | bytes 1769480 | tf_op jit(solution)/shard_map/ppermute | solution.py:558
  209.9 36.6 %collective-permute-start.30 = (bf16[192,1536]{1,0:T(8,128)(2,1)}, bf16[192,1536]{1,0:T(8,128)(2,1)S(1)}, u32[]{:S(2)}, u32[]{:S(2)}) collective-permute-start(bf16[192,1536]{1,0:T(8,128)(2,1)} %get-tuple-element.48), channel_id=1, source_target_pairs={{64,0},{65,1},{66,2},{67,3},{68,4},{69,5},{70,6},{71,7},{72,8},{73... | collective-permute-start | bytes 1769480 | tf_op jit(solution)/shard_map/ppermute | solution.py:558
  218.3 28.2 %collective-permute-start.35 = (bf16[192,1536]{1,0:T(8,128)(2,1)}, bf16[192,1536]{1,0:T(8,128)(2,1)}, u32[]{:S(2)}, u32[]{:S(2)}) collective-permute-start(bf16[192,1536]{1,0:T(8,128)(2,1)} %get-tuple-element.53), channel_id=1, source_target_pairs={{0,1},{1,0},{2,3},{3,2},{4,5},{5,4},{6,7},{7,6},{8,9},{9,8},{10,11... | collective-permute-start | bytes 1769480 | tf_op jit(solution)/shard_map/ppermute | solution.py:564
  222.0 24.4 %collective-permute-start.34 = (bf16[192,1536]{1,0:T(8,128)(2,1)}, bf16[192,1536]{1,0:T(8,128)(2,1)}, u32[]{:S(2)}, u32[]{:S(2)}) collective-permute-start(bf16[192,1536]{1,0:T(8,128)(2,1)} %get-tuple-element.52), channel_id=1, source_target_pairs={{0,65},{1,64},{2,67},{3,66},{4,69},{5,68},{6,71},{7,70},{8,73},{9,... | collective-permute-start | bytes 1769480 | tf_op jit(solution)/shard_map/ppermute | solution.py:564
  226.4 20.0 %collective-permute-start.33 = (bf16[192,1536]{1,0:T(8,128)(2,1)}, bf16[192,1536]{1,0:T(8,128)(2,1)}, u32[]{:S(2)}, u32[]{:S(2)}) collective-permute-start(bf16[192,1536]{1,0:T(8,128)(2,1)} %get-tuple-element.51), channel_id=1, source_target_pairs={{0,64},{1,65},{2,66},{3,67},{4,68},{5,69},{6,70},{7,71},{8,72},{9,... | collective-permute-start | bytes 1769480 | tf_op jit(solution)/shard_map/ppermute | solution.py:564
  (49 other events, 607.8 us)
Sparse Core Ops, SparseCore 0:
  9.7 64.5 all-gather.2
  76.5 47.3 all-gather.4

commit v4 on v3

--- a/solution.py
+++ b/solution.py
@@ -73,18 +73,18 @@
 
 
 def pool_kernel(which, counts, tiles, queries, out):
-    for slide in range(4):
-        live = lax.broadcasted_iota(jnp.int32, (LAT, MAXT), 1) < counts[slide]
-        for head in range(QUARTER // HEAD):
-            cols = slice(head * HEAD, (head + 1) * HEAD)
-            tile = tiles[slide, :, cols]
-            query = queries[:, cols]
-            scores = dot(query, tile, NT) * SCALE
-            scores = jnp.where(live, scores, -1e30)
-            exps = jnp.exp(scores - jnp.max(scores, axis=1, keepdims=True))
-            weights = (exps / jnp.sum(exps, axis=1, keepdims=True)).astype(BF)
-            pooled = dot(weights, tile, NN)
-            out[slide * LAT : (slide + 1) * LAT, cols] = (query.astype(F32) + pooled).astype(BF)
+    heads = [slice(head * HEAD, (head + 1) * HEAD) for head in range(QUARTER // HEAD)]
+    pairs = [(slide, cols) for slide in range(4) for cols in heads]
+    slot = lax.broadcasted_iota(jnp.int32, (LAT, MAXT), 1)
+    tile = [tiles[slide, :, cols] for slide, cols in pairs]
+    query = [queries[:, cols] for _, cols in pairs]
+    scores = [dot(q, t, NT) * SCALE for q, t in zip(query, tile)]
+    scores = [jnp.where(slot < counts[s], x, -1e30) for x, (s, _) in zip(scores, pairs)]
+    exps = [jnp.exp(s - jnp.max(s, axis=1, keepdims=True)) for s in scores]
+    weights = [(e / jnp.sum(e, axis=1, keepdims=True)).astype(BF) for e in exps]
+    pooled = [dot(w, t, NN) for w, t in zip(weights, tile)]
+    for (slide, cols), q, p in zip(pairs, query, pooled):
+        out[slide * LAT : (slide + 1) * LAT, cols] = (q.astype(F32) + p).astype(BF)
 
 
 def pool(which, counts, tiles, queries):
@@ -104,10 +104,12 @@
     )(which, counts, tiles, queries)
 
 
-def gather_chips(block):
-    parts = [block] + [lax.ppermute(block, DP, yz_perm(1, k)) for k in (1, 2, 3)]
-    bundle = jnp.stack(parts)
-    return [bundle] + [lax.ppermute(bundle, DP, yz_perm(2, k)) for k in (1, 2, 3)]
+def gather_chips(blocks):
+    first = [[lax.ppermute(b, DP, yz_perm(1, k)) for k in (1, 2, 3)] for b in blocks]
+    first = lax.optimization_barrier(first)
+    bundles = [jnp.stack([b, *parts]) for b, parts in zip(blocks, first)]
+    bundles = lax.optimization_barrier(bundles)
+    return [[b] + [lax.ppermute(b, DP, yz_perm(2, k)) for k in (1, 2, 3)] for b in bundles]
 
 
 def places(z, y, core):
@@ -172,16 +174,12 @@
     load = pltpu.make_async_copy(x, x_v, sems.at[2])
     load.start()
     half = w_v.shape[0] // 2
-    for part in (1, 0):
-        for a in range(8):
-            for k in range(4):
-                at = pl.multiple_of(meta[ROWS + a * 4 + k], 32)
-
-                @pl.when((at >= half) == (part == 1))
-                def _():
-                    pltpu.make_async_copy(
-                        ins[a].at[k, pl.ds(kind * 32, 32)], w_v.at[pl.ds(at, 32)], sems.at[part]
-                    ).start()
+    for a in range(8):
+        for k in range(4):
+            at = pl.multiple_of(meta[ROWS + a * 4 + k], 32)
+            pltpu.make_async_copy(
+                ins[a].at[k, pl.ds(kind * 32, 32)], w_v.at[pl.ds(at, 32)], sems.at[at // half]
+            ).start()
 
     def group(part):
         return w_v.at[pl.ds(part * half, half)]
@@ -359,7 +357,7 @@
     stat = column(
         jnp.sum(left[tokens:].astype(F32) + right[tokens:].astype(F32), axis=0, keepdims=True)
     )
-    left, right = left[:tokens], right[:tokens]
+    dq = jnp.concatenate([left[:tokens], right[:tokens]], axis=1)
     scale = column(rinv[...])
     share = scale * scale * stat / MODEL_WIDTH
     if following:
@@ -369,7 +367,7 @@
         for copy in copies(tile):
             copy.wait()
         cols = slice(tile * TILE, (tile + 1) * TILE)
-        dnormed = dot(left, wq_v[:half, cols], NN) + dot(right, wq_v[half:, cols], NN)
+        dnormed = dot(dq, wq_v[:, cols], NN)
         upstream = up_v[:, cols].astype(F32)
         if following:
             upstream = jnp.where(live, upstream, 0.0)
@@ -418,12 +416,11 @@
 
 
 def term_kernel(dkv, w_kv, own, *terms):
-    for k in range(4):
-        value = dot(dkv[k], w_kv[...], NT)
-        if k == 0:
-            own[...] = value
-        else:
-            terms[k - 1][...] = value.astype(BF)
+    rows = own.shape[0]
+    value = dot(dkv[...].reshape(4 * rows, dkv.shape[2]), w_kv[...], NT)
+    own[...] = value[:rows]
+    for k, term in enumerate(terms, 1):
+        term[...] = value[k * rows : (k + 1) * rows].astype(BF)
 
 
 def latent_terms(dkv, w_kv):
@@ -496,34 +493,8 @@
     h_all = lax.all_gather(h, "segment")
 
     wq_t = w_query[0].T
-    block = jnp.concatenate([w_out[0], wq_t], axis=0)
-    blocks = gather_chips(block)
-
     pooled = pool(me_x.reshape(1).astype(jnp.int32), tile_counts.reshape(4), tiles, lat_query)
-    lat_blocks = gather_chips(pooled)
-    lat_blocks[3], blocks[1], blocks[3] = lax.optimization_barrier(
-        (lat_blocks[3], blocks[1], blocks[3])
-    )
-    near, across = select(picks, lat_blocks)
-    crossed = lax.ppermute(across, "core", [(0, 1), (1, 0)])
-    is_near = jnp.repeat(source_core[0] == core, LAT)[:, None]
-    chosen = jnp.where(is_near, near, crossed)
-    latents = jnp.concatenate(
-        [chosen] + [lax.ppermute(chosen, X, x_perm(k)) for k in (1, 2, 3)], axis=1
-    )
-    w_kv = jnp.concatenate([w_key[0], w_value[0]], axis=1)
-    w_kv_x = jnp.concatenate(
-        [
-            lax.dynamic_slice_in_dim(w_kv, lax.rem(me_x - k + 4, 4) * QUARTER, QUARTER, 0)
-            for k in range(4)
-        ],
-        axis=0,
-    )
-    kv = dot(latents, w_kv_x, NN).astype(BF)
-    blocks = blocks + [lax.ppermute(b, "core", [(0, 1), (1, 0)]) for b in blocks]
-
-    wq_t, _ = lax.optimization_barrier((wq_t, lat_blocks[0]))
-    wq1 = lax.all_gather(lax.ppermute(wq_t, "segment", [(1, 0)]), DP, axis=0, tiled=True)
+    lat_blocks, blocks = gather_chips([pooled, jnp.concatenate([w_out[0], wq_t], axis=0)])
 
     h32 = h.astype(F32)
     partial = jnp.sum(h32 * h32, axis=1)
@@ -538,13 +509,44 @@
     up1 = jnp.where(live[:, None], cotangent, jnp.zeros((), BF))
     rinv = rinv[None]
     gate = jnp.tanh(attn_gate)
+    w_kv = jnp.concatenate([w_key[0], w_value[0]], axis=1)
+    w_kv_x = jnp.concatenate(
+        [
+            lax.dynamic_slice_in_dim(w_kv, lax.rem(me_x - k + 4, 4) * QUARTER, QUARTER, 0)
+            for k in range(4)
+        ],
+        axis=0,
+    )
+
+    wq_t, _ = lax.optimization_barrier((wq_t, blocks[0]))
+    lat_blocks[0], wq1 = lax.optimization_barrier(
+        (lat_blocks[0], lax.ppermute(wq_t, "segment", [(1, 0)]))
+    )
+    wq1 = lax.all_gather(wq1, DP, axis=0, tiled=True)
+
+    near, across = select(picks, lat_blocks)
+    near, across, blocks[1], blocks[3] = lax.optimization_barrier(
+        (near, across, blocks[1], blocks[3])
+    )
+    crossed = lax.ppermute(across, "core", [(0, 1), (1, 0)])
+    is_near = jnp.repeat(source_core[0] == core, LAT)[:, None]
+    chosen = jnp.where(is_near, near, crossed)
+    chosen, blocks[2], normed, up1, meta, w_kv, w_kv_x = lax.optimization_barrier(
+        (chosen, blocks[2], normed, up1, meta, w_kv, w_kv_x)
+    )
+    latents = [chosen] + [lax.ppermute(chosen, X, x_perm(k)) for k in (1, 2, 3)]
+    blocks = blocks + [lax.ppermute(b, "core", [(0, 1), (1, 0)]) for b in blocks]
+
 
     q_send, wq = project(1, meta, normed, blocks)
     q_got = lax.ppermute(q_send, X, SWAP_MP)
     o_send, wo = project(0, meta, up1, blocks)
     o_got = lax.ppermute(o_send, X, LAST_SWAP)
     q_own = dot(normed, wq[:half], NT)
+    q_own, rinv1, gain1 = lax.optimization_barrier((q_own, rinv1, gain1))
     o_own = dot(up1, wo[:half], NT).astype(BF)
+    latents, o_send = lax.optimization_barrier((latents, o_send))
+    kv = dot(jnp.concatenate(latents, axis=1), w_kv_x, NN).astype(BF)
     probs = forward(meta, q_own, q_got, kv)
     dq1, dkv1 = backward(meta, gate, q_own, q_got, o_own, o_got, kv, probs)
     dqs = [lax.ppermute(dq1, X, LAST_TO_SAME), lax.ppermute(dq1, X, LAST_TO_CROSS)]
@@ -556,15 +558,19 @@
     own1, *terms = latent_terms(dkv1, w_kv)
     moves = (LAST_TO_SAME, LAST_TO_CROSS, LAST_SWAP)
     got = [lax.ppermute(t, X, p) for t, p in zip(terms, moves)]
+    received = jnp.where(last, own1, 0.0)
+    for term in got:
+        received = received + term.astype(F32)
 
     dq0, dkv0 = backward(meta, gate, q_own, q_got, o_own, o_got, kv, probs)
     got0 = lax.ppermute(dq0, X, FIRST_SWAP)
     own0, *terms = latent_terms(dkv0, w_kv)
+    terms, received = lax.optimization_barrier((terms, received))
     moves = (FIRST_TO_SAME, FIRST_TO_CROSS, FIRST_SWAP)
-    got += [lax.ppermute(t, X, p) for t, p in zip(terms, moves)]
+    got = [lax.ppermute(t, X, p) for t, p in zip(terms, moves)]
     (grads,) = back(meta, rinv, gain, [dq1, dq0, got1, got0], up, h, wq)
 
-    latent_grad = jnp.where(last, own1, own0)
+    latent_grad = received + jnp.where(last, 0.0, own0)
     for term in got:
         latent_grad = latent_grad + term.astype(F32)
     return grads[None], latent_grad.reshape(reports, 48, E)

time: 259 us -> 274 us (1.058)
  waiting for transfers between devices: 66 us -> 80.5 us
  local copies, waits for them, and re-layouts: 12.7 us -> 19.2 us
  Pallas kernels: 69.6 us -> 65.4 us
    ppermute x1, waiting for transfers between devices: 0.01 us -> 12.1 us  [per_device(): lax.ppermute(dq1, X, LAST_TO_SAME)]
    ppermute x18 -> x15, waiting for transfers between devices: 26.1 us -> 35.6 us  [the longest x3 14.1 us: per_device(): latents = [chosen] + [lax.ppermute(chosen, X, x_perm(k)) for k in (1, 2, 3)]]
    ppermute x1, waiting for transfers between devices: 13.6 us -> 4.29 us  [per_device(): lax.ppermute(jnp.concatenate([rinv, gain[0]]), 'segment', [(1, 0)])[None]]
    ppermute x18 -> x15, starting transfers between devices: 33.1 us -> 25.1 us  [the longest x6 14.4 us: gather_chips(): lax.ppermute(b, DP, yz_perm(2, k))]
    ppermute x3 -> x6, starting transfers between devices: 3.27 us -> 9.92 us  [per_device(): got = [lax.ppermute(t, X, p) for t, p in zip(terms, moves)]]
    unnamed x72 -> x78, local copies, waits for them, and re-layouts: 3.79 us -> 9.82 us
    ppermute x3 -> x6, waiting for transfers between devices: 10.5 us -> 16.5 us  [per_device(): got = [lax.ppermute(t, X, p) for t, p in zip(terms, moves)]]
    ppermute x1, waiting for transfers between devices: 5.09 us -> 0.01 us  [per_device(): q_got = lax.ppermute(q_send, X, SWAP_MP)]
  transfers between devices with their start and end apart: 38 -> 38, of which waited for: 14 -> 13; matrix products, arithmetic and copies ran while one was open for 17% -> 16% of each run, Pallas kernels for 24% -> 21%
where the time goes in v4:
time: 274 us; the launch traced here: 272 us
  waiting for transfers between devices  80.5 us (29%)
  Pallas kernels  65.4 us (24%)
  starting transfers between devices  57.2 us (21%)
  other arithmetic  19.7 us (7%)
  local copies, waits for them, and re-layouts  19.2 us (7%)
  between operations  15.7 us (6%)
  matrix products  14.1 us (5%)
    ppermute x6, waiting for transfers between devices, per_device(): got = [lax.ppermute(t, X, p) for t, p in zip(terms, moves)]  16.5 us
    pallas_call x2, Pallas kernels, back(): pl.pallas_call(functools.partial(back_kernel, wo is not None), in_specs=i...  15.7 us
    ppermute x6, starting transfers between devices, gather_chips(): lax.ppermute(b, DP, yz_perm(2, k))  14.4 us
    dot_general x4, matrix products, dot(): return lax.dot_general(a, b, dims, preferred_element_type=F32)  14.1 us
    ppermute x3, waiting for transfers between devices, per_device(): latents = [chosen] + [lax.ppermute(chosen, X, x_perm(k)) for k in (1, 2, 3)]  14.1 us
    pallas_call x2, Pallas kernels, project(): pl.pallas_call(functools.partial(project_kernel, kind), in_specs=[SMEM, A...  13.9 us
    pallas_call x2, Pallas kernels, backward(): pl.pallas_call(backward_kernel, grid=(reports,), in_specs=[SMEM, SMEM, to...  12.5 us
    pallas_call x2, Pallas kernels, latent_terms(): pl.pallas_call(term_kernel, grid=(features // tile,), in_specs=[whole(dkv...  12.4 us
  transfers between devices with their start and end apart: 38, of which 13 were waited for; matrix products, arithmetic and copies ran while one was open for 16% of the time, Pallas kernels for 21%

profile of v4, /device:TPU:0, one launch (start us, length us, event | category | flops | bytes accessed | tf_op | source)
XLA Modules:
  0.0 271.8 jit_solution(11451267738641759838)
XLA Ops:
  18.4 4.6 %collective-permute-done = bf16[128,384]{1,0:T(8,128)(2,1)S(1)} collective-permute-done((bf16[128,384]{1,0:T(8,128)(2,1)}, bf16[128,384]{1,0:T(8,128)(2,1)S(1)}, u32[]{:S(2)}, u32[]{:S(2)}) %collective-permute-start) | collective-permute-done | bytes 98336 | tf_op jit(solution)/shard_map/ppermute | solution.py:108
  24.0 3.8 %collective-permute-done.2 = bf16[128,384]{1,0:T(8,128)(2,1)S(1)} collective-permute-done((bf16[128,384]{1,0:T(8,128)(2,1)}, bf16[128,384]{1,0:T(8,128)(2,1)S(1)}, u32[]{:S(2)}, u32[]{:S(2)}) %collective-permute-start.2) | collective-permute-done | bytes 98336 | tf_op jit(solution)/shard_map/ppermute | solution.py:108
  31.6 8.8 %collective-permute-done.6 = bf16[32,2048]{1,0:T(8,128)(2,1)S(1)} collective-permute-done((bf16[32,2048]{1,0:T(8,128)(2,1)}, bf16[32,2048]{1,0:T(8,128)(2,1)S(1)}, u32[]{:S(2)}, u32[]{:S(2)}) %collective-permute-start.6) | collective-permute-done | bytes 131104 | tf_op jit(solution)/shard_map/ppermute | solution.py:523
  65.8 5.9 %collective-permute-done.7.refs_1_ = bf16[4,128,384]{2,1,0:T(8,128)(2,1)} collective-permute-done((bf16[4,128,384]{2,1,0:T(8,128)(2,1)S(1)}, bf16[4,128,384]{2,1,0:T(8,128)(2,1)}, u32[]{:S(2)}, u32[]{:S(2)}) %collective-permute-start.7) | collective-permute-done | bytes 393248 | tf_op jit(solution)/shard_map/ppermute | solution.py:112
  78.8 6.1 %collective-permute-start.13 = (bf16[4,64,2048]{2,1,0:T(8,128)(2,1)S(1)}, bf16[4,64,2048]{2,1,0:T(8,128)(2,1)}, u32[]{:S(2)}, u32[]{:S(2)}) collective-permute-start(bf16[4,64,2048]{2,1,0:T(8,128)(2,1)S(1)} %pad_maximum_fusion.2.refs_0_), channel_id=1, source_target_pairs={{0,32},{2,10},{4,36},{6,14},{8,40},{10,2},{12,44},{14,6},{16,48},{... | collective-permute-start | bytes 3145736 | tf_op jit(solution)/shard_map/ppermute | solution.py:112
  93.0 6.2 %collective-permute-done.13.refs_2_ = bf16[4,64,2048]{2,1,0:T(8,128)(2,1)} collective-permute-done((bf16[4,64,2048]{2,1,0:T(8,128)(2,1)S(1)}, bf16[4,64,2048]{2,1,0:T(8,128)(2,1)}, u32[]{:S(2)}, u32[]{:S(2)}) %collective-permute-start.13) | collective-permute-done | bytes 1048608 | tf_op jit(solution)/shard_map/ppermute | solution.py:112
  100.5 4.3 %collective-permute-done.19 = f32[2560]{0:T(1024)S(1)} collective-permute-done((f32[2560]{0:T(1024)S(1)}, f32[2560]{0:T(1024)S(1)}, u32[]{:S(2)}, u32[]{:S(2)}) %collective-permute-start.19) | collective-permute-done | bytes 10272 | tf_op jit(solution)/shard_map/ppermute | solution.py:504
  113.0 7.0 %shard_map.160 = (bf16[512,512]{1,0:T(8,128)(2,1)}, bf16[1024,2048]{1,0:T(8,128)(2,1)}) custom-call(s32[139]{0:T(256)} %concatenate.42.meta, bf16[512,2048]{1,0:T(8,128)(2,1)} %fusion.2.x, bf16[4,64,2048]{2,1,0:T(8,128)(2,1)} %copy-done.1, bf16[4,64,2048]{2,1,0:T(8,128)(2,1)} %collective-permute-done.10.refs_1_, ...), custom_call_target="tpu_custom_call" | custom-call | flops 1073741824 | bytes 12582912 | tf_op jit(solution)/shard_map/pallas_call | solution.py:202
  123.0 6.9 %shard_map.161 = (bf16[512,512]{1,0:T(8,128)(2,1)}, bf16[1024,2048]{1,0:T(8,128)(2,1)}) custom-call(s32[139]{0:T(256)} %concatenate.42.meta, bf16[512,2048]{1,0:T(8,128)(2,1)} %broadcast_select_fusion.x, bf16[4,64,2048]{2,1,0:T(8,128)(2,1)} %copy-done.1, bf16[4,64,2048]{2,1,0:T(8,128)(2,1)} %collective-permute-done.10.refs_1_, ...), custom_call_target="tpu_custom_call" | custom-call | flops 1073741824 | bytes 12582912 | tf_op jit(solution)/shard_map/pallas_call | solution.py:202
  130.8 14.1 %collective-permute-done.22 = bf16[768,384]{1,0:T(8,128)(2,1)} collective-permute-done((bf16[768,384]{1,0:T(8,128)(2,1)}, bf16[768,384]{1,0:T(8,128)(2,1)}, u32[]{:S(2)}, u32[]{:S(2)}) %collective-permute-start.22) | collective-permute-done | bytes 589856 | tf_op jit(solution)/shard_map/ppermute | solution.py:537
  144.8 6.0 %fusion.17.keys.vals = bf16[768,1024]{1,0:T(8,128)(2,1)} fusion(bf16[1536,1024]{1,0:T(8,128)(2,1)} %pad_maximum_fusion.1, bf16[768,384]{1,0:T(8,128)(2,1)S(1)} %collective-permute-done.24, bf16[768,384]{1,0:T(8,128)(2,1)S(1)} %collective-permute-done.23, bf16[768,384]{1,0:T(8,128)(2,1)} %collective-permute-done.22, bf16[768,384]{1,0:T(8,128)(2,1)} %broadcast_select_fusion.1), kind=kOutput, calls=%fused_computation.32 | convolution fusion | flops 2426142720 | bytes 7077888 | tf_op jit(solution)/shard_map/dot_general | solution.py:57
  157.0 4.7 %shard_map.162.probs = f32[4,512,192]{2,1,0:T(8,128)} custom-call(s32[139]{0:T(256)} %concatenate.42.meta, f32[512,512]{1,0:T(8,128)} %fusion.11.q_own, bf16[512,512]{1,0:T(8,128)(2,1)} %copy-done.7, bf16[768,1024]{1,0:T(8,128)(2,1)} %fusion.17.keys.vals), custom_call_target="tpu_custom_call" | custom-call | flops 100663296 | bytes 6291456 | tf_op jit(solution)/shard_map/pallas_call | solution.py:250
  162.5 6.3 %shard_map.163 = (bf16[528,512]{1,0:T(8,128)(2,1)}, bf16[4,192,1024]{2,1,0:T(8,128)(2,1)}) custom-call(s32[139]{0:T(256)} %concatenate.42.meta, f32[1]{0:T(128)S(6)} %tanh.3.gate, f32[512,512]{1,0:T(8,128)} %fusion.11.q_own, bf16[512,512]{1,0:T(8,128)(2,1)} %copy-done.7, bf16[512,512]{1,0:T(8,128)(2,1)} %fusion.20.o_own, bf16[512,512]{1,0:T(8,128)(2,1)} %copy-done.22, ...), custom_call_target="tpu_custom_call" | custom-call | flops 402653184 | bytes 8388608 | tf_op jit(solution)/shard_map/pallas_call | solution.py:302
  171.3 12.1 %collective-permute-done.25.refs_0_ = bf16[528,512]{1,0:T(8,128)(2,1)S(1)} collective-permute-done((bf16[528,512]{1,0:T(8,128)(2,1)}, bf16[528,512]{1,0:T(8,128)(2,1)S(1)}, u32[]{:S(2)}, u32[]{:S(2)}) %collective-permute-start.25) | collective-permute-done | bytes 540704 | tf_op jit(solution)/shard_map/ppermute | solution.py:552
  186.8 8.4 %shard_map.164 = (bf16[512,2048]{1,0:T(8,128)(2,1)}, bf16[512,512]{1,0:T(8,128)(2,1)}) custom-call(s32[139]{0:T(256)} %concatenate.42.meta, f32[1,512]{1,0:T(1,128)} %slice.25.rinv, f32[1,2048]{1,0:T(1,128)} %slice.26.gain, bf16[528,512]{1,0:T(8,128)(2,1)} %copy-done.19, bf16[528,512]{1,0:T(8,128)(2,1)} %copy-done.20, bf16[512,2048]{1,0:T(8,128)(2,1)} %refs_2_.1, ...), custom_call_target="tpu_custom_call" | custom-call | flops 3221225472 | bytes 12582912 | tf_op jit(solution)/shard_map/pallas_call | solution.py:403
  199.7 6.2 %shard_map.168 = (f32[192,1536]{1,0:T(8,128)}, bf16[192,1536]{1,0:T(8,128)(2,1)}, bf16[192,1536]{1,0:T(8,128)(2,1)}, bf16[192,1536]{1,0:T(8,128)(2,1)}) custom-call(bf16[4,192,1024]{2,1,0:T(8,128)(2,1)} %get-tuple-element.102.dkv, bf16[1536,1024]{1,0:T(8,128)(2,1)} %pad_maximum_fusion.w_kv), custom_call_target="tpu_custom_call" | custom-call | flops 2415919104 | bytes 8388608 | tf_op jit(solution)/shard_map/pallas_call | solution.py:431
  209.2 3.7 %fusion.23.o_own = bf16[512,512]{1,0:T(8,128)(2,1)} fusion(bf16[512,2048]{1,0:T(8,128)(2,1)S(1)} %copy-done.13, bf16[1024,2048]{1,0:T(8,128)(2,1)} %get-tuple-element.80.refs_5_), kind=kOutput, calls=%fused_computation.34 | convolution fusion | flops 1074003968 | bytes 4718592 | tf_op jit(solution)/shard_map/dot_general | solution.py:57
  213.7 6.2 %shard_map.165 = (bf16[528,512]{1,0:T(8,128)(2,1)}, bf16[4,192,1024]{2,1,0:T(8,128)(2,1)}) custom-call(s32[139]{0:T(256)} %concatenate.42.meta, f32[1]{0:T(128)S(6)} %tanh.3.gate, f32[512,512]{1,0:T(8,128)} %fusion.11.q_own, bf16[512,512]{1,0:T(8,128)(2,1)} %copy-done.7, bf16[512,512]{1,0:T(8,128)(2,1)} %fusion.23.o_own, bf16[512,512]{1,0:T(8,128)(2,1)} %copy-done.21, ...), custom_call_target="tpu_custom_call" | custom-call | flops 402653184 | bytes 8388608 | tf_op jit(solution)/shard_map/pallas_call | solution.py:302
  219.9 4.5 %collective-permute-start.29 = (bf16[528,512]{1,0:T(8,128)(2,1)}, bf16[528,512]{1,0:T(8,128)(2,1)}, u32[]{:S(2)}, u32[]{:S(2)}) collective-permute-start(bf16[528,512]{1,0:T(8,128)(2,1)} %get-tuple-element.96.refs_1_), channel_id=1, source_target_pairs={{0,1},{1,0},{2,3},{3,2},{4,5},{5,4},{6,7},{7,6},{8,9},{9,8},{10,11... | collective-permute-start | bytes 1622024 | tf_op jit(solution)/shard_map/ppermute | solution.py:566
  224.5 6.2 %shard_map.167 = (f32[192,1536]{1,0:T(8,128)}, bf16[192,1536]{1,0:T(8,128)(2,1)}, bf16[192,1536]{1,0:T(8,128)(2,1)}, bf16[192,1536]{1,0:T(8,128)(2,1)}) custom-call(bf16[4,192,1024]{2,1,0:T(8,128)(2,1)} %get-tuple-element.97.dkv, bf16[1536,1024]{1,0:T(8,128)(2,1)} %pad_maximum_fusion.w_kv), custom_call_target="tpu_custom_call" | custom-call | flops 2415919104 | bytes 8388608 | tf_op jit(solution)/shard_map/pallas_call | solution.py:431
  236.0 4.0 %collective-permute-start.35 = (bf16[192,1536]{1,0:T(8,128)(2,1)}, bf16[192,1536]{1,0:T(8,128)(2,1)S(1)}, u32[]{:S(2)}, u32[]{:S(2)}) collective-permute-start(bf16[192,1536]{1,0:T(8,128)(2,1)} %get-tuple-element.111), channel_id=1, source_target_pairs={{0,1},{1,0},{2,3},{3,2},{4,5},{5,4},{6,7},{7,6},{8,9},{9,8},{10,11... | collective-permute-start | bytes 1769480 | tf_op jit(solution)/shard_map/ppermute | solution.py:570
  242.7 7.3 %shard_map.166 = bf16[512,2048]{1,0:T(8,128)(2,1)} custom-call(s32[139]{0:T(256)} %concatenate.42.meta, f32[1,512]{1,0:T(1,128)} %bitcast.96, f32[1,2048]{1,0:T(1,128)} %gain.1, bf16[528,512]{1,0:T(8,128)(2,1)} %get-tuple-element.94.refs_0_, bf16[528,512]{1,0:T(8,128)(2,1)} %get-tuple-element.96.refs_1_, bf16[528,512]{1,0:T(8,128)(2,1)} %collective-permute-done.28.refs_2_, ...), custom_call_target="tpu_custom_call" | custom-call | flops 2147483648 | bytes 12582912 | tf_op jit(solution)/shard_map/pallas_call | solution.py:403
  250.0 5.8 %collective-permute-done.35 = bf16[192,1536]{1,0:T(8,128)(2,1)S(1)} collective-permute-done((bf16[192,1536]{1,0:T(8,128)(2,1)}, bf16[192,1536]{1,0:T(8,128)(2,1)S(1)}, u32[]{:S(2)}, u32[]{:S(2)}) %collective-permute-start.35) | collective-permute-done | bytes 589856 | tf_op jit(solution)/shard_map/ppermute | solution.py:570
  255.9 7.7 %collective-permute-done.33 = bf16[192,1536]{1,0:T(8,128)(2,1)S(1)} collective-permute-done((bf16[192,1536]{1,0:T(8,128)(2,1)}, bf16[192,1536]{1,0:T(8,128)(2,1)S(1)}, u32[]{:S(2)}, u32[]{:S(2)}) %collective-permute-start.33) | collective-permute-done | bytes 589856 | tf_op jit(solution)/shard_map/ppermute | solution.py:570
  (184 shorter events, 99.4 us)
Async XLA Ops:
  7.2 178.8 %all-gather.3.cloned.1.call-start = ((), (), s32[]{:S(2)}) async-start(), calls=%async_computation | async-start | bytes 6291456 | tf_op jit(solution)/shard_map/all_gather | solution.py:493
  7.9 178.0 %all-gather.5.cloned.1.call-start = ((), (), s32[]{:S(2)}) async-start(), calls=%async_computation.1 | async-start | bytes 4325376 | tf_op jit(solution)/shard_map/all_gather | solution.py:525
  8.2 19.6 %collective-permute-start.3 = (bf16[64,2048]{1,0:T(8,128)(2,1)S(1)}, bf16[64,2048]{1,0:T(8,128)(2,1)S(1)}, u32[]{:S(2)}, u32[]{:S(2)}) collective-permute-start(bf16[64,2048]{1,0:T(8,128)(2,1)S(1)} %get-tuple-element.120), channel_id=1, source_target_pairs={{0,4},{2,18},{4,8},{6,22},{8,12},{10,26},{12,0},{14,30},{16,20},{1... | collective-permute-start | bytes 786440 | tf_op jit(solution)/shard_map/ppermute | solution.py:108
  9.9 17.9 %collective-permute-start.4 = (bf16[64,2048]{1,0:T(8,128)(2,1)S(1)}, bf16[64,2048]{1,0:T(8,128)(2,1)S(1)}, u32[]{:S(2)}, u32[]{:S(2)}) collective-permute-start(bf16[64,2048]{1,0:T(8,128)(2,1)S(1)} %get-tuple-element.120), channel_id=1, source_target_pairs={{0,8},{2,34},{4,12},{6,38},{8,0},{10,42},{12,4},{14,46},{16,24},{1... | collective-permute-start | bytes 786440 | tf_op jit(solution)/shard_map/ppermute | solution.py:108
  50.7 37.6 %collective-permute-start.10 = (bf16[4,64,2048]{2,1,0:T(8,128)(2,1)S(1)}, bf16[4,64,2048]{2,1,0:T(8,128)(2,1)}, u32[]{:S(2)}, u32[]{:S(2)}) collective-permute-start(bf16[4,64,2048]{2,1,0:T(8,128)(2,1)S(1)} %pad_maximum_fusion.2.refs_0_), channel_id=1, source_target_pairs={{0,16},{2,6},{4,20},{6,10},{8,24},{10,14},{12,28},{14,2},{16,32},{... | collective-permute-start | bytes 3145736 | tf_op jit(solution)/shard_map/ppermute | solution.py:112
  52.4 35.9 %collective-permute-start.11 = (bf16[4,64,2048]{2,1,0:T(8,128)(2,1)S(1)}, bf16[4,64,2048]{2,1,0:T(8,128)(2,1)}, u32[]{:S(2)}, u32[]{:S(2)}) collective-permute-start(bf16[4,64,2048]{2,1,0:T(8,128)(2,1)S(1)} %pad_maximum_fusion.2.refs_0_), channel_id=1, source_target_pairs={{0,48},{2,14},{4,52},{6,2},{8,56},{10,6},{12,60},{14,10},{16,0},{1... | collective-permute-start | bytes 3145736 | tf_op jit(solution)/shard_map/ppermute | solution.py:112
  56.2 22.5 %collective-permute-start.8 = (bf16[4,128,384]{2,1,0:T(8,128)(2,1)S(1)}, bf16[4,128,384]{2,1,0:T(8,128)(2,1)}, u32[]{:S(2)}, u32[]{:S(2)}) collective-permute-start(bf16[4,128,384]{2,1,0:T(8,128)(2,1)S(1)} %pad_maximum_fusion.3.refs_0_), channel_id=1, source_target_pairs={{0,32},{2,10},{4,36},{6,14},{8,40},{10,2},{12,44},{14,6},{16,48},{... | collective-permute-start | bytes 1179656 | tf_op jit(solution)/shard_map/ppermute | solution.py:112
  59.6 25.2 %collective-permute-start.9 = (bf16[4,128,384]{2,1,0:T(8,128)(2,1)S(1)}, bf16[4,128,384]{2,1,0:T(8,128)(2,1)}, u32[]{:S(2)}, u32[]{:S(2)}) collective-permute-start(bf16[4,128,384]{2,1,0:T(8,128)(2,1)S(1)} %pad_maximum_fusion.3.refs_0_), channel_id=1, source_target_pairs={{0,48},{2,14},{4,52},{6,2},{8,56},{10,6},{12,60},{14,10},{16,0},{1... | collective-permute-start | bytes 1179656 | tf_op jit(solution)/shard_map/ppermute | solution.py:112
  71.6 16.8 %collective-permute-start.14 = (f32[512]{0:T(512)S(1)}, f32[512]{0:T(512)}, u32[]{:S(2)}, u32[]{:S(2)}) collective-permute-start(f32[512]{0:T(512)S(1)} %fusion), channel_id=1, source_target_pairs={{0,1},{1,0},{2,3},{3,2},{4,5},{5,4},{6,7},{7,6},{8,9},{9,8},{10,11... | collective-permute-start | bytes 6152 | tf_op jit(solution)/shard_map/ppermute | solution.py:501
  78.8 20.5 %collective-permute-start.13 = (bf16[4,64,2048]{2,1,0:T(8,128)(2,1)S(1)}, bf16[4,64,2048]{2,1,0:T(8,128)(2,1)}, u32[]{:S(2)}, u32[]{:S(2)}) collective-permute-start(bf16[4,64,2048]{2,1,0:T(8,128)(2,1)S(1)} %pad_maximum_fusion.2.refs_0_), channel_id=1, source_target_pairs={{0,32},{2,10},{4,36},{6,14},{8,40},{10,2},{12,44},{14,6},{16,48},{... | collective-permute-start | bytes 3145736 | tf_op jit(solution)/shard_map/ppermute | solution.py:112
  91.6 19.4 %collective-permute-start.18 = (bf16[4,64,2048]{2,1,0:T(8,128)(2,1)}, bf16[4,64,2048]{2,1,0:T(8,128)(2,1)S(1)}, u32[]{:S(2)}, u32[]{:S(2)}) collective-permute-start(bf16[4,64,2048]{2,1,0:T(8,128)(2,1)} %collective-permute-done.11.refs_3_), channel_id=1, source_target_pairs={{0,2},{2,0},{1,3},{3,1},{4,6},{6,4},{5,7},{7,5},{8,10},{10,8},{9,1... | collective-permute-start | bytes 3145736 | tf_op jit(solution)/shard_map/ppermute | solution.py:538
  104.8 40.0 %collective-permute-start.22 = (bf16[768,384]{1,0:T(8,128)(2,1)}, bf16[768,384]{1,0:T(8,128)(2,1)}, u32[]{:S(2)}, u32[]{:S(2)}) collective-permute-start(bf16[768,384]{1,0:T(8,128)(2,1)} %broadcast_select_fusion.1), channel_id=1, source_target_pairs={{0,64},{64,1},{1,65},{65,0},{2,66},{66,3},{3,67},{67,2},{4,68},{68... | collective-permute-start | bytes 1769480 | tf_op jit(solution)/shard_map/ppermute | solution.py:537
  105.8 39.0 %collective-permute-start.23 = (bf16[768,384]{1,0:T(8,128)(2,1)}, bf16[768,384]{1,0:T(8,128)(2,1)S(1)}, u32[]{:S(2)}, u32[]{:S(2)}) collective-permute-start(bf16[768,384]{1,0:T(8,128)(2,1)} %broadcast_select_fusion.1), channel_id=1, source_target_pairs={{0,1},{64,65},{1,0},{65,64},{2,3},{66,67},{3,2},{67,66},{4,5},{68,... | collective-permute-start | bytes 1769480 | tf_op jit(solution)/shard_map/ppermute | solution.py:537
  105.8 39.0 %collective-permute-start.24 = (bf16[768,384]{1,0:T(8,128)(2,1)}, bf16[768,384]{1,0:T(8,128)(2,1)S(1)}, u32[]{:S(2)}, u32[]{:S(2)}) collective-permute-start(bf16[768,384]{1,0:T(8,128)(2,1)} %broadcast_select_fusion.1), channel_id=1, source_target_pairs={{0,65},{64,0},{1,64},{65,1},{2,67},{66,2},{3,66},{67,3},{4,69},{68... | collective-permute-start | bytes 1769480 | tf_op jit(solution)/shard_map/ppermute | solution.py:537
  120.0 36.2 %collective-permute-start.20 = (bf16[512,512]{1,0:T(8,128)(2,1)}, bf16[512,512]{1,0:T(8,128)(2,1)S(1)}, u32[]{:S(2)}, u32[]{:S(2)}) collective-permute-start(bf16[512,512]{1,0:T(8,128)(2,1)} %get-tuple-element.78), channel_id=1, source_target_pairs={{0,1},{1,0},{64,65},{65,64},{2,3},{3,2},{66,67},{67,66},{4,5},{5,4... | collective-permute-start | bytes 1572872 | tf_op jit(solution)/shard_map/ppermute | solution.py:542
  129.9 31.7 %collective-permute-start.21 = (bf16[512,512]{1,0:T(8,128)(2,1)}, bf16[512,512]{1,0:T(8,128)(2,1)S(1)}, u32[]{:S(2)}, u32[]{:S(2)}) collective-permute-start(bf16[512,512]{1,0:T(8,128)(2,1)} %get-tuple-element.81), channel_id=1, source_target_pairs={{64,65},{65,64},{66,67},{67,66},{68,69},{69,68},{70,71},{71,70},{7... | collective-permute-start | bytes 1572872 | tf_op jit(solution)/shard_map/ppermute | solution.py:544
  195.3 17.6 %collective-permute-start.27 = (bf16[512,512]{1,0:T(8,128)(2,1)}, bf16[512,512]{1,0:T(8,128)(2,1)S(1)}, u32[]{:S(2)}, u32[]{:S(2)}) collective-permute-start(bf16[512,512]{1,0:T(8,128)(2,1)} %get-tuple-element.93), channel_id=1, source_target_pairs={{0,1},{1,0},{2,3},{3,2},{4,5},{5,4},{6,7},{7,6},{8,9},{9,8},{10,11... | collective-permute-start | bytes 1572872 | tf_op jit(solution)/shard_map/ppermute | solution.py:554
  198.1 44.6 %collective-permute-start.28 = (bf16[528,512]{1,0:T(8,128)(2,1)}, bf16[528,512]{1,0:T(8,128)(2,1)}, u32[]{:S(2)}, u32[]{:S(2)}) collective-permute-start(bf16[528,512]{1,0:T(8,128)(2,1)} %get-tuple-element.94.refs_0_), channel_id=1, source_target_pairs={{64,65},{65,64},{66,67},{67,66},{68,69},{69,68},{70,71},{71,70},{7... | collective-permute-start | bytes 1622024 | tf_op jit(solution)/shard_map/ppermute | solution.py:557
  205.9 24.8 %collective-permute-start.32 = (bf16[192,1536]{1,0:T(8,128)(2,1)}, bf16[192,1536]{1,0:T(8,128)(2,1)S(1)}, u32[]{:S(2)}, u32[]{:S(2)}) collective-permute-start(bf16[192,1536]{1,0:T(8,128)(2,1)} %get-tuple-element.106), channel_id=1, source_target_pairs={{64,65},{65,64},{66,67},{67,66},{68,69},{69,68},{70,71},{71,70},{7... | collective-permute-start | bytes 1769480 | tf_op jit(solution)/shard_map/ppermute | solution.py:560
  206.6 24.1 %collective-permute-start.31 = (bf16[192,1536]{1,0:T(8,128)(2,1)}, bf16[192,1536]{1,0:T(8,128)(2,1)}, u32[]{:S(2)}, u32[]{:S(2)}) collective-permute-start(bf16[192,1536]{1,0:T(8,128)(2,1)} %get-tuple-element.105), channel_id=1, source_target_pairs={{64,1},{65,0},{66,3},{67,2},{68,5},{69,4},{70,7},{71,6},{72,9},{73... | collective-permute-start | bytes 1769480 | tf_op jit(solution)/shard_map/ppermute | solution.py:560
  207.9 25.8 %collective-permute-start.30 = (bf16[192,1536]{1,0:T(8,128)(2,1)}, bf16[192,1536]{1,0:T(8,128)(2,1)S(1)}, u32[]{:S(2)}, u32[]{:S(2)}) collective-permute-start(bf16[192,1536]{1,0:T(8,128)(2,1)} %get-tuple-element.104), channel_id=1, source_target_pairs={{64,0},{65,1},{66,2},{67,3},{68,4},{69,5},{70,6},{71,7},{72,8},{73... | collective-permute-start | bytes 1769480 | tf_op jit(solution)/shard_map/ppermute | solution.py:560
  219.9 22.8 %collective-permute-start.29 = (bf16[528,512]{1,0:T(8,128)(2,1)}, bf16[528,512]{1,0:T(8,128)(2,1)}, u32[]{:S(2)}, u32[]{:S(2)}) collective-permute-start(bf16[528,512]{1,0:T(8,128)(2,1)} %get-tuple-element.96.refs_1_), channel_id=1, source_target_pairs={{0,1},{1,0},{2,3},{3,2},{4,5},{5,4},{6,7},{7,6},{8,9},{9,8},{10,11... | collective-permute-start | bytes 1622024 | tf_op jit(solution)/shard_map/ppermute | solution.py:566
  236.0 19.9 %collective-permute-start.35 = (bf16[192,1536]{1,0:T(8,128)(2,1)}, bf16[192,1536]{1,0:T(8,128)(2,1)S(1)}, u32[]{:S(2)}, u32[]{:S(2)}) collective-permute-start(bf16[192,1536]{1,0:T(8,128)(2,1)} %get-tuple-element.111), channel_id=1, source_target_pairs={{0,1},{1,0},{2,3},{3,2},{4,5},{5,4},{6,7},{7,6},{8,9},{9,8},{10,11... | collective-permute-start | bytes 1769480 | tf_op jit(solution)/shard_map/ppermute | solution.py:570
  241.3 22.2 %collective-permute-start.33 = (bf16[192,1536]{1,0:T(8,128)(2,1)}, bf16[192,1536]{1,0:T(8,128)(2,1)S(1)}, u32[]{:S(2)}, u32[]{:S(2)}) collective-permute-start(bf16[192,1536]{1,0:T(8,128)(2,1)} %get-tuple-element.109), channel_id=1, source_target_pairs={{0,64},{1,65},{2,66},{3,67},{4,68},{5,69},{6,70},{7,71},{8,72},{9,... | collective-permute-start | bytes 1769480 | tf_op jit(solution)/shard_map/ppermute | solution.py:570
  (52 other events, 513.5 us)
Sparse Core Ops, SparseCore 0:
  9.7 64.5 all-gather.2
  76.5 47.5 all-gather.4

commit v5 on v4

--- a/solution.py
+++ b/solution.py
@@ -16,7 +16,6 @@
 L = 128
 QBLK = 32
 MAXT = 64
-QUARTER = E // 4
 SCALE = HEAD ** (-0.5)
 DP = ("z", "y", "core")
 X = ("segment", "mp")
@@ -34,11 +33,6 @@
 FIRST_TO_SAME = [(0, 2), (1, 3)]
 FIRST_TO_CROSS = [(0, 3), (1, 2)]
 FIRST_SWAP = [(0, 1), (1, 0)]
-AT_X = (0, 2, 1, 3)
-
-
-def x_perm(k):
-    return [(AT_X[x], AT_X[(x + k) % 4]) for x in range(4)]
 
 
 def yz_perm(stage, k):
@@ -69,94 +63,74 @@
 ANY = pl.BlockSpec(memory_space=pl.ANY)
 VMEM = pl.BlockSpec(memory_space=pltpu.VMEM)
 TILE = 512
-ROWS, SLOT, INFO, LENGTHS, PATTERN = 0, 32, 36, 39, 43
-
-
-def pool_kernel(which, counts, tiles, queries, out):
-    heads = [slice(head * HEAD, (head + 1) * HEAD) for head in range(QUARTER // HEAD)]
-    pairs = [(slide, cols) for slide in range(4) for cols in heads]
+ROWS, SLOT, INFO, LENGTHS, PATTERN, PICKS = 0, 32, 36, 39, 43, 139
+ARRAYS = ((0, (0, 1, 2, 3)), (1, (0, 1, 2, 3)), (3, (0, 1, 2, 3)), (2, (0, 1)), (2, (2, 3)))
+
+
+def block_kernel(counts, tiles, queries, w_out, w_query, w_key, w_value, out, w_v, latents, sems):
+    loads = [
+        pltpu.make_async_copy(w, w_v.at[i], sems.at[i]) for i, w in enumerate((w_key, w_value))
+    ]
+    for load in loads:
+        load.start()
+    out[:32] = w_out[...]
+    out[32:64] = w_query[...]
+    heads = [slice(head * HEAD, (head + 1) * HEAD) for head in range(E // HEAD)]
     slot = lax.broadcasted_iota(jnp.int32, (LAT, MAXT), 1)
-    tile = [tiles[slide, :, cols] for slide, cols in pairs]
-    query = [queries[:, cols] for _, cols in pairs]
-    scores = [dot(q, t, NT) * SCALE for q, t in zip(query, tile)]
-    scores = [jnp.where(slot < counts[s], x, -1e30) for x, (s, _) in zip(scores, pairs)]
-    exps = [jnp.exp(s - jnp.max(s, axis=1, keepdims=True)) for s in scores]
-    weights = [(e / jnp.sum(e, axis=1, keepdims=True)).astype(BF) for e in exps]
-    pooled = [dot(w, t, NN) for w, t in zip(weights, tile)]
-    for (slide, cols), q, p in zip(pairs, query, pooled):
-        out[slide * LAT : (slide + 1) * LAT, cols] = (q.astype(F32) + p).astype(BF)
-
-
-def pool(which, counts, tiles, queries):
-    return pl.pallas_call(
-        pool_kernel,
-        grid_spec=pltpu.PrefetchScalarGridSpec(
-            num_scalar_prefetch=2,
-            grid=(1,),
-            in_specs=[
-                pl.BlockSpec((4, MAXT, QUARTER), lambda i, which, counts: (0, 0, which[0])),
-                pl.BlockSpec((LAT, QUARTER), lambda i, which, counts: (0, which[0])),
-            ],
-            out_specs=pl.BlockSpec((4 * LAT, QUARTER), lambda i, which, counts: (0, 0)),
-        ),
-        out_shape=jax.ShapeDtypeStruct((4 * LAT, QUARTER), BF),
-        compiler_params=params(),
-    )(which, counts, tiles, queries)
-
-
-def gather_chips(blocks):
-    first = [[lax.ppermute(b, DP, yz_perm(1, k)) for k in (1, 2, 3)] for b in blocks]
-    first = lax.optimization_barrier(first)
-    bundles = [jnp.stack([b, *parts]) for b, parts in zip(blocks, first)]
-    bundles = lax.optimization_barrier(bundles)
-    return [[b] + [lax.ppermute(b, DP, yz_perm(2, k)) for k in (1, 2, 3)] for b in bundles]
+    for slide in range(tiles.shape[0]):
+        tile = [tiles[slide, :, cols] for cols in heads]
+        query = [queries[:, cols] for cols in heads]
+        scores = [dot(q, t, NT) * SCALE for q, t in zip(query, tile)]
+        scores = [jnp.where(slot < counts[slide], x, -1e30) for x in scores]
+        exps = [jnp.exp(s - jnp.max(s, axis=1, keepdims=True)) for s in scores]
+        weights = [(e / jnp.sum(e, axis=1, keepdims=True)).astype(BF) for e in exps]
+        pooled = [dot(w, t, NN) for w, t in zip(weights, tile)]
+        for cols, q, p in zip(heads, query, pooled):
+            latents[slide * LAT : (slide + 1) * LAT, cols] = (q.astype(F32) + p).astype(BF)
+    for i, load in enumerate(loads):
+        load.wait()
+        value = dot(latents[...], w_v[i], NN).astype(BF)
+        half = value.shape[1]
+        for slide in range(tiles.shape[0]):
+            at = 64 + slide // 2 * LAT
+            col = (slide % 2 * 2 + i) * half
+            out[at : at + LAT, col : col + half] = value[slide * LAT : (slide + 1) * LAT]
+
+
+def make_block(counts, tiles, queries, w_out, w_query, w_key, w_value):
+    slides = tiles.shape[0]
+    return pl.pallas_call(
+        block_kernel,
+        in_specs=[SMEM] + [VMEM] * 4 + [ANY] * 2,
+        out_specs=VMEM,
+        out_shape=jax.ShapeDtypeStruct((64 + slides // 2 * LAT, w_out.shape[1]), BF),
+        scratch_shapes=[
+            pltpu.VMEM((2,) + w_key.shape, BF),
+            pltpu.VMEM((slides * LAT, E), BF),
+            pltpu.SemaphoreType.DMA((2,)),
+        ],
+        compiler_params=params(),
+    )(counts, tiles, queries, w_out, w_query, w_key, w_value)
+
+
+def gather_chips(block):
+    first = [lax.ppermute(block, DP, yz_perm(1, k)) for k in (1, 2, 3)]
+    bundle = jnp.stack([block, *first])
+    one = lax.ppermute(bundle, DP, yz_perm(2, 1))
+    three = lax.ppermute(bundle, DP, yz_perm(2, 3))
+    two = lax.ppermute(one[:2], DP, yz_perm(2, 1)), lax.ppermute(three[2:], DP, yz_perm(2, 3))
+    return [bundle, one, three, *two]
 
 
 def places(z, y, core):
     table = []
-    for a in range(8):
-        c = core if a < 4 else 1 - core
-        for k in range(4):
-            j = a % 4
-            at_z = lax.rem(z - jnp.where(c == 0, j, k) + 4, 4)
-            at_y = lax.rem(y - jnp.where(c == 0, k, j) + 4, 4)
-            table.append((at_z * 4 + at_y) * 2 + c)
+    for c in (core, 1 - core):
+        for j, blocks in ARRAYS:
+            for k in blocks:
+                at_z = lax.rem(z - jnp.where(c == 0, j, k) + 4, 4)
+                at_y = lax.rem(y - jnp.where(c == 0, k, j) + 4, 4)
+                table.append((at_z * 4 + at_y) * 2 + c)
     return jnp.stack(table).astype(jnp.int32)
-
-
-def select_kernel(wanted, picks, *refs):
-    ins, outs, sems = refs[:4], refs[4:6], refs[6]
-
-    def copy(a, which, i):
-        at = which * wanted + i
-        slide = pl.multiple_of(picks[4 * wanted + at] * LAT, LAT)
-        return pltpu.make_async_copy(
-            ins[a].at[picks[2 * wanted + at], pl.ds(slide, LAT)],
-            outs[which].at[pl.ds(i * LAT, LAT)],
-            sems.at[at],
-        )
-
-    for act in ("start", "wait"):
-        for which in range(2):
-            for i in range(wanted):
-                for a in range(4):
-
-                    @pl.when(picks[which * wanted + i] == a)
-                    def _():
-                        getattr(copy(a, which, i), act)()
-
-
-def select(picks, blocks):
-    wanted = picks.shape[0] // 6
-    out = jax.ShapeDtypeStruct((wanted * LAT, QUARTER), BF)
-    return pl.pallas_call(
-        functools.partial(select_kernel, wanted),
-        in_specs=[SMEM] + [ANY] * 4,
-        out_specs=[VMEM, VMEM],
-        out_shape=[out, out],
-        scratch_shapes=[pltpu.SemaphoreType.DMA((2 * wanted,))],
-        compiler_params=params(),
-    )(picks, *blocks)
 
 
 def column(row):
@@ -169,54 +143,83 @@
     return jnp.concatenate([p.astype(F32) for p in parts], axis=0) > 0
 
 
-def project_kernel(kind, meta, x, *refs):
-    ins, (send, weight), (w_v, x_v, sems) = refs[:8], refs[8:10], refs[10:]
-    load = pltpu.make_async_copy(x, x_v, sems.at[2])
+def project_kernel(kind, part, meta, x, *refs):
+    ins, (out, weight), (w_v, x_v, sems) = refs[:10], refs[10:12], refs[12:]
+    load = pltpu.make_async_copy(x, x_v, sems.at[1])
     load.start()
-    half = w_v.shape[0] // 2
-    for a in range(8):
-        for k in range(4):
-            at = pl.multiple_of(meta[ROWS + a * 4 + k], 32)
-            pltpu.make_async_copy(
-                ins[a].at[k, pl.ds(kind * 32, 32)], w_v.at[pl.ds(at, 32)], sems.at[at // half]
-            ).start()
-
-    def group(part):
-        return w_v.at[pl.ds(part * half, half)]
+    half = w_v.shape[0]
+    index = 0
+    for a in range(10):
+        for k in range(len(ARRAYS[a % 5][1])):
+            at = pl.multiple_of(meta[ROWS + index] - part * half, 32)
+            index += 1
+
+            @pl.when((at >= 0) & (at < half))
+            def _():
+                pltpu.make_async_copy(
+                    ins[a].at[k, pl.ds(kind * 32, 32)], w_v.at[pl.ds(at, 32)], sems.at[0]
+                ).start()
 
     load.wait()
-    pltpu.make_async_copy(group(1), group(1), sems.at[1]).wait()
-    store1 = pltpu.make_async_copy(group(1), weight.at[pl.ds(half, half)], sems.at[1])
-    store1.start()
-    send[...] = dot(x_v[...], w_v[half:], NT).astype(BF)
-    pltpu.make_async_copy(group(0), group(0), sems.at[0]).wait()
-    store0 = pltpu.make_async_copy(group(0), weight.at[pl.ds(0, half)], sems.at[0])
-    store0.start()
-    store1.wait()
-    store0.wait()
-
-
-def project(kind, meta, x, blocks):
+    pltpu.make_async_copy(w_v, w_v, sems.at[0]).wait()
+    store = pltpu.make_async_copy(w_v, weight, sems.at[0])
+    store.start()
+    out[...] = dot(x_v[...], w_v[...], NT).astype(out.dtype)
+    store.wait()
+
+
+def project(kind, part, dtype, meta, x, blocks):
     tokens, width = x.shape
-    inner = 32 * 32
-    return pl.pallas_call(
-        functools.partial(project_kernel, kind),
-        in_specs=[SMEM, ANY] + [ANY] * 8,
+    half = 512
+    return pl.pallas_call(
+        functools.partial(project_kernel, kind, part),
+        in_specs=[SMEM, ANY] + [ANY] * 10,
         out_specs=[VMEM, ANY],
         out_shape=[
-            jax.ShapeDtypeStruct((tokens, inner // 2), BF),
-            jax.ShapeDtypeStruct((inner, width), BF),
+            jax.ShapeDtypeStruct((tokens, half), dtype),
+            jax.ShapeDtypeStruct((half, width), BF),
         ],
         scratch_shapes=[
-            pltpu.VMEM((inner, width), BF),
+            pltpu.VMEM((half, width), BF),
             pltpu.VMEM((tokens, width), BF),
-            pltpu.SemaphoreType.DMA((3,)),
+            pltpu.SemaphoreType.DMA((2,)),
         ],
         compiler_params=params(),
         cost_estimate=pl.CostEstimate(
-            flops=tokens * width * inner, bytes_accessed=12 << 20, transcendentals=0
+            flops=2 * tokens * width * half, bytes_accessed=7 << 20, transcendentals=0
         ),
     )(meta, x, *blocks)
+
+
+def select_kernel(wanted, meta, *refs):
+    ins, out, sems = refs[:10], refs[10], refs[11]
+    width = out.shape[1]
+    for i in range(wanted):
+        block = meta[PICKS + wanted + i]
+        slide = meta[PICKS + 2 * wanted + i]
+        rows = pl.ds(pl.multiple_of(64 + slide // 2 * LAT, LAT), LAT)
+        cols = pl.ds(pl.multiple_of(slide % 2 * width, width), width)
+        for a in range(10):
+
+            @pl.when(meta[PICKS + i] == a)
+            def _():
+                pltpu.make_async_copy(
+                    ins[a].at[block, rows, cols], out.at[pl.ds(i * LAT, LAT)], sems.at[0]
+                ).start()
+
+    pltpu.make_async_copy(out, out, sems.at[0]).wait()
+
+
+def select(wanted, meta, blocks):
+    return pl.pallas_call(
+        functools.partial(select_kernel, wanted),
+        in_specs=[SMEM] + [ANY] * 10,
+        out_specs=VMEM,
+        out_shape=jax.ShapeDtypeStruct((wanted * LAT, 1024), BF),
+        scratch_shapes=[pltpu.SemaphoreType.DMA((1,))],
+        compiler_params=params(),
+        cost_estimate=pl.CostEstimate(flops=0, bytes_accessed=3 << 20, transcendentals=0),
+    )(meta, *blocks)
 
 
 def forward_kernel(meta, q_own, q_got, keys, probs):
@@ -325,7 +328,7 @@
         dq_own, dq_got, up, h, wq, wo, grad, o_send, wq_v, up_v, h_v, wo_v, sems = refs
         left, right = dq_own[...], dq_got[...]
     else:
-        dq1, dq0, got1, got0, up, h, wq, grad, wq_v, up_v, h_v, sems = refs
+        dq1, dq0, got1, got0, up, h, wq_own, wq_got, grad, wq_v, up_v, h_v, sems = refs
         left = jnp.where(meta[INFO] == 1, dq1[...].astype(F32), dq0[...].astype(F32)).astype(BF)
         right = (got1[...].astype(F32) + got0[...].astype(F32)).astype(BF)
     if len(h.shape) == 3:
@@ -339,21 +342,23 @@
         cols = slice(tile * TILE, (tile + 1) * TILE)
         out = []
         for part in range(2):
-            at = pl.multiple_of(meta[INFO + 1 + part], half) if following else part * half
-            into = slice(part * half, (part + 1) * half)
-            out.append((wq.at[pl.ds(at, half), cols], wq_v.at[into, cols]))
+            into = wq_v.at[part * half : (part + 1) * half, cols]
+            if following:
+                at = pl.multiple_of(meta[INFO + 1 + part], half)
+                out.append((wq.at[pl.ds(at, half), cols], into))
+            else:
+                out.append(((wq_own, wq_got)[part].at[:, cols], into))
         out.append((up.at[:, cols], up_v.at[:, cols]))
         out.append((h.at[:, cols], h_v.at[:, cols]))
         return [
             pltpu.make_async_copy(a, b, sems.at[tile * 4 + i]) for i, (a, b) in enumerate(out)
         ]
 
-    for tile in range(tiles):
+    for tile in range(2):
         for copy in copies(tile):
             copy.start()
     if following:
-        load = pltpu.make_async_copy(wo.at[pl.ds(half, half)], wo_v, sems.at[tiles * 4])
-        load.start()
+        load = pltpu.make_async_copy(wo, wo_v, sems.at[tiles * 4])
     stat = column(
         jnp.sum(left[tokens:].astype(F32) + right[tokens:].astype(F32), axis=0, keepdims=True)
     )
@@ -366,6 +371,11 @@
     for tile in range(tiles):
         for copy in copies(tile):
             copy.wait()
+        if tile + 2 < tiles:
+            for copy in copies(tile + 2):
+                copy.start()
+        elif following and tile + 2 == tiles:
+            load.start()
         cols = slice(tile * TILE, (tile + 1) * TILE)
         dnormed = dot(dq, wq_v[:, cols], NN)
         upstream = up_v[:, cols].astype(F32)
@@ -385,12 +395,12 @@
         store.wait()
 
 
-def back(meta, rinv, gain, dqs, up, h, wq, wo=None):
+def back(meta, rinv, gain, dqs, up, h, weights, wo=None):
     tokens, width = up.shape
-    inner = wq.shape[0]
-    half = inner // 2
-    inputs = [meta, rinv, gain, *dqs, up, h, wq]
-    in_specs = [SMEM] + [VMEM] * (2 + len(dqs)) + [ANY] * 3
+    half = dqs[0].shape[1]
+    inner = 2 * half
+    inputs = [meta, rinv, gain, *dqs, up, h, *weights]
+    in_specs = [SMEM] + [VMEM] * (2 + len(dqs)) + [ANY] * (2 + len(weights))
     out_specs = [ANY]
     out_shape = [jax.ShapeDtypeStruct((tokens, width), BF)]
     scratch = [pltpu.VMEM((inner, width), BF)] + [pltpu.VMEM((tokens, width), BF)] * 2
@@ -426,7 +436,7 @@
 def latent_terms(dkv, w_kv):
     rows, inner = dkv.shape[1:]
     features = w_kv.shape[0]
-    tile = features // 3
+    tile = features // 6
     result = pl.BlockSpec((rows, tile), lambda i: (0, i))
     return pl.pallas_call(
         term_kernel,
@@ -462,7 +472,6 @@
     me_dp = (z * 4 + y) * 2 + core
     me_mp = lax.axis_index("mp")
     seg = lax.axis_index("segment")
-    me_x = me_mp * 2 + seg
     last = seg == 1
     reports = cross_pattern.shape[0]
     wanted = reports * SPR
@@ -476,25 +485,31 @@
         slot.append(jnp.where(same_seg, jnp.where(same_mp, 0, 3), jnp.where(same_mp, 1, 2)))
     rows = lax.rem(places(z, y, core) * 32 - me_mp * half + 2 * half, 2 * half)
     info = [seg, me_mp * half, (1 - me_mp) * half]
-    meta = jnp.concatenate(
-        [rows, jnp.stack(slot + info).astype(jnp.int32), report_lengths, cross_pattern.reshape(-1)]
+    source = lax.dynamic_index_in_dim(
+        request_source.reshape(32, wanted), me_dp, 0, keepdims=False
     )
-    order = jnp.stack([me_dp, me_dp + 1 - 2 * core])
-    source = request_source.reshape(32, wanted)[order]
-    slide = request_slide.reshape(32, wanted)[order]
+    slide = lax.dynamic_index_in_dim(request_slide.reshape(32, wanted), me_dp, 0, keepdims=False)
     source_core = source % 2
     far_z = lax.rem(z - source // 8 + 4, 4)
     far_y = lax.rem(y - source // 2 % 4 + 4, 4)
-    first = jnp.where(core == 0, far_y, far_z)
-    second = jnp.where(core == 0, far_z, far_y)
-    array = jnp.where(source_core == core, second, 4)
-    picks = jnp.concatenate([array.reshape(-1), first.reshape(-1), slide.reshape(-1)])
+    first = jnp.where(source_core == 0, far_y, far_z)
+    second = jnp.where(source_core == 0, far_z, far_y)
+    array = jnp.where(second < 2, second, jnp.where(second == 3, 2, jnp.where(first < 2, 3, 4)))
+    array = array + jnp.where(source_core == core, 0, 5)
+    block = jnp.where(second == 2, first % 2, first)
+    meta = jnp.concatenate(
+        [rows, jnp.stack(slot + info).astype(jnp.int32), report_lengths]
+        + [cross_pattern.reshape(-1), array, block, slide]
+    )
 
     h_all = lax.all_gather(h, "segment")
 
     wq_t = w_query[0].T
-    pooled = pool(me_x.reshape(1).astype(jnp.int32), tile_counts.reshape(4), tiles, lat_query)
-    lat_blocks, blocks = gather_chips([pooled, jnp.concatenate([w_out[0], wq_t], axis=0)])
+    blocks = gather_chips(
+        make_block(
+            tile_counts.reshape(4), tiles, lat_query, w_out[0], wq_t, w_key[0], w_value[0]
+        )
+    )
 
     h32 = h.astype(F32)
     partial = jnp.sum(h32 * h32, axis=1)
@@ -510,68 +525,49 @@
     rinv = rinv[None]
     gate = jnp.tanh(attn_gate)
     w_kv = jnp.concatenate([w_key[0], w_value[0]], axis=1)
-    w_kv_x = jnp.concatenate(
-        [
-            lax.dynamic_slice_in_dim(w_kv, lax.rem(me_x - k + 4, 4) * QUARTER, QUARTER, 0)
-            for k in range(4)
-        ],
-        axis=0,
-    )
-
-    wq_t, _ = lax.optimization_barrier((wq_t, blocks[0]))
-    lat_blocks[0], wq1 = lax.optimization_barrier(
-        (lat_blocks[0], lax.ppermute(wq_t, "segment", [(1, 0)]))
+    wq_t, _ = lax.optimization_barrier((wq_t, squares))
+    wq1 = lax.ppermute(wq_t, "segment", [(1, 0)])
+    swap = [(0, 1), (1, 0)]
+    others = [lax.ppermute(b, "core", swap) for b in blocks[:3]]
+    blocks, others, normed, up1, rinv1, gain1, meta, w_kv, wq1 = lax.optimization_barrier(
+        (blocks, others, normed, up1, rinv1, gain1, meta, w_kv, wq1)
     )
     wq1 = lax.all_gather(wq1, DP, axis=0, tiled=True)
-
-    near, across = select(picks, lat_blocks)
-    near, across, blocks[1], blocks[3] = lax.optimization_barrier(
-        (near, across, blocks[1], blocks[3])
-    )
-    crossed = lax.ppermute(across, "core", [(0, 1), (1, 0)])
-    is_near = jnp.repeat(source_core[0] == core, LAT)[:, None]
-    chosen = jnp.where(is_near, near, crossed)
-    chosen, blocks[2], normed, up1, meta, w_kv, w_kv_x = lax.optimization_barrier(
-        (chosen, blocks[2], normed, up1, meta, w_kv, w_kv_x)
-    )
-    latents = [chosen] + [lax.ppermute(chosen, X, x_perm(k)) for k in (1, 2, 3)]
-    blocks = blocks + [lax.ppermute(b, "core", [(0, 1), (1, 0)]) for b in blocks]
-
-
-    q_send, wq = project(1, meta, normed, blocks)
+    blocks = blocks + others + [lax.ppermute(b, "core", swap) for b in blocks[3:]]
+
+    q_send, wq_got = project(1, 1, BF, meta, normed, blocks)
     q_got = lax.ppermute(q_send, X, SWAP_MP)
-    o_send, wo = project(0, meta, up1, blocks)
+    o_send, wo_got = project(0, 1, BF, meta, up1, blocks)
     o_got = lax.ppermute(o_send, X, LAST_SWAP)
-    q_own = dot(normed, wq[:half], NT)
-    q_own, rinv1, gain1 = lax.optimization_barrier((q_own, rinv1, gain1))
-    o_own = dot(up1, wo[:half], NT).astype(BF)
-    latents, o_send = lax.optimization_barrier((latents, o_send))
-    kv = dot(jnp.concatenate(latents, axis=1), w_kv_x, NN).astype(BF)
+    q_own, wq_own = project(1, 0, F32, meta, normed, blocks)
+    o_own, wo_own = project(0, 0, BF, meta, up1, blocks)
+    kv = select(wanted, meta, blocks)
     probs = forward(meta, q_own, q_got, kv)
     dq1, dkv1 = backward(meta, gate, q_own, q_got, o_own, o_got, kv, probs)
     dqs = [lax.ppermute(dq1, X, LAST_TO_SAME), lax.ppermute(dq1, X, LAST_TO_CROSS)]
-    up, o_send = back(meta, rinv1, gain1, dqs, cotangent, h_all, wq1, wo)
+    own1, *terms = latent_terms(dkv1, w_kv)
+    dqs, terms = lax.optimization_barrier((dqs, terms))
+    up, o_send = back(meta, rinv1, gain1, dqs, cotangent, h_all, [wq1], wo_got)
     o_got = lax.ppermute(o_send, X, FIRST_SWAP)
-    o_own = dot(up, wo[:half], NT).astype(BF)
-    dq1, dkv1, _ = lax.optimization_barrier((dq1, dkv1, o_send))
+    o_own = dot(up, wo_own, NT).astype(BF)
+    dq1, terms, _ = lax.optimization_barrier((dq1, terms, o_send))
     got1 = lax.ppermute(dq1, X, LAST_SWAP)
-    own1, *terms = latent_terms(dkv1, w_kv)
     moves = (LAST_TO_SAME, LAST_TO_CROSS, LAST_SWAP)
     got = [lax.ppermute(t, X, p) for t, p in zip(terms, moves)]
-    received = jnp.where(last, own1, 0.0)
+
+    dq0, dkv0 = backward(meta, gate, q_own, q_got, o_own, o_got, kv, probs)
+    own0, *terms = latent_terms(dkv0, w_kv)
+    got0 = lax.ppermute(dq0, X, FIRST_SWAP)
+    terms, got = lax.optimization_barrier((terms, got))
+    moves = (FIRST_TO_SAME, FIRST_TO_CROSS, FIRST_SWAP)
+    late = [lax.ppermute(t, X, p) for t, p in zip(terms, moves)]
+    got, got0 = lax.optimization_barrier((got, got0))
+    received = jnp.where(last, own1, own0)
     for term in got:
         received = received + term.astype(F32)
-
-    dq0, dkv0 = backward(meta, gate, q_own, q_got, o_own, o_got, kv, probs)
-    got0 = lax.ppermute(dq0, X, FIRST_SWAP)
-    own0, *terms = latent_terms(dkv0, w_kv)
-    terms, received = lax.optimization_barrier((terms, received))
-    moves = (FIRST_TO_SAME, FIRST_TO_CROSS, FIRST_SWAP)
-    got = [lax.ppermute(t, X, p) for t, p in zip(terms, moves)]
-    (grads,) = back(meta, rinv, gain, [dq1, dq0, got1, got0], up, h, wq)
-
-    latent_grad = received + jnp.where(last, 0.0, own0)
-    for term in got:
+    (grads,) = back(meta, rinv, gain, [dq1, dq0, got1, got0], up, h, [wq_own, wq_got])
+    latent_grad, late = lax.optimization_barrier((received, late))
+    for term in late:
         latent_grad = latent_grad + term.astype(F32)
     return grads[None], latent_grad.reshape(reports, 48, E)
 

time: 274 us -> 249 us (0.909)
  starting transfers between devices: 57.2 us -> 43.3 us
  Pallas kernels: 65.4 us -> 76.2 us
  matrix products: 14.1 us -> 4.3 us
  local copies, waits for them, and re-layouts: 19.2 us -> 12.4 us
    ppermute x6 -> x3, waiting for transfers between devices: 16.5 us -> 6.33 us  [per_device(): got = [lax.ppermute(t, X, p) for t, p in zip(terms, moves)]]
    ppermute x21 -> x16, waiting for transfers between devices: 44.4 us -> 54.5 us  [the longest x1 18.2 us: gather_chips(): one = lax.ppermute(bundle, DP, yz_perm(2, 1))]
    dot_general x4 -> x1, matrix products: 14.1 us -> 4.3 us  [dot(): return lax.dot_general(a, b, dims, preferred_element_type=F32)]
    pallas_call x3 -> x5, Pallas kernels: 16.6 us -> 24.5 us  [the longest x4 20 us: project(): pl.pallas_call(functools.partial(project_kernel, kind, part), in_specs=[S...]
    ppermute x6 -> x3, starting transfers between devices: 9.92 us -> 3.28 us  [per_device(): got = [lax.ppermute(t, X, p) for t, p in zip(terms, moves)]]
    ppermute x1, waiting for transfers between devices: 0.01 us -> 6.15 us  [per_device(): o_got = lax.ppermute(o_send, X, FIRST_SWAP)]
    ppermute x1, waiting for transfers between devices: 12.1 us -> 6.2 us  [per_device(): lax.ppermute(dq1, X, LAST_TO_SAME)]
    ppermute x21 -> x16, starting transfers between devices: 27.5 us -> 22.8 us  [the longest x3 8.1 us: per_device(): late = [lax.ppermute(t, X, p) for t, p in zip(terms, moves)]]
  transfers between devices with their start and end apart: 38 -> 30, of which waited for: 13 -> 13; matrix products, arithmetic and copies ran while one was open for 16% -> 10% of each run, Pallas kernels for 21% -> 26%
where the time goes in v5:
time: 249 us; the launch traced here: 247 us
  waiting for transfers between devices  78.9 us (32%)
  Pallas kernels  76.2 us (31%)
  starting transfers between devices  43.3 us (17%)
  other arithmetic  17 us (7%)
  between operations  15.2 us (6%)
  local copies, waits for them, and re-layouts  12.4 us (5%)
  matrix products  4.3 us (2%)
    pallas_call x4, Pallas kernels, project(): pl.pallas_call(functools.partial(project_kernel, kind, part), in_specs=[S...  20 us
    ppermute x1, waiting for transfers between devices, gather_chips(): one = lax.ppermute(bundle, DP, yz_perm(2, 1))  18.2 us
    pallas_call x2, Pallas kernels, back(): pl.pallas_call(functools.partial(back_kernel, wo is not None), in_specs=i...  16.2 us
    ppermute x3, waiting for transfers between devices, gather_chips(): first = [lax.ppermute(block, DP, yz_perm(1, k)) for k in (1, 2, 3)]  14.9 us
    pallas_call x2, Pallas kernels, latent_terms(): pl.pallas_call(term_kernel, grid=(features // tile,), in_specs=[whole(dkv...  14.6 us
    pallas_call x2, Pallas kernels, backward(): pl.pallas_call(backward_kernel, grid=(reports,), in_specs=[SMEM, SMEM, to...  12.6 us
    ppermute x3, waiting for transfers between devices, per_device(): late = [lax.ppermute(t, X, p) for t, p in zip(terms, moves)]  10.4 us
    ppermute x3, starting transfers between devices, per_device(): late = [lax.ppermute(t, X, p) for t, p in zip(terms, moves)]  8.1 us
  transfers between devices with their start and end apart: 30, of which 13 were waited for; matrix products, arithmetic and copies ran while one was open for 10% of the time, Pallas kernels for 26%

profile of v5, /device:TPU:0, one launch (start us, length us, event | category | flops | bytes accessed | tf_op | source)
XLA Modules:
  0.0 247.3 jit_solution(3116900759159883539)
XLA Ops:
  7.2 4.5 %shard_map.158 = bf16[128,2048]{1,0:T(8,128)(2,1)} custom-call(s32[4]{0:T(128)} %bitcast.107, bf16[4,64,1536]{2,1,0:T(8,128)(2,1)} %tiles.1, bf16[32,1536]{1,0:T(8,128)(2,1)} %queries.1, bf16[32,2048]{1,0:T(8,128)(2,1)} %bitcast.101, bf16[32,2048]{1,0:T(8,128)(2,1)} %bitcast.102, bf16[1536,512]{1,0:T(8,128)(2,1)} %bitcast.91, bf16[1536,512]{1,0:T(8,128)(2,1)} %bitcast.93), custom_call_target="tpu_custom_call" | custom-call | tf_op jit(solution)/shard_map/pallas_call | solution.py:102
  16.5 11.0 %collective-permute-done.2 = bf16[128,2048]{1,0:T(8,128)(2,1)S(1)} collective-permute-done((bf16[128,2048]{1,0:T(8,128)(2,1)}, bf16[128,2048]{1,0:T(8,128)(2,1)S(1)}, u32[]{:S(2)}, u32[]{:S(2)}) %collective-permute-start.2) | collective-permute-done | bytes 524320 | tf_op jit(solution)/shard_map/ppermute | solution.py:117
  27.6 3.9 %collective-permute-done = bf16[128,2048]{1,0:T(8,128)(2,1)S(1)} collective-permute-done((bf16[128,2048]{1,0:T(8,128)(2,1)}, bf16[128,2048]{1,0:T(8,128)(2,1)S(1)}, u32[]{:S(2)}, u32[]{:S(2)}) %collective-permute-start) | collective-permute-done | bytes 524320 | tf_op jit(solution)/shard_map/ppermute | solution.py:117
  42.8 18.2 %collective-permute-done.3.refs_1_ = bf16[4,128,2048]{2,1,0:T(8,128)(2,1)} collective-permute-done((bf16[4,128,2048]{2,1,0:T(8,128)(2,1)S(1)}, bf16[4,128,2048]{2,1,0:T(8,128)(2,1)}, u32[]{:S(2)}, u32[]{:S(2)}) %collective-permute-start.3) | collective-permute-done | bytes 2097184 | tf_op jit(solution)/shard_map/ppermute | solution.py:119
  61.5 3.9 %pad_maximum_fusion.w_kv = bf16[1536,1024]{1,0:T(8,128)(2,1)} fusion(bf16[1536,512]{1,0:T(8,128)(2,1)} %bitcast.94, bf16[1536,512]{1,0:T(8,128)(2,1)} %bitcast.92), kind=kLoop, calls=%fused_computation.5 | loop fusion | flops 6291456 | bytes 6291456 | tf_op jit(solution)/shard_map/concatenate | solution.py:527
  86.4 6.8 %collective-permute-done.5.refs_3_ = bf16[2,128,2048]{2,1,0:T(8,128)(2,1)S(1)} collective-permute-done((bf16[2,128,2048]{2,1,0:T(8,128)(2,1)}, bf16[2,128,2048]{2,1,0:T(8,128)(2,1)S(1)}, u32[]{:S(2)}, u32[]{:S(2)}) %collective-permute-start.5) | collective-permute-done | bytes 1048608 | tf_op jit(solution)/shard_map/ppermute | solution.py:121
  99.0 4.9 %shard_map.160 = (bf16[512,512]{1,0:T(8,128)(2,1)}, bf16[512,2048]{1,0:T(8,128)(2,1)}) custom-call(s32[211]{0:T(256)} %concatenate.10.meta, bf16[512,2048]{1,0:T(8,128)(2,1)} %fusion.2.x, bf16[4,128,2048]{2,1,0:T(8,128)(2,1)} %copy-done, bf16[4,128,2048]{2,1,0:T(8,128)(2,1)} %collective-permute-done.3.refs_1_, ...), custom_call_target="tpu_custom_call" | custom-call | flops 1073741824 | bytes 7340032 | tf_op jit(solution)/shard_map/pallas_call | solution.py:174
  107.1 5.0 %shard_map.162 = (bf16[512,512]{1,0:T(8,128)(2,1)}, bf16[512,2048]{1,0:T(8,128)(2,1)}) custom-call(s32[211]{0:T(256)} %concatenate.10.meta, bf16[512,2048]{1,0:T(8,128)(2,1)} %broadcast_select_fusion.x, bf16[4,128,2048]{2,1,0:T(8,128)(2,1)} %copy-done, bf16[4,128,2048]{2,1,0:T(8,128)(2,1)} %collective-permute-done.3.refs_1_, ...), custom_call_target="tpu_custom_call" | custom-call | flops 1073741824 | bytes 7340032 | tf_op jit(solution)/shard_map/pallas_call | solution.py:174
  113.6 3.3 %shard_map.163.keys.vals = bf16[768,1024]{1,0:T(8,128)(2,1)} custom-call(s32[211]{0:T(256)} %concatenate.10.meta, bf16[4,128,2048]{2,1,0:T(8,128)(2,1)} %copy-done, bf16[4,128,2048]{2,1,0:T(8,128)(2,1)} %collective-permute-done.3.refs_1_, bf16[4,128,2048]{2,1,0:T(8,128)(2,1)} %collective-permute-done.4.refs_2_, bf16[2,128,2048]{2,1,0:T(8,128)(2,1)} %copy-done.2, ...), custom_call_target="tpu_custom_call" | custom-call | bytes 3145728 | tf_op jit(solution)/shard_map/pallas_call | solution.py:214
  116.9 5.1 %shard_map.159 = (f32[512,512]{1,0:T(8,128)}, bf16[512,2048]{1,0:T(8,128)(2,1)}) custom-call(s32[211]{0:T(256)} %concatenate.10.meta, bf16[512,2048]{1,0:T(8,128)(2,1)} %fusion.2.x, bf16[4,128,2048]{2,1,0:T(8,128)(2,1)} %copy-done, bf16[4,128,2048]{2,1,0:T(8,128)(2,1)} %collective-permute-done.3.refs_1_, ...), custom_call_target="tpu_custom_call" | custom-call | flops 1073741824 | bytes 7340032 | tf_op jit(solution)/shard_map/pallas_call | solution.py:174
  122.1 5.0 %shard_map.161 = (bf16[512,512]{1,0:T(8,128)(2,1)}, bf16[512,2048]{1,0:T(8,128)(2,1)}) custom-call(s32[211]{0:T(256)} %concatenate.10.meta, bf16[512,2048]{1,0:T(8,128)(2,1)} %broadcast_select_fusion.x, bf16[4,128,2048]{2,1,0:T(8,128)(2,1)} %copy-done, bf16[4,128,2048]{2,1,0:T(8,128)(2,1)} %collective-permute-done.3.refs_1_, ...), custom_call_target="tpu_custom_call" | custom-call | flops 1073741824 | bytes 7340032 | tf_op jit(solution)/shard_map/pallas_call | solution.py:174
  127.9 4.9 %shard_map.164.probs = f32[4,512,192]{2,1,0:T(8,128)} custom-call(s32[211]{0:T(256)} %concatenate.10.meta, f32[512,512]{1,0:T(8,128)} %get-tuple-element.74.q_own, bf16[512,512]{1,0:T(8,128)(2,1)} %copy-done.5, bf16[768,1024]{1,0:T(8,128)(2,1)} %shard_map.163.keys.vals), custom_call_target="tpu_custom_call" | custom-call | flops 100663296 | bytes 6291456 | tf_op jit(solution)/shard_map/pallas_call | solution.py:253
  133.5 6.4 %shard_map.165 = (bf16[528,512]{1,0:T(8,128)(2,1)}, bf16[4,192,1024]{2,1,0:T(8,128)(2,1)}) custom-call(s32[211]{0:T(256)} %concatenate.10.meta, f32[1]{0:T(128)S(6)} %tanh.3.gate, f32[512,512]{1,0:T(8,128)} %get-tuple-element.74.q_own, bf16[512,512]{1,0:T(8,128)(2,1)} %copy-done.5, bf16[512,512]{1,0:T(8,128)(2,1)} %get-tuple-element.77.o_own, ...), custom_call_target="tpu_custom_call" | custom-call | flops 402653184 | bytes 8388608 | tf_op jit(solution)/shard_map/pallas_call | solution.py:305
  142.5 7.4 %shard_map.166 = (f32[192,1536]{1,0:T(8,128)}, bf16[192,1536]{1,0:T(8,128)(2,1)}, bf16[192,1536]{1,0:T(8,128)(2,1)}, bf16[192,1536]{1,0:T(8,128)(2,1)}) custom-call(bf16[4,192,1024]{2,1,0:T(8,128)(2,1)} %get-tuple-element.80.dkv, bf16[1536,1024]{1,0:T(8,128)(2,1)} %pad_maximum_fusion.w_kv), custom_call_target="tpu_custom_call" | custom-call | flops 2415919104 | bytes 8388608 | tf_op jit(solution)/shard_map/pallas_call | solution.py:441
  149.9 6.2 %collective-permute-done.17.refs_0_ = bf16[528,512]{1,0:T(8,128)(2,1)S(1)} collective-permute-done((bf16[528,512]{1,0:T(8,128)(2,1)}, bf16[528,512]{1,0:T(8,128)(2,1)S(1)}, u32[]{:S(2)}, u32[]{:S(2)}) %collective-permute-start.17) | collective-permute-done | bytes 540704 | tf_op jit(solution)/shard_map/ppermute | solution.py:547
  159.4 8.6 %shard_map.167 = (bf16[512,2048]{1,0:T(8,128)(2,1)}, bf16[512,512]{1,0:T(8,128)(2,1)}) custom-call(s32[211]{0:T(256)} %concatenate.10.meta, f32[1,512]{1,0:T(1,128)} %slice.18.rinv, f32[1,2048]{1,0:T(1,128)} %slice.19.gain, bf16[528,512]{1,0:T(8,128)(2,1)} %copy-done.11, bf16[528,512]{1,0:T(8,128)(2,1)} %copy-done.12, bf16[512,2048]{1,0:T(8,128)(2,1)} %refs_2_.1, ...), custom_call_target="tpu_custom_call" | custom-call | flops 3221225472 | bytes 12582912 | tf_op jit(solution)/shard_map/pallas_call | solution.py:413
  174.1 4.3 %convolution_convert_fusion.o_own = bf16[512,512]{1,0:T(8,128)(2,1)} fusion(bf16[512,2048]{1,0:T(8,128)(2,1)} %get-tuple-element.96.refs_4_, bf16[512,2048]{1,0:T(8,128)(2,1)} %get-tuple-element.97), kind=kOutput, calls=%fused_computation.8 | convolution fusion | flops 1074003968 | bytes 4718592 | tf_op jit(solution)/shard_map/dot_general | solution.py:51
  178.4 6.1 %collective-permute-done.19.o_got = bf16[512,512]{1,0:T(8,128)(2,1)S(1)} collective-permute-done((bf16[512,512]{1,0:T(8,128)(2,1)}, bf16[512,512]{1,0:T(8,128)(2,1)S(1)}, u32[]{:S(2)}, u32[]{:S(2)}) %collective-permute-start.19) | collective-permute-done | bytes 524320 | tf_op jit(solution)/shard_map/ppermute | solution.py:551
  185.4 6.3 %shard_map.168 = (bf16[528,512]{1,0:T(8,128)(2,1)}, bf16[4,192,1024]{2,1,0:T(8,128)(2,1)}) custom-call(s32[211]{0:T(256)} %concatenate.10.meta, f32[1]{0:T(128)S(6)} %tanh.3.gate, f32[512,512]{1,0:T(8,128)} %get-tuple-element.74.q_own, bf16[512,512]{1,0:T(8,128)(2,1)} %copy-done.5, bf16[512,512]{1,0:T(8,128)(2,1)} %convolution_convert_fusion.o_own, ...), custom_call_target="tpu_custom_call" | custom-call | flops 402653184 | bytes 8388608 | tf_op jit(solution)/shard_map/pallas_call | solution.py:305
  195.1 7.2 %shard_map.169 = (f32[192,1536]{1,0:T(8,128)}, bf16[192,1536]{1,0:T(8,128)(2,1)}, bf16[192,1536]{1,0:T(8,128)(2,1)}, bf16[192,1536]{1,0:T(8,128)(2,1)}) custom-call(bf16[4,192,1024]{2,1,0:T(8,128)(2,1)} %get-tuple-element.99.dkv, bf16[1536,1024]{1,0:T(8,128)(2,1)} %pad_maximum_fusion.w_kv), custom_call_target="tpu_custom_call" | custom-call | flops 2415919104 | bytes 8388608 | tf_op jit(solution)/shard_map/pallas_call | solution.py:441
  202.4 6.3 %collective-permute-done.22 = bf16[192,1536]{1,0:T(8,128)(2,1)S(1)} collective-permute-done((bf16[192,1536]{1,0:T(8,128)(2,1)}, bf16[192,1536]{1,0:T(8,128)(2,1)S(1)}, u32[]{:S(2)}, u32[]{:S(2)}) %collective-permute-start.22) | collective-permute-done | bytes 589856 | tf_op jit(solution)/shard_map/ppermute | solution.py:556
  212.9 3.9 %collective-permute-start.27 = (bf16[192,1536]{1,0:T(8,128)(2,1)}, bf16[192,1536]{1,0:T(8,128)(2,1)}, u32[]{:S(2)}, u32[]{:S(2)}) collective-permute-start(bf16[192,1536]{1,0:T(8,128)(2,1)} %get-tuple-element.119), channel_id=1, source_target_pairs={{0,1},{1,0},{2,3},{3,2},{4,5},{5,4},{6,7},{7,6},{8,9},{9,8},{10,11... | collective-permute-start | bytes 1769480 | tf_op jit(solution)/shard_map/ppermute | solution.py:563
  217.8 7.6 %shard_map.170 = bf16[512,2048]{1,0:T(8,128)(2,1)} custom-call(s32[211]{0:T(256)} %concatenate.10.meta, f32[1,512]{1,0:T(1,128)} %bitcast.106, f32[1,2048]{1,0:T(1,128)} %gain.1, bf16[528,512]{1,0:T(8,128)(2,1)} %get-tuple-element.95.refs_0_, bf16[528,512]{1,0:T(8,128)(2,1)} %get-tuple-element.98.refs_1_, bf16[528,512]{1,0:T(8,128)(2,1)} %copy-done.10, ...), custom_call_target="tpu_custom_call" | custom-call | flops 2147483648 | bytes 12582912 | tf_op jit(solution)/shard_map/pallas_call | solution.py:413
  227.3 10.4 %collective-permute-done.27 = bf16[192,1536]{1,0:T(8,128)(2,1)} collective-permute-done((bf16[192,1536]{1,0:T(8,128)(2,1)}, bf16[192,1536]{1,0:T(8,128)(2,1)}, u32[]{:S(2)}, u32[]{:S(2)}) %collective-permute-start.27) | collective-permute-done | bytes 589856 | tf_op jit(solution)/shard_map/ppermute | solution.py:563
  (124 shorter events, 74.8 us)
Async XLA Ops:
  7.2 151.4 %all-gather.3.cloned.1.call-start = ((), (), s32[]{:S(2)}) async-start(), calls=%async_computation | async-start | bytes 6291456 | tf_op jit(solution)/shard_map/all_gather | solution.py:505
  11.8 15.8 %collective-permute-start.2 = (bf16[128,2048]{1,0:T(8,128)(2,1)}, bf16[128,2048]{1,0:T(8,128)(2,1)S(1)}, u32[]{:S(2)}, u32[]{:S(2)}) collective-permute-start(bf16[128,2048]{1,0:T(8,128)(2,1)} %shard_map.158), channel_id=1, source_target_pairs={{0,12},{2,50},{4,0},{6,54},{8,4},{10,58},{12,8},{14,62},{16,28},{1... | collective-permute-start | bytes 1572872 | tf_op jit(solution)/shard_map/ppermute | solution.py:117
  15.6 15.9 %collective-permute-start = (bf16[128,2048]{1,0:T(8,128)(2,1)}, bf16[128,2048]{1,0:T(8,128)(2,1)S(1)}, u32[]{:S(2)}, u32[]{:S(2)}) collective-permute-start(bf16[128,2048]{1,0:T(8,128)(2,1)} %shard_map.158), channel_id=1, source_target_pairs={{0,4},{2,18},{4,8},{6,22},{8,12},{10,26},{12,0},{14,30},{16,20},{1... | collective-permute-start | bytes 1572872 | tf_op jit(solution)/shard_map/ppermute | solution.py:117
  32.8 28.2 %collective-permute-start.3 = (bf16[4,128,2048]{2,1,0:T(8,128)(2,1)S(1)}, bf16[4,128,2048]{2,1,0:T(8,128)(2,1)}, u32[]{:S(2)}, u32[]{:S(2)}) collective-permute-start(bf16[4,128,2048]{2,1,0:T(8,128)(2,1)S(1)} %pad_maximum_fusion.1.refs_0_), channel_id=1, source_target_pairs={{0,16},{2,6},{4,20},{6,10},{8,24},{10,14},{12,28},{14,2},{16,32},{... | collective-permute-start | bytes 6291464 | tf_op jit(solution)/shard_map/ppermute | solution.py:119
  34.7 26.3 %collective-permute-start.4 = (bf16[4,128,2048]{2,1,0:T(8,128)(2,1)S(1)}, bf16[4,128,2048]{2,1,0:T(8,128)(2,1)}, u32[]{:S(2)}, u32[]{:S(2)}) collective-permute-start(bf16[4,128,2048]{2,1,0:T(8,128)(2,1)S(1)} %pad_maximum_fusion.1.refs_0_), channel_id=1, source_target_pairs={{0,48},{2,14},{4,52},{6,2},{8,56},{10,6},{12,60},{14,10},{16,0},{1... | collective-permute-start | bytes 6291464 | tf_op jit(solution)/shard_map/ppermute | solution.py:120
  37.0 121.6 %all-gather.5.cloned.1.call-start = ((), (), s32[]{:S(2)}) async-start(), calls=%async_computation.1 | async-start | bytes 4325376 | tf_op jit(solution)/shard_map/all_gather | solution.py:535
  39.1 26.5 %collective-permute-start.10 = (f32[512]{0:T(512)S(1)}, f32[512]{0:T(512)S(1)}, u32[]{:S(2)}, u32[]{:S(2)}) collective-permute-start(f32[512]{0:T(512)S(1)} %fusion), channel_id=1, source_target_pairs={{0,1},{1,0},{2,3},{3,2},{4,5},{5,4},{6,7},{7,6},{8,9},{9,8},{10,11... | collective-permute-start | bytes 6152 | tf_op jit(solution)/shard_map/ppermute | solution.py:516
  42.7 43.6 %collective-permute-start.7 = (bf16[4,128,2048]{2,1,0:T(8,128)(2,1)S(1)}, bf16[4,128,2048]{2,1,0:T(8,128)(2,1)}, u32[]{:S(2)}, u32[]{:S(2)}) collective-permute-start(bf16[4,128,2048]{2,1,0:T(8,128)(2,1)S(1)} %pad_maximum_fusion.1.refs_0_), channel_id=1, source_target_pairs={{0,2},{2,0},{1,3},{3,1},{4,6},{6,4},{5,7},{7,5},{8,10},{10,8},{9,1... | collective-permute-start | bytes 6291464 | tf_op jit(solution)/shard_map/ppermute | solution.py:531
  61.0 32.5 %collective-permute-start.8 = (bf16[4,128,2048]{2,1,0:T(8,128)(2,1)}, bf16[4,128,2048]{2,1,0:T(8,128)(2,1)}, u32[]{:S(2)}, u32[]{:S(2)}) collective-permute-start(bf16[4,128,2048]{2,1,0:T(8,128)(2,1)} %collective-permute-done.3.refs_1_), channel_id=1, source_target_pairs={{0,2},{2,0},{1,3},{3,1},{4,6},{6,4},{5,7},{7,5},{8,10},{10,8},{9,1... | collective-permute-start | bytes 6291464 | tf_op jit(solution)/shard_map/ppermute | solution.py:531
  61.0 32.5 %collective-permute-start.9 = (bf16[4,128,2048]{2,1,0:T(8,128)(2,1)}, bf16[4,128,2048]{2,1,0:T(8,128)(2,1)}, u32[]{:S(2)}, u32[]{:S(2)}) collective-permute-start(bf16[4,128,2048]{2,1,0:T(8,128)(2,1)} %collective-permute-done.4.refs_2_), channel_id=1, source_target_pairs={{0,2},{2,0},{1,3},{3,1},{4,6},{6,4},{5,7},{7,5},{8,10},{10,8},{9,1... | collective-permute-start | bytes 6291464 | tf_op jit(solution)/shard_map/ppermute | solution.py:531
  76.9 16.2 %collective-permute-start.5 = (bf16[2,128,2048]{2,1,0:T(8,128)(2,1)}, bf16[2,128,2048]{2,1,0:T(8,128)(2,1)S(1)}, u32[]{:S(2)}, u32[]{:S(2)}) collective-permute-start(bf16[2,128,2048]{2,1,0:T(8,128)(2,1)} %slice.16), channel_id=1, source_target_pairs={{0,16},{2,6},{4,20},{6,10},{8,24},{10,14},{12,28},{14,2},{16,32},{... | collective-permute-start | bytes 3145736 | tf_op jit(solution)/shard_map/ppermute | solution.py:121
  104.0 23.1 %collective-permute-start.15 = (bf16[512,512]{1,0:T(8,128)(2,1)}, bf16[512,512]{1,0:T(8,128)(2,1)S(1)}, u32[]{:S(2)}, u32[]{:S(2)}) collective-permute-start(bf16[512,512]{1,0:T(8,128)(2,1)} %get-tuple-element.75), channel_id=1, source_target_pairs={{0,1},{1,0},{64,65},{65,64},{2,3},{3,2},{66,67},{67,66},{4,5},{5,4... | collective-permute-start | bytes 1572872 | tf_op jit(solution)/shard_map/ppermute | solution.py:539
  112.0 20.7 %collective-permute-start.16 = (bf16[512,512]{1,0:T(8,128)(2,1)}, bf16[512,512]{1,0:T(8,128)(2,1)S(1)}, u32[]{:S(2)}, u32[]{:S(2)}) collective-permute-start(bf16[512,512]{1,0:T(8,128)(2,1)} %get-tuple-element.78), channel_id=1, source_target_pairs={{64,65},{65,64},{66,67},{67,66},{68,69},{69,68},{70,71},{71,70},{7... | collective-permute-start | bytes 1572872 | tf_op jit(solution)/shard_map/ppermute | solution.py:541
  139.9 16.2 %collective-permute-start.17 = (bf16[528,512]{1,0:T(8,128)(2,1)}, bf16[528,512]{1,0:T(8,128)(2,1)S(1)}, u32[]{:S(2)}, u32[]{:S(2)}) collective-permute-start(bf16[528,512]{1,0:T(8,128)(2,1)} %get-tuple-element.95.refs_0_), channel_id=1, source_target_pairs={{64,0},{65,1},{66,2},{67,3},{68,4},{69,5},{70,6},{71,7},{72,8},{73... | collective-permute-start | bytes 1622024 | tf_op jit(solution)/shard_map/ppermute | solution.py:547
  141.2 17.4 %collective-permute-start.18 = (bf16[528,512]{1,0:T(8,128)(2,1)}, bf16[528,512]{1,0:T(8,128)(2,1)S(1)}, u32[]{:S(2)}, u32[]{:S(2)}) collective-permute-start(bf16[528,512]{1,0:T(8,128)(2,1)} %get-tuple-element.95.refs_0_), channel_id=1, source_target_pairs={{64,1},{65,0},{66,3},{67,2},{68,5},{69,4},{70,7},{71,6},{72,9},{73... | collective-permute-start | bytes 1622024 | tf_op jit(solution)/shard_map/ppermute | solution.py:547
  168.0 16.6 %collective-permute-start.19 = (bf16[512,512]{1,0:T(8,128)(2,1)}, bf16[512,512]{1,0:T(8,128)(2,1)S(1)}, u32[]{:S(2)}, u32[]{:S(2)}) collective-permute-start(bf16[512,512]{1,0:T(8,128)(2,1)} %get-tuple-element.94), channel_id=1, source_target_pairs={{0,1},{1,0},{2,3},{3,2},{4,5},{5,4},{6,7},{7,6},{8,9},{9,8},{10,11... | collective-permute-start | bytes 1572872 | tf_op jit(solution)/shard_map/ppermute | solution.py:551
  170.8 31.6 %collective-permute-start.21 = (bf16[192,1536]{1,0:T(8,128)(2,1)}, bf16[192,1536]{1,0:T(8,128)(2,1)S(1)}, u32[]{:S(2)}, u32[]{:S(2)}) collective-permute-start(bf16[192,1536]{1,0:T(8,128)(2,1)} %get-tuple-element.103), channel_id=1, source_target_pairs={{64,0},{65,1},{66,2},{67,3},{68,4},{69,5},{70,6},{71,7},{72,8},{73... | collective-permute-start | bytes 1769480 | tf_op jit(solution)/shard_map/ppermute | solution.py:556
  172.1 36.6 %collective-permute-start.22 = (bf16[192,1536]{1,0:T(8,128)(2,1)}, bf16[192,1536]{1,0:T(8,128)(2,1)S(1)}, u32[]{:S(2)}, u32[]{:S(2)}) collective-permute-start(bf16[192,1536]{1,0:T(8,128)(2,1)} %get-tuple-element.104), channel_id=1, source_target_pairs={{64,1},{65,0},{66,3},{67,2},{68,5},{69,4},{70,7},{71,6},{72,9},{73... | collective-permute-start | bytes 1769480 | tf_op jit(solution)/shard_map/ppermute | solution.py:556
  173.4 35.3 %collective-permute-start.23 = (bf16[192,1536]{1,0:T(8,128)(2,1)}, bf16[192,1536]{1,0:T(8,128)(2,1)S(1)}, u32[]{:S(2)}, u32[]{:S(2)}) collective-permute-start(bf16[192,1536]{1,0:T(8,128)(2,1)} %get-tuple-element.105), channel_id=1, source_target_pairs={{64,65},{65,64},{66,67},{67,66},{68,69},{69,68},{70,71},{71,70},{7... | collective-permute-start | bytes 1769480 | tf_op jit(solution)/shard_map/ppermute | solution.py:556
  191.6 25.2 %collective-permute-start.24 = (bf16[528,512]{1,0:T(8,128)(2,1)}, bf16[528,512]{1,0:T(8,128)(2,1)S(1)}, u32[]{:S(2)}, u32[]{:S(2)}) collective-permute-start(bf16[528,512]{1,0:T(8,128)(2,1)} %get-tuple-element.98.refs_1_), channel_id=1, source_target_pairs={{0,1},{1,0},{2,3},{3,2},{4,5},{5,4},{6,7},{7,6},{8,9},{9,8},{10,11... | collective-permute-start | bytes 1622024 | tf_op jit(solution)/shard_map/ppermute | solution.py:560
  194.4 22.4 %collective-permute-start.20 = (bf16[528,512]{1,0:T(8,128)(2,1)S(1)}, bf16[528,512]{1,0:T(8,128)(2,1)S(1)}, u32[]{:S(2)}, u32[]{:S(2)}) collective-permute-start(bf16[528,512]{1,0:T(8,128)(2,1)S(1)} %copy-done.8), channel_id=1, source_target_pairs={{64,65},{65,64},{66,67},{67,66},{68,69},{69,68},{70,71},{71,70},{7... | collective-permute-start | bytes 1622024 | tf_op jit(solution)/shard_map/ppermute | solution.py:554
  208.7 18.6 %collective-permute-start.25 = (bf16[192,1536]{1,0:T(8,128)(2,1)}, bf16[192,1536]{1,0:T(8,128)(2,1)}, u32[]{:S(2)}, u32[]{:S(2)}) collective-permute-start(bf16[192,1536]{1,0:T(8,128)(2,1)} %get-tuple-element.117), channel_id=1, source_target_pairs={{0,64},{1,65},{2,66},{3,67},{4,68},{5,69},{6,70},{7,71},{8,72},{9,... | collective-permute-start | bytes 1769480 | tf_op jit(solution)/shard_map/ppermute | solution.py:563
  210.8 16.5 %collective-permute-start.26 = (bf16[192,1536]{1,0:T(8,128)(2,1)}, bf16[192,1536]{1,0:T(8,128)(2,1)}, u32[]{:S(2)}, u32[]{:S(2)}) collective-permute-start(bf16[192,1536]{1,0:T(8,128)(2,1)} %get-tuple-element.118), channel_id=1, source_target_pairs={{0,65},{1,64},{2,67},{3,66},{4,69},{5,68},{6,71},{7,70},{8,73},{9,... | collective-permute-start | bytes 1769480 | tf_op jit(solution)/shard_map/ppermute | solution.py:563
  212.9 24.8 %collective-permute-start.27 = (bf16[192,1536]{1,0:T(8,128)(2,1)}, bf16[192,1536]{1,0:T(8,128)(2,1)}, u32[]{:S(2)}, u32[]{:S(2)}) collective-permute-start(bf16[192,1536]{1,0:T(8,128)(2,1)} %get-tuple-element.119), channel_id=1, source_target_pairs={{0,1},{1,0},{2,3},{3,2},{4,5},{5,4},{6,7},{7,6},{8,9},{9,8},{10,11... | collective-permute-start | bytes 1769480 | tf_op jit(solution)/shard_map/ppermute | solution.py:563
  (29 other events, 256.8 us)
Sparse Core Ops, SparseCore 0:
  37.1 60.0 all-gather.2
  99.4 47.3 all-gather.4

commit v6 on v5

--- a/solution.py
+++ b/solution.py
@@ -67,14 +67,12 @@
 ARRAYS = ((0, (0, 1, 2, 3)), (1, (0, 1, 2, 3)), (3, (0, 1, 2, 3)), (2, (0, 1)), (2, (2, 3)))
 
 
-def block_kernel(counts, tiles, queries, w_out, w_query, w_key, w_value, out, w_v, latents, sems):
+def kv_kernel(counts, tiles, queries, w_key, w_value, out, w_v, latents, sems):
     loads = [
         pltpu.make_async_copy(w, w_v.at[i], sems.at[i]) for i, w in enumerate((w_key, w_value))
     ]
     for load in loads:
         load.start()
-    out[:32] = w_out[...]
-    out[32:64] = w_query[...]
     heads = [slice(head * HEAD, (head + 1) * HEAD) for head in range(E // HEAD)]
     slot = lax.broadcasted_iota(jnp.int32, (LAT, MAXT), 1)
     for slide in range(tiles.shape[0]):
@@ -92,34 +90,33 @@
         value = dot(latents[...], w_v[i], NN).astype(BF)
         half = value.shape[1]
         for slide in range(tiles.shape[0]):
-            at = 64 + slide // 2 * LAT
+            at = slide // 2 * LAT
             col = (slide % 2 * 2 + i) * half
             out[at : at + LAT, col : col + half] = value[slide * LAT : (slide + 1) * LAT]
 
 
-def make_block(counts, tiles, queries, w_out, w_query, w_key, w_value):
+def make_kv(counts, tiles, queries, w_key, w_value):
     slides = tiles.shape[0]
     return pl.pallas_call(
-        block_kernel,
-        in_specs=[SMEM] + [VMEM] * 4 + [ANY] * 2,
+        kv_kernel,
+        in_specs=[SMEM] + [VMEM] * 2 + [ANY] * 2,
         out_specs=VMEM,
-        out_shape=jax.ShapeDtypeStruct((64 + slides // 2 * LAT, w_out.shape[1]), BF),
+        out_shape=jax.ShapeDtypeStruct((slides // 2 * LAT, 4 * w_key.shape[1]), BF),
         scratch_shapes=[
             pltpu.VMEM((2,) + w_key.shape, BF),
             pltpu.VMEM((slides * LAT, E), BF),
             pltpu.SemaphoreType.DMA((2,)),
         ],
         compiler_params=params(),
-    )(counts, tiles, queries, w_out, w_query, w_key, w_value)
-
-
-def gather_chips(block):
-    first = [lax.ppermute(block, DP, yz_perm(1, k)) for k in (1, 2, 3)]
-    bundle = jnp.stack([block, *first])
-    one = lax.ppermute(bundle, DP, yz_perm(2, 1))
-    three = lax.ppermute(bundle, DP, yz_perm(2, 3))
-    two = lax.ppermute(one[:2], DP, yz_perm(2, 1)), lax.ppermute(three[2:], DP, yz_perm(2, 3))
-    return [bundle, one, three, *two]
+    )(counts, tiles, queries, w_key, w_value)
+
+
+def over_dp(array, stage, k):
+    return lax.ppermute(array, DP, yz_perm(stage, k))
+
+
+def over_core(arrays):
+    return [lax.ppermute(a, "core", [(0, 1), (1, 0)]) for a in arrays]
 
 
 def places(z, y, core):
@@ -197,7 +194,7 @@
     for i in range(wanted):
         block = meta[PICKS + wanted + i]
         slide = meta[PICKS + 2 * wanted + i]
-        rows = pl.ds(pl.multiple_of(64 + slide // 2 * LAT, LAT), LAT)
+        rows = pl.ds(pl.multiple_of(slide // 2 * LAT, LAT), LAT)
         cols = pl.ds(pl.multiple_of(slide % 2 * width, width), width)
         for a in range(10):
 
@@ -425,30 +422,33 @@
     )(*inputs)
 
 
-def term_kernel(dkv, w_kv, own, *terms):
+def term_kernel(dkv, w_key, w_value, own, *terms):
     rows = own.shape[0]
-    value = dot(dkv[...].reshape(4 * rows, dkv.shape[2]), w_kv[...], NT)
+    both = dkv[...].reshape(4 * rows, dkv.shape[2])
+    half = w_key.shape[1]
+    value = dot(both[:, :half], w_key[...], NT) + dot(both[:, half:], w_value[...], NT)
     own[...] = value[:rows]
     for k, term in enumerate(terms, 1):
         term[...] = value[k * rows : (k + 1) * rows].astype(BF)
 
 
-def latent_terms(dkv, w_kv):
+def latent_terms(dkv, w_key, w_value):
     rows, inner = dkv.shape[1:]
-    features = w_kv.shape[0]
-    tile = features // 6
+    features = w_key.shape[0]
+    tile = features // 3
+    weight = pl.BlockSpec((tile, w_key.shape[1]), lambda i: (i, 0))
     result = pl.BlockSpec((rows, tile), lambda i: (0, i))
     return pl.pallas_call(
         term_kernel,
         grid=(features // tile,),
-        in_specs=[whole(dkv.shape), pl.BlockSpec((tile, inner), lambda i: (i, 0))],
+        in_specs=[whole(dkv.shape), weight, weight],
         out_specs=[result] * 4,
         out_shape=[jax.ShapeDtypeStruct((rows, features), t) for t in (F32, BF, BF, BF)],
         compiler_params=params(),
         cost_estimate=pl.CostEstimate(
             flops=8 * rows * inner * features, bytes_accessed=8 << 20, transcendentals=0
         ),
-    )(dkv, w_kv)
+    )(dkv, w_key, w_value)
 
 
 def per_device(
@@ -505,11 +505,17 @@
     h_all = lax.all_gather(h, "segment")
 
     wq_t = w_query[0].T
-    blocks = gather_chips(
-        make_block(
-            tile_counts.reshape(4), tiles, lat_query, w_out[0], wq_t, w_key[0], w_value[0]
-        )
-    )
+    block = jnp.concatenate([w_out[0], wq_t], axis=0)
+    parts = [over_dp(block, 1, k) for k in (1, 2, 3)]
+    kv_block = make_kv(tile_counts.reshape(4), tiles, lat_query, w_key[0], w_value[0])
+    parts, kv_block = lax.optimization_barrier((parts, kv_block))
+    bundle = jnp.stack([block, *parts])
+    one, three = over_dp(bundle, 2, 1), over_dp(bundle, 2, 3)
+    parts = [over_dp(kv_block, 1, k) for k in (1, 2, 3)]
+    one, three, parts = lax.optimization_barrier((one, three, parts))
+    two = [over_dp(one[:2], 2, 1), over_dp(three[2:], 2, 3)]
+    kv_bundle = jnp.stack([kv_block, *parts])
+    kv_one, kv_three = over_dp(kv_bundle, 2, 1), over_dp(kv_bundle, 2, 3)
 
     h32 = h.astype(F32)
     partial = jnp.sum(h32 * h32, axis=1)
@@ -524,28 +530,33 @@
     up1 = jnp.where(live[:, None], cotangent, jnp.zeros((), BF))
     rinv = rinv[None]
     gate = jnp.tanh(attn_gate)
-    w_kv = jnp.concatenate([w_key[0], w_value[0]], axis=1)
     wq_t, _ = lax.optimization_barrier((wq_t, squares))
     wq1 = lax.ppermute(wq_t, "segment", [(1, 0)])
-    swap = [(0, 1), (1, 0)]
-    others = [lax.ppermute(b, "core", swap) for b in blocks[:3]]
-    blocks, others, normed, up1, rinv1, gain1, meta, w_kv, wq1 = lax.optimization_barrier(
-        (blocks, others, normed, up1, rinv1, gain1, meta, w_kv, wq1)
+    others = over_core([bundle, one, three])
+    two, others, normed, up1, rinv1, gain1, meta, wq1 = lax.optimization_barrier(
+        (two, others, normed, up1, rinv1, gain1, meta, wq1)
     )
     wq1 = lax.all_gather(wq1, DP, axis=0, tiled=True)
-    blocks = blocks + others + [lax.ppermute(b, "core", swap) for b in blocks[3:]]
+    blocks = [bundle, one, three, *two, *others, *over_core(two)]
 
     q_send, wq_got = project(1, 1, BF, meta, normed, blocks)
     q_got = lax.ppermute(q_send, X, SWAP_MP)
+    up1, q_send = lax.optimization_barrier((up1, q_send))
     o_send, wo_got = project(0, 1, BF, meta, up1, blocks)
     o_got = lax.ppermute(o_send, X, LAST_SWAP)
+    kv_one, kv_three, o_send = lax.optimization_barrier((kv_one, kv_three, o_send))
+    kv_two = [over_dp(kv_one[:2], 2, 1), over_dp(kv_three[2:], 2, 3)]
+    kv_blocks = [kv_bundle, kv_one, kv_three, *kv_two]
+    kv_blocks += over_core(kv_blocks)
     q_own, wq_own = project(1, 0, F32, meta, normed, blocks)
+    up1, q_got, q_own = lax.optimization_barrier((up1, q_got, q_own))
     o_own, wo_own = project(0, 0, BF, meta, up1, blocks)
-    kv = select(wanted, meta, blocks)
+    kv_blocks, q_own, o_own = lax.optimization_barrier((kv_blocks, q_own, o_own))
+    kv = select(wanted, meta, kv_blocks)
     probs = forward(meta, q_own, q_got, kv)
     dq1, dkv1 = backward(meta, gate, q_own, q_got, o_own, o_got, kv, probs)
     dqs = [lax.ppermute(dq1, X, LAST_TO_SAME), lax.ppermute(dq1, X, LAST_TO_CROSS)]
-    own1, *terms = latent_terms(dkv1, w_kv)
+    own1, *terms = latent_terms(dkv1, w_key[0], w_value[0])
     dqs, terms = lax.optimization_barrier((dqs, terms))
     up, o_send = back(meta, rinv1, gain1, dqs, cotangent, h_all, [wq1], wo_got)
     o_got = lax.ppermute(o_send, X, FIRST_SWAP)
@@ -556,7 +567,7 @@
     got = [lax.ppermute(t, X, p) for t, p in zip(terms, moves)]
 
     dq0, dkv0 = backward(meta, gate, q_own, q_got, o_own, o_got, kv, probs)
-    own0, *terms = latent_terms(dkv0, w_kv)
+    own0, *terms = latent_terms(dkv0, w_key[0], w_value[0])
     got0 = lax.ppermute(dq0, X, FIRST_SWAP)
     terms, got = lax.optimization_barrier((terms, got))
     moves = (FIRST_TO_SAME, FIRST_TO_CROSS, FIRST_SWAP)

time: 249 us -> 246 us (0.988)
  waiting for transfers between devices: 78.9 us -> 60.9 us
  starting transfers between devices: 43.3 us -> 60.1 us
  local copies, waits for them, and re-layouts: 12.4 us -> 16.6 us
  other arithmetic: 17 us -> 13.6 us
    ppermute x12 -> x24, waiting for transfers between devices: 44.1 us -> 18.7 us  [the longest x14 14.9 us: over_dp(): return lax.ppermute(array, DP, yz_perm(stage, k))]
    ppermute x12 -> x24, starting transfers between devices: 13.4 us -> 27.4 us  [the longest x14 25.7 us: over_dp(): return lax.ppermute(array, DP, yz_perm(stage, k))]
    ppermute x1, waiting for transfers between devices: 0.01 us -> 7.94 us  [per_device(): q_got = lax.ppermute(q_send, X, SWAP_MP)]
    concatenate x1 -> x0, other arithmetic: 3.94 us -> none  [per_device(): w_kv = jnp.concatenate([w_key[0], w_value[0]], axis=1)]
    ppermute x1, waiting for transfers between devices: 6.2 us -> 9.5 us  [per_device(): lax.ppermute(dq1, X, LAST_TO_SAME)]
    unnamed x48 -> x58, local copies, waits for them, and re-layouts: 5.46 us -> 4.93 us
  transfers between devices with their start and end apart: 30 -> 42, of which waited for: 13 -> 17; matrix products, arithmetic and copies ran while one was open for 10% -> 11% of each run, Pallas kernels for 26% -> 27%
where the time goes in v6:
time: 246 us; the launch traced here: 244 us
  Pallas kernels  73.8 us (30%)
  waiting for transfers between devices  60.9 us (25%)
  starting transfers between devices  60.1 us (24%)
  local copies, waits for them, and re-layouts  16.6 us (7%)
  between operations  15.3 us (6%)
  other arithmetic  13.6 us (6%)
  matrix products  4.3 us (2%)
    ppermute x14, starting transfers between devices, over_dp(): return lax.ppermute(array, DP, yz_perm(stage, k))  25.7 us
    pallas_call x4, Pallas kernels, project(): pl.pallas_call(functools.partial(project_kernel, kind, part), in_specs=[S...  20.2 us
    pallas_call x2, Pallas kernels, back(): pl.pallas_call(functools.partial(back_kernel, wo is not None), in_specs=i...  16.3 us
    ppermute x14, waiting for transfers between devices, over_dp(): return lax.ppermute(array, DP, yz_perm(stage, k))  14.9 us
    pallas_call x2, Pallas kernels, backward(): pl.pallas_call(backward_kernel, grid=(reports,), in_specs=[SMEM, SMEM, to...  12.6 us
    pallas_call x2, Pallas kernels, latent_terms(): pl.pallas_call(term_kernel, grid=(features // tile,), in_specs=[whole(dkv...  12.3 us
    ppermute x3, waiting for transfers between devices, per_device(): late = [lax.ppermute(t, X, p) for t, p in zip(terms, moves)]  11.1 us
    ppermute x1, waiting for transfers between devices, per_device(): lax.ppermute(dq1, X, LAST_TO_SAME)  9.5 us
  transfers between devices with their start and end apart: 42, of which 17 were waited for; matrix products, arithmetic and copies ran while one was open for 11% of the time, Pallas kernels for 27%

profile of v6, /device:TPU:0, one launch (start us, length us, event | category | flops | bytes accessed | tf_op | source)
XLA Modules:
  0.0 244.5 jit_solution(1622849925781464996)
XLA Ops:
  15.0 4.4 %shard_map.158 = bf16[64,2048]{1,0:T(8,128)(2,1)} custom-call(s32[4]{0:T(128)} %bitcast.114, bf16[4,64,1536]{2,1,0:T(8,128)(2,1)} %tiles.1, bf16[32,1536]{1,0:T(8,128)(2,1)} %queries.1, bf16[1536,512]{1,0:T(8,128)(2,1)} %bitcast.97, bf16[1536,512]{1,0:T(8,128)(2,1)} %bitcast.100), custom_call_target="tpu_custom_call" | custom-call | tf_op jit(solution)/shard_map/pallas_call | solution.py:100
  33.8 4.3 %collective-permute-done.5 = bf16[64,2048]{1,0:T(8,128)(2,1)} collective-permute-done((bf16[64,2048]{1,0:T(8,128)(2,1)S(1)}, bf16[64,2048]{1,0:T(8,128)(2,1)}, u32[]{:S(2)}, u32[]{:S(2)}) %collective-permute-start.5) | collective-permute-done | bytes 262176 | tf_op jit(solution)/shard_map/ppermute | solution.py:115
  63.4 3.6 %collective-permute-done.8.refs_3_ = bf16[2,64,2048]{2,1,0:T(8,128)(2,1)} collective-permute-done((bf16[2,64,2048]{2,1,0:T(8,128)(2,1)}, bf16[2,64,2048]{2,1,0:T(8,128)(2,1)}, u32[]{:S(2)}, u32[]{:S(2)}) %collective-permute-start.8) | collective-permute-done | bytes 524320 | tf_op jit(solution)/shard_map/ppermute | solution.py:115
  77.3 5.1 %shard_map.159 = (bf16[512,512]{1,0:T(8,128)(2,1)}, bf16[512,2048]{1,0:T(8,128)(2,1)}) custom-call(s32[211]{0:T(256)} %concatenate.11.meta, bf16[512,2048]{1,0:T(8,128)(2,1)} %fusion.2.x, bf16[4,64,2048]{2,1,0:T(8,128)(2,1)} %copy-done.1, bf16[4,64,2048]{2,1,0:T(8,128)(2,1)} %collective-permute-done.3.refs_1_, ...), custom_call_target="tpu_custom_call" | custom-call | flops 1073741824 | bytes 7340032 | tf_op jit(solution)/shard_map/pallas_call | solution.py:171
  82.4 4.9 %shard_map.160 = (bf16[512,512]{1,0:T(8,128)(2,1)}, bf16[512,2048]{1,0:T(8,128)(2,1)}) custom-call(s32[211]{0:T(256)} %concatenate.11.meta, bf16[512,2048]{1,0:T(8,128)(2,1)} %broadcast_select_fusion.x, bf16[4,64,2048]{2,1,0:T(8,128)(2,1)} %copy-done.1, bf16[4,64,2048]{2,1,0:T(8,128)(2,1)} %collective-permute-done.3.refs_1_, ...), custom_call_target="tpu_custom_call" | custom-call | flops 1073741824 | bytes 7340032 | tf_op jit(solution)/shard_map/pallas_call | solution.py:171
  95.5 3.7 %collective-permute-done.20.refs_3_ = bf16[2,64,2048]{2,1,0:T(8,128)(2,1)S(1)} collective-permute-done((bf16[2,64,2048]{2,1,0:T(8,128)(2,1)S(1)}, bf16[2,64,2048]{2,1,0:T(8,128)(2,1)S(1)}, u32[]{:S(2)}, u32[]{:S(2)}) %collective-permute-start.20) | collective-permute-done | bytes 524320 | tf_op jit(solution)/shard_map/ppermute | solution.py:115
  99.9 7.9 %collective-permute-done.27.q_got = bf16[512,512]{1,0:T(8,128)(2,1)S(1)} collective-permute-done((bf16[512,512]{1,0:T(8,128)(2,1)S(1)}, bf16[512,512]{1,0:T(8,128)(2,1)S(1)}, u32[]{:S(2)}, u32[]{:S(2)}) %collective-permute-start.27) | collective-permute-done | bytes 524320 | tf_op jit(solution)/shard_map/ppermute | solution.py:543
  110.0 5.1 %shard_map.161 = (f32[512,512]{1,0:T(8,128)}, bf16[512,2048]{1,0:T(8,128)(2,1)}) custom-call(s32[211]{0:T(256)} %concatenate.11.meta, bf16[512,2048]{1,0:T(8,128)(2,1)} %fusion.2.x, bf16[4,64,2048]{2,1,0:T(8,128)(2,1)} %copy-done.1, bf16[4,64,2048]{2,1,0:T(8,128)(2,1)} %collective-permute-done.3.refs_1_, ...), custom_call_target="tpu_custom_call" | custom-call | flops 1073741824 | bytes 7340032 | tf_op jit(solution)/shard_map/pallas_call | solution.py:171
  115.2 5.0 %shard_map.162 = (bf16[512,512]{1,0:T(8,128)(2,1)}, bf16[512,2048]{1,0:T(8,128)(2,1)}) custom-call(s32[211]{0:T(256)} %concatenate.11.meta, bf16[512,2048]{1,0:T(8,128)(2,1)} %broadcast_select_fusion.x, bf16[4,64,2048]{2,1,0:T(8,128)(2,1)} %copy-done.1, bf16[4,64,2048]{2,1,0:T(8,128)(2,1)} %collective-permute-done.3.refs_1_, ...), custom_call_target="tpu_custom_call" | custom-call | flops 1073741824 | bytes 7340032 | tf_op jit(solution)/shard_map/pallas_call | solution.py:171
  124.7 4.7 %shard_map.164.probs = f32[4,512,192]{2,1,0:T(8,128)} custom-call(s32[211]{0:T(256)} %concatenate.11.meta, f32[512,512]{1,0:T(8,128)} %get-tuple-element.113.q_own, bf16[512,512]{1,0:T(8,128)(2,1)} %copy-done.4, bf16[768,1024]{1,0:T(8,128)(2,1)} %shard_map.163.keys.vals), custom_call_target="tpu_custom_call" | custom-call | flops 100663296 | bytes 6291456 | tf_op jit(solution)/shard_map/pallas_call | solution.py:250
  129.4 6.3 %shard_map.165 = (bf16[528,512]{1,0:T(8,128)(2,1)}, bf16[4,192,1024]{2,1,0:T(8,128)(2,1)}) custom-call(s32[211]{0:T(256)} %concatenate.11.meta, f32[1]{0:T(128)S(6)} %tanh.3.gate, f32[512,512]{1,0:T(8,128)} %get-tuple-element.113.q_own, bf16[512,512]{1,0:T(8,128)(2,1)} %copy-done.4, bf16[512,512]{1,0:T(8,128)(2,1)} %get-tuple-element.115.o_own, ...), custom_call_target="tpu_custom_call" | custom-call | flops 402653184 | bytes 8388608 | tf_op jit(solution)/shard_map/pallas_call | solution.py:302
  138.5 6.3 %shard_map.166 = (f32[192,1536]{1,0:T(8,128)}, bf16[192,1536]{1,0:T(8,128)(2,1)}, bf16[192,1536]{1,0:T(8,128)(2,1)}, bf16[192,1536]{1,0:T(8,128)(2,1)}) custom-call(bf16[4,192,1024]{2,1,0:T(8,128)(2,1)} %get-tuple-element.127.dkv, bf16[1536,512]{1,0:T(8,128)(2,1)} %bitcast.98, bf16[1536,512]{1,0:T(8,128)(2,1)} %bitcast.101), custom_call_target="tpu_custom_call" | custom-call | flops 2415919104 | bytes 8388608 | tf_op jit(solution)/shard_map/pallas_call | solution.py:441
  144.8 9.5 %collective-permute-done.29.refs_0_ = bf16[528,512]{1,0:T(8,128)(2,1)S(1)} collective-permute-done((bf16[528,512]{1,0:T(8,128)(2,1)}, bf16[528,512]{1,0:T(8,128)(2,1)S(1)}, u32[]{:S(2)}, u32[]{:S(2)}) %collective-permute-start.29) | collective-permute-done | bytes 540704 | tf_op jit(solution)/shard_map/ppermute | solution.py:558
  156.6 8.6 %shard_map.167 = (bf16[512,2048]{1,0:T(8,128)(2,1)}, bf16[512,512]{1,0:T(8,128)(2,1)}) custom-call(s32[211]{0:T(256)} %concatenate.11.meta, f32[1,512]{1,0:T(1,128)} %slice.24.rinv, f32[1,2048]{1,0:T(1,128)} %slice.25.gain, bf16[528,512]{1,0:T(8,128)(2,1)} %copy-done.14, bf16[528,512]{1,0:T(8,128)(2,1)} %copy-done.15, bf16[512,2048]{1,0:T(8,128)(2,1)} %refs_2_.1, ...), custom_call_target="tpu_custom_call" | custom-call | flops 3221225472 | bytes 12582912 | tf_op jit(solution)/shard_map/pallas_call | solution.py:410
  165.3 3.7 %collective-permute-start.31 = (bf16[512,512]{1,0:T(8,128)(2,1)}, bf16[512,512]{1,0:T(8,128)(2,1)S(1)}, u32[]{:S(2)}, u32[]{:S(2)}) collective-permute-start(bf16[512,512]{1,0:T(8,128)(2,1)} %get-tuple-element.140), channel_id=1, source_target_pairs={{0,1},{1,0},{2,3},{3,2},{4,5},{5,4},{6,7},{7,6},{8,9},{9,8},{10,11... | collective-permute-start | bytes 1572872 | tf_op jit(solution)/shard_map/ppermute | solution.py:562
  172.3 4.3 %convolution_convert_fusion.o_own = bf16[512,512]{1,0:T(8,128)(2,1)} fusion(bf16[512,2048]{1,0:T(8,128)(2,1)} %get-tuple-element.142.refs_4_, bf16[512,2048]{1,0:T(8,128)(2,1)} %get-tuple-element.143), kind=kOutput, calls=%fused_computation.6 | convolution fusion | flops 1074003968 | bytes 4718592 | tf_op jit(solution)/shard_map/dot_general | solution.py:51
  176.6 4.5 %collective-permute-done.31.o_got = bf16[512,512]{1,0:T(8,128)(2,1)S(1)} collective-permute-done((bf16[512,512]{1,0:T(8,128)(2,1)}, bf16[512,512]{1,0:T(8,128)(2,1)S(1)}, u32[]{:S(2)}, u32[]{:S(2)}) %collective-permute-start.31) | collective-permute-done | bytes 524320 | tf_op jit(solution)/shard_map/ppermute | solution.py:562
  181.9 6.3 %shard_map.168 = (bf16[528,512]{1,0:T(8,128)(2,1)}, bf16[4,192,1024]{2,1,0:T(8,128)(2,1)}) custom-call(s32[211]{0:T(256)} %concatenate.11.meta, f32[1]{0:T(128)S(6)} %tanh.3.gate, f32[512,512]{1,0:T(8,128)} %get-tuple-element.113.q_own, bf16[512,512]{1,0:T(8,128)(2,1)} %copy-done.4, bf16[512,512]{1,0:T(8,128)(2,1)} %convolution_convert_fusion.o_own, ...), custom_call_target="tpu_custom_call" | custom-call | flops 402653184 | bytes 8388608 | tf_op jit(solution)/shard_map/pallas_call | solution.py:302
  188.2 3.9 %collective-permute-start.36 = (bf16[528,512]{1,0:T(8,128)(2,1)}, bf16[528,512]{1,0:T(8,128)(2,1)S(1)}, u32[]{:S(2)}, u32[]{:S(2)}) collective-permute-start(bf16[528,512]{1,0:T(8,128)(2,1)} %get-tuple-element.144.refs_1_), channel_id=1, source_target_pairs={{0,1},{1,0},{2,3},{3,2},{4,5},{5,4},{6,7},{7,6},{8,9},{9,8},{10,11... | collective-permute-start | bytes 1622024 | tf_op jit(solution)/shard_map/ppermute | solution.py:571
  192.8 6.1 %shard_map.169 = (f32[192,1536]{1,0:T(8,128)}, bf16[192,1536]{1,0:T(8,128)(2,1)}, bf16[192,1536]{1,0:T(8,128)(2,1)}, bf16[192,1536]{1,0:T(8,128)(2,1)}) custom-call(bf16[4,192,1024]{2,1,0:T(8,128)(2,1)} %get-tuple-element.145.dkv, bf16[1536,512]{1,0:T(8,128)(2,1)} %bitcast.99, bf16[1536,512]{1,0:T(8,128)(2,1)} %bitcast.102), custom_call_target="tpu_custom_call" | custom-call | flops 2415919104 | bytes 8388608 | tf_op jit(solution)/shard_map/pallas_call | solution.py:441
  198.9 6.3 %collective-permute-done.34 = bf16[192,1536]{1,0:T(8,128)(2,1)S(1)} collective-permute-done((bf16[192,1536]{1,0:T(8,128)(2,1)}, bf16[192,1536]{1,0:T(8,128)(2,1)S(1)}, u32[]{:S(2)}, u32[]{:S(2)}) %collective-permute-start.34) | collective-permute-done | bytes 589856 | tf_op jit(solution)/shard_map/ppermute | solution.py:567
  209.7 3.7 %collective-permute-start.39 = (bf16[192,1536]{1,0:T(8,128)(2,1)}, bf16[192,1536]{1,0:T(8,128)(2,1)}, u32[]{:S(2)}, u32[]{:S(2)}) collective-permute-start(bf16[192,1536]{1,0:T(8,128)(2,1)} %get-tuple-element.165), channel_id=1, source_target_pairs={{0,1},{1,0},{2,3},{3,2},{4,5},{5,4},{6,7},{7,6},{8,9},{9,8},{10,11... | collective-permute-start | bytes 1769480 | tf_op jit(solution)/shard_map/ppermute | solution.py:574
  214.4 7.6 %shard_map.170 = bf16[512,2048]{1,0:T(8,128)(2,1)} custom-call(s32[211]{0:T(256)} %concatenate.11.meta, f32[1,512]{1,0:T(1,128)} %bitcast.113, f32[1,2048]{1,0:T(1,128)} %gain.1, bf16[528,512]{1,0:T(8,128)(2,1)} %get-tuple-element.141.refs_0_, bf16[528,512]{1,0:T(8,128)(2,1)} %get-tuple-element.144.refs_1_, bf16[528,512]{1,0:T(8,128)(2,1)} %copy-done.13, ...), custom_call_target="tpu_custom_call" | custom-call | flops 2147483648 | bytes 12582912 | tf_op jit(solution)/shard_map/pallas_call | solution.py:410
  223.9 11.1 %collective-permute-done.39 = bf16[192,1536]{1,0:T(8,128)(2,1)} collective-permute-done((bf16[192,1536]{1,0:T(8,128)(2,1)}, bf16[192,1536]{1,0:T(8,128)(2,1)}, u32[]{:S(2)}, u32[]{:S(2)}) %collective-permute-start.39) | collective-permute-done | bytes 589856 | tf_op jit(solution)/shard_map/ppermute | solution.py:574
  (161 shorter events, 92.3 us)
Async XLA Ops:
  7.2 148.7 %all-gather.3.cloned.1.call-start = ((), (), s32[]{:S(2)}) async-start(), calls=%async_computation | async-start | bytes 6291456 | tf_op jit(solution)/shard_map/all_gather | solution.py:505
  7.9 147.9 %all-gather.5.cloned.1.call-start = ((), (), s32[]{:S(2)}) async-start(), calls=%async_computation.1 | async-start | bytes 4325376 | tf_op jit(solution)/shard_map/all_gather | solution.py:539
  20.1 22.6 %collective-permute-start.3 = (bf16[4,64,2048]{2,1,0:T(8,128)(2,1)S(1)}, bf16[4,64,2048]{2,1,0:T(8,128)(2,1)}, u32[]{:S(2)}, u32[]{:S(2)}) collective-permute-start(bf16[4,64,2048]{2,1,0:T(8,128)(2,1)S(1)} %pad_maximum_fusion.refs_0_), channel_id=1, source_target_pairs={{0,16},{2,6},{4,20},{6,10},{8,24},{10,14},{12,28},{14,2},{16,32},{... | collective-permute-start | bytes 3145736 | tf_op jit(solution)/shard_map/ppermute | solution.py:115
  22.1 20.6 %collective-permute-start.4 = (bf16[4,64,2048]{2,1,0:T(8,128)(2,1)S(1)}, bf16[4,64,2048]{2,1,0:T(8,128)(2,1)}, u32[]{:S(2)}, u32[]{:S(2)}) collective-permute-start(bf16[4,64,2048]{2,1,0:T(8,128)(2,1)S(1)} %pad_maximum_fusion.refs_0_), channel_id=1, source_target_pairs={{0,48},{2,14},{4,52},{6,2},{8,56},{10,6},{12,60},{14,10},{16,0},{1... | collective-permute-start | bytes 3145736 | tf_op jit(solution)/shard_map/ppermute | solution.py:115
  41.9 21.5 %collective-permute-start.10 = (bf16[4,64,2048]{2,1,0:T(8,128)(2,1)S(1)}, bf16[4,64,2048]{2,1,0:T(8,128)(2,1)}, u32[]{:S(2)}, u32[]{:S(2)}) collective-permute-start(bf16[4,64,2048]{2,1,0:T(8,128)(2,1)S(1)} %pad_maximum_fusion.refs_0_), channel_id=1, source_target_pairs={{0,2},{2,0},{1,3},{3,1},{4,6},{6,4},{5,7},{7,5},{8,10},{10,8},{9,1... | collective-permute-start | bytes 3145736 | tf_op jit(solution)/shard_map/ppermute | solution.py:119
  42.7 24.8 %collective-permute-start.11 = (bf16[4,64,2048]{2,1,0:T(8,128)(2,1)}, bf16[4,64,2048]{2,1,0:T(8,128)(2,1)}, u32[]{:S(2)}, u32[]{:S(2)}) collective-permute-start(bf16[4,64,2048]{2,1,0:T(8,128)(2,1)} %collective-permute-done.3.refs_1_), channel_id=1, source_target_pairs={{0,2},{2,0},{1,3},{3,1},{4,6},{6,4},{5,7},{7,5},{8,10},{10,8},{9,1... | collective-permute-start | bytes 3145736 | tf_op jit(solution)/shard_map/ppermute | solution.py:119
  42.7 24.8 %collective-permute-start.12 = (bf16[4,64,2048]{2,1,0:T(8,128)(2,1)}, bf16[4,64,2048]{2,1,0:T(8,128)(2,1)}, u32[]{:S(2)}, u32[]{:S(2)}) collective-permute-start(bf16[4,64,2048]{2,1,0:T(8,128)(2,1)} %collective-permute-done.4.refs_2_), channel_id=1, source_target_pairs={{0,2},{2,0},{1,3},{3,1},{4,6},{6,4},{5,7},{7,5},{8,10},{10,8},{9,1... | collective-permute-start | bytes 3145736 | tf_op jit(solution)/shard_map/ppermute | solution.py:119
  68.8 18.5 %collective-permute-start.16 = (bf16[4,64,2048]{2,1,0:T(8,128)(2,1)S(1)}, bf16[4,64,2048]{2,1,0:T(8,128)(2,1)S(1)}, u32[]{:S(2)}, u32[]{:S(2)}) collective-permute-start(bf16[4,64,2048]{2,1,0:T(8,128)(2,1)S(1)} %pad_maximum_fusion.1.refs_0_), channel_id=1, source_target_pairs={{0,16},{2,6},{4,20},{6,10},{8,24},{10,14},{12,28},{14,2},{16,32},{... | collective-permute-start | bytes 3145736 | tf_op jit(solution)/shard_map/ppermute | solution.py:115
  70.5 16.9 %collective-permute-start.17 = (bf16[4,64,2048]{2,1,0:T(8,128)(2,1)S(1)}, bf16[4,64,2048]{2,1,0:T(8,128)(2,1)}, u32[]{:S(2)}, u32[]{:S(2)}) collective-permute-start(bf16[4,64,2048]{2,1,0:T(8,128)(2,1)S(1)} %pad_maximum_fusion.1.refs_0_), channel_id=1, source_target_pairs={{0,48},{2,14},{4,52},{6,2},{8,56},{10,6},{12,60},{14,10},{16,0},{1... | collective-permute-start | bytes 3145736 | tf_op jit(solution)/shard_map/ppermute | solution.py:115
  72.1 20.3 %collective-permute-start.22 = (bf16[4,64,2048]{2,1,0:T(8,128)(2,1)S(1)}, bf16[4,64,2048]{2,1,0:T(8,128)(2,1)}, u32[]{:S(2)}, u32[]{:S(2)}) collective-permute-start(bf16[4,64,2048]{2,1,0:T(8,128)(2,1)S(1)} %pad_maximum_fusion.1.refs_0_), channel_id=1, source_target_pairs={{0,2},{2,0},{1,3},{3,1},{4,6},{6,4},{5,7},{7,5},{8,10},{10,8},{9,1... | collective-permute-start | bytes 3145736 | tf_op jit(solution)/shard_map/ppermute | solution.py:119
  91.9 28.3 %collective-permute-start.23 = (bf16[4,64,2048]{2,1,0:T(8,128)(2,1)S(1)}, bf16[4,64,2048]{2,1,0:T(8,128)(2,1)S(1)}, u32[]{:S(2)}, u32[]{:S(2)}) collective-permute-start(bf16[4,64,2048]{2,1,0:T(8,128)(2,1)S(1)} %collective-permute-done.16.refs_1_), channel_id=1, source_target_pairs={{0,2},{2,0},{1,3},{3,1},{4,6},{6,4},{5,7},{7,5},{8,10},{10,8},{9,1... | collective-permute-start | bytes 3145736 | tf_op jit(solution)/shard_map/ppermute | solution.py:119
  91.9 28.3 %collective-permute-start.24 = (bf16[4,64,2048]{2,1,0:T(8,128)(2,1)}, bf16[4,64,2048]{2,1,0:T(8,128)(2,1)}, u32[]{:S(2)}, u32[]{:S(2)}) collective-permute-start(bf16[4,64,2048]{2,1,0:T(8,128)(2,1)} %collective-permute-done.17.refs_2_), channel_id=1, source_target_pairs={{0,2},{2,0},{1,3},{3,1},{4,6},{6,4},{5,7},{7,5},{8,10},{10,8},{9,1... | collective-permute-start | bytes 3145736 | tf_op jit(solution)/shard_map/ppermute | solution.py:119
  99.1 21.0 %collective-permute-start.25 = (bf16[2,64,2048]{2,1,0:T(8,128)(2,1)S(1)}, bf16[2,64,2048]{2,1,0:T(8,128)(2,1)S(1)}, u32[]{:S(2)}, u32[]{:S(2)}) collective-permute-start(bf16[2,64,2048]{2,1,0:T(8,128)(2,1)S(1)} %collective-permute-done.20.refs_3_), channel_id=1, source_target_pairs={{0,2},{2,0},{1,3},{3,1},{4,6},{6,4},{5,7},{7,5},{8,10},{10,8},{9,1... | collective-permute-start | bytes 1572872 | tf_op jit(solution)/shard_map/ppermute | solution.py:119
  99.9 20.3 %collective-permute-start.26 = (bf16[2,64,2048]{2,1,0:T(8,128)(2,1)}, bf16[2,64,2048]{2,1,0:T(8,128)(2,1)}, u32[]{:S(2)}, u32[]{:S(2)}) collective-permute-start(bf16[2,64,2048]{2,1,0:T(8,128)(2,1)} %collective-permute-done.21.refs_4_), channel_id=1, source_target_pairs={{0,2},{2,0},{1,3},{3,1},{4,6},{6,4},{5,7},{7,5},{8,10},{10,8},{9,1... | collective-permute-start | bytes 1572872 | tf_op jit(solution)/shard_map/ppermute | solution.py:119
  107.8 21.6 %collective-permute-start.28 = (bf16[512,512]{1,0:T(8,128)(2,1)}, bf16[512,512]{1,0:T(8,128)(2,1)}, u32[]{:S(2)}, u32[]{:S(2)}) collective-permute-start(bf16[512,512]{1,0:T(8,128)(2,1)} %get-tuple-element.106), channel_id=1, source_target_pairs={{64,65},{65,64},{66,67},{67,66},{68,69},{69,68},{70,71},{71,70},{7... | collective-permute-start | bytes 1572872 | tf_op jit(solution)/shard_map/ppermute | solution.py:546
  135.7 18.6 %collective-permute-start.29 = (bf16[528,512]{1,0:T(8,128)(2,1)}, bf16[528,512]{1,0:T(8,128)(2,1)S(1)}, u32[]{:S(2)}, u32[]{:S(2)}) collective-permute-start(bf16[528,512]{1,0:T(8,128)(2,1)} %get-tuple-element.141.refs_0_), channel_id=1, source_target_pairs={{64,0},{65,1},{66,2},{67,3},{68,4},{69,5},{70,6},{71,7},{72,8},{73... | collective-permute-start | bytes 1622024 | tf_op jit(solution)/shard_map/ppermute | solution.py:558
  137.0 18.8 %collective-permute-start.30 = (bf16[528,512]{1,0:T(8,128)(2,1)}, bf16[528,512]{1,0:T(8,128)(2,1)S(1)}, u32[]{:S(2)}, u32[]{:S(2)}) collective-permute-start(bf16[528,512]{1,0:T(8,128)(2,1)} %get-tuple-element.141.refs_0_), channel_id=1, source_target_pairs={{64,1},{65,0},{66,3},{67,2},{68,5},{69,4},{70,7},{71,6},{72,9},{73... | collective-permute-start | bytes 1622024 | tf_op jit(solution)/shard_map/ppermute | solution.py:558
  169.0 29.9 %collective-permute-start.33 = (bf16[192,1536]{1,0:T(8,128)(2,1)}, bf16[192,1536]{1,0:T(8,128)(2,1)S(1)}, u32[]{:S(2)}, u32[]{:S(2)}) collective-permute-start(bf16[192,1536]{1,0:T(8,128)(2,1)} %get-tuple-element.149), channel_id=1, source_target_pairs={{64,0},{65,1},{66,2},{67,3},{68,4},{69,5},{70,6},{71,7},{72,8},{73... | collective-permute-start | bytes 1769480 | tf_op jit(solution)/shard_map/ppermute | solution.py:567
  170.3 34.9 %collective-permute-start.34 = (bf16[192,1536]{1,0:T(8,128)(2,1)}, bf16[192,1536]{1,0:T(8,128)(2,1)S(1)}, u32[]{:S(2)}, u32[]{:S(2)}) collective-permute-start(bf16[192,1536]{1,0:T(8,128)(2,1)} %get-tuple-element.150), channel_id=1, source_target_pairs={{64,1},{65,0},{66,3},{67,2},{68,5},{69,4},{70,7},{71,6},{72,9},{73... | collective-permute-start | bytes 1769480 | tf_op jit(solution)/shard_map/ppermute | solution.py:567
  171.6 33.6 %collective-permute-start.35 = (bf16[192,1536]{1,0:T(8,128)(2,1)}, bf16[192,1536]{1,0:T(8,128)(2,1)S(1)}, u32[]{:S(2)}, u32[]{:S(2)}) collective-permute-start(bf16[192,1536]{1,0:T(8,128)(2,1)} %get-tuple-element.151), channel_id=1, source_target_pairs={{64,65},{65,64},{66,67},{67,66},{68,69},{69,68},{70,71},{71,70},{7... | collective-permute-start | bytes 1769480 | tf_op jit(solution)/shard_map/ppermute | solution.py:567
  188.2 25.2 %collective-permute-start.36 = (bf16[528,512]{1,0:T(8,128)(2,1)}, bf16[528,512]{1,0:T(8,128)(2,1)S(1)}, u32[]{:S(2)}, u32[]{:S(2)}) collective-permute-start(bf16[528,512]{1,0:T(8,128)(2,1)} %get-tuple-element.144.refs_1_), channel_id=1, source_target_pairs={{0,1},{1,0},{2,3},{3,2},{4,5},{5,4},{6,7},{7,6},{8,9},{9,8},{10,11... | collective-permute-start | bytes 1622024 | tf_op jit(solution)/shard_map/ppermute | solution.py:571
  192.1 21.3 %collective-permute-start.32 = (bf16[528,512]{1,0:T(8,128)(2,1)S(1)}, bf16[528,512]{1,0:T(8,128)(2,1)S(1)}, u32[]{:S(2)}, u32[]{:S(2)}) collective-permute-start(bf16[528,512]{1,0:T(8,128)(2,1)S(1)} %copy-done.11), channel_id=1, source_target_pairs={{64,65},{65,64},{66,67},{67,66},{68,69},{69,68},{70,71},{71,70},{7... | collective-permute-start | bytes 1622024 | tf_op jit(solution)/shard_map/ppermute | solution.py:565
  205.2 18.6 %collective-permute-start.37 = (bf16[192,1536]{1,0:T(8,128)(2,1)}, bf16[192,1536]{1,0:T(8,128)(2,1)}, u32[]{:S(2)}, u32[]{:S(2)}) collective-permute-start(bf16[192,1536]{1,0:T(8,128)(2,1)} %get-tuple-element.163), channel_id=1, source_target_pairs={{0,64},{1,65},{2,66},{3,67},{4,68},{5,69},{6,70},{7,71},{8,72},{9,... | collective-permute-start | bytes 1769480 | tf_op jit(solution)/shard_map/ppermute | solution.py:574
  209.7 25.3 %collective-permute-start.39 = (bf16[192,1536]{1,0:T(8,128)(2,1)}, bf16[192,1536]{1,0:T(8,128)(2,1)}, u32[]{:S(2)}, u32[]{:S(2)}) collective-permute-start(bf16[192,1536]{1,0:T(8,128)(2,1)} %get-tuple-element.165), channel_id=1, source_target_pairs={{0,1},{1,0},{2,3},{3,2},{4,5},{5,4},{6,7},{7,6},{8,9},{9,8},{10,11... | collective-permute-start | bytes 1769480 | tf_op jit(solution)/shard_map/ppermute | solution.py:574
  (46 other events, 414.3 us)
Sparse Core Ops, SparseCore 0:
  9.7 64.8 all-gather.2
  76.9 47.7 all-gather.4

commit v7 on v5

--- a/solution.py
+++ b/solution.py
@@ -21,7 +21,7 @@
 X = ("segment", "mp")
 BF = jnp.bfloat16
 F32 = jnp.float32
-LIMIT = 60 * 1024 * 1024
+LIMIT = 64 * 1024 * 1024
 NT = (((1,), (1,)), ((), ()))
 NN = (((1,), (0,)), ((), ()))
 TN = (((0,), (0,)), ((), ()))
@@ -63,8 +63,8 @@
 ANY = pl.BlockSpec(memory_space=pl.ANY)
 VMEM = pl.BlockSpec(memory_space=pltpu.VMEM)
 TILE = 512
+SMALL = pl.CostEstimate(flops=1, bytes_accessed=1, transcendentals=0)
 ROWS, SLOT, INFO, LENGTHS, PATTERN, PICKS = 0, 32, 36, 39, 43, 139
-ARRAYS = ((0, (0, 1, 2, 3)), (1, (0, 1, 2, 3)), (3, (0, 1, 2, 3)), (2, (0, 1)), (2, (2, 3)))
 
 
 def block_kernel(counts, tiles, queries, w_out, w_query, w_key, w_value, out, w_v, latents, sems):
@@ -110,26 +110,27 @@
             pltpu.SemaphoreType.DMA((2,)),
         ],
         compiler_params=params(),
+        cost_estimate=SMALL,
     )(counts, tiles, queries, w_out, w_query, w_key, w_value)
 
 
-def gather_chips(block):
-    first = [lax.ppermute(block, DP, yz_perm(1, k)) for k in (1, 2, 3)]
-    bundle = jnp.stack([block, *first])
-    one = lax.ppermute(bundle, DP, yz_perm(2, 1))
-    three = lax.ppermute(bundle, DP, yz_perm(2, 3))
-    two = lax.ppermute(one[:2], DP, yz_perm(2, 1)), lax.ppermute(three[2:], DP, yz_perm(2, 3))
-    return [bundle, one, three, *two]
+def over_dp(array, stage, k):
+    return lax.ppermute(array, DP, yz_perm(stage, k))
+
+
+def over_core(arrays):
+    return [lax.ppermute(a, "core", [(0, 1), (1, 0)]) for a in arrays]
 
 
 def places(z, y, core):
     table = []
-    for c in (core, 1 - core):
-        for j, blocks in ARRAYS:
-            for k in blocks:
-                at_z = lax.rem(z - jnp.where(c == 0, j, k) + 4, 4)
-                at_y = lax.rem(y - jnp.where(c == 0, k, j) + 4, 4)
-                table.append((at_z * 4 + at_y) * 2 + c)
+    for a in range(8):
+        c = core if a < 4 else 1 - core
+        for k in range(4):
+            j = a % 4
+            at_z = lax.rem(z - jnp.where(c == 0, j, k) + 4, 4)
+            at_y = lax.rem(y - jnp.where(c == 0, k, j) + 4, 4)
+            table.append((at_z * 4 + at_y) * 2 + c)
     return jnp.stack(table).astype(jnp.int32)
 
 
@@ -143,69 +144,81 @@
     return jnp.concatenate([p.astype(F32) for p in parts], axis=0) > 0
 
 
-def project_kernel(kind, part, meta, x, *refs):
-    ins, (out, weight), (w_v, x_v, sems) = refs[:10], refs[10:12], refs[12:]
-    load = pltpu.make_async_copy(x, x_v, sems.at[1])
-    load.start()
-    half = w_v.shape[0]
-    index = 0
-    for a in range(10):
-        for k in range(len(ARRAYS[a % 5][1])):
-            at = pl.multiple_of(meta[ROWS + index] - part * half, 32)
-            index += 1
-
-            @pl.when((at >= 0) & (at < half))
-            def _():
-                pltpu.make_async_copy(
-                    ins[a].at[k, pl.ds(kind * 32, 32)], w_v.at[pl.ds(at, 32)], sems.at[0]
-                ).start()
-
-    load.wait()
-    pltpu.make_async_copy(w_v, w_v, sems.at[0]).wait()
-    store = pltpu.make_async_copy(w_v, weight, sems.at[0])
-    store.start()
-    out[...] = dot(x_v[...], w_v[...], NT).astype(out.dtype)
-    store.wait()
-
-
-def project(kind, part, dtype, meta, x, blocks):
-    tokens, width = x.shape
+def project_kernel(part, meta, normed, upstream, *refs):
+    ins, outs, weights, (w_v, x_v, sems) = refs[:16], refs[16:18], refs[18:20], refs[20:]
+    half = w_v.shape[1]
+
+    def load(i, x):
+        pltpu.make_async_copy(x, x_v.at[i], sems.at[2 * i]).start()
+        for a in range(16):
+            for k in range(2):
+                at = pl.multiple_of(meta[ROWS + a * 2 + k] - part * half, 32)
+
+                @pl.when((at >= 0) & (at < half))
+                def _():
+                    pltpu.make_async_copy(
+                        ins[a].at[k, pl.ds((1 - i) * 32, 32)],
+                        w_v.at[i, pl.ds(at, 32)],
+                        sems.at[2 * i + 1],
+                    ).start()
+
+    load(0, normed)
+    stores = []
+    for i in range(2):
+        pltpu.make_async_copy(x_v.at[i], x_v.at[i], sems.at[2 * i]).wait()
+        pltpu.make_async_copy(w_v.at[i], w_v.at[i], sems.at[2 * i + 1]).wait()
+        if i == 0:
+            load(1, upstream)
+        stores.append(pltpu.make_async_copy(w_v.at[i], weights[i], sems.at[2 * i + 1]))
+        stores[i].start()
+        outs[i][...] = dot(x_v[i], w_v[i], NT).astype(outs[i].dtype)
+    for store in stores:
+        store.wait()
+
+
+def project(part, dtype, meta, normed, upstream, blocks):
+    tokens, width = normed.shape
     half = 512
     return pl.pallas_call(
-        functools.partial(project_kernel, kind, part),
-        in_specs=[SMEM, ANY] + [ANY] * 10,
-        out_specs=[VMEM, ANY],
+        functools.partial(project_kernel, part),
+        in_specs=[SMEM] + [ANY] * 18,
+        out_specs=[VMEM, VMEM, ANY, ANY],
         out_shape=[
             jax.ShapeDtypeStruct((tokens, half), dtype),
+            jax.ShapeDtypeStruct((tokens, half), BF),
+            jax.ShapeDtypeStruct((half, width), BF),
             jax.ShapeDtypeStruct((half, width), BF),
         ],
         scratch_shapes=[
-            pltpu.VMEM((half, width), BF),
-            pltpu.VMEM((tokens, width), BF),
-            pltpu.SemaphoreType.DMA((2,)),
+            pltpu.VMEM((2, half, width), BF),
+            pltpu.VMEM((2, tokens, width), BF),
+            pltpu.SemaphoreType.DMA((4,)),
         ],
         compiler_params=params(),
-        cost_estimate=pl.CostEstimate(
-            flops=2 * tokens * width * half, bytes_accessed=7 << 20, transcendentals=0
-        ),
-    )(meta, x, *blocks)
+        cost_estimate=SMALL,
+    )(meta, normed, upstream, *blocks)
 
 
 def select_kernel(wanted, meta, *refs):
-    ins, out, sems = refs[:10], refs[10], refs[11]
+    ins, out, sems = refs[:16], refs[16], refs[17]
     width = out.shape[1]
     for i in range(wanted):
+        array = meta[PICKS + i]
         block = meta[PICKS + wanted + i]
         slide = meta[PICKS + 2 * wanted + i]
         rows = pl.ds(pl.multiple_of(64 + slide // 2 * LAT, LAT), LAT)
         cols = pl.ds(pl.multiple_of(slide % 2 * width, width), width)
-        for a in range(10):
-
-            @pl.when(meta[PICKS + i] == a)
+        for group in range(4):
+
+            @pl.when(array // 4 == group)
             def _():
-                pltpu.make_async_copy(
-                    ins[a].at[block, rows, cols], out.at[pl.ds(i * LAT, LAT)], sems.at[0]
-                ).start()
+                for a in range(group * 4, group * 4 + 4):
+
+                    @pl.when(array == a)
+                    def _():
+                        pltpu.make_async_copy(
+                            ins[a].at[block, rows, cols], out.at[pl.ds(i * LAT, LAT)], sems.at[0]
+                        ).start()
 
     pltpu.make_async_copy(out, out, sems.at[0]).wait()
 
@@ -213,18 +226,18 @@
 def select(wanted, meta, blocks):
     return pl.pallas_call(
         functools.partial(select_kernel, wanted),
-        in_specs=[SMEM] + [ANY] * 10,
+        in_specs=[SMEM] + [ANY] * 16,
         out_specs=VMEM,
         out_shape=jax.ShapeDtypeStruct((wanted * LAT, 1024), BF),
         scratch_shapes=[pltpu.SemaphoreType.DMA((1,))],
         compiler_params=params(),
-        cost_estimate=pl.CostEstimate(flops=0, bytes_accessed=3 << 20, transcendentals=0),
+        cost_estimate=SMALL,
     )(meta, *blocks)
 
 
-def forward_kernel(meta, q_own, q_got, keys, probs):
+def forward_kernel(meta, q_own, q_got, kv, probs):
     report = pl.program_id(0)
-    span = keys.shape[0]
+    span = kv.shape[0]
     slide = lax.broadcasted_iota(jnp.int32, (QBLK, span), 1) // LAT
     masks = []
     for block in range(L // QBLK):
@@ -236,7 +249,7 @@
     mask = jnp.concatenate(masks, axis=0) == 1
     heads = [slice(head * HEAD, (head + 1) * HEAD) for head in range(probs.shape[0])]
     qb = [(q_own[:, c] + q_got[:, c].astype(F32)).astype(BF) for c in heads]
-    scores = [dot(q, keys[:, c], NT) * SCALE for q, c in zip(qb, heads)]
+    scores = [dot(q, kv[:, c], NT) * SCALE for q, c in zip(qb, heads)]
     scores = [jnp.where(mask, s, -1e30) for s in scores]
     exps = [jnp.exp(s - jnp.max(s, axis=1, keepdims=True)) for s in scores]
     totals = [jnp.sum(e, axis=1, keepdims=True) for e in exps]
@@ -257,9 +270,7 @@
         out_specs=pl.BlockSpec((heads, L, span), lambda i: (0, i, 0)),
         out_shape=jax.ShapeDtypeStruct((heads, tokens, span), F32),
         compiler_params=params(),
-        cost_estimate=pl.CostEstimate(
-            flops=2 * tokens * span * local, bytes_accessed=6 << 20, transcendentals=tokens * span * 4
-        ),
+        cost_estimate=SMALL,
     )(meta, q_own, q_got, kv)
 
 
@@ -317,9 +328,7 @@
             jax.ShapeDtypeStruct((4, reports * 48, 2 * local), BF),
         ],
         compiler_params=params(),
-        cost_estimate=pl.CostEstimate(
-            flops=8 * tokens * span * local, bytes_accessed=8 << 20, transcendentals=0
-        ),
+        cost_estimate=SMALL,
     )(meta, gate, q_own, q_got, o_own, o_got, kv, kv, probs)
 
 
@@ -417,38 +426,41 @@
         out_shape=out_shape,
         scratch_shapes=scratch + [pltpu.SemaphoreType.DMA((width // TILE * 4 + 1,))],
         compiler_params=params(),
-        cost_estimate=pl.CostEstimate(
-            flops=(3 if wo is not None else 2) * tokens * width * inner,
-            bytes_accessed=12 << 20,
-            transcendentals=0,
-        ),
+        cost_estimate=SMALL,
     )(*inputs)
 
 
-def term_kernel(dkv, w_kv, own, *terms):
+def term_kernel(groups, dkv, w_key, w_value, added, own, *terms):
     rows = own.shape[0]
-    value = dot(dkv[...].reshape(4 * rows, dkv.shape[2]), w_kv[...], NT)
+    both = dkv[...].reshape(4 * rows, dkv.shape[2])
+    half = w_key.shape[1]
+    value = dot(both[:, :half], w_key[...], NT) + dot(both[:, half:], w_value[...], NT)
     own[...] = value[:rows]
-    for k, term in enumerate(terms, 1):
-        term[...] = value[k * rows : (k + 1) * rows].astype(BF)
-
-
-def latent_terms(dkv, w_kv):
+    for group, term in zip(groups, terms):
+        for i, k in enumerate(group):
+            part = value[k * rows : (k + 1) * rows]
+            if k == 2:
+                part += added[...].astype(F32)
+            term[i * rows : (i + 1) * rows] = part.astype(BF)
+
+
+def latent_terms(groups, dkv, w_key, w_value, added):
     rows, inner = dkv.shape[1:]
-    features = w_kv.shape[0]
-    tile = features // 6
-    result = pl.BlockSpec((rows, tile), lambda i: (0, i))
+    features = w_key.shape[0]
+    tile = features // 3
+    weight = pl.BlockSpec((tile, w_key.shape[1]), lambda i: (i, 0))
+    sizes = [rows] + [rows * len(group) for group in groups]
     return pl.pallas_call(
-        term_kernel,
+        functools.partial(term_kernel, groups),
         grid=(features // tile,),
-        in_specs=[whole(dkv.shape), pl.BlockSpec((tile, inner), lambda i: (i, 0))],
-        out_specs=[result] * 4,
-        out_shape=[jax.ShapeDtypeStruct((rows, features), t) for t in (F32, BF, BF, BF)],
+        in_specs=[whole(dkv.shape), weight, weight, pl.BlockSpec((rows, tile), lambda i: (0, i))],
+        out_specs=[pl.BlockSpec((n, tile), lambda i: (0, i)) for n in sizes],
+        out_shape=[
+            jax.ShapeDtypeStruct((n, features), BF if i else F32) for i, n in enumerate(sizes)
+        ],
         compiler_params=params(),
-        cost_estimate=pl.CostEstimate(
-            flops=8 * rows * inner * features, bytes_accessed=8 << 20, transcendentals=0
-        ),
-    )(dkv, w_kv)
+        cost_estimate=SMALL,
+    )(dkv, w_key, w_value, added)
 
 
 def per_device(
@@ -494,22 +506,14 @@
     far_y = lax.rem(y - source // 2 % 4 + 4, 4)
     first = jnp.where(source_core == 0, far_y, far_z)
     second = jnp.where(source_core == 0, far_z, far_y)
-    array = jnp.where(second < 2, second, jnp.where(second == 3, 2, jnp.where(first < 2, 3, 4)))
-    array = array + jnp.where(source_core == core, 0, 5)
-    block = jnp.where(second == 2, first % 2, first)
+    array = 2 * second + first // 2 + jnp.where(source_core == core, 0, 8)
+    first = first % 2
     meta = jnp.concatenate(
         [rows, jnp.stack(slot + info).astype(jnp.int32), report_lengths]
-        + [cross_pattern.reshape(-1), array, block, slide]
+        + [cross_pattern.reshape(-1), array, first, slide]
     )
 
-    h_all = lax.all_gather(h, "segment")
-
-    wq_t = w_query[0].T
-    blocks = gather_chips(
-        make_block(
-            tile_counts.reshape(4), tiles, lat_query, w_out[0], wq_t, w_key[0], w_value[0]
-        )
-    )
+    h_all = lax.all_gather(segment_inputs, "segment", axis=0, tiled=True)
 
     h32 = h.astype(F32)
     partial = jnp.sum(h32 * h32, axis=1)
@@ -524,41 +528,54 @@
     up1 = jnp.where(live[:, None], cotangent, jnp.zeros((), BF))
     rinv = rinv[None]
     gate = jnp.tanh(attn_gate)
-    w_kv = jnp.concatenate([w_key[0], w_value[0]], axis=1)
-    wq_t, _ = lax.optimization_barrier((wq_t, squares))
+    wq_t = w_query[0].T
+    block = make_block(
+        tile_counts.reshape(4), tiles, lat_query, w_out[0], wq_t, w_key[0], w_value[0]
+    )
+    parts = [over_dp(block, 1, k) for k in (1, 2, 3)]
+    low, high = jnp.stack([block, parts[0]]), jnp.stack(parts[1:])
+    low1, high3 = over_dp(low, 2, 1), over_dp(high, 2, 3)
+    high1, low3 = over_dp(high, 2, 1), over_dp(low, 2, 3)
+    low2, high2 = over_dp(low1, 2, 1), over_dp(high3, 2, 3)
+    mine = [low, high, low1, high1, low3, high3]
+    others = over_core(mine)
+    last2, mine, others, normed, up1, rinv1, gain1, meta = lax.optimization_barrier(
+        ([low2, high2], mine, others, normed, up1, rinv1, gain1, meta)
+    )
+    others = others[:4] + over_core(last2) + others[4:]
+    blocks = mine[:4] + last2 + mine[4:] + others
+    wq_t, _ = lax.optimization_barrier((wq_t, last2))
     wq1 = lax.ppermute(wq_t, "segment", [(1, 0)])
-    swap = [(0, 1), (1, 0)]
-    others = [lax.ppermute(b, "core", swap) for b in blocks[:3]]
-    blocks, others, normed, up1, rinv1, gain1, meta, w_kv, wq1 = lax.optimization_barrier(
-        (blocks, others, normed, up1, rinv1, gain1, meta, w_kv, wq1)
-    )
+
+    q_send, o_send, wq_got, wo_got = project(1, BF, meta, normed, up1, blocks)
+    q_got = lax.ppermute(q_send, X, SWAP_MP)
+    o_got = lax.ppermute(o_send, X, LAST_SWAP)
+    meta, wq1, o_send = lax.optimization_barrier((meta, wq1, o_send))
     wq1 = lax.all_gather(wq1, DP, axis=0, tiled=True)
-    blocks = blocks + others + [lax.ppermute(b, "core", swap) for b in blocks[3:]]
-
-    q_send, wq_got = project(1, 1, BF, meta, normed, blocks)
-    q_got = lax.ppermute(q_send, X, SWAP_MP)
-    o_send, wo_got = project(0, 1, BF, meta, up1, blocks)
-    o_got = lax.ppermute(o_send, X, LAST_SWAP)
-    q_own, wq_own = project(1, 0, F32, meta, normed, blocks)
-    o_own, wo_own = project(0, 0, BF, meta, up1, blocks)
     kv = select(wanted, meta, blocks)
+    normed, kv = lax.optimization_barrier((normed, kv))
+    q_own, o_own, wq_own, wo_own = project(0, F32, meta, normed, up1, blocks)
     probs = forward(meta, q_own, q_got, kv)
     dq1, dkv1 = backward(meta, gate, q_own, q_got, o_own, o_got, kv, probs)
     dqs = [lax.ppermute(dq1, X, LAST_TO_SAME), lax.ppermute(dq1, X, LAST_TO_CROSS)]
-    own1, *terms = latent_terms(dkv1, w_kv)
+    own1, *terms = latent_terms(
+        ((1, 3), (2,)), dkv1, w_key[0], w_value[0], jnp.zeros((192, E), BF)
+    )
     dqs, terms = lax.optimization_barrier((dqs, terms))
     up, o_send = back(meta, rinv1, gain1, dqs, cotangent, h_all, [wq1], wo_got)
     o_got = lax.ppermute(o_send, X, FIRST_SWAP)
     o_own = dot(up, wo_own, NT).astype(BF)
-    dq1, terms, _ = lax.optimization_barrier((dq1, terms, o_send))
-    got1 = lax.ppermute(dq1, X, LAST_SWAP)
-    moves = (LAST_TO_SAME, LAST_TO_CROSS, LAST_SWAP)
-    got = [lax.ppermute(t, X, p) for t, p in zip(terms, moves)]
+    dq_cross, o_own = lax.optimization_barrier((dqs[1], o_own))
+    got1 = lax.ppermute(dq_cross, X, FIRST_TO_SAME)
+    pair = lax.ppermute(terms[0], X, LAST_TO_SAME)
+    got = [pair[:192], lax.ppermute(terms[1], X, LAST_TO_CROSS)]
+    relayed = pair[192:]
+    o_got, got, relayed = lax.optimization_barrier((o_got, got, relayed))
 
     dq0, dkv0 = backward(meta, gate, q_own, q_got, o_own, o_got, kv, probs)
-    own0, *terms = latent_terms(dkv0, w_kv)
+    dkv0, got1 = lax.optimization_barrier((dkv0, got1))
+    own0, *terms = latent_terms(((1,), (2,), (3,)), dkv0, w_key[0], w_value[0], relayed)
     got0 = lax.ppermute(dq0, X, FIRST_SWAP)
-    terms, got = lax.optimization_barrier((terms, got))
     moves = (FIRST_TO_SAME, FIRST_TO_CROSS, FIRST_SWAP)
     late = [lax.ppermute(t, X, p) for t, p in zip(terms, moves)]
     got, got0 = lax.optimization_barrier((got, got0))

time: 249 us -> 239 us (0.960)
  starting transfers between devices: 43.3 us -> 53.4 us
  Pallas kernels: 76.2 us -> 70.4 us
  other arithmetic: 17 us -> 11.5 us
  local copies, waits for them, and re-layouts: 12.4 us -> 7.56 us
  waiting for transfers between devices: 78.9 us -> 75.8 us
    ppermute x16 -> x20, waiting for transfers between devices: 50.4 us -> 34.4 us  [the longest x9 32.6 us: over_dp(): return lax.ppermute(array, DP, yz_perm(stage, k))]
    ppermute x1, waiting for transfers between devices: 6.2 us -> 13.5 us  [per_device(): lax.ppermute(dq1, X, LAST_TO_SAME)]
    all_gather x1, waiting for transfers between devices: 0.01 us -> 6.01 us  [per_device(): wq1 = lax.all_gather(wq1, DP, axis=0, tiled=True)]
    pallas_call x6 -> x4, Pallas kernels: 34.6 us -> 28.8 us  [the longest x2 16.2 us: project(): pl.pallas_call(functools.partial(project_kernel, part), in_specs=[SMEM] +...]
    concatenate x1 -> x0, other arithmetic: 3.94 us -> none  [per_device(): w_kv = jnp.concatenate([w_key[0], w_value[0]], axis=1)]
    ppermute x16 -> x20, starting transfers between devices: 17.4 us -> 21.1 us  [the longest x9 14.9 us: over_dp(): return lax.ppermute(array, DP, yz_perm(stage, k))]
    unnamed x48 -> x32, local copies, waits for them, and re-layouts: 5.46 us -> 2.08 us
  transfers between devices with their start and end apart: 30 -> 34, of which waited for: 13 -> 16; matrix products, arithmetic and copies ran while one was open for 10% -> 8% of each run, Pallas kernels for 26% -> 28%
where the time goes in v7:
time: 239 us; the launch traced here: 238 us
  waiting for transfers between devices  75.8 us (32%)
  Pallas kernels  70.4 us (29%)
  starting transfers between devices  53.4 us (22%)
  between operations  15.1 us (6%)
  other arithmetic  11.5 us (5%)
  local copies, waits for them, and re-layouts  7.56 us (3%)
  matrix products  4.3 us (2%)
    ppermute x9, waiting for transfers between devices, over_dp(): return lax.ppermute(array, DP, yz_perm(stage, k))  32.6 us
    pallas_call x2, Pallas kernels, project(): pl.pallas_call(functools.partial(project_kernel, part), in_specs=[SMEM] +...  16.2 us
    pallas_call x2, Pallas kernels, back(): pl.pallas_call(functools.partial(back_kernel, wo is not None), in_specs=i...  16.1 us
    ppermute x9, starting transfers between devices, over_dp(): return lax.ppermute(array, DP, yz_perm(stage, k))  14.9 us
    ppermute x1, waiting for transfers between devices, per_device(): lax.ppermute(dq1, X, LAST_TO_SAME)  13.5 us
    pallas_call x2, Pallas kernels, backward(): pl.pallas_call(backward_kernel, grid=(reports,), in_specs=[SMEM, SMEM, to...  12.6 us
    pallas_call x2, Pallas kernels, latent_terms(): pl.pallas_call(functools.partial(term_kernel, groups), grid=(features //...  12.6 us
    ppermute x3, waiting for transfers between devices, per_device(): late = [lax.ppermute(t, X, p) for t, p in zip(terms, moves)]  12.1 us
  transfers between devices with their start and end apart: 34, of which 16 were waited for; matrix products, arithmetic and copies ran while one was open for 8% of the time, Pallas kernels for 28%

profile of v7, /device:TPU:0, one launch (start us, length us, event | category | flops | bytes accessed | tf_op | source)
XLA Modules:
  0.0 238.1 jit_solution(18259911691756172809)
XLA Ops:
  7.2 4.5 %shard_map.158 = bf16[128,2048]{1,0:T(8,128)(2,1)} custom-call(s32[4]{0:T(128)} %bitcast.107, bf16[4,64,1536]{2,1,0:T(8,128)(2,1)} %tiles.1, bf16[32,1536]{1,0:T(8,128)(2,1)} %queries.1, bf16[32,2048]{1,0:T(8,128)(2,1)} %bitcast.103, bf16[32,2048]{1,0:T(8,128)(2,1)} %bitcast.3.w_query, bf16[1536,512]{1,0:T(8,128)(2,1)} %bitcast.91, bf16[1536,512]{1,0:T(8,128)(2,1)} %bitcast.94), custom_call_target="tpu_custom_call" | custom-call | flops 1 | bytes 1 | tf_op jit(solution)/shard_map/pallas_call | solution.py:102
  17.2 5.7 %collective-permute-done.3 = bf16[128,2048]{1,0:T(8,128)(2,1)S(1)} collective-permute-done((bf16[128,2048]{1,0:T(8,128)(2,1)}, bf16[128,2048]{1,0:T(8,128)(2,1)S(1)}, u32[]{:S(2)}, u32[]{:S(2)}) %collective-permute-start.3) | collective-permute-done | bytes 524320 | tf_op jit(solution)/shard_map/ppermute | solution.py:118
  22.9 6.0 %collective-permute-done.4 = bf16[128,2048]{1,0:T(8,128)(2,1)S(1)} collective-permute-done((bf16[128,2048]{1,0:T(8,128)(2,1)}, bf16[128,2048]{1,0:T(8,128)(2,1)S(1)}, u32[]{:S(2)}, u32[]{:S(2)}) %collective-permute-start.4) | collective-permute-done | bytes 524320 | tf_op jit(solution)/shard_map/ppermute | solution.py:118
  28.9 4.1 %collective-permute-start.5 = (bf16[2,128,2048]{2,1,0:T(8,128)(2,1)S(1)}, bf16[2,128,2048]{2,1,0:T(8,128)(2,1)}, u32[]{:S(2)}, u32[]{:S(2)}) collective-permute-start(bf16[2,128,2048]{2,1,0:T(8,128)(2,1)S(1)} %pad_maximum_fusion.1.refs_1_), channel_id=1, source_target_pairs={{0,48},{2,14},{4,52},{6,2},{8,56},{10,6},{12,60},{14,10},{16,0},{1... | collective-permute-start | bytes 3145736 | tf_op jit(solution)/shard_map/ppermute | solution.py:118
  51.9 9.8 %collective-permute-done.7.refs_3_ = bf16[2,128,2048]{2,1,0:T(8,128)(2,1)} collective-permute-done((bf16[2,128,2048]{2,1,0:T(8,128)(2,1)S(1)}, bf16[2,128,2048]{2,1,0:T(8,128)(2,1)}, u32[]{:S(2)}, u32[]{:S(2)}) %collective-permute-start.7) | collective-permute-done | bytes 1048608 | tf_op jit(solution)/shard_map/ppermute | solution.py:118
  70.5 6.2 %collective-permute-done.6.refs_5_ = bf16[2,128,2048]{2,1,0:T(8,128)(2,1)S(1)} collective-permute-done((bf16[2,128,2048]{2,1,0:T(8,128)(2,1)}, bf16[2,128,2048]{2,1,0:T(8,128)(2,1)S(1)}, u32[]{:S(2)}, u32[]{:S(2)}) %collective-permute-start.6) | collective-permute-done | bytes 1048608 | tf_op jit(solution)/shard_map/ppermute | solution.py:118
  82.4 8.0 %shard_map.159 = (bf16[512,512]{1,0:T(8,128)(2,1)}, bf16[512,512]{1,0:T(8,128)(2,1)}, bf16[512,2048]{1,0:T(8,128)(2,1)}, bf16[512,2048]{1,0:T(8,128)(2,1)}) custom-call(s32[211]{0:T(256)} %concatenate.7.meta, bf16[512,2048]{1,0:T(8,128)(2,1)} %fusion.2.normed, bf16[512,2048]{1,0:T(8,128)(2,1)} %broadcast_select_fusion.upstream, ...), custom_call_target="tpu_custom_call" | custom-call | flops 1 | bytes 1 | tf_op jit(solution)/shard_map/pallas_call | solution.py:182
  95.7 3.7 %shard_map.160.kv.keys.vals = bf16[768,1024]{1,0:T(8,128)(2,1)} custom-call(s32[211]{0:T(256)} %concatenate.7.meta, bf16[2,128,2048]{2,1,0:T(8,128)(2,1)} %pad_maximum_fusion.refs_0_, bf16[2,128,2048]{2,1,0:T(8,128)(2,1)} %copy-done.1, bf16[2,128,2048]{2,1,0:T(8,128)(2,1)} %collective-permute-done.1.refs_2_, ...), custom_call_target="tpu_custom_call" | custom-call | flops 1 | bytes 1 | tf_op jit(solution)/shard_map/pallas_call | solution.py:227
  99.4 8.2 %shard_map.161 = (f32[512,512]{1,0:T(8,128)}, bf16[512,512]{1,0:T(8,128)(2,1)}, bf16[512,2048]{1,0:T(8,128)(2,1)}, bf16[512,2048]{1,0:T(8,128)(2,1)}) custom-call(s32[211]{0:T(256)} %concatenate.7.meta, bf16[512,2048]{1,0:T(8,128)(2,1)} %fusion.2.normed, bf16[512,2048]{1,0:T(8,128)(2,1)} %broadcast_select_fusion.upstream, ...), custom_call_target="tpu_custom_call" | custom-call | flops 1 | bytes 1 | tf_op jit(solution)/shard_map/pallas_call | solution.py:182
  107.7 4.7 %shard_map.162.probs = f32[4,512,192]{2,1,0:T(8,128)} custom-call(s32[211]{0:T(256)} %concatenate.7.meta, f32[512,512]{1,0:T(8,128)} %get-tuple-element.87.q_own, bf16[512,512]{1,0:T(8,128)(2,1)} %collective-permute-done.20.q_got, bf16[768,1024]{1,0:T(8,128)(2,1)} %shard_map.160.kv.keys.vals), custom_call_target="tpu_custom_call" | custom-call | flops 1 | bytes 1 | tf_op jit(solution)/shard_map/pallas_call | solution.py:266
  112.3 6.3 %shard_map.163 = (bf16[528,512]{1,0:T(8,128)(2,1)}, bf16[4,192,1024]{2,1,0:T(8,128)(2,1)}) custom-call(s32[211]{0:T(256)} %concatenate.7.meta, f32[1]{0:T(128)S(6)} %tanh.3.gate, f32[512,512]{1,0:T(8,128)} %get-tuple-element.87.q_own, bf16[512,512]{1,0:T(8,128)(2,1)} %collective-permute-done.20.q_got, bf16[512,512]{1,0:T(8,128)(2,1)} %get-tuple-element.89.o_own, ...), custom_call_target="tpu_custom_call" | custom-call | flops 1 | bytes 1 | tf_op jit(solution)/shard_map/pallas_call | solution.py:316
  122.1 6.3 %shard_map.164 = (f32[192,1536]{1,0:T(8,128)}, bf16[384,1536]{1,0:T(8,128)(2,1)}, bf16[192,1536]{1,0:T(8,128)(2,1)}) custom-call(bf16[4,192,1024]{2,1,0:T(8,128)(2,1)} %get-tuple-element.92.dkv, bf16[1536,512]{1,0:T(8,128)(2,1)} %bitcast.92, bf16[1536,512]{1,0:T(8,128)(2,1)} %bitcast.95, bf16[192,1536]{1,0:T(8,128)(2,1)} %broadcast_in_dim.38.added), custom_call_target="tpu_custom_call" | custom-call | flops 1 | bytes 1 | tf_op jit(solution)/shard_map/pallas_call | solution.py:453
  128.4 13.5 %collective-permute-done.22.refs_0_ = bf16[528,512]{1,0:T(8,128)(2,1)} collective-permute-done((bf16[528,512]{1,0:T(8,128)(2,1)}, bf16[528,512]{1,0:T(8,128)(2,1)}, u32[]{:S(2)}, u32[]{:S(2)}) %collective-permute-start.22) | collective-permute-done | bytes 540704 | tf_op jit(solution)/shard_map/ppermute | solution.py:560
  147.2 6.0 %all-gather.5.cloned.1.call-done.refs_4_ = bf16[1024,2048]{1,0:T(8,128)(2,1)} async-done(((bf16[32,2048]{1,0:T(8,128)(2,1)}), bf16[1024,2048]{1,0:T(8,128)(2,1)}) %all-gather.5.cloned.1.call-update) | async-done | bytes 4194320 | tf_op jit(solution)/shard_map/all_gather | solution.py:554
  153.2 8.6 %shard_map.165 = (bf16[512,2048]{1,0:T(8,128)(2,1)}, bf16[512,512]{1,0:T(8,128)(2,1)}) custom-call(s32[211]{0:T(256)} %concatenate.7.meta, f32[1,512]{1,0:T(1,128)} %slice.16.rinv, f32[1,2048]{1,0:T(1,128)} %slice.17.gain, bf16[528,512]{1,0:T(8,128)(2,1)} %collective-permute-done.22.refs_0_, bf16[528,512]{1,0:T(8,128)(2,1)} %collective-permute-done.23.refs_1_, ...), custom_call_target="tpu_custom_call" | custom-call | flops 1 | bytes 1 | tf_op jit(solution)/shard_map/pallas_call | solution.py:422
  161.8 5.1 %collective-permute-start.24 = (bf16[512,512]{1,0:T(8,128)(2,1)}, bf16[512,512]{1,0:T(8,128)(2,1)}, u32[]{:S(2)}, u32[]{:S(2)}) collective-permute-start(bf16[512,512]{1,0:T(8,128)(2,1)} %get-tuple-element.104), channel_id=1, source_target_pairs={{0,1},{1,0},{2,3},{3,2},{4,5},{5,4},{6,7},{7,6},{8,9},{9,8},{10,11... | collective-permute-start | bytes 1572872 | tf_op jit(solution)/shard_map/ppermute | solution.py:566
  166.9 4.3 %convolution_convert_fusion.o_own = bf16[512,512]{1,0:T(8,128)(2,1)} fusion(bf16[512,2048]{1,0:T(8,128)(2,1)} %get-tuple-element.101.refs_4_, bf16[512,2048]{1,0:T(8,128)(2,1)} %get-tuple-element.102), kind=kOutput, calls=%fused_computation.6 | convolution fusion | flops 1074003968 | bytes 4718592 | tf_op jit(solution)/shard_map/dot_general | solution.py:51
  176.2 4.1 %collective-permute-done.24.o_got = bf16[512,512]{1,0:T(8,128)(2,1)} collective-permute-done((bf16[512,512]{1,0:T(8,128)(2,1)}, bf16[512,512]{1,0:T(8,128)(2,1)}, u32[]{:S(2)}, u32[]{:S(2)}) %collective-permute-start.24) | collective-permute-done | bytes 524320 | tf_op jit(solution)/shard_map/ppermute | solution.py:566
  180.3 6.3 %shard_map.166 = (bf16[528,512]{1,0:T(8,128)(2,1)}, bf16[4,192,1024]{2,1,0:T(8,128)(2,1)}) custom-call(s32[211]{0:T(256)} %concatenate.7.meta, f32[1]{0:T(128)S(6)} %tanh.3.gate, f32[512,512]{1,0:T(8,128)} %get-tuple-element.87.q_own, bf16[512,512]{1,0:T(8,128)(2,1)} %collective-permute-done.20.q_got, bf16[512,512]{1,0:T(8,128)(2,1)} %convolution_convert_fusion.o_own, ...), custom_call_target="tpu_custom_call" | custom-call | flops 1 | bytes 1 | tf_op jit(solution)/shard_map/pallas_call | solution.py:316
  186.5 4.9 %collective-permute-start.28 = (bf16[528,512]{1,0:T(8,128)(2,1)}, bf16[528,512]{1,0:T(8,128)(2,1)}, u32[]{:S(2)}, u32[]{:S(2)}) collective-permute-start(bf16[528,512]{1,0:T(8,128)(2,1)} %get-tuple-element.108.refs_1_), channel_id=1, source_target_pairs={{0,1},{1,0},{2,3},{3,2},{4,5},{5,4},{6,7},{7,6},{8,9},{9,8},{10,11... | collective-permute-start | bytes 1622024 | tf_op jit(solution)/shard_map/ppermute | solution.py:578
  191.4 6.3 %shard_map.168 = (f32[192,1536]{1,0:T(8,128)}, bf16[192,1536]{1,0:T(8,128)(2,1)}, bf16[192,1536]{1,0:T(8,128)(2,1)}, bf16[192,1536]{1,0:T(8,128)(2,1)}) custom-call(bf16[4,192,1024]{2,1,0:T(8,128)(2,1)} %get-tuple-element.118.dkv, bf16[1536,512]{1,0:T(8,128)(2,1)} %bitcast.93, bf16[1536,512]{1,0:T(8,128)(2,1)} %bitcast.96, ...), custom_call_target="tpu_custom_call" | custom-call | flops 1 | bytes 1 | tf_op jit(solution)/shard_map/pallas_call | solution.py:453
  197.7 3.9 %collective-permute-start.29 = (bf16[192,1536]{1,0:T(8,128)(2,1)}, bf16[192,1536]{1,0:T(8,128)(2,1)}, u32[]{:S(2)}, u32[]{:S(2)}) collective-permute-start(bf16[192,1536]{1,0:T(8,128)(2,1)} %get-tuple-element.123), channel_id=1, source_target_pairs={{0,64},{1,65},{2,66},{3,67},{4,68},{5,69},{6,70},{7,71},{8,72},{9,... | collective-permute-start | bytes 1769480 | tf_op jit(solution)/shard_map/ppermute | solution.py:580
  206.9 7.5 %shard_map.167 = bf16[512,2048]{1,0:T(8,128)(2,1)} custom-call(s32[211]{0:T(256)} %concatenate.7.meta, f32[1,512]{1,0:T(1,128)} %bitcast.106, f32[1,2048]{1,0:T(1,128)} %gain.1, bf16[528,512]{1,0:T(8,128)(2,1)} %get-tuple-element.91.refs_0_, bf16[528,512]{1,0:T(8,128)(2,1)} %get-tuple-element.108.refs_1_, bf16[528,512]{1,0:T(8,128)(2,1)} %collective-permute-done.27.refs_2_, ...), custom_call_target="tpu_custom_call" | custom-call | flops 1 | bytes 1 | tf_op jit(solution)/shard_map/pallas_call | solution.py:422
  216.4 12.1 %collective-permute-done.31 = bf16[192,1536]{1,0:T(8,128)(2,1)} collective-permute-done((bf16[192,1536]{1,0:T(8,128)(2,1)}, bf16[192,1536]{1,0:T(8,128)(2,1)}, u32[]{:S(2)}, u32[]{:S(2)}) %collective-permute-start.31) | collective-permute-done | bytes 589856 | tf_op jit(solution)/shard_map/ppermute | solution.py:580
  (114 shorter events, 67.0 us)
Async XLA Ops:
  7.2 140.0 %all-gather.3.cloned.1.call-start = ((), (), s32[]{:S(2)}) async-start(), calls=%async_computation | async-start | bytes 6291456 | tf_op jit(solution)/shard_map/all_gather | solution.py:516
  16.2 16.9 %collective-permute-start = (bf16[128,2048]{1,0:T(8,128)(2,1)}, bf16[128,2048]{1,0:T(8,128)(2,1)S(1)}, u32[]{:S(2)}, u32[]{:S(2)}) collective-permute-start(bf16[128,2048]{1,0:T(8,128)(2,1)} %shard_map.158), channel_id=1, source_target_pairs={{0,4},{2,18},{4,8},{6,22},{8,12},{10,26},{12,0},{14,30},{16,20},{1... | collective-permute-start | bytes 1572872 | tf_op jit(solution)/shard_map/ppermute | solution.py:118
  28.9 17.4 %collective-permute-start.5 = (bf16[2,128,2048]{2,1,0:T(8,128)(2,1)S(1)}, bf16[2,128,2048]{2,1,0:T(8,128)(2,1)}, u32[]{:S(2)}, u32[]{:S(2)}) collective-permute-start(bf16[2,128,2048]{2,1,0:T(8,128)(2,1)S(1)} %pad_maximum_fusion.1.refs_1_), channel_id=1, source_target_pairs={{0,48},{2,14},{4,52},{6,2},{8,56},{10,6},{12,60},{14,10},{16,0},{1... | collective-permute-start | bytes 3145736 | tf_op jit(solution)/shard_map/ppermute | solution.py:118
  34.1 16.3 %collective-permute-start.1 = (bf16[2,128,2048]{2,1,0:T(8,128)(2,1)}, bf16[2,128,2048]{2,1,0:T(8,128)(2,1)}, u32[]{:S(2)}, u32[]{:S(2)}) collective-permute-start(bf16[2,128,2048]{2,1,0:T(8,128)(2,1)} %pad_maximum_fusion.refs_0_), channel_id=1, source_target_pairs={{0,16},{2,6},{4,20},{6,10},{8,24},{10,14},{12,28},{14,2},{16,32},{... | collective-permute-start | bytes 3145736 | tf_op jit(solution)/shard_map/ppermute | solution.py:118
  34.2 119.0 %all-gather.5.cloned.1.call-start = ((), (), s32[]{:S(2)}) async-start(), calls=%async_computation.1 | async-start | bytes 4325376 | tf_op jit(solution)/shard_map/all_gather | solution.py:554
  42.0 19.7 %collective-permute-start.7 = (bf16[2,128,2048]{2,1,0:T(8,128)(2,1)S(1)}, bf16[2,128,2048]{2,1,0:T(8,128)(2,1)}, u32[]{:S(2)}, u32[]{:S(2)}) collective-permute-start(bf16[2,128,2048]{2,1,0:T(8,128)(2,1)S(1)} %pad_maximum_fusion.1.refs_1_), channel_id=1, source_target_pairs={{0,16},{2,6},{4,20},{6,10},{8,24},{10,14},{12,28},{14,2},{16,32},{... | collective-permute-start | bytes 3145736 | tf_op jit(solution)/shard_map/ppermute | solution.py:118
  42.1 19.6 %collective-permute-start.8 = (bf16[2,128,2048]{2,1,0:T(8,128)(2,1)}, bf16[2,128,2048]{2,1,0:T(8,128)(2,1)}, u32[]{:S(2)}, u32[]{:S(2)}) collective-permute-start(bf16[2,128,2048]{2,1,0:T(8,128)(2,1)} %pad_maximum_fusion.refs_0_), channel_id=1, source_target_pairs={{0,48},{2,14},{4,52},{6,2},{8,56},{10,6},{12,60},{14,10},{16,0},{1... | collective-permute-start | bytes 3145736 | tf_op jit(solution)/shard_map/ppermute | solution.py:118
  46.3 15.4 %collective-permute-start.10 = (bf16[2,128,2048]{2,1,0:T(8,128)(2,1)S(1)}, bf16[2,128,2048]{2,1,0:T(8,128)(2,1)}, u32[]{:S(2)}, u32[]{:S(2)}) collective-permute-start(bf16[2,128,2048]{2,1,0:T(8,128)(2,1)S(1)} %pad_maximum_fusion.1.refs_1_), channel_id=1, source_target_pairs={{0,2},{2,0},{1,3},{3,1},{4,6},{6,4},{5,7},{7,5},{8,10},{10,8},{9,1... | collective-permute-start | bytes 3145736 | tf_op jit(solution)/shard_map/ppermute | solution.py:122
  46.3 17.5 %collective-permute-start.9 = (bf16[2,128,2048]{2,1,0:T(8,128)(2,1)}, bf16[2,128,2048]{2,1,0:T(8,128)(2,1)}, u32[]{:S(2)}, u32[]{:S(2)}) collective-permute-start(bf16[2,128,2048]{2,1,0:T(8,128)(2,1)} %pad_maximum_fusion.refs_0_), channel_id=1, source_target_pairs={{0,2},{2,0},{1,3},{3,1},{4,6},{6,4},{5,7},{7,5},{8,10},{10,8},{9,1... | collective-permute-start | bytes 3145736 | tf_op jit(solution)/shard_map/ppermute | solution.py:122
  61.7 15.0 %collective-permute-start.6 = (bf16[2,128,2048]{2,1,0:T(8,128)(2,1)}, bf16[2,128,2048]{2,1,0:T(8,128)(2,1)S(1)}, u32[]{:S(2)}, u32[]{:S(2)}) collective-permute-start(bf16[2,128,2048]{2,1,0:T(8,128)(2,1)} %collective-permute-done.5.refs_7_), channel_id=1, source_target_pairs={{0,48},{2,14},{4,52},{6,2},{8,56},{10,6},{12,60},{14,10},{16,0},{1... | collective-permute-start | bytes 3145736 | tf_op jit(solution)/shard_map/ppermute | solution.py:118
  61.7 15.0 %collective-permute-start.11 = (bf16[2,128,2048]{2,1,0:T(8,128)(2,1)}, bf16[2,128,2048]{2,1,0:T(8,128)(2,1)S(1)}, u32[]{:S(2)}, u32[]{:S(2)}) collective-permute-start(bf16[2,128,2048]{2,1,0:T(8,128)(2,1)} %collective-permute-done.1.refs_2_), channel_id=1, source_target_pairs={{0,2},{2,0},{1,3},{3,1},{4,6},{6,4},{5,7},{7,5},{8,10},{10,8},{9,1... | collective-permute-start | bytes 3145736 | tf_op jit(solution)/shard_map/ppermute | solution.py:122
  61.7 16.3 %collective-permute-start.2 = (bf16[2,128,2048]{2,1,0:T(8,128)(2,1)}, bf16[2,128,2048]{2,1,0:T(8,128)(2,1)S(1)}, u32[]{:S(2)}, u32[]{:S(2)}) collective-permute-start(bf16[2,128,2048]{2,1,0:T(8,128)(2,1)} %collective-permute-done.1.refs_2_), channel_id=1, source_target_pairs={{0,16},{2,6},{4,20},{6,10},{8,24},{10,14},{12,28},{14,2},{16,32},{... | collective-permute-start | bytes 3145736 | tf_op jit(solution)/shard_map/ppermute | solution.py:118
  90.4 17.2 %collective-permute-start.20 = (bf16[512,512]{1,0:T(8,128)(2,1)}, bf16[512,512]{1,0:T(8,128)(2,1)}, u32[]{:S(2)}, u32[]{:S(2)}) collective-permute-start(bf16[512,512]{1,0:T(8,128)(2,1)} %get-tuple-element.88), channel_id=1, source_target_pairs={{0,1},{1,0},{64,65},{65,64},{2,3},{3,2},{66,67},{67,66},{4,5},{5,4... | collective-permute-start | bytes 1572872 | tf_op jit(solution)/shard_map/ppermute | solution.py:551
  93.5 18.8 %collective-permute-start.21 = (bf16[512,512]{1,0:T(8,128)(2,1)}, bf16[512,512]{1,0:T(8,128)(2,1)}, u32[]{:S(2)}, u32[]{:S(2)}) collective-permute-start(bf16[512,512]{1,0:T(8,128)(2,1)} %get-tuple-element.84), channel_id=1, source_target_pairs={{64,65},{65,64},{66,67},{67,66},{68,69},{69,68},{70,71},{71,70},{7... | collective-permute-start | bytes 1572872 | tf_op jit(solution)/shard_map/ppermute | solution.py:552
  118.7 23.2 %collective-permute-start.22 = (bf16[528,512]{1,0:T(8,128)(2,1)}, bf16[528,512]{1,0:T(8,128)(2,1)}, u32[]{:S(2)}, u32[]{:S(2)}) collective-permute-start(bf16[528,512]{1,0:T(8,128)(2,1)} %get-tuple-element.91.refs_0_), channel_id=1, source_target_pairs={{64,0},{65,1},{66,2},{67,3},{68,4},{69,5},{70,6},{71,7},{72,8},{73... | collective-permute-start | bytes 1622024 | tf_op jit(solution)/shard_map/ppermute | solution.py:560
  119.9 24.6 %collective-permute-start.23 = (bf16[528,512]{1,0:T(8,128)(2,1)}, bf16[528,512]{1,0:T(8,128)(2,1)}, u32[]{:S(2)}, u32[]{:S(2)}) collective-permute-start(bf16[528,512]{1,0:T(8,128)(2,1)} %get-tuple-element.91.refs_0_), channel_id=1, source_target_pairs={{64,1},{65,0},{66,3},{67,2},{68,5},{69,4},{70,7},{71,6},{72,9},{73... | collective-permute-start | bytes 1622024 | tf_op jit(solution)/shard_map/ppermute | solution.py:560
  144.5 29.2 %collective-permute-start.25 = (bf16[384,1536]{1,0:T(8,128)(2,1)}, bf16[384,1536]{1,0:T(8,128)(2,1)}, u32[]{:S(2)}, u32[]{:S(2)}) collective-permute-start(bf16[384,1536]{1,0:T(8,128)(2,1)} %get-tuple-element.105), channel_id=1, source_target_pairs={{64,0},{65,1},{66,2},{67,3},{68,4},{69,5},{70,6},{71,7},{72,8},{73... | collective-permute-start | bytes 3538952 | tf_op jit(solution)/shard_map/ppermute | solution.py:570
  145.8 30.4 %collective-permute-start.26 = (bf16[192,1536]{1,0:T(8,128)(2,1)}, bf16[192,1536]{1,0:T(8,128)(2,1)}, u32[]{:S(2)}, u32[]{:S(2)}) collective-permute-start(bf16[192,1536]{1,0:T(8,128)(2,1)} %get-tuple-element.106), channel_id=1, source_target_pairs={{64,1},{65,0},{66,3},{67,2},{68,5},{69,4},{70,7},{71,6},{72,9},{73... | collective-permute-start | bytes 1769480 | tf_op jit(solution)/shard_map/ppermute | solution.py:571
  161.8 18.5 %collective-permute-start.24 = (bf16[512,512]{1,0:T(8,128)(2,1)}, bf16[512,512]{1,0:T(8,128)(2,1)}, u32[]{:S(2)}, u32[]{:S(2)}) collective-permute-start(bf16[512,512]{1,0:T(8,128)(2,1)} %get-tuple-element.104), channel_id=1, source_target_pairs={{0,1},{1,0},{2,3},{3,2},{4,5},{5,4},{6,7},{7,6},{8,9},{9,8},{10,11... | collective-permute-start | bytes 1572872 | tf_op jit(solution)/shard_map/ppermute | solution.py:566
  171.2 20.2 %collective-permute-start.27 = (bf16[528,512]{1,0:T(8,128)(2,1)}, bf16[528,512]{1,0:T(8,128)(2,1)}, u32[]{:S(2)}, u32[]{:S(2)}) collective-permute-start(bf16[528,512]{1,0:T(8,128)(2,1)} %collective-permute-done.23.refs_1_), channel_id=1, source_target_pairs={{0,64},{1,65},{2,66},{3,67},{4,68},{5,69},{6,70},{7,71},{8,72},{9,... | collective-permute-start | bytes 1622024 | tf_op jit(solution)/shard_map/ppermute | solution.py:569
  186.5 20.4 %collective-permute-start.28 = (bf16[528,512]{1,0:T(8,128)(2,1)}, bf16[528,512]{1,0:T(8,128)(2,1)}, u32[]{:S(2)}, u32[]{:S(2)}) collective-permute-start(bf16[528,512]{1,0:T(8,128)(2,1)} %get-tuple-element.108.refs_1_), channel_id=1, source_target_pairs={{0,1},{1,0},{2,3},{3,2},{4,5},{5,4},{6,7},{7,6},{8,9},{9,8},{10,11... | collective-permute-start | bytes 1622024 | tf_op jit(solution)/shard_map/ppermute | solution.py:578
  197.7 18.7 %collective-permute-start.29 = (bf16[192,1536]{1,0:T(8,128)(2,1)}, bf16[192,1536]{1,0:T(8,128)(2,1)}, u32[]{:S(2)}, u32[]{:S(2)}) collective-permute-start(bf16[192,1536]{1,0:T(8,128)(2,1)} %get-tuple-element.123), channel_id=1, source_target_pairs={{0,64},{1,65},{2,66},{3,67},{4,68},{5,69},{6,70},{7,71},{8,72},{9,... | collective-permute-start | bytes 1769480 | tf_op jit(solution)/shard_map/ppermute | solution.py:580
  201.6 14.8 %collective-permute-start.30 = (bf16[192,1536]{1,0:T(8,128)(2,1)}, bf16[192,1536]{1,0:T(8,128)(2,1)}, u32[]{:S(2)}, u32[]{:S(2)}) collective-permute-start(bf16[192,1536]{1,0:T(8,128)(2,1)} %get-tuple-element.124), channel_id=1, source_target_pairs={{0,65},{1,64},{2,67},{3,66},{4,69},{5,68},{6,71},{7,70},{8,73},{9,... | collective-permute-start | bytes 1769480 | tf_op jit(solution)/shard_map/ppermute | solution.py:580
  203.7 24.7 %collective-permute-start.31 = (bf16[192,1536]{1,0:T(8,128)(2,1)}, bf16[192,1536]{1,0:T(8,128)(2,1)}, u32[]{:S(2)}, u32[]{:S(2)}) collective-permute-start(bf16[192,1536]{1,0:T(8,128)(2,1)} %get-tuple-element.125), channel_id=1, source_target_pairs={{0,1},{1,0},{2,3},{3,2},{4,5},{5,4},{6,7},{7,6},{8,9},{9,8},{10,11... | collective-permute-start | bytes 1769480 | tf_op jit(solution)/shard_map/ppermute | solution.py:580
  (25 other events, 249.9 us)
Sparse Core Ops, SparseCore 0:
  34.3 64.6 all-gather.2
  101.3 51.8 all-gather.4

commit v8 on v7

--- a/solution.py
+++ b/solution.py
@@ -430,37 +430,31 @@
     )(*inputs)
 
 
-def term_kernel(groups, dkv, w_key, w_value, added, own, *terms):
+def term_kernel(dkv, w_key, w_value, own, *terms):
     rows = own.shape[0]
     both = dkv[...].reshape(4 * rows, dkv.shape[2])
     half = w_key.shape[1]
     value = dot(both[:, :half], w_key[...], NT) + dot(both[:, half:], w_value[...], NT)
     own[...] = value[:rows]
-    for group, term in zip(groups, terms):
-        for i, k in enumerate(group):
-            part = value[k * rows : (k + 1) * rows]
-            if k == 2:
-                part += added[...].astype(F32)
-            term[i * rows : (i + 1) * rows] = part.astype(BF)
-
-
-def latent_terms(groups, dkv, w_key, w_value, added):
+    for k, term in enumerate(terms, 1):
+        term[...] = value[k * rows : (k + 1) * rows].astype(BF)
+
+
+def latent_terms(dkv, w_key, w_value):
     rows, inner = dkv.shape[1:]
     features = w_key.shape[0]
     tile = features // 3
     weight = pl.BlockSpec((tile, w_key.shape[1]), lambda i: (i, 0))
-    sizes = [rows] + [rows * len(group) for group in groups]
+    result = pl.BlockSpec((rows, tile), lambda i: (0, i))
     return pl.pallas_call(
-        functools.partial(term_kernel, groups),
+        term_kernel,
         grid=(features // tile,),
-        in_specs=[whole(dkv.shape), weight, weight, pl.BlockSpec((rows, tile), lambda i: (0, i))],
-        out_specs=[pl.BlockSpec((n, tile), lambda i: (0, i)) for n in sizes],
-        out_shape=[
-            jax.ShapeDtypeStruct((n, features), BF if i else F32) for i, n in enumerate(sizes)
-        ],
+        in_specs=[whole(dkv.shape), weight, weight],
+        out_specs=[result] * 4,
+        out_shape=[jax.ShapeDtypeStruct((rows, features), t) for t in (F32, BF, BF, BF)],
         compiler_params=params(),
         cost_estimate=SMALL,
-    )(dkv, w_key, w_value, added)
+    )(dkv, w_key, w_value)
 
 
 def per_device(
@@ -533,51 +527,51 @@
         tile_counts.reshape(4), tiles, lat_query, w_out[0], wq_t, w_key[0], w_value[0]
     )
     parts = [over_dp(block, 1, k) for k in (1, 2, 3)]
+    wq1 = lax.ppermute(wq_t, "segment", [(1, 0)])
+    parts, wq1, rinv, rinv1, gain1 = lax.optimization_barrier((parts, wq1, rinv, rinv1, gain1))
     low, high = jnp.stack([block, parts[0]]), jnp.stack(parts[1:])
     low1, high3 = over_dp(low, 2, 1), over_dp(high, 2, 3)
     high1, low3 = over_dp(high, 2, 1), over_dp(low, 2, 3)
+    others = over_core([low, high])
+    low1, high3, others = lax.optimization_barrier((low1, high3, others))
     low2, high2 = over_dp(low1, 2, 1), over_dp(high3, 2, 3)
     mine = [low, high, low1, high1, low3, high3]
-    others = over_core(mine)
-    last2, mine, others, normed, up1, rinv1, gain1, meta = lax.optimization_barrier(
-        ([low2, high2], mine, others, normed, up1, rinv1, gain1, meta)
+    others += over_core(mine[2:])
+    last2, mine, others, normed, up1, meta = lax.optimization_barrier(
+        ([low2, high2], mine, others, normed, up1, meta)
     )
     others = others[:4] + over_core(last2) + others[4:]
     blocks = mine[:4] + last2 + mine[4:] + others
-    wq_t, _ = lax.optimization_barrier((wq_t, last2))
-    wq1 = lax.ppermute(wq_t, "segment", [(1, 0)])
+    wq1, _ = lax.optimization_barrier((wq1, last2))
+    wq1 = lax.all_gather(wq1, DP, axis=0, tiled=True)
 
     q_send, o_send, wq_got, wo_got = project(1, BF, meta, normed, up1, blocks)
     q_got = lax.ppermute(q_send, X, SWAP_MP)
     o_got = lax.ppermute(o_send, X, LAST_SWAP)
-    meta, wq1, o_send = lax.optimization_barrier((meta, wq1, o_send))
-    wq1 = lax.all_gather(wq1, DP, axis=0, tiled=True)
+    meta, o_send = lax.optimization_barrier((meta, o_send))
     kv = select(wanted, meta, blocks)
     normed, kv = lax.optimization_barrier((normed, kv))
     q_own, o_own, wq_own, wo_own = project(0, F32, meta, normed, up1, blocks)
     probs = forward(meta, q_own, q_got, kv)
     dq1, dkv1 = backward(meta, gate, q_own, q_got, o_own, o_got, kv, probs)
     dqs = [lax.ppermute(dq1, X, LAST_TO_SAME), lax.ppermute(dq1, X, LAST_TO_CROSS)]
-    own1, *terms = latent_terms(
-        ((1, 3), (2,)), dkv1, w_key[0], w_value[0], jnp.zeros((192, E), BF)
-    )
-    dqs, terms = lax.optimization_barrier((dqs, terms))
+    own1, *terms = latent_terms(dkv1, w_key[0], w_value[0])
+    got1 = lax.ppermute(dq1, X, LAST_SWAP)
+    moves = (LAST_SWAP, LAST_TO_CROSS, LAST_TO_SAME)
+    got = [lax.ppermute(t, X, p) for t, p in zip(terms[::-1], moves)]
+    dqs, own1 = lax.optimization_barrier((dqs, own1))
     up, o_send = back(meta, rinv1, gain1, dqs, cotangent, h_all, [wq1], wo_got)
+    o_send, got1 = lax.optimization_barrier((o_send, got1))
     o_got = lax.ppermute(o_send, X, FIRST_SWAP)
     o_own = dot(up, wo_own, NT).astype(BF)
-    dq_cross, o_own = lax.optimization_barrier((dqs[1], o_own))
-    got1 = lax.ppermute(dq_cross, X, FIRST_TO_SAME)
-    pair = lax.ppermute(terms[0], X, LAST_TO_SAME)
-    got = [pair[:192], lax.ppermute(terms[1], X, LAST_TO_CROSS)]
-    relayed = pair[192:]
-    o_got, got, relayed = lax.optimization_barrier((o_got, got, relayed))
+    o_got, got[:2] = lax.optimization_barrier((o_got, got[:2]))
 
     dq0, dkv0 = backward(meta, gate, q_own, q_got, o_own, o_got, kv, probs)
-    dkv0, got1 = lax.optimization_barrier((dkv0, got1))
-    own0, *terms = latent_terms(((1,), (2,), (3,)), dkv0, w_key[0], w_value[0], relayed)
+    own0, *terms = latent_terms(dkv0, w_key[0], w_value[0])
     got0 = lax.ppermute(dq0, X, FIRST_SWAP)
-    moves = (FIRST_TO_SAME, FIRST_TO_CROSS, FIRST_SWAP)
-    late = [lax.ppermute(t, X, p) for t, p in zip(terms, moves)]
+    terms, got = lax.optimization_barrier((terms, got))
+    moves = (FIRST_SWAP, FIRST_TO_CROSS, FIRST_TO_SAME)
+    late = [lax.ppermute(t, X, p) for t, p in zip(terms[::-1], moves)]
     got, got0 = lax.optimization_barrier((got, got0))
     received = jnp.where(last, own1, own0)
     for term in got:

time: 239 us -> 225 us (0.941)
  waiting for transfers between devices: 75.8 us -> 63 us
  starting transfers between devices: 53.4 us -> 50.4 us
  other arithmetic: 11.5 us -> 14.1 us
    ppermute x9, waiting for transfers between devices: 32.6 us -> 23.3 us  [over_dp(): return lax.ppermute(array, DP, yz_perm(stage, k))]
    ppermute x6 -> x7, waiting for transfers between devices: 12.5 us -> 19.8 us  [the longest x3 10.1 us: per_device(): got = [lax.ppermute(t, X, p) for t, p in zip(terms[::-1], moves)]]
    ppermute x1, waiting for transfers between devices: 13.5 us -> 7.3 us  [per_device(): lax.ppermute(dq1, X, LAST_TO_SAME)]
    all_gather x1, waiting for transfers between devices: 6.01 us -> 0.01 us  [per_device(): wq1 = lax.all_gather(wq1, DP, axis=0, tiled=True)]
    ppermute x1, waiting for transfers between devices: 4.06 us -> 0.01 us  [per_device(): o_got = lax.ppermute(o_send, X, FIRST_SWAP)]
    ppermute x1, waiting for transfers between devices: 0.98 us -> 4.29 us  [per_device(): lax.ppermute(jnp.concatenate([rinv, gain[0]]), 'segment', [(1, 0)])[None]]
    ppermute x8, waiting for transfers between devices: 1.29 us -> 3.87 us  [over_core(): return [lax.ppermute(a, 'core', [(0, 1), (1, 0)]) for a in arrays]]
    slice x1 -> x0, local copies, waits for them, and re-layouts: 2.41 us -> none  [per_device(): relayed = pair[192:]]
  transfers between devices with their start and end apart: 34 -> 35, of which waited for: 16 -> 15; matrix products, arithmetic and copies ran while one was open for 8% -> 8% of each run, Pallas kernels for 28% -> 30%
where the time goes in v8:
time: 225 us; the launch traced here: 223 us
  Pallas kernels  70.3 us (31%)
  waiting for transfers between devices  63 us (28%)
  starting transfers between devices  50.4 us (22%)
  between operations  15.1 us (7%)
  other arithmetic  14.1 us (6%)
  local copies, waits for them, and re-layouts  5.45 us (2%)
  matrix products  4.29 us (2%)
    ppermute x9, waiting for transfers between devices, over_dp(): return lax.ppermute(array, DP, yz_perm(stage, k))  23.3 us
    pallas_call x2, Pallas kernels, project(): pl.pallas_call(functools.partial(project_kernel, part), in_specs=[SMEM] +...  16.3 us
    pallas_call x2, Pallas kernels, back(): pl.pallas_call(functools.partial(back_kernel, wo is not None), in_specs=i...  16.2 us
    ppermute x9, starting transfers between devices, over_dp(): return lax.ppermute(array, DP, yz_perm(stage, k))  16.1 us
    pallas_call x2, Pallas kernels, backward(): pl.pallas_call(backward_kernel, grid=(reports,), in_specs=[SMEM, SMEM, to...  12.7 us
    pallas_call x2, Pallas kernels, latent_terms(): pl.pallas_call(term_kernel, grid=(features // tile,), in_specs=[whole(dkv...  12.2 us
    ppermute x3, waiting for transfers between devices, per_device(): got = [lax.ppermute(t, X, p) for t, p in zip(terms[::-1], moves)]  10.1 us
    ppermute x3, waiting for transfers between devices, per_device(): late = [lax.ppermute(t, X, p) for t, p in zip(terms[::-1], moves)]  9.75 us
  transfers between devices with their start and end apart: 35, of which 15 were waited for; matrix products, arithmetic and copies ran while one was open for 8% of the time, Pallas kernels for 30%

profile of v8, /device:TPU:0, one launch (start us, length us, event | category | flops | bytes accessed | tf_op | source)
XLA Modules:
  0.0 222.7 jit_solution(9793469710816627967)
XLA Ops:
  7.2 4.5 %shard_map.158 = bf16[128,2048]{1,0:T(8,128)(2,1)} custom-call(s32[4]{0:T(128)} %bitcast.108, bf16[4,64,1536]{2,1,0:T(8,128)(2,1)} %tiles.1, bf16[32,1536]{1,0:T(8,128)(2,1)} %queries.1, bf16[32,2048]{1,0:T(8,128)(2,1)} %bitcast.102, bf16[32,2048]{1,0:T(8,128)(2,1)} %bitcast.103, bf16[1536,512]{1,0:T(8,128)(2,1)} %bitcast.91, bf16[1536,512]{1,0:T(8,128)(2,1)} %bitcast.94), custom_call_target="tpu_custom_call" | custom-call | flops 1 | bytes 1 | tf_op jit(solution)/shard_map/pallas_call | solution.py:102
  18.3 3.1 %collective-permute-start.4 = (f32[512]{0:T(512)S(1)}, f32[512]{0:T(512)S(1)}, u32[]{:S(2)}, u32[]{:S(2)}) collective-permute-start(f32[512]{0:T(512)S(1)} %fusion), channel_id=1, source_target_pairs={{0,1},{1,0},{2,3},{3,2},{4,5},{5,4},{6,7},{7,6},{8,9},{9,8},{10,11... | collective-permute-start | bytes 6152 | tf_op jit(solution)/shard_map/ppermute | solution.py:514
  24.8 4.3 %collective-permute-done.5 = f32[2560]{0:T(1024)S(1)} collective-permute-done((f32[2560]{0:T(1024)S(1)}, f32[2560]{0:T(1024)S(1)}, u32[]{:S(2)}, u32[]{:S(2)}) %collective-permute-start.5) | collective-permute-done | bytes 10272 | tf_op jit(solution)/shard_map/ppermute | solution.py:517
  39.9 9.9 %collective-permute-done.6.refs_2_ = bf16[2,128,2048]{2,1,0:T(8,128)(2,1)} collective-permute-done((bf16[2,128,2048]{2,1,0:T(8,128)(2,1)S(1)}, bf16[2,128,2048]{2,1,0:T(8,128)(2,1)}, u32[]{:S(2)}, u32[]{:S(2)}) %collective-permute-start.6) | collective-permute-done | bytes 1048608 | tf_op jit(solution)/shard_map/ppermute | solution.py:118
  61.1 3.7 %collective-permute-done.13.refs_6_ = bf16[2,128,2048]{2,1,0:T(8,128)(2,1)} collective-permute-done((bf16[2,128,2048]{2,1,0:T(8,128)(2,1)S(1)}, bf16[2,128,2048]{2,1,0:T(8,128)(2,1)}, u32[]{:S(2)}, u32[]{:S(2)}) %collective-permute-start.13) | collective-permute-done | bytes 1048608 | tf_op jit(solution)/shard_map/ppermute | solution.py:118
  64.8 7.6 %collective-permute-done.10.refs_4_ = bf16[2,128,2048]{2,1,0:T(8,128)(2,1)} collective-permute-done((bf16[2,128,2048]{2,1,0:T(8,128)(2,1)}, bf16[2,128,2048]{2,1,0:T(8,128)(2,1)}, u32[]{:S(2)}, u32[]{:S(2)}) %collective-permute-start.10) | collective-permute-done | bytes 1048608 | tf_op jit(solution)/shard_map/ppermute | solution.py:118
  72.3 3.2 %broadcast_select_fusion.upstream = bf16[512,2048]{1,0:T(8,128)(2,1)} fusion(bf16[512,2048]{1,0:T(8,128)(2,1)} %refs_2_.1, pred[512]{0:T(512)(128)(4,1)S(1)} %fusion.3), kind=kLoop, calls=%fused_computation.5 | loop fusion | flops 1048576 | bytes 4194816 | tf_op jit(solution)/shard_map/jit(_where)/select_n | solution.py:522
  82.1 8.0 %shard_map.159 = (bf16[512,512]{1,0:T(8,128)(2,1)}, bf16[512,512]{1,0:T(8,128)(2,1)}, bf16[512,2048]{1,0:T(8,128)(2,1)}, bf16[512,2048]{1,0:T(8,128)(2,1)}) custom-call(s32[211]{0:T(256)} %concatenate.7.meta, bf16[512,2048]{1,0:T(8,128)(2,1)} %fusion.2.normed, bf16[512,2048]{1,0:T(8,128)(2,1)} %broadcast_select_fusion.upstream, ...), custom_call_target="tpu_custom_call" | custom-call | flops 1 | bytes 1 | tf_op jit(solution)/shard_map/pallas_call | solution.py:182
  90.1 3.1 %collective-permute-start.20 = (bf16[512,512]{1,0:T(8,128)(2,1)}, bf16[512,512]{1,0:T(8,128)(2,1)}, u32[]{:S(2)}, u32[]{:S(2)}) collective-permute-start(bf16[512,512]{1,0:T(8,128)(2,1)} %get-tuple-element.107), channel_id=1, source_target_pairs={{0,1},{1,0},{64,65},{65,64},{2,3},{3,2},{66,67},{67,66},{4,5},{5,4... | collective-permute-start | bytes 1572872 | tf_op jit(solution)/shard_map/ppermute | solution.py:549
  95.4 3.7 %shard_map.160.kv.keys.vals = bf16[768,1024]{1,0:T(8,128)(2,1)} custom-call(s32[211]{0:T(256)} %concatenate.7.meta, bf16[2,128,2048]{2,1,0:T(8,128)(2,1)} %copy-done.1, bf16[2,128,2048]{2,1,0:T(8,128)(2,1)} %pad_maximum_fusion.1.refs_1_, bf16[2,128,2048]{2,1,0:T(8,128)(2,1)} %collective-permute-done.6.refs_2_, ...), custom_call_target="tpu_custom_call" | custom-call | flops 1 | bytes 1 | tf_op jit(solution)/shard_map/pallas_call | solution.py:227
  99.1 8.3 %shard_map.161 = (f32[512,512]{1,0:T(8,128)}, bf16[512,512]{1,0:T(8,128)(2,1)}, bf16[512,2048]{1,0:T(8,128)(2,1)}, bf16[512,2048]{1,0:T(8,128)(2,1)}) custom-call(s32[211]{0:T(256)} %concatenate.7.meta, bf16[512,2048]{1,0:T(8,128)(2,1)} %fusion.2.normed, bf16[512,2048]{1,0:T(8,128)(2,1)} %broadcast_select_fusion.upstream, bf16[2,128,2048]{2,1,0:T(8,128)(2,1)} %copy-done.1, ...), custom_call_target="tpu_custom_call" | custom-call | flops 1 | bytes 1 | tf_op jit(solution)/shard_map/pallas_call | solution.py:182
  107.4 4.8 %shard_map.162.probs = f32[4,512,192]{2,1,0:T(8,128)} custom-call(s32[211]{0:T(256)} %concatenate.7.meta, f32[512,512]{1,0:T(8,128)} %get-tuple-element.106.q_own, bf16[512,512]{1,0:T(8,128)(2,1)} %collective-permute-done.20.q_got, bf16[768,1024]{1,0:T(8,128)(2,1)} %shard_map.160.kv.keys.vals), custom_call_target="tpu_custom_call" | custom-call | flops 1 | bytes 1 | tf_op jit(solution)/shard_map/pallas_call | solution.py:266
  112.3 6.4 %shard_map.163 = (bf16[528,512]{1,0:T(8,128)(2,1)}, bf16[4,192,1024]{2,1,0:T(8,128)(2,1)}) custom-call(s32[211]{0:T(256)} %concatenate.7.meta, f32[1]{0:T(128)S(6)} %tanh.3.gate, f32[512,512]{1,0:T(8,128)} %get-tuple-element.106.q_own, bf16[512,512]{1,0:T(8,128)(2,1)} %collective-permute-done.20.q_got, bf16[512,512]{1,0:T(8,128)(2,1)} %get-tuple-element.108.o_own, ...), custom_call_target="tpu_custom_call" | custom-call | flops 1 | bytes 1 | tf_op jit(solution)/shard_map/pallas_call | solution.py:316
  122.8 6.1 %shard_map.164 = (f32[192,1536]{1,0:T(8,128)}, bf16[192,1536]{1,0:T(8,128)(2,1)}, bf16[192,1536]{1,0:T(8,128)(2,1)}, bf16[192,1536]{1,0:T(8,128)(2,1)}) custom-call(bf16[4,192,1024]{2,1,0:T(8,128)(2,1)} %get-tuple-element.113.dkv, bf16[1536,512]{1,0:T(8,128)(2,1)} %bitcast.92, bf16[1536,512]{1,0:T(8,128)(2,1)} %bitcast.95), custom_call_target="tpu_custom_call" | custom-call | flops 1 | bytes 1 | tf_op jit(solution)/shard_map/pallas_call | solution.py:449
  131.6 7.3 %collective-permute-done.22.refs_0_ = bf16[528,512]{1,0:T(8,128)(2,1)} collective-permute-done((bf16[528,512]{1,0:T(8,128)(2,1)}, bf16[528,512]{1,0:T(8,128)(2,1)}, u32[]{:S(2)}, u32[]{:S(2)}) %collective-permute-start.22) | collective-permute-done | bytes 540704 | tf_op jit(solution)/shard_map/ppermute | solution.py:557
  141.2 8.6 %shard_map.165 = (bf16[512,2048]{1,0:T(8,128)(2,1)}, bf16[512,512]{1,0:T(8,128)(2,1)}) custom-call(s32[211]{0:T(256)} %concatenate.7.meta, f32[1,512]{1,0:T(1,128)} %slice.8.rinv, f32[1,2048]{1,0:T(1,128)} %slice.9.gain, bf16[528,512]{1,0:T(8,128)(2,1)} %collective-permute-done.22.refs_0_, bf16[528,512]{1,0:T(8,128)(2,1)} %collective-permute-done.23.refs_1_, ...), custom_call_target="tpu_custom_call" | custom-call | flops 1 | bytes 1 | tf_op jit(solution)/shard_map/pallas_call | solution.py:422
  154.1 4.3 %convolution_convert_fusion.o_own = bf16[512,512]{1,0:T(8,128)(2,1)} fusion(bf16[512,2048]{1,0:T(8,128)(2,1)} %get-tuple-element.120.refs_4_, bf16[512,2048]{1,0:T(8,128)(2,1)} %get-tuple-element.121), kind=kOutput, calls=%fused_computation.6 | convolution fusion | flops 1074003968 | bytes 4718592 | tf_op jit(solution)/shard_map/dot_general | solution.py:51
  158.4 10.1 %collective-permute-done.27 = bf16[192,1536]{1,0:T(8,128)(2,1)} collective-permute-done((bf16[192,1536]{1,0:T(8,128)(2,1)}, bf16[192,1536]{1,0:T(8,128)(2,1)}, u32[]{:S(2)}, u32[]{:S(2)}) %collective-permute-start.27) | collective-permute-done | bytes 589856 | tf_op jit(solution)/shard_map/ppermute | solution.py:561
  168.5 6.3 %shard_map.166 = (bf16[528,512]{1,0:T(8,128)(2,1)}, bf16[4,192,1024]{2,1,0:T(8,128)(2,1)}) custom-call(s32[211]{0:T(256)} %concatenate.7.meta, f32[1]{0:T(128)S(6)} %tanh.3.gate, f32[512,512]{1,0:T(8,128)} %get-tuple-element.106.q_own, bf16[512,512]{1,0:T(8,128)(2,1)} %collective-permute-done.20.q_got, bf16[512,512]{1,0:T(8,128)(2,1)} %convolution_convert_fusion.o_own, ...), custom_call_target="tpu_custom_call" | custom-call | flops 1 | bytes 1 | tf_op jit(solution)/shard_map/pallas_call | solution.py:316
  177.5 6.1 %shard_map.167 = (f32[192,1536]{1,0:T(8,128)}, bf16[192,1536]{1,0:T(8,128)(2,1)}, bf16[192,1536]{1,0:T(8,128)(2,1)}, bf16[192,1536]{1,0:T(8,128)(2,1)}) custom-call(bf16[4,192,1024]{2,1,0:T(8,128)(2,1)} %get-tuple-element.129.dkv, bf16[1536,512]{1,0:T(8,128)(2,1)} %bitcast.93, bf16[1536,512]{1,0:T(8,128)(2,1)} %bitcast.96), custom_call_target="tpu_custom_call" | custom-call | flops 1 | bytes 1 | tf_op jit(solution)/shard_map/pallas_call | solution.py:449
  183.6 4.6 %collective-permute-start.30 = (bf16[192,1536]{1,0:T(8,128)(2,1)}, bf16[192,1536]{1,0:T(8,128)(2,1)}, u32[]{:S(2)}, u32[]{:S(2)}) collective-permute-start(bf16[192,1536]{1,0:T(8,128)(2,1)} %get-tuple-element.147), channel_id=1, source_target_pairs={{0,1},{1,0},{2,3},{3,2},{4,5},{5,4},{6,7},{7,6},{8,9},{9,8},{10,11... | collective-permute-start | bytes 1769480 | tf_op jit(solution)/shard_map/ppermute | solution.py:574
  193.7 7.5 %shard_map.168 = bf16[512,2048]{1,0:T(8,128)(2,1)} custom-call(s32[211]{0:T(256)} %concatenate.7.meta, f32[1,512]{1,0:T(1,128)} %bitcast.107, f32[1,2048]{1,0:T(1,128)} %gain.1, bf16[528,512]{1,0:T(8,128)(2,1)} %get-tuple-element.110.refs_0_, bf16[528,512]{1,0:T(8,128)(2,1)} %get-tuple-element.127.refs_1_, bf16[528,512]{1,0:T(8,128)(2,1)} %collective-permute-done.24.refs_2_, ...), custom_call_target="tpu_custom_call" | custom-call | flops 1 | bytes 1 | tf_op jit(solution)/shard_map/pallas_call | solution.py:422
  203.4 2.9 %collective-permute-done.30 = bf16[192,1536]{1,0:T(8,128)(2,1)} collective-permute-done((bf16[192,1536]{1,0:T(8,128)(2,1)}, bf16[192,1536]{1,0:T(8,128)(2,1)}, u32[]{:S(2)}, u32[]{:S(2)}) %collective-permute-start.30) | collective-permute-done | bytes 589856 | tf_op jit(solution)/shard_map/ppermute | solution.py:574
  206.3 6.8 %collective-permute-done.32 = bf16[192,1536]{1,0:T(8,128)(2,1)} collective-permute-done((bf16[192,1536]{1,0:T(8,128)(2,1)}, bf16[192,1536]{1,0:T(8,128)(2,1)}, u32[]{:S(2)}, u32[]{:S(2)}) %collective-permute-start.32) | collective-permute-done | bytes 589856 | tf_op jit(solution)/shard_map/ppermute | solution.py:574
  (114 shorter events, 66.3 us)
Async XLA Ops:
  7.2 134.0 %all-gather.3.cloned.1.call-start = ((), (), s32[]{:S(2)}) async-start(), calls=%async_computation | async-start | bytes 6291456 | tf_op jit(solution)/shard_map/all_gather | solution.py:510
  11.8 18.5 %collective-permute-start = (bf16[128,2048]{1,0:T(8,128)(2,1)}, bf16[128,2048]{1,0:T(8,128)(2,1)S(1)}, u32[]{:S(2)}, u32[]{:S(2)}) collective-permute-start(bf16[128,2048]{1,0:T(8,128)(2,1)} %shard_map.158), channel_id=1, source_target_pairs={{0,4},{2,18},{4,8},{6,22},{8,12},{10,26},{12,0},{14,30},{16,20},{1... | collective-permute-start | bytes 1572872 | tf_op jit(solution)/shard_map/ppermute | solution.py:118
  13.5 16.8 %collective-permute-start.1 = (bf16[128,2048]{1,0:T(8,128)(2,1)}, bf16[128,2048]{1,0:T(8,128)(2,1)S(1)}, u32[]{:S(2)}, u32[]{:S(2)}) collective-permute-start(bf16[128,2048]{1,0:T(8,128)(2,1)} %shard_map.158), channel_id=1, source_target_pairs={{0,8},{2,34},{4,12},{6,38},{8,0},{10,42},{12,4},{14,46},{16,24},{1... | collective-permute-start | bytes 1572872 | tf_op jit(solution)/shard_map/ppermute | solution.py:118
  17.8 123.4 %all-gather.5.cloned.1.call-start = ((), (), s32[]{:S(2)}) async-start(), calls=%async_computation.1 | async-start | bytes 4325376 | tf_op jit(solution)/shard_map/all_gather | solution.py:546
  32.9 17.0 %collective-permute-start.6 = (bf16[2,128,2048]{2,1,0:T(8,128)(2,1)S(1)}, bf16[2,128,2048]{2,1,0:T(8,128)(2,1)}, u32[]{:S(2)}, u32[]{:S(2)}) collective-permute-start(bf16[2,128,2048]{2,1,0:T(8,128)(2,1)S(1)} %pad_maximum_fusion.refs_0_), channel_id=1, source_target_pairs={{0,16},{2,6},{4,20},{6,10},{8,24},{10,14},{12,28},{14,2},{16,32},{... | collective-permute-start | bytes 3145736 | tf_op jit(solution)/shard_map/ppermute | solution.py:118
  37.0 15.1 %collective-permute-start.7 = (bf16[2,128,2048]{2,1,0:T(8,128)(2,1)}, bf16[2,128,2048]{2,1,0:T(8,128)(2,1)}, u32[]{:S(2)}, u32[]{:S(2)}) collective-permute-start(bf16[2,128,2048]{2,1,0:T(8,128)(2,1)} %pad_maximum_fusion.1.refs_1_), channel_id=1, source_target_pairs={{0,48},{2,14},{4,52},{6,2},{8,56},{10,6},{12,60},{14,10},{16,0},{1... | collective-permute-start | bytes 3145736 | tf_op jit(solution)/shard_map/ppermute | solution.py:118
  39.9 21.2 %collective-permute-start.12 = (bf16[2,128,2048]{2,1,0:T(8,128)(2,1)}, bf16[2,128,2048]{2,1,0:T(8,128)(2,1)}, u32[]{:S(2)}, u32[]{:S(2)}) collective-permute-start(bf16[2,128,2048]{2,1,0:T(8,128)(2,1)} %pad_maximum_fusion.1.refs_1_), channel_id=1, source_target_pairs={{0,16},{2,6},{4,20},{6,10},{8,24},{10,14},{12,28},{14,2},{16,32},{... | collective-permute-start | bytes 3145736 | tf_op jit(solution)/shard_map/ppermute | solution.py:118
  54.1 18.3 %collective-permute-start.10 = (bf16[2,128,2048]{2,1,0:T(8,128)(2,1)}, bf16[2,128,2048]{2,1,0:T(8,128)(2,1)}, u32[]{:S(2)}, u32[]{:S(2)}) collective-permute-start(bf16[2,128,2048]{2,1,0:T(8,128)(2,1)} %collective-permute-done.6.refs_2_), channel_id=1, source_target_pairs={{0,16},{2,6},{4,20},{6,10},{8,24},{10,14},{12,28},{14,2},{16,32},{... | collective-permute-start | bytes 3145736 | tf_op jit(solution)/shard_map/ppermute | solution.py:118
  57.4 19.9 %collective-permute-start.14 = (bf16[2,128,2048]{2,1,0:T(8,128)(2,1)}, bf16[2,128,2048]{2,1,0:T(8,128)(2,1)}, u32[]{:S(2)}, u32[]{:S(2)}) collective-permute-start(bf16[2,128,2048]{2,1,0:T(8,128)(2,1)} %collective-permute-done.6.refs_2_), channel_id=1, source_target_pairs={{0,2},{2,0},{1,3},{3,1},{4,6},{6,4},{5,7},{7,5},{8,10},{10,8},{9,1... | collective-permute-start | bytes 3145736 | tf_op jit(solution)/shard_map/ppermute | solution.py:122
  57.4 19.9 %collective-permute-start.11 = (bf16[2,128,2048]{2,1,0:T(8,128)(2,1)}, bf16[2,128,2048]{2,1,0:T(8,128)(2,1)}, u32[]{:S(2)}, u32[]{:S(2)}) collective-permute-start(bf16[2,128,2048]{2,1,0:T(8,128)(2,1)} %collective-permute-done.7.refs_7_), channel_id=1, source_target_pairs={{0,48},{2,14},{4,52},{6,2},{8,56},{10,6},{12,60},{14,10},{16,0},{1... | collective-permute-start | bytes 3145736 | tf_op jit(solution)/shard_map/ppermute | solution.py:118
  61.1 16.3 %collective-permute-start.17 = (bf16[2,128,2048]{2,1,0:T(8,128)(2,1)}, bf16[2,128,2048]{2,1,0:T(8,128)(2,1)}, u32[]{:S(2)}, u32[]{:S(2)}) collective-permute-start(bf16[2,128,2048]{2,1,0:T(8,128)(2,1)} %collective-permute-done.7.refs_7_), channel_id=1, source_target_pairs={{0,2},{2,0},{1,3},{3,1},{4,6},{6,4},{5,7},{7,5},{8,10},{10,8},{9,1... | collective-permute-start | bytes 3145736 | tf_op jit(solution)/shard_map/ppermute | solution.py:122
  90.1 17.3 %collective-permute-start.20 = (bf16[512,512]{1,0:T(8,128)(2,1)}, bf16[512,512]{1,0:T(8,128)(2,1)}, u32[]{:S(2)}, u32[]{:S(2)}) collective-permute-start(bf16[512,512]{1,0:T(8,128)(2,1)} %get-tuple-element.107), channel_id=1, source_target_pairs={{0,1},{1,0},{64,65},{65,64},{2,3},{3,2},{66,67},{67,66},{4,5},{5,4... | collective-permute-start | bytes 1572872 | tf_op jit(solution)/shard_map/ppermute | solution.py:549
  93.3 19.0 %collective-permute-start.21 = (bf16[512,512]{1,0:T(8,128)(2,1)}, bf16[512,512]{1,0:T(8,128)(2,1)}, u32[]{:S(2)}, u32[]{:S(2)}) collective-permute-start(bf16[512,512]{1,0:T(8,128)(2,1)} %get-tuple-element.102), channel_id=1, source_target_pairs={{64,65},{65,64},{66,67},{67,66},{68,69},{69,68},{70,71},{71,70},{7... | collective-permute-start | bytes 1572872 | tf_op jit(solution)/shard_map/ppermute | solution.py:550
  118.7 20.3 %collective-permute-start.22 = (bf16[528,512]{1,0:T(8,128)(2,1)}, bf16[528,512]{1,0:T(8,128)(2,1)}, u32[]{:S(2)}, u32[]{:S(2)}) collective-permute-start(bf16[528,512]{1,0:T(8,128)(2,1)} %get-tuple-element.110.refs_0_), channel_id=1, source_target_pairs={{64,0},{65,1},{66,2},{67,3},{68,4},{69,5},{70,6},{71,7},{72,8},{73... | collective-permute-start | bytes 1622024 | tf_op jit(solution)/shard_map/ppermute | solution.py:557
  120.0 21.3 %collective-permute-start.23 = (bf16[528,512]{1,0:T(8,128)(2,1)}, bf16[528,512]{1,0:T(8,128)(2,1)}, u32[]{:S(2)}, u32[]{:S(2)}) collective-permute-start(bf16[528,512]{1,0:T(8,128)(2,1)} %get-tuple-element.110.refs_0_), channel_id=1, source_target_pairs={{64,1},{65,0},{66,3},{67,2},{68,5},{69,4},{70,7},{71,6},{72,9},{73... | collective-permute-start | bytes 1622024 | tf_op jit(solution)/shard_map/ppermute | solution.py:557
  121.3 28.6 %collective-permute-start.24 = (bf16[528,512]{1,0:T(8,128)(2,1)}, bf16[528,512]{1,0:T(8,128)(2,1)}, u32[]{:S(2)}, u32[]{:S(2)}) collective-permute-start(bf16[528,512]{1,0:T(8,128)(2,1)} %get-tuple-element.110.refs_0_), channel_id=1, source_target_pairs={{64,65},{65,64},{66,67},{67,66},{68,69},{69,68},{70,71},{71,70},{7... | collective-permute-start | bytes 1622024 | tf_op jit(solution)/shard_map/ppermute | solution.py:559
  128.9 29.5 %collective-permute-start.26 = (bf16[192,1536]{1,0:T(8,128)(2,1)}, bf16[192,1536]{1,0:T(8,128)(2,1)}, u32[]{:S(2)}, u32[]{:S(2)}) collective-permute-start(bf16[192,1536]{1,0:T(8,128)(2,1)} %get-tuple-element.124), channel_id=1, source_target_pairs={{64,65},{65,64},{66,67},{67,66},{68,69},{69,68},{70,71},{71,70},{7... | collective-permute-start | bytes 1769480 | tf_op jit(solution)/shard_map/ppermute | solution.py:561
  130.3 38.1 %collective-permute-start.27 = (bf16[192,1536]{1,0:T(8,128)(2,1)}, bf16[192,1536]{1,0:T(8,128)(2,1)}, u32[]{:S(2)}, u32[]{:S(2)}) collective-permute-start(bf16[192,1536]{1,0:T(8,128)(2,1)} %get-tuple-element.125), channel_id=1, source_target_pairs={{64,1},{65,0},{66,3},{67,2},{68,5},{69,4},{70,7},{71,6},{72,9},{73... | collective-permute-start | bytes 1769480 | tf_op jit(solution)/shard_map/ppermute | solution.py:561
  149.9 18.6 %collective-permute-start.25 = (bf16[512,512]{1,0:T(8,128)(2,1)}, bf16[512,512]{1,0:T(8,128)(2,1)}, u32[]{:S(2)}, u32[]{:S(2)}) collective-permute-start(bf16[512,512]{1,0:T(8,128)(2,1)} %get-tuple-element.123), channel_id=1, source_target_pairs={{0,1},{1,0},{2,3},{3,2},{4,5},{5,4},{6,7},{7,6},{8,9},{9,8},{10,11... | collective-permute-start | bytes 1572872 | tf_op jit(solution)/shard_map/ppermute | solution.py:565
  152.6 31.0 %collective-permute-start.28 = (bf16[192,1536]{1,0:T(8,128)(2,1)}, bf16[192,1536]{1,0:T(8,128)(2,1)}, u32[]{:S(2)}, u32[]{:S(2)}) collective-permute-start(bf16[192,1536]{1,0:T(8,128)(2,1)} %get-tuple-element.135), channel_id=1, source_target_pairs={{64,0},{65,1},{66,2},{67,3},{68,4},{69,5},{70,6},{71,7},{72,8},{73... | collective-permute-start | bytes 1769480 | tf_op jit(solution)/shard_map/ppermute | solution.py:561
  174.7 18.9 %collective-permute-start.29 = (bf16[528,512]{1,0:T(8,128)(2,1)}, bf16[528,512]{1,0:T(8,128)(2,1)}, u32[]{:S(2)}, u32[]{:S(2)}) collective-permute-start(bf16[528,512]{1,0:T(8,128)(2,1)} %get-tuple-element.127.refs_1_), channel_id=1, source_target_pairs={{0,1},{1,0},{2,3},{3,2},{4,5},{5,4},{6,7},{7,6},{8,9},{9,8},{10,11... | collective-permute-start | bytes 1622024 | tf_op jit(solution)/shard_map/ppermute | solution.py:571
  183.6 22.7 %collective-permute-start.30 = (bf16[192,1536]{1,0:T(8,128)(2,1)}, bf16[192,1536]{1,0:T(8,128)(2,1)}, u32[]{:S(2)}, u32[]{:S(2)}) collective-permute-start(bf16[192,1536]{1,0:T(8,128)(2,1)} %get-tuple-element.147), channel_id=1, source_target_pairs={{0,1},{1,0},{2,3},{3,2},{4,5},{5,4},{6,7},{7,6},{8,9},{9,8},{10,11... | collective-permute-start | bytes 1769480 | tf_op jit(solution)/shard_map/ppermute | solution.py:574
  188.2 18.1 %collective-permute-start.31 = (bf16[192,1536]{1,0:T(8,128)(2,1)}, bf16[192,1536]{1,0:T(8,128)(2,1)}, u32[]{:S(2)}, u32[]{:S(2)}) collective-permute-start(bf16[192,1536]{1,0:T(8,128)(2,1)} %get-tuple-element.148), channel_id=1, source_target_pairs={{0,65},{1,64},{2,67},{3,66},{4,69},{5,68},{6,71},{7,70},{8,73},{9,... | collective-permute-start | bytes 1769480 | tf_op jit(solution)/shard_map/ppermute | solution.py:574
  190.3 22.8 %collective-permute-start.32 = (bf16[192,1536]{1,0:T(8,128)(2,1)}, bf16[192,1536]{1,0:T(8,128)(2,1)}, u32[]{:S(2)}, u32[]{:S(2)}) collective-permute-start(bf16[192,1536]{1,0:T(8,128)(2,1)} %get-tuple-element.149), channel_id=1, source_target_pairs={{0,64},{1,65},{2,66},{3,67},{4,68},{5,69},{6,70},{7,71},{8,72},{9,... | collective-permute-start | bytes 1769480 | tf_op jit(solution)/shard_map/ppermute | solution.py:574
  (26 other events, 370.0 us)
Sparse Core Ops, SparseCore 0:
  17.9 59.1 all-gather.2
  79.3 47.3 all-gather.4

commit v9 on v8

--- a/solution.py
+++ b/solution.py
@@ -528,8 +528,11 @@
     )
     parts = [over_dp(block, 1, k) for k in (1, 2, 3)]
     wq1 = lax.ppermute(wq_t, "segment", [(1, 0)])
-    parts, wq1, rinv, rinv1, gain1 = lax.optimization_barrier((parts, wq1, rinv, rinv1, gain1))
-    low, high = jnp.stack([block, parts[0]]), jnp.stack(parts[1:])
+    low = jnp.stack([block, parts[0]])
+    parts[1:], wq1, rinv, rinv1, gain1 = lax.optimization_barrier(
+        (parts[1:], wq1, rinv, rinv1, gain1)
+    )
+    high = jnp.stack(parts[1:])
     low1, high3 = over_dp(low, 2, 1), over_dp(high, 2, 3)
     high1, low3 = over_dp(high, 2, 1), over_dp(low, 2, 3)
     others = over_core([low, high])
@@ -557,8 +560,8 @@
     dqs = [lax.ppermute(dq1, X, LAST_TO_SAME), lax.ppermute(dq1, X, LAST_TO_CROSS)]
     own1, *terms = latent_terms(dkv1, w_key[0], w_value[0])
     got1 = lax.ppermute(dq1, X, LAST_SWAP)
-    moves = (LAST_SWAP, LAST_TO_CROSS, LAST_TO_SAME)
-    got = [lax.ppermute(t, X, p) for t, p in zip(terms[::-1], moves)]
+    moves = (LAST_TO_SAME, LAST_TO_CROSS, LAST_SWAP)
+    got = [lax.ppermute(t, X, p) for t, p in zip(terms, moves)]
     dqs, own1 = lax.optimization_barrier((dqs, own1))
     up, o_send = back(meta, rinv1, gain1, dqs, cotangent, h_all, [wq1], wo_got)
     o_send, got1 = lax.optimization_barrier((o_send, got1))

time: 225 us -> 222 us (0.987)
  waiting for transfers between devices: 63 us -> 60.4 us
    ppermute x1, starting transfers between devices: 3.12 us -> 0.6 us  [per_device(): q_got = lax.ppermute(q_send, X, SWAP_MP)]
where the time goes in v9:
time: 222 us; the launch traced here: 220 us
  Pallas kernels  70.3 us (32%)
  waiting for transfers between devices  60.4 us (27%)
  starting transfers between devices  50 us (23%)
  between operations  15.1 us (7%)
  other arithmetic  14.2 us (6%)
  local copies, waits for them, and re-layouts  5.25 us (2%)
  matrix products  4.3 us (2%)
    ppermute x9, waiting for transfers between devices, over_dp(): return lax.ppermute(array, DP, yz_perm(stage, k))  23.1 us
    ppermute x9, starting transfers between devices, over_dp(): return lax.ppermute(array, DP, yz_perm(stage, k))  17.7 us
    pallas_call x2, Pallas kernels, project(): pl.pallas_call(functools.partial(project_kernel, part), in_specs=[SMEM] +...  16.3 us
    pallas_call x2, Pallas kernels, back(): pl.pallas_call(functools.partial(back_kernel, wo is not None), in_specs=i...  16.2 us
    pallas_call x2, Pallas kernels, backward(): pl.pallas_call(backward_kernel, grid=(reports,), in_specs=[SMEM, SMEM, to...  12.6 us
    pallas_call x2, Pallas kernels, latent_terms(): pl.pallas_call(term_kernel, grid=(features // tile,), in_specs=[whole(dkv...  12.2 us
    ppermute x3, waiting for transfers between devices, per_device(): late = [lax.ppermute(t, X, p) for t, p in zip(terms[::-1], moves)]  10 us
    ppermute x1, waiting for transfers between devices, per_device(): lax.ppermute(dq1, X, LAST_TO_SAME)  8.95 us
  transfers between devices with their start and end apart: 35, of which 15 were waited for; matrix products, arithmetic and copies ran while one was open for 8% of the time, Pallas kernels for 30%

profile of v9, /device:TPU:0, one launch (start us, length us, event | category | flops | bytes accessed | tf_op | source)
XLA Modules:
  0.0 219.6 jit_solution(554503614309583192)
XLA Ops:
  7.2 4.5 %shard_map.158 = bf16[128,2048]{1,0:T(8,128)(2,1)} custom-call(s32[4]{0:T(128)} %bitcast.106, bf16[4,64,1536]{2,1,0:T(8,128)(2,1)} %tiles.1, bf16[32,1536]{1,0:T(8,128)(2,1)} %queries.1, bf16[32,2048]{1,0:T(8,128)(2,1)} %bitcast.100, bf16[32,2048]{1,0:T(8,128)(2,1)} %bitcast.101, bf16[1536,512]{1,0:T(8,128)(2,1)} %bitcast.91, bf16[1536,512]{1,0:T(8,128)(2,1)} %bitcast.94), custom_call_target="tpu_custom_call" | custom-call | flops 1 | bytes 1 | tf_op jit(solution)/shard_map/pallas_call | solution.py:102
  36.3 4.0 %collective-permute-start.7 = (bf16[2,128,2048]{2,1,0:T(8,128)(2,1)}, bf16[2,128,2048]{2,1,0:T(8,128)(2,1)}, u32[]{:S(2)}, u32[]{:S(2)}) collective-permute-start(bf16[2,128,2048]{2,1,0:T(8,128)(2,1)} %pad_maximum_fusion.1.refs_1_), channel_id=1, source_target_pairs={{0,48},{2,14},{4,52},{6,2},{8,56},{10,6},{12,60},{14,10},{16,0},{1... | collective-permute-start | bytes 3145736 | tf_op jit(solution)/shard_map/ppermute | solution.py:118
  40.9 6.7 %collective-permute-done.1.refs_2_ = bf16[2,128,2048]{2,1,0:T(8,128)(2,1)} collective-permute-done((bf16[2,128,2048]{2,1,0:T(8,128)(2,1)S(1)}, bf16[2,128,2048]{2,1,0:T(8,128)(2,1)}, u32[]{:S(2)}, u32[]{:S(2)}) %collective-permute-start.1) | collective-permute-done | bytes 1048608 | tf_op jit(solution)/shard_map/ppermute | solution.py:118
  49.5 3.4 %collective-permute-done.7.refs_7_ = bf16[2,128,2048]{2,1,0:T(8,128)(2,1)} collective-permute-done((bf16[2,128,2048]{2,1,0:T(8,128)(2,1)}, bf16[2,128,2048]{2,1,0:T(8,128)(2,1)}, u32[]{:S(2)}, u32[]{:S(2)}) %collective-permute-start.7) | collective-permute-done | bytes 1048608 | tf_op jit(solution)/shard_map/ppermute | solution.py:118
  56.8 3.3 %collective-permute-start.11 = (bf16[2,128,2048]{2,1,0:T(8,128)(2,1)}, bf16[2,128,2048]{2,1,0:T(8,128)(2,1)}, u32[]{:S(2)}, u32[]{:S(2)}) collective-permute-start(bf16[2,128,2048]{2,1,0:T(8,128)(2,1)} %collective-permute-done.7.refs_7_), channel_id=1, source_target_pairs={{0,48},{2,14},{4,52},{6,2},{8,56},{10,6},{12,60},{14,10},{16,0},{1... | collective-permute-start | bytes 3145736 | tf_op jit(solution)/shard_map/ppermute | solution.py:118
  60.1 4.0 %collective-permute-done.13.refs_6_ = bf16[2,128,2048]{2,1,0:T(8,128)(2,1)} collective-permute-done((bf16[2,128,2048]{2,1,0:T(8,128)(2,1)S(1)}, bf16[2,128,2048]{2,1,0:T(8,128)(2,1)}, u32[]{:S(2)}, u32[]{:S(2)}) %collective-permute-start.13) | collective-permute-done | bytes 1048608 | tf_op jit(solution)/shard_map/ppermute | solution.py:118
  64.1 7.6 %collective-permute-done.10.refs_4_ = bf16[2,128,2048]{2,1,0:T(8,128)(2,1)} collective-permute-done((bf16[2,128,2048]{2,1,0:T(8,128)(2,1)}, bf16[2,128,2048]{2,1,0:T(8,128)(2,1)}, u32[]{:S(2)}, u32[]{:S(2)}) %collective-permute-start.10) | collective-permute-done | bytes 1048608 | tf_op jit(solution)/shard_map/ppermute | solution.py:118
  81.5 8.0 %shard_map.159 = (bf16[512,512]{1,0:T(8,128)(2,1)}, bf16[512,512]{1,0:T(8,128)(2,1)}, bf16[512,2048]{1,0:T(8,128)(2,1)}, bf16[512,2048]{1,0:T(8,128)(2,1)}) custom-call(s32[211]{0:T(256)} %concatenate.7.meta, bf16[512,2048]{1,0:T(8,128)(2,1)} %fusion.2.normed, bf16[512,2048]{1,0:T(8,128)(2,1)} %broadcast_select_fusion.upstream, ...), custom_call_target="tpu_custom_call" | custom-call | flops 1 | bytes 1 | tf_op jit(solution)/shard_map/pallas_call | solution.py:182
  92.3 3.7 %shard_map.160.kv.keys.vals = bf16[768,1024]{1,0:T(8,128)(2,1)} custom-call(s32[211]{0:T(256)} %concatenate.7.meta, bf16[2,128,2048]{2,1,0:T(8,128)(2,1)} %copy-done.1, bf16[2,128,2048]{2,1,0:T(8,128)(2,1)} %pad_maximum_fusion.1.refs_1_, bf16[2,128,2048]{2,1,0:T(8,128)(2,1)} %collective-permute-done.1.refs_2_, ...), custom_call_target="tpu_custom_call" | custom-call | flops 1 | bytes 1 | tf_op jit(solution)/shard_map/pallas_call | solution.py:227
  96.0 8.3 %shard_map.161 = (f32[512,512]{1,0:T(8,128)}, bf16[512,512]{1,0:T(8,128)(2,1)}, bf16[512,2048]{1,0:T(8,128)(2,1)}, bf16[512,2048]{1,0:T(8,128)(2,1)}) custom-call(s32[211]{0:T(256)} %concatenate.7.meta, bf16[512,2048]{1,0:T(8,128)(2,1)} %fusion.2.normed, bf16[512,2048]{1,0:T(8,128)(2,1)} %broadcast_select_fusion.upstream, bf16[2,128,2048]{2,1,0:T(8,128)(2,1)} %copy-done.1, ...), custom_call_target="tpu_custom_call" | custom-call | flops 1 | bytes 1 | tf_op jit(solution)/shard_map/pallas_call | solution.py:182
  105.7 4.9 %shard_map.162.probs = f32[4,512,192]{2,1,0:T(8,128)} custom-call(s32[211]{0:T(256)} %concatenate.7.meta, f32[512,512]{1,0:T(8,128)} %get-tuple-element.104.q_own, bf16[512,512]{1,0:T(8,128)(2,1)} %collective-permute-done.20.q_got, bf16[768,1024]{1,0:T(8,128)(2,1)} %shard_map.160.kv.keys.vals), custom_call_target="tpu_custom_call" | custom-call | flops 1 | bytes 1 | tf_op jit(solution)/shard_map/pallas_call | solution.py:266
  110.5 6.3 %shard_map.163 = (bf16[528,512]{1,0:T(8,128)(2,1)}, bf16[4,192,1024]{2,1,0:T(8,128)(2,1)}) custom-call(s32[211]{0:T(256)} %concatenate.7.meta, f32[1]{0:T(128)S(6)} %tanh.3.gate, f32[512,512]{1,0:T(8,128)} %get-tuple-element.104.q_own, bf16[512,512]{1,0:T(8,128)(2,1)} %collective-permute-done.20.q_got, bf16[512,512]{1,0:T(8,128)(2,1)} %get-tuple-element.106.o_own, ...), custom_call_target="tpu_custom_call" | custom-call | flops 1 | bytes 1 | tf_op jit(solution)/shard_map/pallas_call | solution.py:316
  121.0 6.1 %shard_map.164 = (f32[192,1536]{1,0:T(8,128)}, bf16[192,1536]{1,0:T(8,128)(2,1)}, bf16[192,1536]{1,0:T(8,128)(2,1)}, bf16[192,1536]{1,0:T(8,128)(2,1)}) custom-call(bf16[4,192,1024]{2,1,0:T(8,128)(2,1)} %get-tuple-element.111.dkv, bf16[1536,512]{1,0:T(8,128)(2,1)} %bitcast.92, bf16[1536,512]{1,0:T(8,128)(2,1)} %bitcast.95), custom_call_target="tpu_custom_call" | custom-call | flops 1 | bytes 1 | tf_op jit(solution)/shard_map/pallas_call | solution.py:449
  129.7 9.0 %collective-permute-done.22.refs_0_ = bf16[528,512]{1,0:T(8,128)(2,1)} collective-permute-done((bf16[528,512]{1,0:T(8,128)(2,1)}, bf16[528,512]{1,0:T(8,128)(2,1)}, u32[]{:S(2)}, u32[]{:S(2)}) %collective-permute-start.22) | collective-permute-done | bytes 540704 | tf_op jit(solution)/shard_map/ppermute | solution.py:560
  140.1 8.6 %shard_map.165 = (bf16[512,2048]{1,0:T(8,128)(2,1)}, bf16[512,512]{1,0:T(8,128)(2,1)}) custom-call(s32[211]{0:T(256)} %concatenate.7.meta, f32[1,512]{1,0:T(1,128)} %slice.8.rinv, f32[1,2048]{1,0:T(1,128)} %slice.9.gain, bf16[528,512]{1,0:T(8,128)(2,1)} %collective-permute-done.22.refs_0_, bf16[528,512]{1,0:T(8,128)(2,1)} %collective-permute-done.23.refs_1_, ...), custom_call_target="tpu_custom_call" | custom-call | flops 1 | bytes 1 | tf_op jit(solution)/shard_map/pallas_call | solution.py:422
  148.7 3.4 %collective-permute-start.25 = (bf16[512,512]{1,0:T(8,128)(2,1)}, bf16[512,512]{1,0:T(8,128)(2,1)}, u32[]{:S(2)}, u32[]{:S(2)}) collective-permute-start(bf16[512,512]{1,0:T(8,128)(2,1)} %get-tuple-element.121), channel_id=1, source_target_pairs={{0,1},{1,0},{2,3},{3,2},{4,5},{5,4},{6,7},{7,6},{8,9},{9,8},{10,11... | collective-permute-start | bytes 1572872 | tf_op jit(solution)/shard_map/ppermute | solution.py:568
  153.6 4.3 %convolution_convert_fusion.o_own = bf16[512,512]{1,0:T(8,128)(2,1)} fusion(bf16[512,2048]{1,0:T(8,128)(2,1)} %get-tuple-element.118.refs_4_, bf16[512,2048]{1,0:T(8,128)(2,1)} %get-tuple-element.119), kind=kOutput, calls=%fused_computation.6 | convolution fusion | flops 1074003968 | bytes 4718592 | tf_op jit(solution)/shard_map/dot_general | solution.py:51
  157.9 4.9 %collective-permute-done.26 = bf16[192,1536]{1,0:T(8,128)(2,1)} collective-permute-done((bf16[192,1536]{1,0:T(8,128)(2,1)}, bf16[192,1536]{1,0:T(8,128)(2,1)}, u32[]{:S(2)}, u32[]{:S(2)}) %collective-permute-start.26) | collective-permute-done | bytes 589856 | tf_op jit(solution)/shard_map/ppermute | solution.py:564
  162.9 3.5 %collective-permute-done.27 = bf16[192,1536]{1,0:T(8,128)(2,1)} collective-permute-done((bf16[192,1536]{1,0:T(8,128)(2,1)}, bf16[192,1536]{1,0:T(8,128)(2,1)}, u32[]{:S(2)}, u32[]{:S(2)}) %collective-permute-start.27) | collective-permute-done | bytes 589856 | tf_op jit(solution)/shard_map/ppermute | solution.py:564
  166.4 6.3 %shard_map.166 = (bf16[528,512]{1,0:T(8,128)(2,1)}, bf16[4,192,1024]{2,1,0:T(8,128)(2,1)}) custom-call(s32[211]{0:T(256)} %concatenate.7.meta, f32[1]{0:T(128)S(6)} %tanh.3.gate, f32[512,512]{1,0:T(8,128)} %get-tuple-element.104.q_own, bf16[512,512]{1,0:T(8,128)(2,1)} %collective-permute-done.20.q_got, bf16[512,512]{1,0:T(8,128)(2,1)} %convolution_convert_fusion.o_own, ...), custom_call_target="tpu_custom_call" | custom-call | flops 1 | bytes 1 | tf_op jit(solution)/shard_map/pallas_call | solution.py:316
  175.4 6.1 %shard_map.167 = (f32[192,1536]{1,0:T(8,128)}, bf16[192,1536]{1,0:T(8,128)(2,1)}, bf16[192,1536]{1,0:T(8,128)(2,1)}, bf16[192,1536]{1,0:T(8,128)(2,1)}) custom-call(bf16[4,192,1024]{2,1,0:T(8,128)(2,1)} %get-tuple-element.127.dkv, bf16[1536,512]{1,0:T(8,128)(2,1)} %bitcast.93, bf16[1536,512]{1,0:T(8,128)(2,1)} %bitcast.96), custom_call_target="tpu_custom_call" | custom-call | flops 1 | bytes 1 | tf_op jit(solution)/shard_map/pallas_call | solution.py:449
  181.5 4.6 %collective-permute-start.30 = (bf16[192,1536]{1,0:T(8,128)(2,1)}, bf16[192,1536]{1,0:T(8,128)(2,1)}, u32[]{:S(2)}, u32[]{:S(2)}) collective-permute-start(bf16[192,1536]{1,0:T(8,128)(2,1)} %get-tuple-element.145), channel_id=1, source_target_pairs={{0,1},{1,0},{2,3},{3,2},{4,5},{5,4},{6,7},{7,6},{8,9},{9,8},{10,11... | collective-permute-start | bytes 1769480 | tf_op jit(solution)/shard_map/ppermute | solution.py:577
  190.3 7.5 %shard_map.168 = bf16[512,2048]{1,0:T(8,128)(2,1)} custom-call(s32[211]{0:T(256)} %concatenate.7.meta, f32[1,512]{1,0:T(1,128)} %bitcast.105, f32[1,2048]{1,0:T(1,128)} %gain.1, bf16[528,512]{1,0:T(8,128)(2,1)} %get-tuple-element.108.refs_0_, bf16[528,512]{1,0:T(8,128)(2,1)} %get-tuple-element.125.refs_1_, bf16[528,512]{1,0:T(8,128)(2,1)} %collective-permute-done.24.refs_2_, ...), custom_call_target="tpu_custom_call" | custom-call | flops 1 | bytes 1 | tf_op jit(solution)/shard_map/pallas_call | solution.py:422
  202.5 7.5 %collective-permute-done.32 = bf16[192,1536]{1,0:T(8,128)(2,1)} collective-permute-done((bf16[192,1536]{1,0:T(8,128)(2,1)}, bf16[192,1536]{1,0:T(8,128)(2,1)}, u32[]{:S(2)}, u32[]{:S(2)}) %collective-permute-start.32) | collective-permute-done | bytes 589856 | tf_op jit(solution)/shard_map/ppermute | solution.py:577
  (110 shorter events, 67.8 us)
Async XLA Ops:
  7.2 132.9 %all-gather.3.cloned.1.call-start = ((), (), s32[]{:S(2)}) async-start(), calls=%async_computation | async-start | bytes 6291456 | tf_op jit(solution)/shard_map/all_gather | solution.py:510
  11.8 16.6 %collective-permute-start = (bf16[128,2048]{1,0:T(8,128)(2,1)}, bf16[128,2048]{1,0:T(8,128)(2,1)S(1)}, u32[]{:S(2)}, u32[]{:S(2)}) collective-permute-start(bf16[128,2048]{1,0:T(8,128)(2,1)} %shard_map.158), channel_id=1, source_target_pairs={{0,4},{2,18},{4,8},{6,22},{8,12},{10,26},{12,0},{14,30},{16,20},{1... | collective-permute-start | bytes 1572872 | tf_op jit(solution)/shard_map/ppermute | solution.py:118
  13.6 126.5 %all-gather.5.cloned.1.call-start = ((), (), s32[]{:S(2)}) async-start(), calls=%async_computation.1 | async-start | bytes 4325376 | tf_op jit(solution)/shard_map/all_gather | solution.py:549
  30.7 16.8 %collective-permute-start.1 = (bf16[2,128,2048]{2,1,0:T(8,128)(2,1)S(1)}, bf16[2,128,2048]{2,1,0:T(8,128)(2,1)}, u32[]{:S(2)}, u32[]{:S(2)}) collective-permute-start(bf16[2,128,2048]{2,1,0:T(8,128)(2,1)S(1)} %pad_maximum_fusion.refs_0_), channel_id=1, source_target_pairs={{0,16},{2,6},{4,20},{6,10},{8,24},{10,14},{12,28},{14,2},{16,32},{... | collective-permute-start | bytes 3145736 | tf_op jit(solution)/shard_map/ppermute | solution.py:118
  36.3 16.7 %collective-permute-start.7 = (bf16[2,128,2048]{2,1,0:T(8,128)(2,1)}, bf16[2,128,2048]{2,1,0:T(8,128)(2,1)}, u32[]{:S(2)}, u32[]{:S(2)}) collective-permute-start(bf16[2,128,2048]{2,1,0:T(8,128)(2,1)} %pad_maximum_fusion.1.refs_1_), channel_id=1, source_target_pairs={{0,48},{2,14},{4,52},{6,2},{8,56},{10,6},{12,60},{14,10},{16,0},{1... | collective-permute-start | bytes 3145736 | tf_op jit(solution)/shard_map/ppermute | solution.py:118
  40.9 19.2 %collective-permute-start.12 = (bf16[2,128,2048]{2,1,0:T(8,128)(2,1)}, bf16[2,128,2048]{2,1,0:T(8,128)(2,1)}, u32[]{:S(2)}, u32[]{:S(2)}) collective-permute-start(bf16[2,128,2048]{2,1,0:T(8,128)(2,1)} %pad_maximum_fusion.1.refs_1_), channel_id=1, source_target_pairs={{0,16},{2,6},{4,20},{6,10},{8,24},{10,14},{12,28},{14,2},{16,32},{... | collective-permute-start | bytes 3145736 | tf_op jit(solution)/shard_map/ppermute | solution.py:118
  47.5 16.6 %collective-permute-start.13 = (bf16[2,128,2048]{2,1,0:T(8,128)(2,1)S(1)}, bf16[2,128,2048]{2,1,0:T(8,128)(2,1)}, u32[]{:S(2)}, u32[]{:S(2)}) collective-permute-start(bf16[2,128,2048]{2,1,0:T(8,128)(2,1)S(1)} %pad_maximum_fusion.refs_0_), channel_id=1, source_target_pairs={{0,48},{2,14},{4,52},{6,2},{8,56},{10,6},{12,60},{14,10},{16,0},{1... | collective-permute-start | bytes 3145736 | tf_op jit(solution)/shard_map/ppermute | solution.py:118
  55.0 16.8 %collective-permute-start.10 = (bf16[2,128,2048]{2,1,0:T(8,128)(2,1)}, bf16[2,128,2048]{2,1,0:T(8,128)(2,1)}, u32[]{:S(2)}, u32[]{:S(2)}) collective-permute-start(bf16[2,128,2048]{2,1,0:T(8,128)(2,1)} %collective-permute-done.1.refs_2_), channel_id=1, source_target_pairs={{0,16},{2,6},{4,20},{6,10},{8,24},{10,14},{12,28},{14,2},{16,32},{... | collective-permute-start | bytes 3145736 | tf_op jit(solution)/shard_map/ppermute | solution.py:118
  56.8 20.0 %collective-permute-start.14 = (bf16[2,128,2048]{2,1,0:T(8,128)(2,1)}, bf16[2,128,2048]{2,1,0:T(8,128)(2,1)}, u32[]{:S(2)}, u32[]{:S(2)}) collective-permute-start(bf16[2,128,2048]{2,1,0:T(8,128)(2,1)} %collective-permute-done.1.refs_2_), channel_id=1, source_target_pairs={{0,2},{2,0},{1,3},{3,1},{4,6},{6,4},{5,7},{7,5},{8,10},{10,8},{9,1... | collective-permute-start | bytes 3145736 | tf_op jit(solution)/shard_map/ppermute | solution.py:122
  56.8 20.0 %collective-permute-start.11 = (bf16[2,128,2048]{2,1,0:T(8,128)(2,1)}, bf16[2,128,2048]{2,1,0:T(8,128)(2,1)}, u32[]{:S(2)}, u32[]{:S(2)}) collective-permute-start(bf16[2,128,2048]{2,1,0:T(8,128)(2,1)} %collective-permute-done.7.refs_7_), channel_id=1, source_target_pairs={{0,48},{2,14},{4,52},{6,2},{8,56},{10,6},{12,60},{14,10},{16,0},{1... | collective-permute-start | bytes 3145736 | tf_op jit(solution)/shard_map/ppermute | solution.py:118
  60.1 16.7 %collective-permute-start.17 = (bf16[2,128,2048]{2,1,0:T(8,128)(2,1)}, bf16[2,128,2048]{2,1,0:T(8,128)(2,1)}, u32[]{:S(2)}, u32[]{:S(2)}) collective-permute-start(bf16[2,128,2048]{2,1,0:T(8,128)(2,1)} %collective-permute-done.7.refs_7_), channel_id=1, source_target_pairs={{0,2},{2,0},{1,3},{3,1},{4,6},{6,4},{5,7},{7,5},{8,10},{10,8},{9,1... | collective-permute-start | bytes 3145736 | tf_op jit(solution)/shard_map/ppermute | solution.py:122
  89.5 16.1 %collective-permute-start.20 = (bf16[512,512]{1,0:T(8,128)(2,1)}, bf16[512,512]{1,0:T(8,128)(2,1)}, u32[]{:S(2)}, u32[]{:S(2)}) collective-permute-start(bf16[512,512]{1,0:T(8,128)(2,1)} %get-tuple-element.105), channel_id=1, source_target_pairs={{0,1},{1,0},{64,65},{65,64},{2,3},{3,2},{66,67},{67,66},{4,5},{5,4... | collective-permute-start | bytes 1572872 | tf_op jit(solution)/shard_map/ppermute | solution.py:552
  90.1 20.4 %collective-permute-start.21 = (bf16[512,512]{1,0:T(8,128)(2,1)}, bf16[512,512]{1,0:T(8,128)(2,1)}, u32[]{:S(2)}, u32[]{:S(2)}) collective-permute-start(bf16[512,512]{1,0:T(8,128)(2,1)} %get-tuple-element.100), channel_id=1, source_target_pairs={{64,65},{65,64},{66,67},{67,66},{68,69},{69,68},{70,71},{71,70},{7... | collective-permute-start | bytes 1572872 | tf_op jit(solution)/shard_map/ppermute | solution.py:553
  116.9 21.8 %collective-permute-start.22 = (bf16[528,512]{1,0:T(8,128)(2,1)}, bf16[528,512]{1,0:T(8,128)(2,1)}, u32[]{:S(2)}, u32[]{:S(2)}) collective-permute-start(bf16[528,512]{1,0:T(8,128)(2,1)} %get-tuple-element.108.refs_0_), channel_id=1, source_target_pairs={{64,0},{65,1},{66,2},{67,3},{68,4},{69,5},{70,6},{71,7},{72,8},{73... | collective-permute-start | bytes 1622024 | tf_op jit(solution)/shard_map/ppermute | solution.py:560
  118.1 21.9 %collective-permute-start.23 = (bf16[528,512]{1,0:T(8,128)(2,1)}, bf16[528,512]{1,0:T(8,128)(2,1)}, u32[]{:S(2)}, u32[]{:S(2)}) collective-permute-start(bf16[528,512]{1,0:T(8,128)(2,1)} %get-tuple-element.108.refs_0_), channel_id=1, source_target_pairs={{64,1},{65,0},{66,3},{67,2},{68,5},{69,4},{70,7},{71,6},{72,9},{73... | collective-permute-start | bytes 1622024 | tf_op jit(solution)/shard_map/ppermute | solution.py:560
  119.4 29.3 %collective-permute-start.24 = (bf16[528,512]{1,0:T(8,128)(2,1)}, bf16[528,512]{1,0:T(8,128)(2,1)}, u32[]{:S(2)}, u32[]{:S(2)}) collective-permute-start(bf16[528,512]{1,0:T(8,128)(2,1)} %get-tuple-element.108.refs_0_), channel_id=1, source_target_pairs={{64,65},{65,64},{66,67},{67,66},{68,69},{69,68},{70,71},{71,70},{7... | collective-permute-start | bytes 1622024 | tf_op jit(solution)/shard_map/ppermute | solution.py:562
  127.1 35.8 %collective-permute-start.26 = (bf16[192,1536]{1,0:T(8,128)(2,1)}, bf16[192,1536]{1,0:T(8,128)(2,1)}, u32[]{:S(2)}, u32[]{:S(2)}) collective-permute-start(bf16[192,1536]{1,0:T(8,128)(2,1)} %get-tuple-element.122), channel_id=1, source_target_pairs={{64,0},{65,1},{66,2},{67,3},{68,4},{69,5},{70,6},{71,7},{72,8},{73... | collective-permute-start | bytes 1769480 | tf_op jit(solution)/shard_map/ppermute | solution.py:564
  128.4 38.0 %collective-permute-start.27 = (bf16[192,1536]{1,0:T(8,128)(2,1)}, bf16[192,1536]{1,0:T(8,128)(2,1)}, u32[]{:S(2)}, u32[]{:S(2)}) collective-permute-start(bf16[192,1536]{1,0:T(8,128)(2,1)} %get-tuple-element.123), channel_id=1, source_target_pairs={{64,1},{65,0},{66,3},{67,2},{68,5},{69,4},{70,7},{71,6},{72,9},{73... | collective-permute-start | bytes 1769480 | tf_op jit(solution)/shard_map/ppermute | solution.py:564
  148.7 17.6 %collective-permute-start.25 = (bf16[512,512]{1,0:T(8,128)(2,1)}, bf16[512,512]{1,0:T(8,128)(2,1)}, u32[]{:S(2)}, u32[]{:S(2)}) collective-permute-start(bf16[512,512]{1,0:T(8,128)(2,1)} %get-tuple-element.121), channel_id=1, source_target_pairs={{0,1},{1,0},{2,3},{3,2},{4,5},{5,4},{6,7},{7,6},{8,9},{9,8},{10,11... | collective-permute-start | bytes 1572872 | tf_op jit(solution)/shard_map/ppermute | solution.py:568
  152.1 29.4 %collective-permute-start.28 = (bf16[192,1536]{1,0:T(8,128)(2,1)}, bf16[192,1536]{1,0:T(8,128)(2,1)}, u32[]{:S(2)}, u32[]{:S(2)}) collective-permute-start(bf16[192,1536]{1,0:T(8,128)(2,1)} %get-tuple-element.133), channel_id=1, source_target_pairs={{64,65},{65,64},{66,67},{67,66},{68,69},{69,68},{70,71},{71,70},{7... | collective-permute-start | bytes 1769480 | tf_op jit(solution)/shard_map/ppermute | solution.py:564
  172.6 17.7 %collective-permute-start.29 = (bf16[528,512]{1,0:T(8,128)(2,1)}, bf16[528,512]{1,0:T(8,128)(2,1)}, u32[]{:S(2)}, u32[]{:S(2)}) collective-permute-start(bf16[528,512]{1,0:T(8,128)(2,1)} %get-tuple-element.125.refs_1_), channel_id=1, source_target_pairs={{0,1},{1,0},{2,3},{3,2},{4,5},{5,4},{6,7},{7,6},{8,9},{9,8},{10,11... | collective-permute-start | bytes 1622024 | tf_op jit(solution)/shard_map/ppermute | solution.py:574
  181.5 21.0 %collective-permute-start.30 = (bf16[192,1536]{1,0:T(8,128)(2,1)}, bf16[192,1536]{1,0:T(8,128)(2,1)}, u32[]{:S(2)}, u32[]{:S(2)}) collective-permute-start(bf16[192,1536]{1,0:T(8,128)(2,1)} %get-tuple-element.145), channel_id=1, source_target_pairs={{0,1},{1,0},{2,3},{3,2},{4,5},{5,4},{6,7},{7,6},{8,9},{9,8},{10,11... | collective-permute-start | bytes 1769480 | tf_op jit(solution)/shard_map/ppermute | solution.py:577
  186.1 16.4 %collective-permute-start.31 = (bf16[192,1536]{1,0:T(8,128)(2,1)}, bf16[192,1536]{1,0:T(8,128)(2,1)}, u32[]{:S(2)}, u32[]{:S(2)}) collective-permute-start(bf16[192,1536]{1,0:T(8,128)(2,1)} %get-tuple-element.146), channel_id=1, source_target_pairs={{0,65},{1,64},{2,67},{3,66},{4,69},{5,68},{6,71},{7,70},{8,73},{9,... | collective-permute-start | bytes 1769480 | tf_op jit(solution)/shard_map/ppermute | solution.py:577
  188.2 21.8 %collective-permute-start.32 = (bf16[192,1536]{1,0:T(8,128)(2,1)}, bf16[192,1536]{1,0:T(8,128)(2,1)}, u32[]{:S(2)}, u32[]{:S(2)}) collective-permute-start(bf16[192,1536]{1,0:T(8,128)(2,1)} %get-tuple-element.147), channel_id=1, source_target_pairs={{0,64},{1,65},{2,66},{3,67},{4,68},{5,69},{6,70},{7,71},{8,72},{9,... | collective-permute-start | bytes 1769480 | tf_op jit(solution)/shard_map/ppermute | solution.py:577
  (24 other events, 368.7 us)
Sparse Core Ops, SparseCore 0:
  13.7 61.3 all-gather.2
  77.3 47.3 all-gather.4

commit v10 on v9

--- a/solution.py
+++ b/solution.py
@@ -559,17 +559,18 @@
     dq1, dkv1 = backward(meta, gate, q_own, q_got, o_own, o_got, kv, probs)
     dqs = [lax.ppermute(dq1, X, LAST_TO_SAME), lax.ppermute(dq1, X, LAST_TO_CROSS)]
     own1, *terms = latent_terms(dkv1, w_key[0], w_value[0])
-    got1 = lax.ppermute(dq1, X, LAST_SWAP)
     moves = (LAST_TO_SAME, LAST_TO_CROSS, LAST_SWAP)
     got = [lax.ppermute(t, X, p) for t, p in zip(terms, moves)]
     dqs, own1 = lax.optimization_barrier((dqs, own1))
     up, o_send = back(meta, rinv1, gain1, dqs, cotangent, h_all, [wq1], wo_got)
-    o_send, got1 = lax.optimization_barrier((o_send, got1))
     o_got = lax.ppermute(o_send, X, FIRST_SWAP)
     o_own = dot(up, wo_own, NT).astype(BF)
+    dq1, o_own = lax.optimization_barrier((dq1, o_own))
+    got1 = lax.ppermute(dq1, X, LAST_SWAP)
     o_got, got[:2] = lax.optimization_barrier((o_got, got[:2]))
 
     dq0, dkv0 = backward(meta, gate, q_own, q_got, o_own, o_got, kv, probs)
+    dkv0, got1 = lax.optimization_barrier((dkv0, got1))
     own0, *terms = latent_terms(dkv0, w_key[0], w_value[0])
     got0 = lax.ppermute(dq0, X, FIRST_SWAP)
     terms, got = lax.optimization_barrier((terms, got))

time: 222 us -> 220 us (level)
  waiting for transfers between devices: 60.4 us -> 56.4 us
  starting transfers between devices: 50 us -> 52.5 us
    ppermute x3, waiting for transfers between devices: 8.47 us -> 0.01 us  [per_device(): got = [lax.ppermute(t, X, p) for t, p in zip(terms, moves)]]
    ppermute x1, waiting for transfers between devices: 0.01 us -> 4.52 us  [per_device(): o_got = lax.ppermute(o_send, X, FIRST_SWAP)]
    ppermute x3, waiting for transfers between devices: 10 us -> 7.38 us  [per_device(): late = [lax.ppermute(t, X, p) for t, p in zip(terms[::-1], moves)]]
  transfers between devices with their start and end apart: 35 -> 35, of which waited for: 15 -> 13; matrix products, arithmetic and copies ran while one was open for 8% -> 8% of each run, Pallas kernels for 30% -> 30%
where the time goes in v10:
time: 220 us; the launch traced here: 218 us
  Pallas kernels  70.4 us (32%)
  waiting for transfers between devices  56.4 us (26%)
  starting transfers between devices  52.5 us (24%)
  between operations  15.1 us (7%)
  other arithmetic  14.2 us (6%)
  local copies, waits for them, and re-layouts  5.25 us (2%)
  matrix products  4.31 us (2%)
    ppermute x9, waiting for transfers between devices, over_dp(): return lax.ppermute(array, DP, yz_perm(stage, k))  23.1 us
    ppermute x9, starting transfers between devices, over_dp(): return lax.ppermute(array, DP, yz_perm(stage, k))  17.7 us
    pallas_call x2, Pallas kernels, project(): pl.pallas_call(functools.partial(project_kernel, part), in_specs=[SMEM] +...  16.3 us
    pallas_call x2, Pallas kernels, back(): pl.pallas_call(functools.partial(back_kernel, wo is not None), in_specs=i...  16.1 us
    pallas_call x2, Pallas kernels, backward(): pl.pallas_call(backward_kernel, grid=(reports,), in_specs=[SMEM, SMEM, to...  12.6 us
    pallas_call x2, Pallas kernels, latent_terms(): pl.pallas_call(term_kernel, grid=(features // tile,), in_specs=[whole(dkv...  12.4 us
    ppermute x3, starting transfers between devices, per_device(): late = [lax.ppermute(t, X, p) for t, p in zip(terms[::-1], moves)]  10.7 us
    ppermute x1, waiting for transfers between devices, per_device(): lax.ppermute(dq1, X, LAST_TO_SAME)  10.3 us
  transfers between devices with their start and end apart: 35, of which 13 were waited for; matrix products, arithmetic and copies ran while one was open for 8% of the time, Pallas kernels for 30%

profile of v10, /device:TPU:0, one launch (start us, length us, event | category | flops | bytes accessed | tf_op | source)
XLA Modules:
  0.0 218.3 jit_solution(17408494477629144370)
XLA Ops:
  7.2 4.5 %shard_map.158 = bf16[128,2048]{1,0:T(8,128)(2,1)} custom-call(s32[4]{0:T(128)} %bitcast.106, bf16[4,64,1536]{2,1,0:T(8,128)(2,1)} %tiles.1, bf16[32,1536]{1,0:T(8,128)(2,1)} %queries.1, bf16[32,2048]{1,0:T(8,128)(2,1)} %bitcast.100, bf16[32,2048]{1,0:T(8,128)(2,1)} %bitcast.101, bf16[1536,512]{1,0:T(8,128)(2,1)} %bitcast.91, bf16[1536,512]{1,0:T(8,128)(2,1)} %bitcast.94), custom_call_target="tpu_custom_call" | custom-call | flops 1 | bytes 1 | tf_op jit(solution)/shard_map/pallas_call | solution.py:102
  36.3 4.0 %collective-permute-start.7 = (bf16[2,128,2048]{2,1,0:T(8,128)(2,1)}, bf16[2,128,2048]{2,1,0:T(8,128)(2,1)}, u32[]{:S(2)}, u32[]{:S(2)}) collective-permute-start(bf16[2,128,2048]{2,1,0:T(8,128)(2,1)} %pad_maximum_fusion.1.refs_1_), channel_id=1, source_target_pairs={{0,48},{2,14},{4,52},{6,2},{8,56},{10,6},{12,60},{14,10},{16,0},{1... | collective-permute-start | bytes 3145736 | tf_op jit(solution)/shard_map/ppermute | solution.py:118
  40.9 6.7 %collective-permute-done.1.refs_2_ = bf16[2,128,2048]{2,1,0:T(8,128)(2,1)} collective-permute-done((bf16[2,128,2048]{2,1,0:T(8,128)(2,1)S(1)}, bf16[2,128,2048]{2,1,0:T(8,128)(2,1)}, u32[]{:S(2)}, u32[]{:S(2)}) %collective-permute-start.1) | collective-permute-done | bytes 1048608 | tf_op jit(solution)/shard_map/ppermute | solution.py:118
  49.5 3.4 %collective-permute-done.7.refs_7_ = bf16[2,128,2048]{2,1,0:T(8,128)(2,1)} collective-permute-done((bf16[2,128,2048]{2,1,0:T(8,128)(2,1)}, bf16[2,128,2048]{2,1,0:T(8,128)(2,1)}, u32[]{:S(2)}, u32[]{:S(2)}) %collective-permute-start.7) | collective-permute-done | bytes 1048608 | tf_op jit(solution)/shard_map/ppermute | solution.py:118
  56.8 3.3 %collective-permute-start.11 = (bf16[2,128,2048]{2,1,0:T(8,128)(2,1)}, bf16[2,128,2048]{2,1,0:T(8,128)(2,1)}, u32[]{:S(2)}, u32[]{:S(2)}) collective-permute-start(bf16[2,128,2048]{2,1,0:T(8,128)(2,1)} %collective-permute-done.7.refs_7_), channel_id=1, source_target_pairs={{0,48},{2,14},{4,52},{6,2},{8,56},{10,6},{12,60},{14,10},{16,0},{1... | collective-permute-start | bytes 3145736 | tf_op jit(solution)/shard_map/ppermute | solution.py:118
  60.1 4.0 %collective-permute-done.13.refs_6_ = bf16[2,128,2048]{2,1,0:T(8,128)(2,1)} collective-permute-done((bf16[2,128,2048]{2,1,0:T(8,128)(2,1)S(1)}, bf16[2,128,2048]{2,1,0:T(8,128)(2,1)}, u32[]{:S(2)}, u32[]{:S(2)}) %collective-permute-start.13) | collective-permute-done | bytes 1048608 | tf_op jit(solution)/shard_map/ppermute | solution.py:118
  64.1 7.6 %collective-permute-done.10.refs_4_ = bf16[2,128,2048]{2,1,0:T(8,128)(2,1)} collective-permute-done((bf16[2,128,2048]{2,1,0:T(8,128)(2,1)}, bf16[2,128,2048]{2,1,0:T(8,128)(2,1)}, u32[]{:S(2)}, u32[]{:S(2)}) %collective-permute-start.10) | collective-permute-done | bytes 1048608 | tf_op jit(solution)/shard_map/ppermute | solution.py:118
  81.5 8.0 %shard_map.159 = (bf16[512,512]{1,0:T(8,128)(2,1)}, bf16[512,512]{1,0:T(8,128)(2,1)}, bf16[512,2048]{1,0:T(8,128)(2,1)}, bf16[512,2048]{1,0:T(8,128)(2,1)}) custom-call(s32[211]{0:T(256)} %concatenate.7.meta, bf16[512,2048]{1,0:T(8,128)(2,1)} %fusion.2.normed, bf16[512,2048]{1,0:T(8,128)(2,1)} %broadcast_select_fusion.upstream, ...), custom_call_target="tpu_custom_call" | custom-call | flops 1 | bytes 1 | tf_op jit(solution)/shard_map/pallas_call | solution.py:182
  92.3 3.7 %shard_map.160.kv.keys.vals = bf16[768,1024]{1,0:T(8,128)(2,1)} custom-call(s32[211]{0:T(256)} %concatenate.7.meta, bf16[2,128,2048]{2,1,0:T(8,128)(2,1)} %copy-done.1, bf16[2,128,2048]{2,1,0:T(8,128)(2,1)} %pad_maximum_fusion.1.refs_1_, bf16[2,128,2048]{2,1,0:T(8,128)(2,1)} %collective-permute-done.1.refs_2_, ...), custom_call_target="tpu_custom_call" | custom-call | flops 1 | bytes 1 | tf_op jit(solution)/shard_map/pallas_call | solution.py:227
  96.0 8.3 %shard_map.161 = (f32[512,512]{1,0:T(8,128)}, bf16[512,512]{1,0:T(8,128)(2,1)}, bf16[512,2048]{1,0:T(8,128)(2,1)}, bf16[512,2048]{1,0:T(8,128)(2,1)}) custom-call(s32[211]{0:T(256)} %concatenate.7.meta, bf16[512,2048]{1,0:T(8,128)(2,1)} %fusion.2.normed, bf16[512,2048]{1,0:T(8,128)(2,1)} %broadcast_select_fusion.upstream, bf16[2,128,2048]{2,1,0:T(8,128)(2,1)} %copy-done.1, ...), custom_call_target="tpu_custom_call" | custom-call | flops 1 | bytes 1 | tf_op jit(solution)/shard_map/pallas_call | solution.py:182
  105.7 4.9 %shard_map.162.probs = f32[4,512,192]{2,1,0:T(8,128)} custom-call(s32[211]{0:T(256)} %concatenate.7.meta, f32[512,512]{1,0:T(8,128)} %get-tuple-element.106.q_own, bf16[512,512]{1,0:T(8,128)(2,1)} %collective-permute-done.20.q_got, bf16[768,1024]{1,0:T(8,128)(2,1)} %shard_map.160.kv.keys.vals), custom_call_target="tpu_custom_call" | custom-call | flops 1 | bytes 1 | tf_op jit(solution)/shard_map/pallas_call | solution.py:266
  110.5 6.3 %shard_map.163 = (bf16[528,512]{1,0:T(8,128)(2,1)}, bf16[4,192,1024]{2,1,0:T(8,128)(2,1)}) custom-call(s32[211]{0:T(256)} %concatenate.7.meta, f32[1]{0:T(128)S(6)} %tanh.3.gate, f32[512,512]{1,0:T(8,128)} %get-tuple-element.106.q_own, bf16[512,512]{1,0:T(8,128)(2,1)} %collective-permute-done.20.q_got, bf16[512,512]{1,0:T(8,128)(2,1)} %get-tuple-element.108.o_own, ...), custom_call_target="tpu_custom_call" | custom-call | flops 1 | bytes 1 | tf_op jit(solution)/shard_map/pallas_call | solution.py:316
  119.4 6.3 %shard_map.164 = (f32[192,1536]{1,0:T(8,128)}, bf16[192,1536]{1,0:T(8,128)(2,1)}, bf16[192,1536]{1,0:T(8,128)(2,1)}, bf16[192,1536]{1,0:T(8,128)(2,1)}) custom-call(bf16[4,192,1024]{2,1,0:T(8,128)(2,1)} %get-tuple-element.113.dkv, bf16[1536,512]{1,0:T(8,128)(2,1)} %bitcast.92, bf16[1536,512]{1,0:T(8,128)(2,1)} %bitcast.95), custom_call_target="tpu_custom_call" | custom-call | flops 1 | bytes 1 | tf_op jit(solution)/shard_map/pallas_call | solution.py:449
  128.3 10.3 %collective-permute-done.22.refs_0_ = bf16[528,512]{1,0:T(8,128)(2,1)} collective-permute-done((bf16[528,512]{1,0:T(8,128)(2,1)}, bf16[528,512]{1,0:T(8,128)(2,1)}, u32[]{:S(2)}, u32[]{:S(2)}) %collective-permute-start.22) | collective-permute-done | bytes 540704 | tf_op jit(solution)/shard_map/ppermute | solution.py:560
  141.3 8.6 %shard_map.165 = (bf16[512,2048]{1,0:T(8,128)(2,1)}, bf16[512,512]{1,0:T(8,128)(2,1)}) custom-call(s32[211]{0:T(256)} %concatenate.7.meta, f32[1,512]{1,0:T(1,128)} %slice.8.rinv, f32[1,2048]{1,0:T(1,128)} %slice.9.gain, bf16[528,512]{1,0:T(8,128)(2,1)} %collective-permute-done.22.refs_0_, bf16[528,512]{1,0:T(8,128)(2,1)} %collective-permute-done.23.refs_1_, ...), custom_call_target="tpu_custom_call" | custom-call | flops 1 | bytes 1 | tf_op jit(solution)/shard_map/pallas_call | solution.py:422
  149.9 3.4 %collective-permute-start.24 = (bf16[512,512]{1,0:T(8,128)(2,1)}, bf16[512,512]{1,0:T(8,128)(2,1)}, u32[]{:S(2)}, u32[]{:S(2)}) collective-permute-start(bf16[512,512]{1,0:T(8,128)(2,1)} %get-tuple-element.124), channel_id=1, source_target_pairs={{0,1},{1,0},{2,3},{3,2},{4,5},{5,4},{6,7},{7,6},{8,9},{9,8},{10,11... | collective-permute-start | bytes 1572872 | tf_op jit(solution)/shard_map/ppermute | solution.py:566
  154.9 4.3 %convolution_convert_fusion.o_own = bf16[512,512]{1,0:T(8,128)(2,1)} fusion(bf16[512,2048]{1,0:T(8,128)(2,1)} %get-tuple-element.120.refs_4_, bf16[512,2048]{1,0:T(8,128)(2,1)} %get-tuple-element.121), kind=kOutput, calls=%fused_computation.6 | convolution fusion | flops 1074003968 | bytes 4718592 | tf_op jit(solution)/shard_map/dot_general | solution.py:51
  160.7 4.5 %collective-permute-done.24.o_got = bf16[512,512]{1,0:T(8,128)(2,1)} collective-permute-done((bf16[512,512]{1,0:T(8,128)(2,1)}, bf16[512,512]{1,0:T(8,128)(2,1)}, u32[]{:S(2)}, u32[]{:S(2)}) %collective-permute-start.24) | collective-permute-done | bytes 524320 | tf_op jit(solution)/shard_map/ppermute | solution.py:566
  165.2 6.3 %shard_map.166 = (bf16[528,512]{1,0:T(8,128)(2,1)}, bf16[4,192,1024]{2,1,0:T(8,128)(2,1)}) custom-call(s32[211]{0:T(256)} %concatenate.7.meta, f32[1]{0:T(128)S(6)} %tanh.3.gate, f32[512,512]{1,0:T(8,128)} %get-tuple-element.106.q_own, bf16[512,512]{1,0:T(8,128)(2,1)} %collective-permute-done.20.q_got, bf16[512,512]{1,0:T(8,128)(2,1)} %convolution_convert_fusion.o_own, ...), custom_call_target="tpu_custom_call" | custom-call | flops 1 | bytes 1 | tf_op jit(solution)/shard_map/pallas_call | solution.py:316
  174.8 6.1 %shard_map.167 = (f32[192,1536]{1,0:T(8,128)}, bf16[192,1536]{1,0:T(8,128)(2,1)}, bf16[192,1536]{1,0:T(8,128)(2,1)}, bf16[192,1536]{1,0:T(8,128)(2,1)}) custom-call(bf16[4,192,1024]{2,1,0:T(8,128)(2,1)} %get-tuple-element.131.dkv, bf16[1536,512]{1,0:T(8,128)(2,1)} %bitcast.93, bf16[1536,512]{1,0:T(8,128)(2,1)} %bitcast.96), custom_call_target="tpu_custom_call" | custom-call | flops 1 | bytes 1 | tf_op jit(solution)/shard_map/pallas_call | solution.py:449
  180.9 4.0 %collective-permute-start.30 = (bf16[192,1536]{1,0:T(8,128)(2,1)}, bf16[192,1536]{1,0:T(8,128)(2,1)}, u32[]{:S(2)}, u32[]{:S(2)}) collective-permute-start(bf16[192,1536]{1,0:T(8,128)(2,1)} %get-tuple-element.149), channel_id=1, source_target_pairs={{0,1},{1,0},{2,3},{3,2},{4,5},{5,4},{6,7},{7,6},{8,9},{9,8},{10,11... | collective-permute-start | bytes 1769480 | tf_op jit(solution)/shard_map/ppermute | solution.py:578
  184.9 4.6 %collective-permute-start.31 = (bf16[192,1536]{1,0:T(8,128)(2,1)}, bf16[192,1536]{1,0:T(8,128)(2,1)}, u32[]{:S(2)}, u32[]{:S(2)}) collective-permute-start(bf16[192,1536]{1,0:T(8,128)(2,1)} %get-tuple-element.150), channel_id=1, source_target_pairs={{0,65},{1,64},{2,67},{3,66},{4,69},{5,68},{6,71},{7,70},{8,73},{9,... | collective-permute-start | bytes 1769480 | tf_op jit(solution)/shard_map/ppermute | solution.py:578
  191.6 7.5 %shard_map.168 = bf16[512,2048]{1,0:T(8,128)(2,1)} custom-call(s32[211]{0:T(256)} %concatenate.7.meta, f32[1,512]{1,0:T(1,128)} %bitcast.105, f32[1,2048]{1,0:T(1,128)} %gain.1, bf16[528,512]{1,0:T(8,128)(2,1)} %get-tuple-element.122.refs_0_, bf16[528,512]{1,0:T(8,128)(2,1)} %get-tuple-element.128.refs_1_, bf16[528,512]{1,0:T(8,128)(2,1)} %collective-permute-done.27.refs_2_, ...), custom_call_target="tpu_custom_call" | custom-call | flops 1 | bytes 1 | tf_op jit(solution)/shard_map/pallas_call | solution.py:422
  201.3 7.4 %collective-permute-done.32 = bf16[192,1536]{1,0:T(8,128)(2,1)} collective-permute-done((bf16[192,1536]{1,0:T(8,128)(2,1)}, bf16[192,1536]{1,0:T(8,128)(2,1)}, u32[]{:S(2)}, u32[]{:S(2)}) %collective-permute-start.32) | collective-permute-done | bytes 589856 | tf_op jit(solution)/shard_map/ppermute | solution.py:578
  (110 shorter events, 65.0 us)
Async XLA Ops:
  7.2 134.1 %all-gather.3.cloned.1.call-start = ((), (), s32[]{:S(2)}) async-start(), calls=%async_computation | async-start | bytes 6291456 | tf_op jit(solution)/shard_map/all_gather | solution.py:510
  11.8 16.6 %collective-permute-start = (bf16[128,2048]{1,0:T(8,128)(2,1)}, bf16[128,2048]{1,0:T(8,128)(2,1)S(1)}, u32[]{:S(2)}, u32[]{:S(2)}) collective-permute-start(bf16[128,2048]{1,0:T(8,128)(2,1)} %shard_map.158), channel_id=1, source_target_pairs={{0,4},{2,18},{4,8},{6,22},{8,12},{10,26},{12,0},{14,30},{16,20},{1... | collective-permute-start | bytes 1572872 | tf_op jit(solution)/shard_map/ppermute | solution.py:118
  13.6 127.8 %all-gather.5.cloned.1.call-start = ((), (), s32[]{:S(2)}) async-start(), calls=%async_computation.1 | async-start | bytes 4325376 | tf_op jit(solution)/shard_map/all_gather | solution.py:549
  17.2 15.5 %collective-permute-start.2 = (bf16[128,2048]{1,0:T(8,128)(2,1)}, bf16[128,2048]{1,0:T(8,128)(2,1)}, u32[]{:S(2)}, u32[]{:S(2)}) collective-permute-start(bf16[128,2048]{1,0:T(8,128)(2,1)} %shard_map.158), channel_id=1, source_target_pairs={{0,8},{2,34},{4,12},{6,38},{8,0},{10,42},{12,4},{14,46},{16,24},{1... | collective-permute-start | bytes 1572872 | tf_op jit(solution)/shard_map/ppermute | solution.py:118
  30.7 16.8 %collective-permute-start.1 = (bf16[2,128,2048]{2,1,0:T(8,128)(2,1)S(1)}, bf16[2,128,2048]{2,1,0:T(8,128)(2,1)}, u32[]{:S(2)}, u32[]{:S(2)}) collective-permute-start(bf16[2,128,2048]{2,1,0:T(8,128)(2,1)S(1)} %pad_maximum_fusion.refs_0_), channel_id=1, source_target_pairs={{0,16},{2,6},{4,20},{6,10},{8,24},{10,14},{12,28},{14,2},{16,32},{... | collective-permute-start | bytes 3145736 | tf_op jit(solution)/shard_map/ppermute | solution.py:118
  36.3 16.7 %collective-permute-start.7 = (bf16[2,128,2048]{2,1,0:T(8,128)(2,1)}, bf16[2,128,2048]{2,1,0:T(8,128)(2,1)}, u32[]{:S(2)}, u32[]{:S(2)}) collective-permute-start(bf16[2,128,2048]{2,1,0:T(8,128)(2,1)} %pad_maximum_fusion.1.refs_1_), channel_id=1, source_target_pairs={{0,48},{2,14},{4,52},{6,2},{8,56},{10,6},{12,60},{14,10},{16,0},{1... | collective-permute-start | bytes 3145736 | tf_op jit(solution)/shard_map/ppermute | solution.py:118
  40.9 19.2 %collective-permute-start.12 = (bf16[2,128,2048]{2,1,0:T(8,128)(2,1)}, bf16[2,128,2048]{2,1,0:T(8,128)(2,1)}, u32[]{:S(2)}, u32[]{:S(2)}) collective-permute-start(bf16[2,128,2048]{2,1,0:T(8,128)(2,1)} %pad_maximum_fusion.1.refs_1_), channel_id=1, source_target_pairs={{0,16},{2,6},{4,20},{6,10},{8,24},{10,14},{12,28},{14,2},{16,32},{... | collective-permute-start | bytes 3145736 | tf_op jit(solution)/shard_map/ppermute | solution.py:118
  47.5 16.6 %collective-permute-start.13 = (bf16[2,128,2048]{2,1,0:T(8,128)(2,1)S(1)}, bf16[2,128,2048]{2,1,0:T(8,128)(2,1)}, u32[]{:S(2)}, u32[]{:S(2)}) collective-permute-start(bf16[2,128,2048]{2,1,0:T(8,128)(2,1)S(1)} %pad_maximum_fusion.refs_0_), channel_id=1, source_target_pairs={{0,48},{2,14},{4,52},{6,2},{8,56},{10,6},{12,60},{14,10},{16,0},{1... | collective-permute-start | bytes 3145736 | tf_op jit(solution)/shard_map/ppermute | solution.py:118
  55.0 16.8 %collective-permute-start.10 = (bf16[2,128,2048]{2,1,0:T(8,128)(2,1)}, bf16[2,128,2048]{2,1,0:T(8,128)(2,1)}, u32[]{:S(2)}, u32[]{:S(2)}) collective-permute-start(bf16[2,128,2048]{2,1,0:T(8,128)(2,1)} %collective-permute-done.1.refs_2_), channel_id=1, source_target_pairs={{0,16},{2,6},{4,20},{6,10},{8,24},{10,14},{12,28},{14,2},{16,32},{... | collective-permute-start | bytes 3145736 | tf_op jit(solution)/shard_map/ppermute | solution.py:118
  56.8 20.0 %collective-permute-start.14 = (bf16[2,128,2048]{2,1,0:T(8,128)(2,1)}, bf16[2,128,2048]{2,1,0:T(8,128)(2,1)}, u32[]{:S(2)}, u32[]{:S(2)}) collective-permute-start(bf16[2,128,2048]{2,1,0:T(8,128)(2,1)} %collective-permute-done.1.refs_2_), channel_id=1, source_target_pairs={{0,2},{2,0},{1,3},{3,1},{4,6},{6,4},{5,7},{7,5},{8,10},{10,8},{9,1... | collective-permute-start | bytes 3145736 | tf_op jit(solution)/shard_map/ppermute | solution.py:122
  56.8 20.0 %collective-permute-start.11 = (bf16[2,128,2048]{2,1,0:T(8,128)(2,1)}, bf16[2,128,2048]{2,1,0:T(8,128)(2,1)}, u32[]{:S(2)}, u32[]{:S(2)}) collective-permute-start(bf16[2,128,2048]{2,1,0:T(8,128)(2,1)} %collective-permute-done.7.refs_7_), channel_id=1, source_target_pairs={{0,48},{2,14},{4,52},{6,2},{8,56},{10,6},{12,60},{14,10},{16,0},{1... | collective-permute-start | bytes 3145736 | tf_op jit(solution)/shard_map/ppermute | solution.py:118
  60.1 16.7 %collective-permute-start.17 = (bf16[2,128,2048]{2,1,0:T(8,128)(2,1)}, bf16[2,128,2048]{2,1,0:T(8,128)(2,1)}, u32[]{:S(2)}, u32[]{:S(2)}) collective-permute-start(bf16[2,128,2048]{2,1,0:T(8,128)(2,1)} %collective-permute-done.7.refs_7_), channel_id=1, source_target_pairs={{0,2},{2,0},{1,3},{3,1},{4,6},{6,4},{5,7},{7,5},{8,10},{10,8},{9,1... | collective-permute-start | bytes 3145736 | tf_op jit(solution)/shard_map/ppermute | solution.py:122
  89.5 16.1 %collective-permute-start.20 = (bf16[512,512]{1,0:T(8,128)(2,1)}, bf16[512,512]{1,0:T(8,128)(2,1)}, u32[]{:S(2)}, u32[]{:S(2)}) collective-permute-start(bf16[512,512]{1,0:T(8,128)(2,1)} %get-tuple-element.107), channel_id=1, source_target_pairs={{0,1},{1,0},{64,65},{65,64},{2,3},{3,2},{66,67},{67,66},{4,5},{5,4... | collective-permute-start | bytes 1572872 | tf_op jit(solution)/shard_map/ppermute | solution.py:552
  90.1 20.4 %collective-permute-start.21 = (bf16[512,512]{1,0:T(8,128)(2,1)}, bf16[512,512]{1,0:T(8,128)(2,1)}, u32[]{:S(2)}, u32[]{:S(2)}) collective-permute-start(bf16[512,512]{1,0:T(8,128)(2,1)} %get-tuple-element.102), channel_id=1, source_target_pairs={{64,65},{65,64},{66,67},{67,66},{68,69},{69,68},{70,71},{71,70},{7... | collective-permute-start | bytes 1572872 | tf_op jit(solution)/shard_map/ppermute | solution.py:553
  116.9 21.8 %collective-permute-start.22 = (bf16[528,512]{1,0:T(8,128)(2,1)}, bf16[528,512]{1,0:T(8,128)(2,1)}, u32[]{:S(2)}, u32[]{:S(2)}) collective-permute-start(bf16[528,512]{1,0:T(8,128)(2,1)} %get-tuple-element.122.refs_0_), channel_id=1, source_target_pairs={{64,0},{65,1},{66,2},{67,3},{68,4},{69,5},{70,6},{71,7},{72,8},{73... | collective-permute-start | bytes 1622024 | tf_op jit(solution)/shard_map/ppermute | solution.py:560
  118.1 23.2 %collective-permute-start.23 = (bf16[528,512]{1,0:T(8,128)(2,1)}, bf16[528,512]{1,0:T(8,128)(2,1)}, u32[]{:S(2)}, u32[]{:S(2)}) collective-permute-start(bf16[528,512]{1,0:T(8,128)(2,1)} %get-tuple-element.122.refs_0_), channel_id=1, source_target_pairs={{64,1},{65,0},{66,3},{67,2},{68,5},{69,4},{70,7},{71,6},{72,9},{73... | collective-permute-start | bytes 1622024 | tf_op jit(solution)/shard_map/ppermute | solution.py:560
  125.7 35.0 %collective-permute-start.25 = (bf16[192,1536]{1,0:T(8,128)(2,1)}, bf16[192,1536]{1,0:T(8,128)(2,1)}, u32[]{:S(2)}, u32[]{:S(2)}) collective-permute-start(bf16[192,1536]{1,0:T(8,128)(2,1)} %get-tuple-element.125), channel_id=1, source_target_pairs={{64,0},{65,1},{66,2},{67,3},{68,4},{69,5},{70,6},{71,7},{72,8},{73... | collective-permute-start | bytes 1769480 | tf_op jit(solution)/shard_map/ppermute | solution.py:563
  127.0 33.7 %collective-permute-start.26 = (bf16[192,1536]{1,0:T(8,128)(2,1)}, bf16[192,1536]{1,0:T(8,128)(2,1)}, u32[]{:S(2)}, u32[]{:S(2)}) collective-permute-start(bf16[192,1536]{1,0:T(8,128)(2,1)} %get-tuple-element.126), channel_id=1, source_target_pairs={{64,1},{65,0},{66,3},{67,2},{68,5},{69,4},{70,7},{71,6},{72,9},{73... | collective-permute-start | bytes 1769480 | tf_op jit(solution)/shard_map/ppermute | solution.py:563
  153.4 27.5 %collective-permute-start.28 = (bf16[192,1536]{1,0:T(8,128)(2,1)}, bf16[192,1536]{1,0:T(8,128)(2,1)}, u32[]{:S(2)}, u32[]{:S(2)}) collective-permute-start(bf16[192,1536]{1,0:T(8,128)(2,1)} %get-tuple-element.137), channel_id=1, source_target_pairs={{64,65},{65,64},{66,67},{67,66},{68,69},{69,68},{70,71},{71,70},{7... | collective-permute-start | bytes 1769480 | tf_op jit(solution)/shard_map/ppermute | solution.py:563
  159.2 15.6 %collective-permute-start.27 = (bf16[528,512]{1,0:T(8,128)(2,1)}, bf16[528,512]{1,0:T(8,128)(2,1)}, u32[]{:S(2)}, u32[]{:S(2)}) collective-permute-start(bf16[528,512]{1,0:T(8,128)(2,1)} %get-tuple-element.122.refs_0_), channel_id=1, source_target_pairs={{64,65},{65,64},{66,67},{67,66},{68,69},{69,68},{70,71},{71,70},{7... | collective-permute-start | bytes 1622024 | tf_op jit(solution)/shard_map/ppermute | solution.py:569
  171.5 20.2 %collective-permute-start.29 = (bf16[528,512]{1,0:T(8,128)(2,1)}, bf16[528,512]{1,0:T(8,128)(2,1)}, u32[]{:S(2)}, u32[]{:S(2)}) collective-permute-start(bf16[528,512]{1,0:T(8,128)(2,1)} %get-tuple-element.128.refs_1_), channel_id=1, source_target_pairs={{0,1},{1,0},{2,3},{3,2},{4,5},{5,4},{6,7},{7,6},{8,9},{9,8},{10,11... | collective-permute-start | bytes 1622024 | tf_op jit(solution)/shard_map/ppermute | solution.py:575
  180.9 20.4 %collective-permute-start.30 = (bf16[192,1536]{1,0:T(8,128)(2,1)}, bf16[192,1536]{1,0:T(8,128)(2,1)}, u32[]{:S(2)}, u32[]{:S(2)}) collective-permute-start(bf16[192,1536]{1,0:T(8,128)(2,1)} %get-tuple-element.149), channel_id=1, source_target_pairs={{0,1},{1,0},{2,3},{3,2},{4,5},{5,4},{6,7},{7,6},{8,9},{9,8},{10,11... | collective-permute-start | bytes 1769480 | tf_op jit(solution)/shard_map/ppermute | solution.py:578
  184.9 16.4 %collective-permute-start.31 = (bf16[192,1536]{1,0:T(8,128)(2,1)}, bf16[192,1536]{1,0:T(8,128)(2,1)}, u32[]{:S(2)}, u32[]{:S(2)}) collective-permute-start(bf16[192,1536]{1,0:T(8,128)(2,1)} %get-tuple-element.150), channel_id=1, source_target_pairs={{0,65},{1,64},{2,67},{3,66},{4,69},{5,68},{6,71},{7,70},{8,73},{9,... | collective-permute-start | bytes 1769480 | tf_op jit(solution)/shard_map/ppermute | solution.py:578
  189.5 19.2 %collective-permute-start.32 = (bf16[192,1536]{1,0:T(8,128)(2,1)}, bf16[192,1536]{1,0:T(8,128)(2,1)}, u32[]{:S(2)}, u32[]{:S(2)}) collective-permute-start(bf16[192,1536]{1,0:T(8,128)(2,1)} %get-tuple-element.151), channel_id=1, source_target_pairs={{0,64},{1,65},{2,66},{3,67},{4,68},{5,69},{6,70},{7,71},{8,72},{9,... | collective-permute-start | bytes 1769480 | tf_op jit(solution)/shard_map/ppermute | solution.py:578
  (24 other events, 368.5 us)
Sparse Core Ops, SparseCore 0:
  13.7 61.3 all-gather.2
  77.3 47.3 all-gather.4
